TPU v7x, 128 devices: a whole 4x4x4 slice. The times are simulated.
128 devices in a mesh: exp: 32 (over x, z, core), ws: 4 (over y).
Axes of the slice: x: 4, y: 4, z: 4, core: 2. Of those that a mesh axis runs over, the one named last changes fastest.
Arguments:
- tokens: bfloat16 [16384, 1536], P(('exp', 'ws')), may hold values from -6 to 6
- cotangent: bfloat16 [16384, 1536], P(('exp', 'ws')), may hold values from -6 to 6
- seg_lengths: int32 [32, 13], P('exp'), may hold values from 1 to 256, 512 in all within a row
- parents: int32 [32, 13], P('exp'), may hold values from 0 to 11, as said below
- routes: int32 [16384, 8], P(('exp', 'ws')), may hold values from 0 to 31, all different within a row; in each aligned block of 128 rows (0 to 127, 128 to 255, ...) at most 48 rows name the same one
- norm_attn: bfloat16 [1536], P('ws'), may hold values from 0.5 to 1.5
- w_query: bfloat16 [1536, 1536], P('ws'), may hold values from -0.15625 to 0.15625
- w_key: bfloat16 [1536, 512], P('ws'), may hold values from -0.15625 to 0.15625
- w_value: bfloat16 [1536, 512], P('ws'), may hold values from -0.15625 to 0.15625
- w_out: bfloat16 [1536, 1536], P('ws'), may hold values from -1.25 to 1.25
- norm_moe: bfloat16 [1536], P('ws'), may hold values from 0.5 to 1.5
- w_router: bfloat16 [1536, 32], P('ws'), may hold values from -0.078125 to 0.078125
- w_gate: bfloat16 [32, 1536, 512], P('exp', None, 'ws'), may hold values from -0.15625 to 0.15625
- w_up: bfloat16 [32, 1536, 512], P('exp', None, 'ws'), may hold values from -0.15625 to 0.15625
- w_down: bfloat16 [32, 512, 1536], P('exp', 'ws'), may hold values from -1 to 1
Outputs:
- layer_out: bfloat16 [16384, 1536], P(('exp', 'ws'))
- grad_tokens: float32 [16384, 1536], P(('exp', 'ws'))
- grad_norm_attn: float32 [1536], P('ws')
- grad_w_query: float32 [1536, 1536], P('ws')
- grad_w_key: float32 [1536, 512], P('ws')
- grad_w_value: float32 [1536, 512], P('ws')
- grad_w_out: float32 [1536, 1536], P('ws')
- grad_norm_moe: float32 [1536], P('ws')
- grad_w_router: float32 [1536, 32], P('ws')
- grad_w_gate: float32 [32, 1536, 512], P('exp', None, 'ws')
- grad_w_up: float32 [32, 1536, 512], P('exp', None, 'ws')
- grad_w_down: float32 [32, 512, 1536], P('exp', 'ws')
Inputs may be any that keep to these rules, and one draw needn't show every extreme that they name: parents[t, 0] is 0; for every other segment s, parents[t, s] is a segment before s; the parent of the last segment is segment 13 - 2. `seg_lengths`: each tree's lengths sum to 512, and the longest is 256. `routes`: each row names 8 different experts; among the 128 rows of one device no expert is named more than 48 times, and on some device one expert is named exactly 48 times.
All inputs are finite; a program needn't handle non-finite values.
Results may differ from a plain program's by a relative error of at most 0.025.
Values may be sent and summed in bfloat16 or wider, within the bound.
No kernel may reach another device: no remote copies, remote signals or barrier semaphores. Data moves between devices by JAX's collectives and lax.ppermute only.
A program may use at most 192 MiB of HBM per device.

v0:
```python
import jax
import jax.numpy as jnp
from jax import lax
from jax.sharding import PartitionSpec as P

HEADS = 24
KV_HEADS = 8
HEAD = 64


EPS = 1e-06
THETA = 10000.0
MASKED = -1e30


def tree_layout(lengths, parents, tree_size):
    seg_count = lengths.shape[0]
    labels = jnp.arange(seg_count, dtype=jnp.int32)
    segment_end = jnp.cumsum(lengths, dtype=jnp.int32)
    starts = segment_end - lengths
    token_index = jnp.arange(tree_size, dtype=jnp.int32)
    segment = jnp.sum(
        (token_index[:, None] >= segment_end[None, :]).astype(jnp.int32), axis=1, dtype=jnp.int32
    )
    current = labels
    ancestry = (current[:, None] == labels[None, :]).astype(jnp.int32)
    for repeat in range(seg_count - 1):
        current = jnp.sum(
            jnp.where(current[:, None] == labels[None, :], parents[None, :], 0),
            axis=1,
            dtype=jnp.int32,
        )
        ancestry = jnp.maximum(ancestry, (current[:, None] == labels[None, :]).astype(jnp.int32))
    above_count = jnp.sum(ancestry * lengths[None, :], axis=1, dtype=jnp.int32) - lengths
    members = (segment[:, None] == labels[None, :]).astype(jnp.int32)
    position = (
        jnp.sum(members * (above_count - starts)[None, :], axis=1, dtype=jnp.int32) + token_index
    )
    reaches = jnp.dot(members, ancestry)
    return (members, reaches, position)


def angles_for(position, head_size):
    middle = head_size // 2
    inverse = THETA ** (-jnp.arange(middle, dtype=jnp.float32) * 2.0 / head_size)
    angles = position.astype(jnp.float32)[:, None] * inverse[None, :]
    return (jnp.cos(angles), jnp.sin(angles))


def turn_forward(vectors, cosines, sines):
    middle = vectors.shape[-1] // 2
    first_half = vectors[..., :middle]
    second_half = vectors[..., middle:]
    cosines = cosines[:, None, :]
    sines = sines[:, None, :]
    return jnp.concatenate(
        [first_half * cosines - second_half * sines, second_half * cosines + first_half * sines],
        axis=-1,
    )


def turn_back(slopes, cosines, sines):
    middle = slopes.shape[-1] // 2
    first_half = slopes[..., :middle]
    second_half = slopes[..., middle:]
    cosines = cosines[:, None, :]
    sines = sines[:, None, :]
    return jnp.concatenate(
        [first_half * cosines + second_half * sines, second_half * cosines - first_half * sines],
        axis=-1,
    )


def contract_last(left, right, precision=None):
    return lax.dot_general(
        left,
        right,
        (((1,), (1,)), ((), ())),
        precision=precision,
        preferred_element_type=jnp.float32,
    )


def contract_first(left, right, precision=None):
    return lax.dot_general(
        left,
        right,
        (((0,), (0,)), ((), ())),
        precision=precision,
        preferred_element_type=jnp.float32,
    )


def norm_back(resid, scale, gain, slope):
    gain_slope = jnp.sum(slope * resid * scale, axis=0)
    inner = jnp.mean(gain * slope * resid, axis=-1, keepdims=True)
    return (scale * gain * slope - resid * scale * scale * scale * inner, gain_slope)


def shards(
    tokens,
    cotangent,
    seg_lengths,
    parents,
    routes,
    norm_attn,
    w_query,
    w_key,
    w_value,
    w_out,
    norm_moe,
    w_router,
    w_gate,
    w_up,
    w_down,
):
    owner_count = lax.axis_size("exp")
    shard_count = lax.axis_size("ws")
    shard_index = lax.axis_index("ws")
    rows_here, model_width = tokens.shape
    top_count = routes.shape[1]
    local_experts = w_gate.shape[0]
    expert_count = local_experts * owner_count
    capacity = min(rows_here, 3 * rows_here * top_count // (2 * expert_count))
    (
        query_full,
        key_full,
        value_full,
        out_full,
        router_full,
        gain_attn,
        gain_moe,
        gate_full,
        up_full,
        down_full,
    ) = (
        lax.all_gather(w_query, "ws", axis=0, tiled=True),
        lax.all_gather(w_key, "ws", axis=0, tiled=True),
        lax.all_gather(w_value, "ws", axis=0, tiled=True),
        lax.all_gather(w_out, "ws", axis=0, tiled=True),
        lax.all_gather(w_router, "ws", axis=0, tiled=True),
        lax.all_gather(norm_attn, "ws", axis=0, tiled=True),
        lax.all_gather(norm_moe, "ws", axis=0, tiled=True),
        lax.all_gather(w_gate, "ws", axis=2, tiled=True),
        lax.all_gather(w_up, "ws", axis=2, tiled=True),
        lax.all_gather(w_down, "ws", axis=1, tiled=True),
    )
    kv_width = KV_HEADS * HEAD
    group_size = HEADS // KV_HEADS
    score_scale = HEAD ** (-0.5)
    tree_size = rows_here * shard_count
    members, reaches, positions = tree_layout(seg_lengths[0], parents[0], tree_size)
    first_row = shard_index * rows_here
    own_reach = lax.dynamic_slice_in_dim(reaches, first_row, rows_here, 0)
    own_position = lax.dynamic_slice_in_dim(positions, first_row, rows_here, 0)
    row_index = first_row + jnp.arange(rows_here, dtype=jnp.int32)
    col_index = jnp.arange(tree_size, dtype=jnp.int32)
    visible = (jnp.dot(own_reach, members.T) > 0) & (col_index[None, :] <= row_index[:, None])
    cosines, sines = angles_for(own_position, HEAD)
    resid = tokens.astype(jnp.float32)
    gain_one = gain_attn.astype(jnp.float32)
    scale_one = lax.rsqrt(jnp.mean(resid * resid, axis=-1, keepdims=True) + EPS)
    normed_one = (resid * scale_one * gain_one).astype(jnp.bfloat16)
    query_pre = jnp.dot(normed_one, query_full, preferred_element_type=jnp.float32)
    key_pre = jnp.dot(normed_one, key_full, preferred_element_type=jnp.float32)
    value_rows = jnp.dot(normed_one, value_full, preferred_element_type=jnp.float32).astype(
        jnp.bfloat16
    )
    queries = turn_forward(query_pre.reshape(rows_here, HEADS, HEAD), cosines, sines).astype(
        jnp.bfloat16
    )
    key_rows = (
        turn_forward(key_pre.reshape(rows_here, KV_HEADS, HEAD), cosines, sines)
        .astype(jnp.bfloat16)
        .reshape(rows_here, kv_width)
    )
    keys_all, values_all = (
        lax.all_gather(key_rows, "ws", axis=0, tiled=True),
        lax.all_gather(value_rows, "ws", axis=0, tiled=True),
    )
    grouped = queries.reshape(rows_here, KV_HEADS, group_size, HEAD)
    keys_heads = keys_all.reshape(tree_size, KV_HEADS, HEAD)
    values_heads = values_all.reshape(tree_size, KV_HEADS, HEAD)

    def score_rows():
        raw = (
            jnp.einsum("tkgd,skd->kgts", grouped, keys_heads, preferred_element_type=jnp.float32)
            * score_scale
        )
        return jnp.where(visible[None, None], raw, MASKED)

    scores = score_rows()
    row_peak = jnp.max(scores, axis=-1, keepdims=True)
    lifted = jnp.exp(scores - row_peak)
    row_total = jnp.sum(lifted, axis=-1, keepdims=True)
    logsum = row_peak + jnp.log(row_total)
    attention = lifted / row_total
    mixed_heads = (
        jnp.einsum(
            "kgts,skd->tkgd",
            attention.astype(jnp.bfloat16),
            values_heads,
            preferred_element_type=jnp.float32,
        )
        .reshape(rows_here, HEADS * HEAD)
        .astype(jnp.bfloat16)
    )
    resid_two = resid + jnp.dot(mixed_heads, out_full, preferred_element_type=jnp.float32)
    gain_two = gain_moe.astype(jnp.float32)
    scale_two = lax.rsqrt(jnp.mean(resid_two * resid_two, axis=-1, keepdims=True) + EPS)
    normed_two = (resid_two * scale_two * gain_two).astype(jnp.bfloat16)
    logits = jnp.dot(normed_two, router_full, preferred_element_type=jnp.float32)
    labels = jnp.arange(expert_count, dtype=jnp.int32)
    chosen = (routes[:, :, None] == labels[None, None, :]).astype(jnp.float32)
    picked = jnp.einsum("tke,te->tk", chosen, logits, precision=lax.Precision.HIGHEST)
    gates = jax.nn.softmax(picked, axis=-1)
    flat_routes = routes.reshape(-1)
    pair_count = flat_routes.shape[0]
    onehot = (flat_routes[:, None] == labels[None, :]).astype(jnp.int32)
    slot_rank = jnp.sum(
        (jnp.cumsum(onehot, axis=0, dtype=jnp.int32) - onehot) * onehot, axis=1, dtype=jnp.int32
    )
    target = flat_routes * capacity + slot_rank
    source = (
        jnp.full((expert_count * capacity,), pair_count, jnp.int32)
        .at[target]
        .set(jnp.arange(pair_count, dtype=jnp.int32))
    )
    filled = source < pair_count
    token_of = jnp.minimum(source // top_count, rows_here - 1)
    send_rows = jnp.where(
        filled[:, None], normed_two[token_of], jnp.zeros((), jnp.bfloat16)
    ).reshape(expert_count, capacity, model_width)

    def pre_acts(rows):
        slot_count = rows.shape[1]
        blocks = rows.reshape(owner_count, local_experts, slot_count, model_width)
        gate_pre = jnp.einsum(
            "slcd,ldf->slcf", blocks, gate_full, preferred_element_type=jnp.float32
        )
        up_pre = jnp.einsum("slcd,ldf->slcf", blocks, up_full, preferred_element_type=jnp.float32)
        return (gate_pre, up_pre)

    rows = lax.all_to_all(send_rows, "exp", split_axis=0, concat_axis=0, tiled=True)
    slot_count = rows.shape[1]
    gate_pre, up_pre = pre_acts(rows)
    hidden = (jax.nn.silu(gate_pre) * up_pre).astype(jnp.bfloat16)
    result = jnp.einsum(
        "slcf,lfd->slcd", hidden, down_full, preferred_element_type=jnp.float32
    ).astype(jnp.bfloat16)
    expert_out = result.reshape(expert_count, slot_count, model_width)
    returned = lax.all_to_all(expert_out, "exp", split_axis=0, concat_axis=0, tiled=True)
    pair_rows = (
        returned.reshape(expert_count * capacity, model_width)[target]
        .reshape(rows_here, top_count, model_width)
        .astype(jnp.float32)
    )
    final = resid_two + jnp.sum(gates[:, :, None] * pair_rows, axis=1)
    layer_out = final.astype(jnp.bfloat16)
    grad_out = cotangent.astype(jnp.float32)
    grad_gates = jnp.sum(pair_rows * grad_out[:, None, :], axis=-1)
    grad_picked = gates * (grad_gates - jnp.sum(gates * grad_gates, axis=-1, keepdims=True))
    grad_logits = jnp.einsum("tke,tk->te", chosen, grad_picked, precision=lax.Precision.HIGHEST)
    grad_pairs = (
        (gates[:, :, None] * grad_out[:, None, :])
        .astype(jnp.bfloat16)
        .reshape(pair_count, model_width)
    )
    grad_send = jnp.where(
        filled[:, None],
        grad_pairs[jnp.minimum(source, pair_count - 1)],
        jnp.zeros((), jnp.bfloat16),
    ).reshape(expert_count, capacity, model_width)
    grad_recv = lax.all_to_all(grad_send, "exp", split_axis=0, concat_axis=0, tiled=True)
    rows_back = lax.all_to_all(send_rows, "exp", split_axis=0, concat_axis=0, tiled=True)
    gate_back, up_back = pre_acts(rows_back)
    rows_blocks = rows_back.reshape(owner_count, local_experts, capacity, model_width)
    slope_blocks = grad_recv.reshape(owner_count, local_experts, capacity, model_width)
    hidden = (jax.nn.silu(gate_back) * up_back).astype(jnp.bfloat16)
    grad_hidden = jnp.einsum(
        "slcd,lfd->slcf", slope_blocks, down_full, preferred_element_type=jnp.float32
    )
    grad_down = jnp.einsum(
        "slcf,slcd->lfd", hidden, slope_blocks, preferred_element_type=jnp.float32
    )
    sigmoid_gate = jax.nn.sigmoid(gate_back)
    grad_gate_pre = (
        grad_hidden * up_back * sigmoid_gate * (1.0 + gate_back * (1.0 - sigmoid_gate))
    ).astype(jnp.bfloat16)
    grad_up_pre = (grad_hidden * jax.nn.silu(gate_back)).astype(jnp.bfloat16)
    grad_wgate = jnp.einsum(
        "slcd,slcf->ldf", rows_blocks, grad_gate_pre, preferred_element_type=jnp.float32
    )
    grad_wup = jnp.einsum(
        "slcd,slcf->ldf", rows_blocks, grad_up_pre, preferred_element_type=jnp.float32
    )
    grad_rows = jnp.einsum(
        "slcf,ldf->slcd", grad_gate_pre, gate_full, preferred_element_type=jnp.float32
    ) + jnp.einsum("slcf,ldf->slcd", grad_up_pre, up_full, preferred_element_type=jnp.float32)
    grad_rows = grad_rows.astype(jnp.bfloat16).reshape(expert_count, capacity, model_width)
    grad_back = lax.all_to_all(grad_rows, "exp", split_axis=0, concat_axis=0, tiled=True)
    grad_normed_two = jnp.sum(
        grad_back.reshape(expert_count * capacity, model_width)[target]
        .reshape(rows_here, top_count, model_width)
        .astype(jnp.float32),
        axis=1,
    )
    grad_normed_two = grad_normed_two + contract_last(
        grad_logits, router_full.astype(jnp.float32), lax.Precision.HIGHEST
    )
    grad_router = contract_first(normed_two.astype(jnp.float32), grad_logits, lax.Precision.HIGHEST)
    grad_resid_norm, grad_gain_moe = norm_back(resid_two, scale_two, gain_two, grad_normed_two)
    grad_resid_two = grad_out + grad_resid_norm
    grad_attn = grad_resid_two.astype(jnp.bfloat16)
    grad_wout = contract_first(mixed_heads, grad_attn)
    grad_mixed = contract_last(grad_attn, out_full).astype(jnp.bfloat16)
    grad_grouped = grad_mixed.reshape(rows_here, KV_HEADS, group_size, HEAD)
    attention_again = jnp.exp(score_rows() - logsum)
    grad_attention = jnp.einsum(
        "tkgd,skd->kgts", grad_grouped, values_heads, preferred_element_type=jnp.float32
    )
    row_delta = jnp.sum(attention_again * grad_attention, axis=-1, keepdims=True)
    grad_scores = (attention_again * (grad_attention - row_delta)).astype(jnp.bfloat16)
    grad_queries = (
        jnp.einsum("kgts,skd->tkgd", grad_scores, keys_heads, preferred_element_type=jnp.float32)
        * score_scale
    )
    grad_keys_all = (
        jnp.einsum("kgts,tkgd->skd", grad_scores, grouped, preferred_element_type=jnp.float32)
        * score_scale
    )
    grad_values_all = jnp.einsum(
        "kgts,tkgd->skd",
        attention_again.astype(jnp.bfloat16),
        grad_grouped,
        preferred_element_type=jnp.float32,
    )
    grad_keys, grad_values = (
        lax.psum_scatter(
            grad_keys_all.reshape(tree_size, kv_width).astype(jnp.bfloat16),
            "ws",
            scatter_dimension=0,
            tiled=True,
        ).astype(jnp.float32),
        lax.psum_scatter(
            grad_values_all.reshape(tree_size, kv_width).astype(jnp.bfloat16),
            "ws",
            scatter_dimension=0,
            tiled=True,
        ).astype(jnp.float32),
    )
    grad_query_pre = (
        turn_back(grad_queries.reshape(rows_here, HEADS, HEAD), cosines, sines)
        .reshape(rows_here, HEADS * HEAD)
        .astype(jnp.bfloat16)
    )
    grad_key_pre = (
        turn_back(grad_keys.reshape(rows_here, KV_HEADS, HEAD), cosines, sines)
        .reshape(rows_here, kv_width)
        .astype(jnp.bfloat16)
    )
    grad_value_rows = grad_values.astype(jnp.bfloat16)
    grad_normed_one = (
        contract_last(grad_query_pre, query_full)
        + contract_last(grad_key_pre, key_full)
        + contract_last(grad_value_rows, value_full)
    )
    grad_wquery = contract_first(normed_one, grad_query_pre)
    grad_wkey = contract_first(normed_one, grad_key_pre)
    grad_wvalue = contract_first(normed_one, grad_value_rows)
    grad_resid_one, grad_gain_attn = norm_back(resid, scale_one, gain_one, grad_normed_one)
    grad_tokens = grad_resid_two + grad_resid_one
    (
        red_query,
        red_key,
        red_value,
        red_out,
        red_router,
        red_gain_attn,
        red_gain_moe,
        red_gate,
        red_up,
        red_down,
    ) = (
        lax.psum_scatter(
            grad_wquery.astype(jnp.bfloat16), "ws", scatter_dimension=0, tiled=True
        ).astype(jnp.float32),
        lax.psum_scatter(
            grad_wkey.astype(jnp.bfloat16), "ws", scatter_dimension=0, tiled=True
        ).astype(jnp.float32),
        lax.psum_scatter(
            grad_wvalue.astype(jnp.bfloat16), "ws", scatter_dimension=0, tiled=True
        ).astype(jnp.float32),
        lax.psum_scatter(
            grad_wout.astype(jnp.bfloat16), "ws", scatter_dimension=0, tiled=True
        ).astype(jnp.float32),
        lax.psum_scatter(
            grad_router.astype(jnp.bfloat16), "ws", scatter_dimension=0, tiled=True
        ).astype(jnp.float32),
        lax.psum_scatter(
            grad_gain_attn.astype(jnp.bfloat16), "ws", scatter_dimension=0, tiled=True
        ).astype(jnp.float32),
        lax.psum_scatter(
            grad_gain_moe.astype(jnp.bfloat16), "ws", scatter_dimension=0, tiled=True
        ).astype(jnp.float32),
        lax.psum_scatter(
            grad_wgate.astype(jnp.bfloat16), "ws", scatter_dimension=2, tiled=True
        ).astype(jnp.float32),
        lax.psum_scatter(
            grad_wup.astype(jnp.bfloat16), "ws", scatter_dimension=2, tiled=True
        ).astype(jnp.float32),
        lax.psum_scatter(
            grad_down.astype(jnp.bfloat16), "ws", scatter_dimension=1, tiled=True
        ).astype(jnp.float32),
    )
    sum_query, sum_key, sum_value, sum_out, sum_router, sum_gain_attn, sum_gain_moe = (
        lax.psum(red_query.astype(jnp.bfloat16), "exp").astype(jnp.float32),
        lax.psum(red_key.astype(jnp.bfloat16), "exp").astype(jnp.float32),
        lax.psum(red_value.astype(jnp.bfloat16), "exp").astype(jnp.float32),
        lax.psum(red_out.astype(jnp.bfloat16), "exp").astype(jnp.float32),
        lax.psum(red_router.astype(jnp.bfloat16), "exp").astype(jnp.float32),
        lax.psum(red_gain_attn.astype(jnp.bfloat16), "exp").astype(jnp.float32),
        lax.psum(red_gain_moe.astype(jnp.bfloat16), "exp").astype(jnp.float32),
    )
    return (
        layer_out,
        grad_tokens,
        sum_gain_attn,
        sum_query,
        sum_key,
        sum_value,
        sum_out,
        sum_gain_moe,
        sum_router,
        red_gate,
        red_up,
        red_down,
    )


def solution(mesh):
    placed = (
        P(("exp", "ws"), None),
        P(("exp", "ws"), None),
        P("exp", None),
        P("exp", None),
        P(("exp", "ws"), None),
        P("ws"),
        P("ws", None),
        P("ws", None),
        P("ws", None),
        P("ws", None),
        P("ws"),
        P("ws", None),
        P("exp", None, "ws"),
        P("exp", None, "ws"),
        P("exp", "ws", None),
    )
    return jax.shard_map(
        shards,
        mesh=mesh,
        in_specs=placed,
        out_specs=(
            P(("exp", "ws"), None),
            P(("exp", "ws"), None),
            P("ws"),
            P("ws", None),
            P("ws", None),
            P("ws", None),
            P("ws", None),
            P("ws"),
            P("ws", None),
            P("exp", None, "ws"),
            P("exp", None, "ws"),
            P("exp", "ws", None),
        ),
        check_vma=False,
    )
```

profile of v0, /device:TPU:1, one launch (start us, length us, event | category | flops | bytes accessed | tf_op | source)
XLA Modules:
  0.0 990.9 jit_solution(15315948576997709827)
XLA Ops:
  12.8 9.4 all-gather.1
  22.3 8.8 all-gather
  32.3 9.0 reduce-window.11
  41.8 4.3 scatter_custom_fusion
  47.2 9.6 all_gather.44
  59.5 12.2 %all_gather.38 = bf16[512,512]{1,0:T(8,128)(2,1)S(1)} all-gather(bf16[128,512]{1,0:T(8,128)(2,1)S(1)} %convolution_convert_fusion.7), channel_id=1, replica_groups=mesh['exp'=32,'ws'=4] {'ws'}, dimensions={0}, use_global_device_ids=true | all-gather | bytes 655360 | tf_op jit(solution)/shard_map/all_gather | solution.py:179
  74.5 10.3 %all_gather.40 = bf16[512,512]{0,1:T(8,128)(2,1)S(1)} all-gather(bf16[128,512]{0,1:T(8,128)(2,1)S(1)} %bitcast.313), channel_id=1, replica_groups=mesh['exp'=32,'ws'=4] {'ws'}, dimensions={0}, use_global_device_ids=true | all-gather | bytes 655360 | tf_op jit(solution)/shard_map/all_gather | solution.py:178
  84.8 43.3 %all-gather.14.cloned.1.call-done = bf16[1536,1536]{1,0:T(8,128)(2,1)} async-done(((bf16[384,1536]{1,0:T(8,128)(2,1)}), bf16[1536,1536]{1,0:T(8,128)(2,1)}) %all-gather.14.cloned.1.call-update) | async-done | bytes 4718608 | tf_op jit(solution)/shard_map/all_gather | solution.py:137
  128.1 4.3 fusion.91
  137.6 45.1 %all-gather.16.cloned.1.call-done = bf16[1536,1536]{1,0:T(8,128)(2,1)} async-done(((bf16[384,1536]{1,0:T(8,128)(2,1)}), bf16[1536,1536]{1,0:T(8,128)(2,1)}) %all-gather.16.cloned.1.call-update) | async-done | bytes 4718608 | tf_op jit(solution)/shard_map/all_gather | solution.py:140
  189.3 6.3 gather_fusion
  197.2 6.3 gather_fusion.2
  203.5 8.4 broadcast_select_fusion
  211.9 7.7 all-to-all-start
  220.2 57.8 %all-to-all-done = bf16[32,48,1536]{2,1,0:T(8,128)(2,1)} async-done(((bf16[32,48,1536]{2,1,0:T(8,128)(2,1)}), bf16[32,48,1536]{2,1,0:T(8,128)(2,1)}, u32[]{:S(2)}, u32[]{:S(2)}) %all-to-all-start) | async-done | bytes 4718624 | tf_op jit(solution)/shard_map/all_to_all | solution.py:244
  278.0 7.8 all-to-all-start.2
  287.2 7.1 fusion.36
  294.3 20.4 %all-gather.22.cloned.1.call-done = bf16[1,512,1536]{2,1,0:T(8,128)(2,1)} async-done(((bf16[1,128,1536]{2,1,0:T(8,128)(2,1)}), bf16[1,512,1536]{2,1,0:T(8,128)(2,1)}) %all-gather.22.cloned.1.call-update) | async-done | bytes 1572880 | tf_op jit(solution)/shard_map/all_gather | solution.py:146
  314.7 29.7 %all-to-all-done.2 = bf16[32,48,1536]{2,1,0:T(8,128)(2,1)} async-done(((bf16[32,48,1536]{2,1,0:T(8,128)(2,1)}), bf16[32,48,1536]{2,1,0:T(8,128)(2,1)}, u32[]{:S(2)}, u32[]{:S(2)}) %all-to-all-start.2) | async-done | bytes 4718624 | tf_op jit(solution)/shard_map/all_to_all | solution.py:274
  344.4 7.2 fusion.32
  351.6 9.9 %fusion.28 = (bf16[32,48,512]{2,1,0:T(8,128)(2,1)S(1)}, bf16[32,1,48,512]{3,2,0,1:T(8,128)(2,1)}, bf16[32,48,512]{2,1,0:T(8,128)(2,1)S(1)}) fusion(f32[32,48,512]{2,1,0:T(8,128)} %fusion.32, f32[32,48,512]{2,1,0:T(8,128)} %fusion.36, bf16[32,48,1536]{2,1,0:T(8,128)(2,1)} %all-to-all-done, bf16[1,1536,512]{2,1,0:T(8,128)(2,1)} %all-gather.18.cloned.1.call-done), kind=kOutput, calls=%fused_computation.65 | convolution fusion | flops 2427715584 | bytes 17301504 | tf_op jit(solution)/shard_map/slcd,ldf->slcf/dot_general | solution.py:238
  362.7 4.3 convolution_convert_fusion.2
  367.0 7.5 all-to-all-start.1
  374.5 4.2 fusion.30
  378.7 4.7 add_convert_fusion
  383.4 49.5 %all-to-all-done.1 = bf16[32,48,1536]{2,1,0:T(8,128)(2,1)} async-done(((bf16[32,48,1536]{2,1,0:T(8,128)(2,1)}), bf16[32,48,1536]{2,1,0:T(8,128)(2,1)}, u32[]{:S(2)}, u32[]{:S(2)}) %all-to-all-start.1) | async-done | bytes 4718624 | tf_op jit(solution)/shard_map/all_to_all | solution.py:252
  432.9 7.8 all-to-all-start.3
  441.0 9.6 gather_fusion.1
  450.7 4.4 fusion.1
  456.1 43.2 %all-to-all-done.3 = bf16[32,48,1536]{2,1,0:T(8,128)(2,1)} async-done(((bf16[32,48,1536]{2,1,0:T(8,128)(2,1)}), bf16[32,48,1536]{2,1,0:T(8,128)(2,1)}, u32[]{:S(2)}, u32[]{:S(2)}) %all-to-all-start.3) | async-done | bytes 4718624 | tf_op jit(solution)/shard_map/all_to_all | solution.py:301
  499.2 9.6 gather_fusion.3
  528.0 4.3 fusion.4
  536.3 6.7 fusion.26
  543.0 8.5 copy.108
  554.9 6.7 fusion.25
  561.7 8.5 copy.110
  573.8 6.7 fusion.24
  589.6 4.8 convolution_convert_fusion
  606.3 17.5 %reduce-scatter.39.cloned.1.call-done = bf16[128,1536]{1,0:T(8,128)(2,1)} async-done(((bf16[512,1536]{1,0:T(8,128)(2,1)}), bf16[128,1536]{1,0:T(8,128)(2,1)}) %reduce-scatter.39.cloned.1.call-update) | async-done | bytes 393232
  626.9 24.7 %reduce-scatter.29.cloned.1.call-done = bf16[1,128,1536]{2,1,0:T(8,128)(2,1)} async-done(((bf16[1,512,1536]{2,1,0:T(8,128)(2,1)}), bf16[1,128,1536]{2,1,0:T(8,128)(2,1)}) %reduce-scatter.29.cloned.1.call-update) | async-done | bytes 393232 | tf_op jit(solution)/shard_map/reduce_scatter | solution.py:412
  653.6 26.5 %reduce-scatter.25.cloned.1.call-done = bf16[384,512]{1,0:T(8,128)(2,1)} async-done(((bf16[1536,512]{1,0:T(8,128)(2,1)}), bf16[384,512]{1,0:T(8,128)(2,1)}) %reduce-scatter.25.cloned.1.call-update) | async-done | bytes 393232 | tf_op jit(solution)/shard_map/reduce_scatter | solution.py:391
  680.1 28.3 %reduce-scatter.23.cloned.1.call-done = bf16[384,512]{1,0:T(8,128)(2,1)} async-done(((bf16[1536,512]{1,0:T(8,128)(2,1)}), bf16[384,512]{1,0:T(8,128)(2,1)}) %reduce-scatter.23.cloned.1.call-update) | async-done | bytes 393232 | tf_op jit(solution)/shard_map/reduce_scatter | solution.py:388
  708.4 54.2 %reduce-scatter.27.cloned.1.call-done = bf16[384,1536]{1,0:T(8,128)(2,1)} async-done(((bf16[1536,1536]{1,0:T(8,128)(2,1)}), bf16[384,1536]{1,0:T(8,128)(2,1)}) %reduce-scatter.27.cloned.1.call-update) | async-done | bytes 1179664 | tf_op jit(solution)/shard_map/reduce_scatter | solution.py:394
  762.6 53.1 %reduce-scatter.21.cloned.1.call-done = bf16[384,1536]{1,0:T(8,128)(2,1)} async-done(((bf16[1536,1536]{1,0:T(8,128)(2,1)}), bf16[384,1536]{1,0:T(8,128)(2,1)}) %reduce-scatter.21.cloned.1.call-update) | async-done | bytes 1179664 | tf_op jit(solution)/shard_map/reduce_scatter | solution.py:385
  815.7 4.1 fusion.100
  819.8 17.2 %reduce-scatter.35.cloned.1.call-done = bf16[384,32]{1,0:T(8,128)(2,1)} async-done(((bf16[1536,32]{1,0:T(8,128)(2,1)}), bf16[384,32]{1,0:T(8,128)(2,1)}) %reduce-scatter.35.cloned.1.call-update) | async-done | bytes 24592
  842.0 7.1 all-reduce.4
  849.3 123.9 %all-reduce.2 = (bf16[384]{0:T(512)(128)(2,1)S(1)}, bf16[384]{0:T(512)(128)(2,1)S(1)}, bf16[384,32]{0,1:T(8,128)(2,1)S(1)}) all-reduce(bf16[384]{0:T(512)(128)(2,1)S(1)} %dynamic-slice.1, bf16[384]{0:T(512)(128)(2,1)S(1)} %dynamic-slice.3, bf16[384,32]{0,1:T(8,128)(2,1)S(1)} %copy-done.45), channel_id=1, replica_groups=mesh['exp'=32,'ws'=4] {'exp'}, use_global_device_ids=true, to_apply=%region_37.38 | all-reduce | flops 13056 | bytes 52224 | tf_op jit(solution)/shard_map/psum | solution.py:422
  (311 shorter events, 101.5 us)
Async XLA Ops:
  7.2 50.4 %all-gather.10.cloned.1.call-start = ((), (), s32[]{:S(2)}) async-start(), calls=%async_computation.14 | async-start | bytes 1966080 | tf_op jit(solution)/shard_map/all_gather | solution.py:139
  7.3 39.0 %copy-start.22 = (bf16[128,1536]{1,0:T(8,128)(2,1)S(1)}, bf16[128,1536]{1,0:T(8,128)(2,1)}, u32[]{:S(2)}) copy-start(bf16[128,1536]{1,0:T(8,128)(2,1)} %param.16) | copy-start | bytes 1179652
  8.0 64.1 %all-gather.12.cloned.1.call-start = ((), (), s32[]{:S(2)}) async-start(), calls=%async_computation.15 | async-start | bytes 1966080 | tf_op jit(solution)/shard_map/all_gather | solution.py:138
  8.7 38.5 %copy-start.50 = (bf16[384,32]{0,1:T(8,128)(2,1)S(1)}, bf16[384,32]{0,1:T(8,128)(2,1)}, u32[]{:S(2)}) copy-start(bf16[384,32]{0,1:T(8,128)(2,1)} %param.26) | copy-start | bytes 73732
  8.7 119.3 %all-gather.14.cloned.1.call-start = ((), (), s32[]{:S(2)}) async-start(), calls=%async_computation.16 | async-start | bytes 5898240 | tf_op jit(solution)/shard_map/all_gather | solution.py:137
  9.5 47.8 %copy-start.3 = (bf16[128,1536]{1,0:T(8,128)(2,1)S(1)}, bf16[128,1536]{1,0:T(8,128)(2,1)}, u32[]{:S(2)}) copy-start(bf16[128,1536]{1,0:T(8,128)(2,1)} %param.15) | copy-start | bytes 1179652
  9.5 173.2 %all-gather.16.cloned.1.call-start = ((), (), s32[]{:S(2)}) async-start(), calls=%async_computation.17 | async-start | bytes 5898240 | tf_op jit(solution)/shard_map/all_gather | solution.py:140
  10.2 177.1 %copy-start.33 = (s32[128,8]{1,0:T(8,128)}, s32[128,8]{1,0:T(8,128)S(1)}, u32[]{:S(2)}) copy-start(s32[128,8]{1,0:T(8,128)S(1)} %copy.78) | copy-start | bytes 12292
  22.3 163.7 %copy-start.43 = (f32[1536]{0:T(1024)}, f32[1536]{0:T(1024)S(1)}, u32[]{:S(2)}) copy-start(f32[1536]{0:T(1024)S(1)} %reshape.401) | copy-start | bytes 18436
  31.2 96.9 %copy-start.29 = (f32[1536]{0:T(1024)}, f32[1536]{0:T(1024)S(1)}, u32[]{:S(2)}) copy-start(f32[1536]{0:T(1024)S(1)} %reshape.400) | copy-start | bytes 18436
  41.8 15.6 %copy-start.53 = (s32[1024,1]{0,1:T(1,128)}, s32[1024,1]{0,1:T(1,128)S(1)}, u32[]{:S(2)}) copy-start(s32[1024,1]{0,1:T(1,128)S(1)} %compare_select_fusion) | copy-start | bytes 12292
  56.8 130.1 %copy-start.27 = (bf16[1536,32]{0,1:T(8,128)(2,1)}, bf16[1536,32]{0,1:T(8,128)(2,1)S(1)}, u32[]{:S(2)}) copy-start(bf16[1536,32]{0,1:T(8,128)(2,1)S(1)} %all_gather.44) | copy-start | bytes 294916
  57.5 70.6 %copy-start.48 = (f32[128]{0:T(128)}, f32[128]{0:T(128)S(1)}, u32[]{:S(2)}) copy-start(f32[128]{0:T(128)S(1)} %add_rsqrt_fusion.1) | copy-start | bytes 1540
  57.6 74.8 %copy-start.35 = (f32[128,32]{0,1:T(8,128)}, f32[128,32]{0,1:T(8,128)S(1)}, u32[]{:S(2)}) copy-start(f32[128,32]{0,1:T(8,128)S(1)} %get-tuple-element.44) | copy-start | bytes 49156
  57.6 74.8 %copy-start.37 = (f32[128,32]{0,1:T(8,128)}, f32[128,32]{0,1:T(8,128)S(1)}, u32[]{:S(2)}) copy-start(f32[128,32]{0,1:T(8,128)S(1)} %get-tuple-element.45) | copy-start | bytes 49156
  72.0 62.7 %copy-start.13 = (bf16[512,512]{0,1:T(8,128)(2,1)}, bf16[512,512]{0,1:T(8,128)(2,1)S(1)}, u32[]{:S(2)}) copy-start(bf16[512,512]{0,1:T(8,128)(2,1)S(1)} %copy.73) | copy-start | bytes 1572868
  84.8 47.7 %copy-start.10 = (bf16[512,512]{0,1:T(8,128)(2,1)}, bf16[512,512]{0,1:T(8,128)(2,1)S(1)}, u32[]{:S(2)}) copy-start(bf16[512,512]{0,1:T(8,128)(2,1)S(1)} %all_gather.40) | copy-start | bytes 1572868
  137.6 48.3 %copy-start.12 = (bf16[8,64,3,128]{3,1,2,0:T(8,128)(2,1)}, bf16[8,64,3,128]{3,1,2,0:T(8,128)(2,1)S(1)}, u32[]{:S(2)}) copy-start(bf16[8,64,3,128]{3,1,2,0:T(8,128)(2,1)S(1)} %fusion.49) | copy-start | bytes 1179652
  187.0 8.6 copy-start
  211.9 66.1 %all-to-all-start = ((bf16[32,48,1536]{2,1,0:T(8,128)(2,1)}), bf16[32,48,1536]{2,1,0:T(8,128)(2,1)}, u32[]{:S(2)}, u32[]{:S(2)}) async-start(bf16[32,48,1536]{2,1,0:T(8,128)(2,1)} %get-tuple-element.43), calls=%async_computation | async-start | bytes 9437184 | tf_op jit(solution)/shard_map/all_to_all | solution.py:244
  219.6 67.6 %all-gather.20.cloned.1.call-start = ((), (), s32[]{:S(2)}) async-start(), calls=%async_computation.19 | async-start | bytes 1966080 | tf_op jit(solution)/shard_map/all_gather | solution.py:145
  278.0 66.4 %all-to-all-start.2 = ((bf16[32,48,1536]{2,1,0:T(8,128)(2,1)}), bf16[32,48,1536]{2,1,0:T(8,128)(2,1)}, u32[]{:S(2)}, u32[]{:S(2)}) async-start(bf16[32,48,1536]{2,1,0:T(8,128)(2,1)} %get-tuple-element.42), calls=%async_computation.2 | async-start | bytes 9437184 | tf_op jit(solution)/shard_map/all_to_all | solution.py:274
  285.8 28.9 %all-gather.22.cloned.1.call-start = ((), (), s32[]{:S(2)}) async-start(), calls=%async_computation.20 | async-start | bytes 1966080 | tf_op jit(solution)/shard_map/all_gather | solution.py:146
  286.4 65.2 %all-gather.18.cloned.1.call-start = ((), (), s32[]{:S(2)}) async-start(), calls=%async_computation.18 | async-start | bytes 1966080 | tf_op jit(solution)/shard_map/all_gather | solution.py:144
  351.6 11.1 %copy-start.65 = (bf16[1,512,1536]{2,1,0:T(8,128)(2,1)S(1)}, bf16[1,512,1536]{2,1,0:T(8,128)(2,1)}, u32[]{:S(2)}) copy-start(bf16[1,512,1536]{2,1,0:T(8,128)(2,1)} %all-gather.22.cloned.1.call-done) | copy-start | bytes 4718596
  361.5 17.1 %copy-start.69 = (bf16[32,48,512]{2,1,0:T(8,128)(2,1)}, bf16[32,48,512]{2,1,0:T(8,128)(2,1)S(1)}, u32[]{:S(2)}) copy-start(bf16[32,48,512]{2,1,0:T(8,128)(2,1)S(1)} %get-tuple-element.27) | copy-start | bytes 4718596
  367.0 7.5 copy-start.66
  367.0 65.9 %all-to-all-start.1 = ((bf16[32,48,1536]{2,1,0:T(8,128)(2,1)}), bf16[32,48,1536]{2,1,0:T(8,128)(2,1)}, u32[]{:S(2)}, u32[]{:S(2)}) async-start(bf16[32,48,1536]{2,1,0:T(8,128)(2,1)} %convolution_convert_fusion.2), calls=%async_computation.1 | async-start | bytes 9437184 | tf_op jit(solution)/shard_map/all_to_all | solution.py:252
  383.4 57.5 %copy-start.54 = (s32[1024,1]{0,1:T(1,128)S(1)}, s32[1024,1]{0,1:T(1,128)}, u32[]{:S(2)}) copy-start(s32[1024,1]{0,1:T(1,128)} %copy-done.53) | copy-start | bytes 12292
  383.4 57.6 %copy-start.42 = (f32[8,3,128]{2,1,0:T(4,128)S(1)}, f32[8,3,128]{2,1,0:T(4,128)}, u32[]{:S(2)}) copy-start(f32[8,3,128]{2,1,0:T(4,128)} %copy-done.41) | copy-start | bytes 36868
  383.4 57.6 %copy-start.47 = (f32[8,3,128]{2,1,0:T(4,128)S(1)}, f32[8,3,128]{2,1,0:T(4,128)}, u32[]{:S(2)}) copy-start(f32[8,3,128]{2,1,0:T(4,128)} %copy-done.46) | copy-start | bytes 36868
  432.9 66.4 %all-to-all-start.3 = ((bf16[32,48,1536]{2,1,0:T(8,128)(2,1)}), bf16[32,48,1536]{2,1,0:T(8,128)(2,1)}, u32[]{:S(2)}, u32[]{:S(2)}) async-start(bf16[32,48,1536]{2,1,0:T(8,128)(2,1)} %add_convert_fusion), calls=%async_computation.3 | async-start | bytes 9437184 | tf_op jit(solution)/shard_map/all_to_all | solution.py:301
  440.7 139.8 %reduce-scatter.33.cloned.1.call-start = ((), (), s32[]{:S(2)}) async-start(), calls=%async_computation.27 | async-start | bytes 655360
  441.0 9.7 copy-start.32
  456.1 55.0 %copy-start.39 = (f32[128,1,32]{2,1,0:T(1,128)}, f32[128,1,32]{2,1,0:T(1,128)S(1)}, u32[]{:S(2)}) copy-start(f32[128,1,32]{2,1,0:T(1,128)S(1)} %fusion.62) | copy-start | bytes 49156
  523.5 60.1 %reduce-scatter.31.cloned.1.call-start = ((), (), s32[]{:S(2)}) async-start(), calls=%async_computation.26 | async-start | bytes 655360
  536.3 65.7 %reduce-scatter.37.cloned.1.call-start = ((), (), s32[]{:S(2)}) async-start(), calls=%async_computation.29 | async-start | bytes 1966080
  554.9 69.0 %reduce-scatter.39.cloned.1.call-start = ((), (), s32[]{:S(2)}) async-start(), calls=%async_computation.30 | async-start | bytes 1966080
  573.7 77.9 %reduce-scatter.29.cloned.1.call-start = ((), (), s32[]{:S(2)}) async-start(), calls=%async_computation.25 | async-start | bytes 1966080 | tf_op jit(solution)/shard_map/reduce_scatter | solution.py:412
  580.5 99.6 %reduce-scatter.25.cloned.1.call-start = ((), (), s32[]{:S(2)}) async-start(), calls=%async_computation.23 | async-start | bytes 1966080 | tf_op jit(solution)/shard_map/reduce_scatter | solution.py:391
  583.3 125.0 %reduce-scatter.23.cloned.1.call-start = ((), (), s32[]{:S(2)}) async-start(), calls=%async_computation.22 | async-start | bytes 1966080 | tf_op jit(solution)/shard_map/reduce_scatter | solution.py:388
  589.5 173.0 %reduce-scatter.27.cloned.1.call-start = ((), (), s32[]{:S(2)}) async-start(), calls=%async_computation.24 | async-start | bytes 5898240 | tf_op jit(solution)/shard_map/reduce_scatter | solution.py:394
  594.4 221.3 %reduce-scatter.21.cloned.1.call-start = ((), (), s32[]{:S(2)}) async-start(), calls=%async_computation.21 | async-start | bytes 5898240 | tf_op jit(solution)/shard_map/reduce_scatter | solution.py:385
  600.1 236.9 %reduce-scatter.35.cloned.1.call-start = ((), (), s32[]{:S(2)}) async-start(), calls=%async_computation.28 | async-start | bytes 491520
  606.3 369.8 %all-reduce.7.cloned.1.call-start = ((), (), s32[]{:S(2)}) async-start(), calls=%async_computation.31 | async-start | bytes 6291456 | tf_op jit(solution)/shard_map/psum | solution.py:417
  815.7 22.9 %copy-start.9 = (bf16[1536,512]{1,0:T(8,128)(2,1)S(1)}, bf16[1536,512]{1,0:T(8,128)(2,1)}, u32[]{:S(2)}) copy-start(bf16[1536,512]{1,0:T(8,128)(2,1)} %all-gather.12.cloned.1.call-done) | copy-start | bytes 4718596
  838.6 136.3 %copy-start.8 = (f32[128,1536]{1,0:T(8,128)S(1)}, f32[128,1536]{1,0:T(8,128)}, u32[]{:S(2)}) copy-start(f32[128,1536]{1,0:T(8,128)} %copy-done.7) | copy-start | bytes 2359300
  840.3 9.0 copy-start.45
  (45 other events, 143.2 us)
Sparse Core Ops, SparseCore 0:
  9.7 29.8 all-gather.9
  41.3 28.6 all-gather.11
  71.6 56.4 all-gather.13
  129.6 53.1 all-gather.15
  221.8 29.4 all-gather.19
  288.0 26.6 all-gather.21
  316.3 29.3 all-gather.17
  523.7 19.8 reduce-scatter.32
  546.5 21.1 reduce-scatter.30
  569.9 26.0 reduce-scatter.36
  598.4 25.4 reduce-scatter.38
  626.1 25.4 reduce-scatter.28
  654.6 25.4 reduce-scatter.24
  682.9 25.4 reduce-scatter.22
  710.6 51.8 reduce-scatter.26
  764.8 50.8 reduce-scatter.20
  818.5 18.4 reduce-scatter.34
  841.0 112.1 all-reduce.6
where the time goes:
time: 1000 us; the launch traced here: 991 us
  waiting for transfers between devices  515 us (52%)
  blocking collectives  181 us (18%)
  matrix products  111 us (11%)
  local copies, waits for them, and re-layouts  80.6 us (8%)
  other arithmetic  53.3 us (5%)
  starting transfers between devices  32.6 us (3%)
  between operations  16.8 us (2%)
    psum x1, blocking collectives, shards(): lax.psum(red_gain_attn.astype(jnp.bfloat16), 'exp').astype(jnp.float32)  124 us
    all_to_all x1, waiting for transfers between devices, shards(): lax.all_to_all(send_rows, 'exp', split_axis=0, concat_axis=0, tiled=True)  57.8 us
    reduce_scatter x1, waiting for transfers between devices, shards(): lax.psum_scatter(grad_wout.astype(jnp.bfloat16), 'ws', scatter_dimension=...  54.2 us
    reduce_scatter x1, waiting for transfers between devices, shards(): lax.psum_scatter(grad_wquery.astype(jnp.bfloat16), 'ws', scatter_dimensio...  53.1 us
    all_to_all x1, waiting for transfers between devices, shards(): lax.all_to_all(expert_out, 'exp', split_axis=0, concat_axis=0, tiled=True)  49.5 us
    all_gather x1, waiting for transfers between devices, shards(): lax.all_gather(w_out, 'ws', axis=0, tiled=True)  45.1 us
    all_gather x1, waiting for transfers between devices, shards(): lax.all_gather(w_query, 'ws', axis=0, tiled=True)  43.3 us
    all_to_all x1, waiting for transfers between devices, shards(): lax.all_to_all(grad_rows, 'exp', split_axis=0, concat_axis=0, tiled=True)  43.2 us
  transfers between devices with their start and end apart: 22, of which 14 were waited for; matrix products, arithmetic and copies ran while one was open for 17% of the time, Pallas kernels for 0%

commit v1 on v0

v1 whole, which is shorter than its diff:
```python
import jax
import jax.numpy as jnp
from jax import lax
from jax.sharding import PartitionSpec as P

HEADS = 24
KV_HEADS = 8
HEAD = 64
EPS = 1e-06
THETA = 10000.0
MASKED = -1e30
BF = jnp.bfloat16
F32 = jnp.float32
WS = 4
CHIPS = 16
CAP = 48


def dot(a, b):
    return jnp.dot(a, b, preferred_element_type=F32)


def dot_t(a, b):
    return lax.dot_general(a, b, (((1,), (1,)), ((), ())), preferred_element_type=F32)


def tdot(a, b):
    return lax.dot_general(a, b, (((0,), (0,)), ((), ())), preferred_element_type=F32)


def split(v):
    hi = v.astype(BF)
    return hi, (v - hi.astype(F32)).astype(BF)


def from_peer(v, k):
    return lax.ppermute(v, "ws", [(s, (s - k) % WS) for s in range(WS)])


def to_peer(v, k):
    return lax.ppermute(v, "ws", [(s, (s + k) % WS) for s in range(WS)])


def other_core(v):
    return lax.ppermute(v, "exp", [(s, s ^ 1) for s in range(2 * CHIPS)])


def same_core(v):
    groups = [[2 * chip + core for chip in range(CHIPS)] for core in range(2)]
    return lax.all_to_all(v, "exp", 0, 0, tiled=True, axis_index_groups=groups)


def tree_layout(lengths, parents, token_index):
    seg = lengths.shape[0]
    labels = jnp.arange(seg, dtype=jnp.int32)
    segment_end = jnp.cumsum(lengths, dtype=jnp.int32)
    starts = segment_end - lengths
    segment = jnp.sum((token_index[:, None] >= segment_end[None, :]).astype(jnp.int32), axis=1)
    reach = ((parents[:, None] == labels[None, :]) | (labels[:, None] == labels[None, :])).astype(
        BF
    )
    for _ in range(4):
        reach = (dot(reach, reach) > 0.5).astype(BF)
    above = jnp.sum(reach.astype(jnp.int32) * lengths[None, :], axis=1) - lengths
    members = segment[:, None] == labels[None, :]
    position = jnp.sum(jnp.where(members, (above - starts)[None, :], 0), axis=1) + token_index
    members = members.astype(BF)
    reaches = dot(members, reach).astype(BF)
    visible = (dot_t(reaches, members) > 0.5) & (token_index[None, :] <= token_index[:, None])
    return visible, position


def rope(vectors, cosines, sines, sign):
    rows, width = vectors.shape
    v = vectors.reshape(rows, width // HEAD, HEAD)
    a, b = v[..., : HEAD // 2], v[..., HEAD // 2 :]
    c, s = cosines[:, None, :], sines[:, None, :] * sign
    return jnp.concatenate([a * c - b * s, b * c + a * s], axis=-1).reshape(rows, width)


def norm_back(resid, scale, gain, slope):
    gain_slope = jnp.sum(slope * resid * scale, axis=0)
    inner = jnp.mean(gain * slope * resid, axis=-1, keepdims=True)
    return scale * gain * slope - resid * scale * scale * scale * inner, gain_slope


def masked_softmax(logits, mask):
    top = jnp.max(jnp.where(mask, logits, MASKED), axis=-1, keepdims=True)
    lifted = jnp.where(mask, jnp.exp(jnp.where(mask, logits, MASKED) - top), 0.0)
    return lifted / jnp.maximum(jnp.sum(lifted, axis=-1, keepdims=True), 1e-30)


def shards(
    tokens,
    cotangent,
    seg_lengths,
    parents,
    routes,
    norm_attn,
    w_query,
    w_key,
    w_value,
    w_out,
    norm_moe,
    w_router,
    w_gate,
    w_up,
    w_down,
):
    me = lax.axis_index("ws")
    expert = lax.axis_index("exp")
    core = expert % 2
    rows, width = tokens.shape
    tree = rows * WS
    shard = width // WS
    experts = 2 * CHIPS
    group = HEADS // KV_HEADS
    my_heads = HEADS // WS
    my_kv = KV_HEADS // WS
    q_w, kv_w = my_heads * HEAD, my_kv * HEAD
    slots = experts * CAP

    def gathered(v):
        return [v] + [from_peer(v, k) for k in (1, 2, 3)]

    def absolute(parts):
        out = jnp.zeros((WS,) + parts[0].shape, parts[0].dtype)
        for r, part in enumerate(parts):
            out = lax.dynamic_update_index_in_dim(out, part, (me + r) % WS, 0)
        return out.reshape((WS * parts[0].shape[0],) + parts[0].shape[1:])

    x_all16 = jnp.concatenate(gathered(tokens), axis=0)
    small = jnp.concatenate(
        [
            w_router,
            norm_attn[:, None],
            norm_moe[:, None],
            jnp.zeros((shard, 128 - experts - 2), BF),
        ],
        axis=1,
    )
    small_full = absolute(gathered(small))
    router = small_full[:, :experts]
    gain_one = small_full[:, experts].astype(F32)
    gain_two = small_full[:, experts + 1].astype(F32)

    def piece(d):
        return jnp.concatenate(
            [
                lax.dynamic_slice_in_dim(w_query, d * q_w, q_w, 1),
                lax.dynamic_slice_in_dim(w_key, d * kv_w, kv_w, 1),
                lax.dynamic_slice_in_dim(w_value, d * kv_w, kv_w, 1),
            ],
            axis=1,
        )

    qkv_parts = [piece(me)] + [from_peer(piece((me - k) % WS), k) for k in (1, 2, 3)]
    w_qkv = absolute(qkv_parts)

    labels = jnp.arange(experts, dtype=jnp.int32)
    chosen = jnp.any(routes[:, :, None] == labels[None, None, :], axis=1)
    row_id = jnp.arange(rows, dtype=jnp.int32)
    before = (row_id[None, :] < row_id[:, None]).astype(BF)
    rank = dot(before, chosen.astype(BF))
    col = jnp.arange(slots, dtype=jnp.int32)
    spread = (col[None, :] // CAP == labels[:, None]).astype(BF)
    place = dot(jnp.where(chosen, rank + 1.0, 0.0).astype(BF), spread)
    taken = place == (col % CAP + 1).astype(F32)[None, :]
    to_slot = taken.astype(BF)
    extra = jnp.concatenate(
        [cotangent, chosen.astype(BF), jnp.zeros((rows, 128 - experts), BF)], axis=1
    )
    dy_send = tdot(to_slot, extra).astype(BF).reshape(experts, CAP, width + 128)
    dy_slots = lax.all_to_all(dy_send, "exp", 0, 0, tiled=True).reshape(slots, width + 128)

    order = (
        ((me + jnp.arange(WS, dtype=jnp.int32)) % WS)[:, None] * rows + row_id[None, :]
    ).reshape(-1)
    visible, position = tree_layout(seg_lengths[0], parents[0], order)
    inverse = THETA ** (-jnp.arange(HEAD // 2, dtype=F32) * 2.0 / HEAD)
    angles = position.astype(F32)[:, None] * inverse[None, :]
    cosines, sines = jnp.cos(angles), jnp.sin(angles)
    x_all = x_all16.astype(F32)
    scale_one = lax.rsqrt(jnp.mean(x_all * x_all, axis=-1, keepdims=True) + EPS)
    h1 = (x_all * scale_one * gain_one).astype(BF)
    qkv = dot(h1, w_qkv)
    q = rope(qkv[:, :q_w], cosines, sines, 1.0).astype(BF).reshape(tree, my_kv, group, HEAD)
    k = rope(qkv[:, q_w : q_w + kv_w], cosines, sines, 1.0).astype(BF).reshape(tree, my_kv, HEAD)
    v = qkv[:, q_w + kv_w :].astype(BF).reshape(tree, my_kv, HEAD)
    score_scale = HEAD ** (-0.5)

    def score_rows():
        raw = jnp.einsum("tkgd,skd->kgts", q, k, preferred_element_type=F32) * score_scale
        return jnp.where(visible[None, None], raw, MASKED)

    scores = score_rows()
    row_peak = jnp.max(scores, axis=-1, keepdims=True)
    lifted = jnp.exp(scores - row_peak)
    row_total = jnp.sum(lifted, axis=-1, keepdims=True)
    logsum = row_peak + jnp.log(row_total)
    attention = (lifted / row_total).astype(BF)
    o = (
        jnp.einsum("kgts,skd->tkgd", attention, v, preferred_element_type=F32)
        .reshape(tree, q_w)
        .astype(BF)
    )

    def to_owners(partial):
        blocks = partial.reshape(WS, rows, width)
        total = blocks[0]
        for k in (1, 2, 3):
            total = total + to_peer(blocks[k].astype(BF), k).astype(F32)
        return total

    x2 = tokens.astype(F32) + to_owners(dot(o, w_out))
    scale_two = lax.rsqrt(jnp.mean(x2 * x2, axis=-1, keepdims=True) + EPS)
    h2 = (x2 * scale_two * gain_two).astype(BF)
    x_send = tdot(to_slot, h2).astype(BF).reshape(experts, CAP, width)
    x_send, wg_own, wu_own, wd_own = lax.optimization_barrier(
        (x_send, w_gate[0], w_up[0], w_down[0])
    )
    x_slots = lax.all_to_all(x_send, "exp", 0, 0, tiled=True).reshape(slots, width)
    gates = masked_softmax(dot(h2, router), chosen)

    wg = jnp.concatenate(gathered(wg_own), axis=1)
    wu = jnp.concatenate(gathered(wu_own), axis=1)
    wd = jnp.concatenate(gathered(wd_own), axis=0)
    g_pre = dot(x_slots, wg)
    u_pre = dot(x_slots, wu)
    sig = jax.nn.sigmoid(g_pre)
    hidden = (g_pre * sig * u_pre).astype(BF)
    y = dot(hidden, wd).astype(BF)
    dy = dy_slots[:, :width].astype(F32)
    slot_mask = dy_slots[:, width : width + experts] > 0.5
    slot_gates = masked_softmax(dot(x_slots, router), slot_mask)
    mine = (labels == expert)[None, :]
    gate_here = jnp.sum(jnp.where(mine, slot_gates, 0.0), axis=1, keepdims=True)
    dgate = jnp.sum(dy * y.astype(F32), axis=1, keepdims=True)
    d_y = (gate_here * dy).astype(BF)
    d_h = dot_t(d_y, wd)
    d_g = (d_h * u_pre * sig * (1.0 + g_pre * (1.0 - sig))).astype(BF)
    d_u = (d_h * g_pre * sig).astype(BF)
    d_x = (dot_t(d_g, wg) + dot_t(d_u, wu)).astype(BF)
    hi, lo = split(dgate)
    none = jnp.zeros((), BF)
    tail = jnp.concatenate(
        [
            jnp.where(mine, hi, none),
            jnp.where(mine, lo, none),
            jnp.zeros((slots, 128 - 2 * experts), BF),
        ],
        axis=1,
    )
    dx_send = jnp.concatenate([d_x, tail], axis=1).reshape(experts, CAP, width + 128)
    dx_back = lax.all_to_all(dx_send, "exp", 0, 0, tiled=True).reshape(slots, width + 128)
    y, dx_back = lax.optimization_barrier((y, dx_back))
    y_back = lax.all_to_all(y.reshape(experts, CAP, width), "exp", 0, 0, tiled=True).reshape(
        slots, width
    )

    part = w_gate.shape[2]

    def shard_sum(blocks):
        total = blocks[0]
        for k in (1, 2, 3):
            total = total + to_peer(blocks[k].astype(BF), k).astype(F32)
        return total

    grad_wg = shard_sum(
        [tdot(x_slots, d_g[:, r * part : (r + 1) * part]) for r in range(WS)]
    )[None]
    grad_wu = shard_sum(
        [tdot(x_slots, d_u[:, r * part : (r + 1) * part]) for r in range(WS)]
    )[None]
    grad_wd = shard_sum(
        [tdot(hidden[:, r * part : (r + 1) * part], d_y) for r in range(WS)]
    )[None]

    back = dot(to_slot, dx_back)
    dgate_dense = back[:, width : width + experts] + back[:, width + experts : width + 2 * experts]
    dlogits = gates * (dgate_dense - jnp.sum(gates * dgate_dense, axis=-1, keepdims=True))
    dl_hi, dl_lo = split(dlogits)
    dh2 = back[:, :width] + dot_t(dl_hi, router) + dot_t(dl_lo, router)
    grad_router = tdot(h2, dl_hi) + tdot(h2, dl_lo)
    dres, grad_gain_two = norm_back(x2, scale_two, gain_two, dh2)
    dx2 = cotangent.astype(F32) + dres
    d_a = jnp.concatenate(gathered(dx2.astype(BF)), axis=0)
    grad_wout = tdot(o, d_a)
    d_o = dot_t(d_a, w_out).astype(BF).reshape(tree, my_kv, group, HEAD)
    probs = jnp.exp(score_rows() - logsum)
    d_p = jnp.einsum("tkgd,skd->kgts", d_o, v, preferred_element_type=F32)
    delta = jnp.sum(probs * d_p, axis=-1, keepdims=True)
    d_s = (probs * (d_p - delta)).astype(BF)
    d_q = jnp.einsum("kgts,skd->tkgd", d_s, k, preferred_element_type=F32) * score_scale
    d_k = jnp.einsum("kgts,tkgd->skd", d_s, q, preferred_element_type=F32) * score_scale
    d_v = jnp.einsum("kgts,tkgd->skd", probs.astype(BF), d_o, preferred_element_type=F32)
    d_qkv = jnp.concatenate(
        [
            rope(d_q.reshape(tree, q_w), cosines, sines, -1.0).astype(BF),
            rope(d_k.reshape(tree, kv_w), cosines, sines, -1.0).astype(BF),
            d_v.reshape(tree, kv_w).astype(BF),
        ],
        axis=1,
    )
    dh1_part = dot_t(d_qkv, w_qkv)
    grad_gain_one = jnp.sum(dh1_part * x_all * scale_one, axis=0)
    dh1 = to_owners(dh1_part)
    dres_one, _ = norm_back(tokens.astype(F32), scale_one[:rows], gain_one, dh1)
    grad_tokens = dx2 + dres_one
    grad_wqkv = tdot(h1, d_qkv)

    half = (q_w + 2 * kv_w + 128) // 2
    load = jnp.concatenate(
        [
            grad_wqkv,
            grad_router,
            grad_gain_two[:, None],
            grad_gain_one[:, None],
            jnp.zeros((width, 128 - experts - 2), F32),
        ],
        axis=1,
    )
    load_o = jnp.concatenate([grad_wout[:, i * half : (i + 1) * half] for i in range(WS)], axis=0)
    load_o = jnp.concatenate([load_o[: 2 * shard], load_o[2 * shard :]], axis=1)
    load = jnp.concatenate([load, load_o], axis=0)
    keep = jnp.where(core == 0, load[:, :half], load[:, half:])
    give = jnp.where(core == 0, load[:, half:], load[:, :half]).astype(BF)
    chip_sum = (keep + other_core(give).astype(F32)).astype(BF)
    step = shard // CHIPS
    sets = chip_sum.shape[0] // shard
    sent = chip_sum.reshape(sets, CHIPS, step, half).transpose(1, 0, 2, 3)
    got = same_core(sent)
    total = jnp.sum(got.astype(F32), axis=0).astype(BF)
    turned = absolute(
        [lax.dynamic_index_in_dim(total, me, 0, False)]
        + [
            from_peer(lax.dynamic_index_in_dim(total, (me - k) % WS, 0, False), k)
            for k in (1, 2, 3)
        ]
    ).reshape(WS, step, half)
    final = jnp.concatenate([turned, total[WS:]], axis=0)
    spread_out = same_core(jnp.broadcast_to(final, (CHIPS,) + final.shape))
    twin = other_core(spread_out)
    first = jnp.where(core == 0, spread_out, twin).transpose(1, 0, 2, 3).reshape(sets, shard, half)
    second = jnp.where(core == 0, twin, spread_out).transpose(1, 0, 2, 3).reshape(sets, shard, half)
    first, second = first.astype(F32), second.astype(F32)
    sum_query = jnp.concatenate([first[i] for i in range(WS)], axis=1)
    sum_key = jnp.concatenate([second[i][:, :kv_w] for i in range(WS)], axis=1)
    sum_value = jnp.concatenate([second[i][:, kv_w : 2 * kv_w] for i in range(WS)], axis=1)
    sum_small = sum(second[i][:, 2 * kv_w :] for i in range(WS))
    sum_out = jnp.concatenate([first[WS], first[WS + 1], second[WS], second[WS + 1]], axis=1)

    gates_slot = jnp.where(taken, dot(split(gates)[0], spread) + dot(split(gates)[1], spread), 0.0)
    gs_hi, gs_lo = split(gates_slot)
    layer_out = (x2 + dot(gs_hi, y_back) + dot(gs_lo, y_back)).astype(BF)
    return (
        layer_out,
        grad_tokens,
        sum_small[:, experts + 1],
        sum_query,
        sum_key,
        sum_value,
        sum_out,
        sum_small[:, experts],
        sum_small[:, :experts],
        grad_wg,
        grad_wu,
        grad_wd,
    )


def solution(mesh):
    rows = P(("exp", "ws"), None)
    placed = (
        rows,
        rows,
        P("exp", None),
        P("exp", None),
        rows,
        P("ws"),
        P("ws", None),
        P("ws", None),
        P("ws", None),
        P("ws", None),
        P("ws"),
        P("ws", None),
        P("exp", None, "ws"),
        P("exp", None, "ws"),
        P("exp", "ws", None),
    )
    return jax.shard_map(
        shards,
        mesh=mesh,
        in_specs=placed,
        out_specs=(
            rows,
            rows,
            P("ws"),
            P("ws", None),
            P("ws", None),
            P("ws", None),
            P("ws", None),
            P("ws"),
            P("ws", None),
            P("exp", None, "ws"),
            P("exp", None, "ws"),
            P("exp", "ws", None),
        ),
        check_vma=False,
    )
```

time: 1000 us -> 582 us (0.58)
  waiting for transfers between devices: 515 us -> 203 us
  blocking collectives: 181 us -> 0 us
  starting transfers between devices: 32.6 us -> 108 us
  matrix products: 111 us -> 125 us
  between operations: 16.8 us -> 3.02 us
  other arithmetic: 53.3 us -> 42.8 us
  local copies, waits for them, and re-layouts: 80.6 us -> 90.9 us
    reduce_scatter x5 -> x0, waiting for transfers between devices: 187 us -> none  [the longest x1 54.2 us: shards(): lax.psum_scatter(grad_wout.astype(jnp.bfloat16), 'ws', scatter_dimension=...]
    psum x1 -> x0, blocking collectives: 124 us -> none  [shards(): lax.psum(red_gain_attn.astype(jnp.bfloat16), 'exp').astype(jnp.float32)]
    ppermute x0 -> x41, waiting for transfers between devices: none -> 116 us  [the longest x24 73.4 us: from_peer(): return lax.ppermute(v, 'ws', [(s, (s - k) % WS) for s in range(WS)])]
    all_gather x7 -> x0, waiting for transfers between devices: 109 us -> none  [the longest x1 45.1 us: shards(): lax.all_gather(w_out, 'ws', axis=0, tiled=True)]
    all_to_all x4 -> x6, waiting for transfers between devices: 180 us -> 87.1 us  [the longest x1 62.1 us: shards(): lax.all_to_all(dx_send, 'exp', 0, 0, tiled=True).reshape(slots, width + 128)]
    ppermute x0 -> x41, starting transfers between devices: none -> 55.6 us  [the longest x24 33.8 us: from_peer(): return lax.ppermute(v, 'ws', [(s, (s - k) % WS) for s in range(WS)])]
    all_gather x5 -> x0, blocking collectives: 50.4 us -> none  [the longest x1 12.2 us: shards(): lax.all_gather(value_rows, 'ws', axis=0, tiled=True)]
    unnamed x23 -> x0, waiting for transfers between devices: 38.8 us -> none
  transfers between devices with their start and end apart: 22 -> 47, of which waited for: 14 -> 21; matrix products, arithmetic and copies ran while one was open for 17% -> 23% of each run, Pallas kernels for 0% -> 0%
where the time goes in v1:
time: 582 us; the launch traced here: 573 us
  waiting for transfers between devices  203 us (35%)
  matrix products  125 us (21%)
  starting transfers between devices  108 us (19%)
  local copies, waits for them, and re-layouts  90.9 us (16%)
  other arithmetic  42.8 us (7%)
    ppermute x24, waiting for transfers between devices, from_peer(): return lax.ppermute(v, 'ws', [(s, (s - k) % WS) for s in range(WS)])  73.4 us
    dot_general x18, matrix products, tdot(): lax.dot_general(a, b, (((0,), (0,)), ((), ())), preferred_element_type=F32)  62.5 us
    all_to_all x1, waiting for transfers between devices, shards(): lax.all_to_all(dx_send, 'exp', 0, 0, tiled=True).reshape(slots, width + 128)  62.1 us
    ppermute x15, waiting for transfers between devices, to_peer(): return lax.ppermute(v, 'ws', [(s, (s + k) % WS) for s in range(WS)])  39.4 us
    dot_general x15, matrix products, dot(): return jnp.dot(a, b, preferred_element_type=F32)  38.4 us
    ppermute x24, starting transfers between devices, from_peer(): return lax.ppermute(v, 'ws', [(s, (s - k) % WS) for s in range(WS)])  33.8 us
    all_to_all x2, waiting for transfers between devices, same_core(): return lax.all_to_all(v, 'exp', 0, 0, tiled=True, axis_index_groups=groups)  25 us
    unnamed x228, local copies, waits for them, and re-layouts  19.6 us
  transfers between devices with their start and end apart: 47, of which 21 were waited for; matrix products, arithmetic and copies ran while one was open for 23% of the time, Pallas kernels for 0%

profile of v1, /device:TPU:1, one launch (start us, length us, event | category | flops | bytes accessed | tf_op | source)
XLA Modules:
  0.0 573.2 jit_solution(17284975930172324365)
XLA Ops:
  14.7 3.8 convolution_convert_fusion
  18.5 10.2 %all-to-all-start.1 = ((bf16[32,48,1664]{2,1,0:T(8,128)(2,1)}), bf16[32,48,1664]{2,1,0:T(8,128)(2,1)}, u32[]{:S(2)}, u32[]{:S(2)}) async-start(bf16[32,48,1664]{2,1,0:T(8,128)(2,1)} %bitcast.199), calls=%async_computation.1 | async-start | bytes 10223616 | tf_op jit(solution)/shard_map/all_to_all | solution.py:174
  49.1 11.0 %collective-permute-done.2 = bf16[128,1536]{1,0:T(8,128)(2,1)} collective-permute-done((bf16[128,1536]{1,0:T(8,128)(2,1)S(1)}, bf16[128,1536]{1,0:T(8,128)(2,1)}, u32[]{:S(2)}, u32[]{:S(2)}) %collective-permute-start.2) | collective-permute-done | bytes 393248 | tf_op jit(solution)/shard_map/ppermute | solution.py:37
  66.8 4.2 collective-permute-done.8
  88.5 9.1 %collective-permute-done.9 = bf16[128,1536]{1,0:T(8,128)(2,1)S(1)} collective-permute-done((bf16[128,1536]{1,0:T(8,128)(2,1)S(1)}, bf16[128,1536]{1,0:T(8,128)(2,1)S(1)}, u32[]{:S(2)}, u32[]{:S(2)}) %collective-permute-start.9) | collective-permute-done | bytes 393248 | tf_op jit(solution)/shard_map/ppermute | solution.py:41
  97.6 6.4 %collective-permute-done.10 = bf16[128,1536]{1,0:T(8,128)(2,1)S(1)} collective-permute-done((bf16[128,1536]{1,0:T(8,128)(2,1)S(1)}, bf16[128,1536]{1,0:T(8,128)(2,1)S(1)}, u32[]{:S(2)}, u32[]{:S(2)}) %collective-permute-start.10) | collective-permute-done | bytes 393248 | tf_op jit(solution)/shard_map/ppermute | solution.py:41
  108.2 10.0 %all-to-all-start = ((bf16[32,48,1536]{2,1,0:T(8,128)(2,1)}), bf16[32,48,1536]{2,1,0:T(8,128)(2,1)}, u32[]{:S(2)}, u32[]{:S(2)}) async-start(bf16[32,48,1536]{2,1,0:T(8,128)(2,1)} %bitcast.200), calls=%async_computation | async-start | bytes 9437184 | tf_op jit(solution)/shard_map/all_to_all | solution.py:222
  125.9 13.1 %collective-permute-done.12 = bf16[1536,128]{1,0:T(8,128)(2,1)S(1)} collective-permute-done((bf16[1536,128]{1,0:T(8,128)(2,1)S(1)}, bf16[1536,128]{1,0:T(8,128)(2,1)S(1)}, u32[]{:S(2)}, u32[]{:S(2)}) %collective-permute-start.12) | collective-permute-done | bytes 393248 | tf_op jit(solution)/shard_map/ppermute | solution.py:37
  139.0 4.0 collective-permute-start.15
  145.1 10.9 %collective-permute-done.15 = bf16[1536,128]{1,0:T(8,128)(2,1)S(1)} collective-permute-done((bf16[1536,128]{1,0:T(8,128)(2,1)}, bf16[1536,128]{1,0:T(8,128)(2,1)S(1)}, u32[]{:S(2)}, u32[]{:S(2)}) %collective-permute-start.15) | collective-permute-done | bytes 393248 | tf_op jit(solution)/shard_map/ppermute | solution.py:37
  156.0 3.9 collective-permute-start.18
  160.2 12.6 %collective-permute-done.18 = bf16[128,1536]{1,0:T(8,128)(2,1)S(1)} collective-permute-done((bf16[128,1536]{1,0:T(8,128)(2,1)S(1)}, bf16[128,1536]{1,0:T(8,128)(2,1)S(1)}, u32[]{:S(2)}, u32[]{:S(2)}) %collective-permute-start.18) | collective-permute-done | bytes 393248 | tf_op jit(solution)/shard_map/ppermute | solution.py:37
  176.5 4.7 slice.353
  182.4 6.7 %copy.191 = bf16[1536,1536]{0,1:T(8,128)(2,1)} copy(bf16[1536,1536]{1,0:T(8,128)(2,1)} %slice.353) | data formatting | bytes 9437184
  189.1 3.9 fusion.157
  193.2 4.6 fusion.158
  200.7 6.4 %multiply_convert_fusion.1 = (bf16[1536,512]{1,0:T(8,128)(2,1)S(1)}, bf16[1536,512]{1,0:T(8,128)(2,1)S(1)}, bf16[1536,512]{1,0:T(8,128)(2,1)S(1)}) fusion(f32[1536,512]{1,0:T(8,128)S(1)} %fusion.26, f32[1536,512]{1,0:T(8,128)S(1)} %fusion.158, bf16[1536,1536]{1,0:T(8,128)(2,1)} %bitcast.32, bf16[1536,512]{1,0:T(8,128)(2,1)S(1)} %copy-done.66), kind=kOutput, calls=%fused_computation.36 | convolution fusion | flops 2428502016 | bytes 17301504 | tf_op jit(solution)/shard_map/dot_general | solution.py:20
  207.1 4.6 fusion.1
  217.4 8.2 %maximum_maximum_fusion.1 = bf16[1536,1664]{0,1:T(8,128)(2,1)} fusion(bf16[1536,32]{0,1:T(8,128)(2,1)S(1)} %get-tuple-element.168, bf16[1536,32]{0,1:T(8,128)(2,1)S(1)} %get-tuple-element.167, bf16[1536,1536]{0,1:T(8,128)(2,1)S(1)} %add_convert_fusion, bf16[1664]{0:T(1024)(128)(2,1)S(1)} %pad.37.clone), kind=kLoop, calls=%fused_computation.19 | loop fusion | flops 20447232 | bytes 10030336 | tf_op jit(solution)/shard_map/concatenate | solution.py:254
  225.6 7.7 %copy.163 = bf16[1536,1664]{1,0:T(8,128)(2,1)} copy(bf16[1536,1664]{0,1:T(8,128)(2,1)} %maximum_maximum_fusion.1) | data formatting | bytes 10223616 | tf_op jit(solution)/shard_map/concatenate | solution.py:254
  233.4 8.2 %all-to-all-start.2 = ((bf16[32,48,1664]{2,1,0:T(8,128)(2,1)}), bf16[32,48,1664]{2,1,0:T(8,128)(2,1)}, u32[]{:S(2)}, u32[]{:S(2)}) async-start(bf16[32,48,1664]{2,1,0:T(8,128)(2,1)} %bitcast.201), calls=%async_computation.2 | async-start | bytes 10223616 | tf_op jit(solution)/shard_map/all_to_all | solution.py:255
  242.6 62.1 %all-to-all-done.2 = bf16[32,48,1664]{2,1,0:T(8,128)(2,1)} async-done(((bf16[32,48,1664]{2,1,0:T(8,128)(2,1)}), bf16[32,48,1664]{2,1,0:T(8,128)(2,1)}, u32[]{:S(2)}, u32[]{:S(2)}) %all-to-all-start.2) | async-done | bytes 5111840 | tf_op jit(solution)/shard_map/all_to_all | solution.py:255
  318.4 6.2 %collective-permute-done.23 = bf16[128,1536]{1,0:T(8,128)(2,1)S(1)} collective-permute-done((bf16[128,1536]{1,0:T(8,128)(2,1)S(1)}, bf16[128,1536]{1,0:T(8,128)(2,1)S(1)}, u32[]{:S(2)}, u32[]{:S(2)}) %collective-permute-start.23) | collective-permute-done | bytes 393248 | tf_op jit(solution)/shard_map/ppermute | solution.py:37
  324.6 8.9 %collective-permute-done.22 = bf16[128,1536]{1,0:T(8,128)(2,1)S(1)} collective-permute-done((bf16[128,1536]{1,0:T(8,128)(2,1)S(1)}, bf16[128,1536]{1,0:T(8,128)(2,1)S(1)}, u32[]{:S(2)}, u32[]{:S(2)}) %collective-permute-start.22) | collective-permute-done | bytes 393248 | tf_op jit(solution)/shard_map/ppermute | solution.py:37
  345.0 4.6 fusion.11
  349.6 4.5 fusion.61
  355.0 14.4 %concatenate.103 = f32[1536,768]{0,1:T(8,128)} concatenate(f32[1536,640]{0,1:T(8,128)} %fusion.61, f32[1536,32]{0,1:T(8,128)S(1)} %copy-done.31, f32[1536,1]{0,1:T(1,128)S(1)} %copy-done.74, f32[1536,1]{0,1:T(1,128)S(1)} %broadcast_in_dim.250, f32[1536,94]{0,1:T(8,128)} %broadcast_in_dim.251), dimensions={1} | concatenate | bytes 9437184 | tf_op jit(solution)/shard_map/concatenate | solution.py:313
  369.5 4.5 maximum_maximum_fusion
  381.6 3.9 copy.174
  388.3 8.6 %all-to-all-start.4 = ((bf16[16,6,24,384]{3,2,1,0:T(8,128)(2,1)}), bf16[16,6,24,384]{3,2,1,0:T(8,128)(2,1)}, u32[]{:S(2)}, u32[]{:S(2)}) async-start(bf16[16,6,24,384]{3,2,1,0:T(8,128)(2,1)} %copy.175), calls=%async_computation.4 | async-start | bytes 3538944 | tf_op jit(solution)/shard_map/all_to_all | solution.py:50
  396.9 25.0 %all-to-all-done.4 = bf16[16,6,24,384]{3,2,1,0:T(8,128)(2,1)} async-done(((bf16[16,6,24,384]{3,2,1,0:T(8,128)(2,1)}), bf16[16,6,24,384]{3,2,1,0:T(8,128)(2,1)}, u32[]{:S(2)}, u32[]{:S(2)}) %all-to-all-start.4) | async-done | bytes 1769504 | tf_op jit(solution)/shard_map/all_to_all | solution.py:50
  432.9 5.2 all-to-all-start.5
  439.6 4.7 convolution_convert_fusion.6
  444.3 4.6 convolution_convert_fusion.3
  448.9 3.8 convolution_convert_fusion.4
  456.2 6.6 %copy.164 = bf16[1536,1536]{1,0:T(8,128)(2,1)} copy(bf16[1536,1536]{0,1:T(8,128)(2,1)} %get-tuple-element.22) | data formatting | bytes 9437184 | tf_op jit(solution)/shard_map/optimization_barrier | solution.py:256
  462.8 10.4 %all-to-all-start.3 = ((bf16[32,48,1536]{2,1,0:T(8,128)(2,1)}), bf16[32,48,1536]{2,1,0:T(8,128)(2,1)}, u32[]{:S(2)}, u32[]{:S(2)}) async-start(bf16[32,48,1536]{2,1,0:T(8,128)(2,1)} %bitcast.202), calls=%async_computation.3 | async-start | bytes 9437184 | tf_op jit(solution)/shard_map/all_to_all | solution.py:257
  473.2 4.0 convolution_convert_fusion.5
  477.5 3.9 collective-permute-start.36
  481.5 4.0 fusion.31
  485.6 4.2 fusion.28
  489.8 3.9 convolution_convert_fusion.7
  503.5 4.7 add_bitcast_fusion.1
  509.6 6.2 %collective-permute-done.39 = bf16[128,1536]{1,0:T(8,128)(2,1)S(1)} collective-permute-done((bf16[128,1536]{1,0:T(8,128)(2,1)S(1)}, bf16[128,1536]{1,0:T(8,128)(2,1)S(1)}, u32[]{:S(2)}, u32[]{:S(2)}) %collective-permute-start.39) | collective-permute-done | bytes 393248 | tf_op jit(solution)/shard_map/ppermute | solution.py:41
  525.4 7.1 %collective-permute-done.33 = bf16[1536,128]{1,0:T(8,128)(2,1)S(1)} collective-permute-done((bf16[1536,128]{1,0:T(8,128)(2,1)S(1)}, bf16[1536,128]{1,0:T(8,128)(2,1)S(1)}, u32[]{:S(2)}, u32[]{:S(2)}) %collective-permute-start.33) | collective-permute-done | bytes 393248 | tf_op jit(solution)/shard_map/ppermute | solution.py:41
  532.5 4.7 add_bitcast_fusion.2
  542.1 7.2 %collective-permute-done.25 = bf16[128,1536]{1,0:T(8,128)(2,1)S(1)} collective-permute-done((bf16[128,1536]{1,0:T(8,128)(2,1)S(1)}, bf16[128,1536]{1,0:T(8,128)(2,1)S(1)}, u32[]{:S(2)}, u32[]{:S(2)}) %collective-permute-start.25) | collective-permute-done | bytes 393248 | tf_op jit(solution)/shard_map/ppermute | solution.py:41
  554.5 3.9 fusion.37
  (443 shorter events, 184.0 us)
Async XLA Ops:
  4.2 35.0 %collective-permute-start.4 = (bf16[384,128]{1,0:T(8,128)(2,1)}, bf16[384,128]{1,0:T(8,128)(2,1)}, u32[]{:S(2)}, u32[]{:S(2)}) collective-permute-start(bf16[384,128]{1,0:T(8,128)(2,1)} %get-tuple-element.99), channel_id=1, source_target_pairs={{0,2},{1,3},{2,0},{3,1},{4,6},{5,7},{6,4},{7,5},{8,10},{9,11},{10,... | collective-permute-start | bytes 294920 | tf_op jit(solution)/shard_map/ppermute | solution.py:37
  7.9 30.3 %collective-permute-start.3 = (bf16[384,128]{1,0:T(8,128)(2,1)}, bf16[384,128]{1,0:T(8,128)(2,1)}, u32[]{:S(2)}, u32[]{:S(2)}) collective-permute-start(bf16[384,128]{1,0:T(8,128)(2,1)} %get-tuple-element.99), channel_id=1, source_target_pairs={{0,3},{1,0},{2,1},{3,2},{4,7},{5,4},{6,5},{7,6},{8,11},{9,8},{10,9... | collective-permute-start | bytes 294920 | tf_op jit(solution)/shard_map/ppermute | solution.py:37
  8.7 33.4 %collective-permute-start.5 = (bf16[384,128]{1,0:T(8,128)(2,1)}, bf16[384,128]{1,0:T(8,128)(2,1)}, u32[]{:S(2)}, u32[]{:S(2)}) collective-permute-start(bf16[384,128]{1,0:T(8,128)(2,1)} %get-tuple-element.99), channel_id=1, source_target_pairs={{0,1},{1,2},{2,3},{3,0},{4,5},{5,6},{6,7},{7,4},{8,9},{9,10},{10,1... | collective-permute-start | bytes 294920 | tf_op jit(solution)/shard_map/ppermute | solution.py:37
  9.4 39.4 %collective-permute-start.1 = (bf16[128,1536]{1,0:T(8,128)(2,1)}, bf16[128,1536]{1,0:T(8,128)(2,1)}, u32[]{:S(2)}, u32[]{:S(2)}) collective-permute-start(bf16[128,1536]{1,0:T(8,128)(2,1)} %param.15), channel_id=1, source_target_pairs={{0,2},{1,3},{2,0},{3,1},{4,6},{5,7},{6,4},{7,5},{8,10},{9,11},{10,... | collective-permute-start | bytes 1179656 | tf_op jit(solution)/shard_map/ppermute | solution.py:37
  10.1 39.0 %collective-permute-start = (bf16[128,1536]{1,0:T(8,128)(2,1)}, bf16[128,1536]{1,0:T(8,128)(2,1)}, u32[]{:S(2)}, u32[]{:S(2)}) collective-permute-start(bf16[128,1536]{1,0:T(8,128)(2,1)} %param.15), channel_id=1, source_target_pairs={{0,3},{1,0},{2,1},{3,2},{4,7},{5,4},{6,5},{7,6},{8,11},{9,8},{10,9... | collective-permute-start | bytes 1179656 | tf_op jit(solution)/shard_map/ppermute | solution.py:37
  13.5 291.1 %copy-start.8 = (pred[128,1536]{1,0:T(32,128)(4,1)}, pred[128,1536]{1,0:T(32,128)(4,1)S(1)}, u32[]{:S(2)}) copy-start(pred[128,1536]{1,0:T(32,128)(4,1)S(1)} %convolution_compare_fusion) | copy-start | bytes 589828
  18.5 89.6 %all-to-all-start.1 = ((bf16[32,48,1664]{2,1,0:T(8,128)(2,1)}), bf16[32,48,1664]{2,1,0:T(8,128)(2,1)}, u32[]{:S(2)}, u32[]{:S(2)}) async-start(bf16[32,48,1664]{2,1,0:T(8,128)(2,1)} %bitcast.199), calls=%async_computation.1 | async-start | bytes 10223616 | tf_op jit(solution)/shard_map/all_to_all | solution.py:174
  38.3 21.8 %collective-permute-start.2 = (bf16[128,1536]{1,0:T(8,128)(2,1)S(1)}, bf16[128,1536]{1,0:T(8,128)(2,1)}, u32[]{:S(2)}, u32[]{:S(2)}) collective-permute-start(bf16[128,1536]{1,0:T(8,128)(2,1)S(1)} %copy-done.3), channel_id=1, source_target_pairs={{0,1},{1,2},{2,3},{3,0},{4,5},{5,6},{6,7},{7,4},{8,9},{9,10},{10,1... | collective-permute-start | bytes 1179656 | tf_op jit(solution)/shard_map/ppermute | solution.py:37
  39.2 26.8 %collective-permute-start.7 = (bf16[384,640]{1,0:T(8,128)(2,1)}, bf16[384,640]{1,0:T(8,128)(2,1)S(1)}, u32[]{:S(2)}, u32[]{:S(2)}) collective-permute-start(bf16[384,640]{1,0:T(8,128)(2,1)} %pad_maximum_fusion.8), channel_id=1, source_target_pairs={{0,2},{1,3},{2,0},{3,1},{4,6},{5,7},{6,4},{7,5},{8,10},{9,11},{10,... | collective-permute-start | bytes 1474568 | tf_op jit(solution)/shard_map/ppermute | solution.py:37
  42.1 22.1 %collective-permute-start.6 = (bf16[384,640]{1,0:T(8,128)(2,1)}, bf16[384,640]{1,0:T(8,128)(2,1)}, u32[]{:S(2)}, u32[]{:S(2)}) collective-permute-start(bf16[384,640]{1,0:T(8,128)(2,1)} %pad_maximum_fusion.7), channel_id=1, source_target_pairs={{0,3},{1,0},{2,1},{3,2},{4,7},{5,4},{6,5},{7,6},{8,11},{9,8},{10,9... | collective-permute-start | bytes 1474568 | tf_op jit(solution)/shard_map/ppermute | solution.py:37
  48.8 22.2 %collective-permute-start.8 = (bf16[384,640]{1,0:T(8,128)(2,1)}, bf16[384,640]{1,0:T(8,128)(2,1)S(1)}, u32[]{:S(2)}, u32[]{:S(2)}) collective-permute-start(bf16[384,640]{1,0:T(8,128)(2,1)} %pad_maximum_fusion.9), channel_id=1, source_target_pairs={{0,1},{1,2},{2,3},{3,0},{4,5},{5,6},{6,7},{7,4},{8,9},{9,10},{10,1... | collective-permute-start | bytes 1474568 | tf_op jit(solution)/shard_map/ppermute | solution.py:37
  85.7 11.9 %collective-permute-start.9 = (bf16[128,1536]{1,0:T(8,128)(2,1)S(1)}, bf16[128,1536]{1,0:T(8,128)(2,1)S(1)}, u32[]{:S(2)}, u32[]{:S(2)}) collective-permute-start(bf16[128,1536]{1,0:T(8,128)(2,1)S(1)} %get-tuple-element.126), channel_id=1, source_target_pairs={{0,1},{1,2},{2,3},{3,0},{4,5},{5,6},{6,7},{7,4},{8,9},{9,10},{10,1... | collective-permute-start | bytes 1179656 | tf_op jit(solution)/shard_map/ppermute | solution.py:41
  85.8 11.8 %collective-permute-start.11 = (bf16[128,1536]{1,0:T(8,128)(2,1)S(1)}, bf16[128,1536]{1,0:T(8,128)(2,1)S(1)}, u32[]{:S(2)}, u32[]{:S(2)}) collective-permute-start(bf16[128,1536]{1,0:T(8,128)(2,1)S(1)} %get-tuple-element.127), channel_id=1, source_target_pairs={{0,3},{1,0},{2,1},{3,2},{4,7},{5,4},{6,5},{7,6},{8,11},{9,8},{10,9... | collective-permute-start | bytes 1179656 | tf_op jit(solution)/shard_map/ppermute | solution.py:41
  88.5 15.5 %collective-permute-start.10 = (bf16[128,1536]{1,0:T(8,128)(2,1)S(1)}, bf16[128,1536]{1,0:T(8,128)(2,1)S(1)}, u32[]{:S(2)}, u32[]{:S(2)}) collective-permute-start(bf16[128,1536]{1,0:T(8,128)(2,1)S(1)} %get-tuple-element.128), channel_id=1, source_target_pairs={{0,2},{1,3},{2,0},{3,1},{4,6},{5,7},{6,4},{7,5},{8,10},{9,11},{10,... | collective-permute-start | bytes 1179656 | tf_op jit(solution)/shard_map/ppermute | solution.py:41
  108.2 80.9 %all-to-all-start = ((bf16[32,48,1536]{2,1,0:T(8,128)(2,1)}), bf16[32,48,1536]{2,1,0:T(8,128)(2,1)}, u32[]{:S(2)}, u32[]{:S(2)}) async-start(bf16[32,48,1536]{2,1,0:T(8,128)(2,1)} %bitcast.200), calls=%async_computation | async-start | bytes 9437184 | tf_op jit(solution)/shard_map/all_to_all | solution.py:222
  118.3 25.4 %collective-permute-start.14 = (bf16[1536,128]{1,0:T(8,128)(2,1)S(1)}, bf16[1536,128]{1,0:T(8,128)(2,1)S(1)}, u32[]{:S(2)}, u32[]{:S(2)}) collective-permute-start(bf16[1536,128]{1,0:T(8,128)(2,1)S(1)} %bitcast.242), channel_id=1, source_target_pairs={{0,1},{1,2},{2,3},{3,0},{4,5},{5,6},{6,7},{7,4},{8,9},{9,10},{10,1... | collective-permute-start | bytes 1179656 | tf_op jit(solution)/shard_map/ppermute | solution.py:37
  118.9 24.2 %collective-permute-start.13 = (bf16[1536,128]{1,0:T(8,128)(2,1)S(1)}, bf16[1536,128]{1,0:T(8,128)(2,1)S(1)}, u32[]{:S(2)}, u32[]{:S(2)}) collective-permute-start(bf16[1536,128]{1,0:T(8,128)(2,1)S(1)} %bitcast.243), channel_id=1, source_target_pairs={{0,2},{1,3},{2,0},{3,1},{4,6},{5,7},{6,4},{7,5},{8,10},{9,11},{10,... | collective-permute-start | bytes 1179656 | tf_op jit(solution)/shard_map/ppermute | solution.py:37
  122.2 16.8 %collective-permute-start.12 = (bf16[1536,128]{1,0:T(8,128)(2,1)S(1)}, bf16[1536,128]{1,0:T(8,128)(2,1)S(1)}, u32[]{:S(2)}, u32[]{:S(2)}) collective-permute-start(bf16[1536,128]{1,0:T(8,128)(2,1)S(1)} %bitcast.244), channel_id=1, source_target_pairs={{0,3},{1,0},{2,1},{3,2},{4,7},{5,4},{6,5},{7,6},{8,11},{9,8},{10,9... | collective-permute-start | bytes 1179656 | tf_op jit(solution)/shard_map/ppermute | solution.py:37
  122.2 37.9 %collective-permute-start.17 = (bf16[1536,128]{1,0:T(8,128)(2,1)}, bf16[1536,128]{1,0:T(8,128)(2,1)S(1)}, u32[]{:S(2)}, u32[]{:S(2)}) collective-permute-start(bf16[1536,128]{1,0:T(8,128)(2,1)} %bitcast.246), channel_id=1, source_target_pairs={{0,1},{1,2},{2,3},{3,0},{4,5},{5,6},{6,7},{7,4},{8,9},{9,10},{10,1... | collective-permute-start | bytes 1179656 | tf_op jit(solution)/shard_map/ppermute | solution.py:37
  123.7 36.3 %collective-permute-start.16 = (bf16[1536,128]{1,0:T(8,128)(2,1)}, bf16[1536,128]{1,0:T(8,128)(2,1)S(1)}, u32[]{:S(2)}, u32[]{:S(2)}) collective-permute-start(bf16[1536,128]{1,0:T(8,128)(2,1)} %bitcast.247), channel_id=1, source_target_pairs={{0,2},{1,3},{2,0},{3,1},{4,6},{5,7},{6,4},{7,5},{8,10},{9,11},{10,... | collective-permute-start | bytes 1179656 | tf_op jit(solution)/shard_map/ppermute | solution.py:37
  139.0 17.0 %collective-permute-start.15 = (bf16[1536,128]{1,0:T(8,128)(2,1)}, bf16[1536,128]{1,0:T(8,128)(2,1)S(1)}, u32[]{:S(2)}, u32[]{:S(2)}) collective-permute-start(bf16[1536,128]{1,0:T(8,128)(2,1)} %bitcast.249), channel_id=1, source_target_pairs={{0,3},{1,0},{2,1},{3,2},{4,7},{5,4},{6,5},{7,6},{8,11},{9,8},{10,9... | collective-permute-start | bytes 1179656 | tf_op jit(solution)/shard_map/ppermute | solution.py:37
  143.1 30.4 %collective-permute-start.20 = (bf16[128,1536]{1,0:T(8,128)(2,1)S(1)}, bf16[128,1536]{1,0:T(8,128)(2,1)S(1)}, u32[]{:S(2)}, u32[]{:S(2)}) collective-permute-start(bf16[128,1536]{1,0:T(8,128)(2,1)S(1)} %bitcast.251), channel_id=1, source_target_pairs={{0,1},{1,2},{2,3},{3,0},{4,5},{5,6},{6,7},{7,4},{8,9},{9,10},{10,1... | collective-permute-start | bytes 1179656 | tf_op jit(solution)/shard_map/ppermute | solution.py:37
  143.7 29.8 %collective-permute-start.19 = (bf16[128,1536]{1,0:T(8,128)(2,1)S(1)}, bf16[128,1536]{1,0:T(8,128)(2,1)S(1)}, u32[]{:S(2)}, u32[]{:S(2)}) collective-permute-start(bf16[128,1536]{1,0:T(8,128)(2,1)S(1)} %bitcast.252), channel_id=1, source_target_pairs={{0,2},{1,3},{2,0},{3,1},{4,6},{5,7},{6,4},{7,5},{8,10},{9,11},{10,... | collective-permute-start | bytes 1179656 | tf_op jit(solution)/shard_map/ppermute | solution.py:37
  156.0 16.8 %collective-permute-start.18 = (bf16[128,1536]{1,0:T(8,128)(2,1)S(1)}, bf16[128,1536]{1,0:T(8,128)(2,1)S(1)}, u32[]{:S(2)}, u32[]{:S(2)}) collective-permute-start(bf16[128,1536]{1,0:T(8,128)(2,1)S(1)} %bitcast.253), channel_id=1, source_target_pairs={{0,3},{1,0},{2,1},{3,2},{4,7},{5,4},{6,5},{7,6},{8,11},{9,8},{10,9... | collective-permute-start | bytes 1179656 | tf_op jit(solution)/shard_map/ppermute | solution.py:37
  233.4 71.3 %all-to-all-start.2 = ((bf16[32,48,1664]{2,1,0:T(8,128)(2,1)}), bf16[32,48,1664]{2,1,0:T(8,128)(2,1)}, u32[]{:S(2)}, u32[]{:S(2)}) async-start(bf16[32,48,1664]{2,1,0:T(8,128)(2,1)} %bitcast.201), calls=%async_computation.2 | async-start | bytes 10223616 | tf_op jit(solution)/shard_map/all_to_all | solution.py:255
  313.5 11.0 %collective-permute-start.23 = (bf16[128,1536]{1,0:T(8,128)(2,1)S(1)}, bf16[128,1536]{1,0:T(8,128)(2,1)S(1)}, u32[]{:S(2)}, u32[]{:S(2)}) collective-permute-start(bf16[128,1536]{1,0:T(8,128)(2,1)S(1)} %fusion.145), channel_id=1, source_target_pairs={{0,1},{1,2},{2,3},{3,0},{4,5},{5,6},{6,7},{7,4},{8,9},{9,10},{10,1... | collective-permute-start | bytes 1179656 | tf_op jit(solution)/shard_map/ppermute | solution.py:37
  313.6 19.8 %collective-permute-start.22 = (bf16[128,1536]{1,0:T(8,128)(2,1)S(1)}, bf16[128,1536]{1,0:T(8,128)(2,1)S(1)}, u32[]{:S(2)}, u32[]{:S(2)}) collective-permute-start(bf16[128,1536]{1,0:T(8,128)(2,1)S(1)} %fusion.145), channel_id=1, source_target_pairs={{0,2},{1,3},{2,0},{3,1},{4,6},{5,7},{6,4},{7,5},{8,10},{9,11},{10,... | collective-permute-start | bytes 1179656 | tf_op jit(solution)/shard_map/ppermute | solution.py:37
  316.7 17.1 %collective-permute-start.21 = (bf16[128,1536]{1,0:T(8,128)(2,1)S(1)}, bf16[128,1536]{1,0:T(8,128)(2,1)S(1)}, u32[]{:S(2)}, u32[]{:S(2)}) collective-permute-start(bf16[128,1536]{1,0:T(8,128)(2,1)S(1)} %fusion.145), channel_id=1, source_target_pairs={{0,3},{1,0},{2,1},{3,2},{4,7},{5,4},{6,5},{7,6},{8,11},{9,8},{10,9... | collective-permute-start | bytes 1179656 | tf_op jit(solution)/shard_map/ppermute | solution.py:37
  374.3 5.4 collective-permute-start.27
  388.3 33.6 %all-to-all-start.4 = ((bf16[16,6,24,384]{3,2,1,0:T(8,128)(2,1)}), bf16[16,6,24,384]{3,2,1,0:T(8,128)(2,1)}, u32[]{:S(2)}, u32[]{:S(2)}) async-start(bf16[16,6,24,384]{3,2,1,0:T(8,128)(2,1)} %copy.175), calls=%async_computation.4 | async-start | bytes 3538944 | tf_op jit(solution)/shard_map/all_to_all | solution.py:50
  423.7 4.8 collective-permute-start.28
  427.3 4.2 collective-permute-start.30
  427.3 4.2 collective-permute-start.29
  432.9 29.9 %all-to-all-start.5 = ((bf16[16,6,24,384]{3,2,1,0:T(8,128)(2,1)}), bf16[16,6,24,384]{3,2,1,0:T(8,128)(2,1)}, u32[]{:S(2)}, u32[]{:S(2)}) async-start(bf16[16,6,24,384]{3,2,1,0:T(8,128)(2,1)} %broadcast_in_dim.255), calls=%async_computation.5 | async-start | bytes 3538944 | tf_op jit(solution)/shard_map/all_to_all | solution.py:50
  462.8 88.6 %all-to-all-start.3 = ((bf16[32,48,1536]{2,1,0:T(8,128)(2,1)}), bf16[32,48,1536]{2,1,0:T(8,128)(2,1)}, u32[]{:S(2)}, u32[]{:S(2)}) async-start(bf16[32,48,1536]{2,1,0:T(8,128)(2,1)} %bitcast.202), calls=%async_computation.3 | async-start | bytes 9437184 | tf_op jit(solution)/shard_map/all_to_all | solution.py:257
  477.2 21.8 %collective-permute-start.35 = (bf16[1536,128]{1,0:T(8,128)(2,1)S(1)}, bf16[1536,128]{1,0:T(8,128)(2,1)S(1)}, u32[]{:S(2)}, u32[]{:S(2)}) collective-permute-start(bf16[1536,128]{1,0:T(8,128)(2,1)S(1)} %convolution_convert_fusion.5), channel_id=1, source_target_pairs={{0,1},{1,2},{2,3},{3,0},{4,5},{5,6},{6,7},{7,4},{8,9},{9,10},{10,1... | collective-permute-start | bytes 1179656 | tf_op jit(solution)/shard_map/ppermute | solution.py:41
  477.5 24.1 %collective-permute-start.36 = (bf16[1536,128]{1,0:T(8,128)(2,1)S(1)}, bf16[1536,128]{1,0:T(8,128)(2,1)S(1)}, u32[]{:S(2)}, u32[]{:S(2)}) collective-permute-start(bf16[1536,128]{1,0:T(8,128)(2,1)S(1)} %convolution_convert_fusion.4), channel_id=1, source_target_pairs={{0,2},{1,3},{2,0},{3,1},{4,6},{5,7},{6,4},{7,5},{8,10},{9,11},{10,... | collective-permute-start | bytes 1179656 | tf_op jit(solution)/shard_map/ppermute | solution.py:41
  481.3 20.2 %collective-permute-start.37 = (bf16[1536,128]{1,0:T(8,128)(2,1)}, bf16[1536,128]{1,0:T(8,128)(2,1)S(1)}, u32[]{:S(2)}, u32[]{:S(2)}) collective-permute-start(bf16[1536,128]{1,0:T(8,128)(2,1)} %convolution_convert_fusion.3), channel_id=1, source_target_pairs={{0,3},{1,0},{2,1},{3,2},{4,7},{5,4},{6,5},{7,6},{8,11},{9,8},{10,9... | collective-permute-start | bytes 1179656 | tf_op jit(solution)/shard_map/ppermute | solution.py:41
  493.7 14.7 %collective-permute-start.38 = (bf16[128,1536]{1,0:T(8,128)(2,1)S(1)}, bf16[128,1536]{1,0:T(8,128)(2,1)S(1)}, u32[]{:S(2)}, u32[]{:S(2)}) collective-permute-start(bf16[128,1536]{1,0:T(8,128)(2,1)S(1)} %fusion.28), channel_id=1, source_target_pairs={{0,1},{1,2},{2,3},{3,0},{4,5},{5,6},{6,7},{7,4},{8,9},{9,10},{10,1... | collective-permute-start | bytes 1179656 | tf_op jit(solution)/shard_map/ppermute | solution.py:41
  495.2 20.5 %collective-permute-start.39 = (bf16[128,1536]{1,0:T(8,128)(2,1)S(1)}, bf16[128,1536]{1,0:T(8,128)(2,1)S(1)}, u32[]{:S(2)}, u32[]{:S(2)}) collective-permute-start(bf16[128,1536]{1,0:T(8,128)(2,1)S(1)} %fusion.31), channel_id=1, source_target_pairs={{0,2},{1,3},{2,0},{3,1},{4,6},{5,7},{6,4},{7,5},{8,10},{9,11},{10,... | collective-permute-start | bytes 1179656 | tf_op jit(solution)/shard_map/ppermute | solution.py:41
  499.0 16.7 %collective-permute-start.40 = (bf16[128,1536]{1,0:T(8,128)(2,1)}, bf16[128,1536]{1,0:T(8,128)(2,1)S(1)}, u32[]{:S(2)}, u32[]{:S(2)}) collective-permute-start(bf16[128,1536]{1,0:T(8,128)(2,1)} %fusion.34), channel_id=1, source_target_pairs={{0,3},{1,0},{2,1},{3,2},{4,7},{5,4},{6,5},{7,6},{8,11},{9,8},{10,9... | collective-permute-start | bytes 1179656 | tf_op jit(solution)/shard_map/ppermute | solution.py:41
  501.6 23.6 %collective-permute-start.32 = (bf16[1536,128]{1,0:T(8,128)(2,1)S(1)}, bf16[1536,128]{1,0:T(8,128)(2,1)S(1)}, u32[]{:S(2)}, u32[]{:S(2)}) collective-permute-start(bf16[1536,128]{1,0:T(8,128)(2,1)S(1)} %convolution_convert_fusion.8), channel_id=1, source_target_pairs={{0,1},{1,2},{2,3},{3,0},{4,5},{5,6},{6,7},{7,4},{8,9},{9,10},{10,1... | collective-permute-start | bytes 1179656 | tf_op jit(solution)/shard_map/ppermute | solution.py:41
  501.6 30.9 %collective-permute-start.33 = (bf16[1536,128]{1,0:T(8,128)(2,1)S(1)}, bf16[1536,128]{1,0:T(8,128)(2,1)S(1)}, u32[]{:S(2)}, u32[]{:S(2)}) collective-permute-start(bf16[1536,128]{1,0:T(8,128)(2,1)S(1)} %convolution_convert_fusion.7), channel_id=1, source_target_pairs={{0,2},{1,3},{2,0},{3,1},{4,6},{5,7},{6,4},{7,5},{8,10},{9,11},{10,... | collective-permute-start | bytes 1179656 | tf_op jit(solution)/shard_map/ppermute | solution.py:41
  508.4 24.1 %collective-permute-start.34 = (bf16[1536,128]{1,0:T(8,128)(2,1)S(1)}, bf16[1536,128]{1,0:T(8,128)(2,1)S(1)}, u32[]{:S(2)}, u32[]{:S(2)}) collective-permute-start(bf16[1536,128]{1,0:T(8,128)(2,1)S(1)} %copy-done.88), channel_id=1, source_target_pairs={{0,3},{1,0},{2,1},{3,2},{4,7},{5,4},{6,5},{7,6},{8,11},{9,8},{10,9... | collective-permute-start | bytes 1179656 | tf_op jit(solution)/shard_map/ppermute | solution.py:41
  518.5 23.6 %collective-permute-start.24 = (bf16[128,1536]{1,0:T(8,128)(2,1)S(1)}, bf16[128,1536]{1,0:T(8,128)(2,1)S(1)}, u32[]{:S(2)}, u32[]{:S(2)}) collective-permute-start(bf16[128,1536]{1,0:T(8,128)(2,1)S(1)} %get-tuple-element.123), channel_id=1, source_target_pairs={{0,1},{1,2},{2,3},{3,0},{4,5},{5,6},{6,7},{7,4},{8,9},{9,10},{10,1... | collective-permute-start | bytes 1179656 | tf_op jit(solution)/shard_map/ppermute | solution.py:41
  520.7 21.4 %collective-permute-start.26 = (bf16[128,1536]{1,0:T(8,128)(2,1)S(1)}, bf16[128,1536]{1,0:T(8,128)(2,1)S(1)}, u32[]{:S(2)}, u32[]{:S(2)}) collective-permute-start(bf16[128,1536]{1,0:T(8,128)(2,1)S(1)} %get-tuple-element.124), channel_id=1, source_target_pairs={{0,3},{1,0},{2,1},{3,2},{4,7},{5,4},{6,5},{7,6},{8,11},{9,8},{10,9... | collective-permute-start | bytes 1179656 | tf_op jit(solution)/shard_map/ppermute | solution.py:41
  525.2 24.2 %collective-permute-start.25 = (bf16[128,1536]{1,0:T(8,128)(2,1)S(1)}, bf16[128,1536]{1,0:T(8,128)(2,1)S(1)}, u32[]{:S(2)}, u32[]{:S(2)}) collective-permute-start(bf16[128,1536]{1,0:T(8,128)(2,1)S(1)} %get-tuple-element.125), channel_id=1, source_target_pairs={{0,2},{1,3},{2,0},{3,1},{4,6},{5,7},{6,4},{7,5},{8,10},{9,11},{10,... | collective-permute-start | bytes 1179656 | tf_op jit(solution)/shard_map/ppermute | solution.py:41
  540.3 18.2 %collective-permute-start.31 = (bf16[16,6,24,384]{3,2,0,1:T(8,128)(2,1)}, bf16[16,6,24,384]{3,2,0,1:T(8,128)(2,1)}, u32[]{:S(2)}, u32[]{:S(2)}) collective-permute-start(bf16[16,6,24,384]{3,2,0,1:T(8,128)(2,1)} %copy.176), channel_id=1, source_target_pairs={{0,4},{4,0},{8,12},{12,8},{16,20},{20,16},{24,28},{28,24},{32,36},... | collective-permute-start | bytes 5308424 | tf_op jit(solution)/shard_map/ppermute | solution.py:45
  (106 other events, 1185.1 us)

commit v2 on v1

--- a/solution.py
+++ b/solution.py
@@ -1,6 +1,10 @@
+import functools
+
 import jax
 import jax.numpy as jnp
 from jax import lax
+from jax.experimental import pallas as pl
+from jax.experimental.pallas import tpu as pltpu
 from jax.sharding import PartitionSpec as P
 
 HEADS = 24
@@ -14,6 +18,7 @@
 WS = 4
 CHIPS = 16
 CAP = 48
+VM = 60 * 1024 * 1024
 
 
 def dot(a, b):
@@ -88,6 +93,212 @@
     top = jnp.max(jnp.where(mask, logits, MASKED), axis=-1, keepdims=True)
     lifted = jnp.where(mask, jnp.exp(jnp.where(mask, logits, MASKED) - top), 0.0)
     return lifted / jnp.maximum(jnp.sum(lifted, axis=-1, keepdims=True), 1e-30)
+
+
+def expert_body(width, ff, x_ref, dy_ref, sel_ref, wr_ref, *rest):
+    wg, wu, wd = rest[0:4], rest[4:8], rest[8:12]
+    y_ref, dx_ref, h_ref, dgu_ref, dyo_ref = rest[12:17]
+    wgu, wdn = rest[17:]
+    part = wg[0].shape[1]
+
+    @pl.when(pl.program_id(0) == 0)
+    def _():
+        for r in range(4):
+            wgu[:, r * part : (r + 1) * part] = wg[r][...]
+            wgu[:, ff + r * part : ff + (r + 1) * part] = wu[r][...]
+            wdn[r * part : (r + 1) * part, :] = wd[r][...]
+        wgu[:, 2 * ff :] = wr_ref[...]
+
+    x = x_ref[...]
+    pre = dot(x, wgu[...])
+    g, u, logits = pre[:, :ff], pre[:, ff : 2 * ff], pre[:, 2 * ff :]
+    mask = dy_ref[:, width:].astype(F32) > 0.5
+    logits = jnp.where(mask, logits, MASKED)
+    lifted = jnp.where(mask, jnp.exp(logits - jnp.max(logits, axis=1, keepdims=True)), 0.0)
+    total = jnp.maximum(jnp.sum(lifted, axis=1, keepdims=True), 1e-30)
+    gate = jnp.sum(lifted * sel_ref[0:1, :], axis=1, keepdims=True) / total
+    sig = 1.0 / (1.0 + jnp.exp(-g))
+    silu = g * sig
+    h = (silu * u).astype(BF)
+    h_ref[...] = h
+    y = dot(h, wdn[...]).astype(BF)
+    y_ref[...] = y
+    dy = dy_ref[:, :width].astype(F32)
+    dgate = jnp.sum(dy * y.astype(F32), axis=1, keepdims=True)
+    d_y = (gate * dy).astype(BF)
+    dyo_ref[...] = d_y
+    dh = dot_t(d_y, wdn[...])
+    dgu_ref[:, :ff] = (dh * u * sig * (1.0 + g * (1.0 - sig))).astype(BF)
+    dgu_ref[:, ff:] = (dh * silu).astype(BF)
+    dx_ref[:, :width] = dot_t(dgu_ref[...], wgu[:, : 2 * ff]).astype(BF)
+    hi = dgate.astype(BF).astype(F32)
+    dx_ref[:, width:] = (hi * sel_ref[0:1, :] + (dgate - hi) * sel_ref[1:2, :]).astype(BF)
+
+def expert_pass(x, dy, sel, wr, wg, wu, wd, tile):
+    slots, width = x.shape
+    part = wg[0].shape[1]; ff = 4 * part
+    row = lambda w: pl.BlockSpec((tile, w), lambda i: (i, 0))
+    whole = lambda a: pl.BlockSpec(a.shape, lambda i: (0, 0))
+    return pl.pallas_call(
+        functools.partial(expert_body, width, ff),
+        grid=(slots // tile,),
+        in_specs=[row(width), row(width + 128), whole(sel), whole(wr)] + [whole(a) for a in (*wg, *wu, *wd)],
+        out_specs=[row(width), row(width + 128), row(ff), row(2 * ff), row(width)],
+        out_shape=[jax.ShapeDtypeStruct((slots, w), BF) for w in (width, width + 128, ff, 2 * ff, width)],
+        scratch_shapes=[pltpu.VMEM((width, 2 * ff + 128), BF), pltpu.VMEM((ff, width), BF)],
+        compiler_params=pltpu.CompilerParams(vmem_limit_bytes=VM),
+        cost_estimate=pl.CostEstimate(flops=12*slots*width*ff, bytes_accessed=12*slots*width, transcendentals=slots*ff),
+        name="expert_pass",
+    )(x, dy, sel, wr, *wg, *wu, *wd)
+
+def slope_body(x_ref, dgu_ref, h_ref, dy_ref, own_g, own_u, own_d, *peers):
+    part = own_g.shape[1]
+    ff = h_ref.shape[1]
+    gu = tdot(x_ref[...], dgu_ref[...])
+    dn = tdot(h_ref[...], dy_ref[...])
+    own_g[...] = gu[:, :part]
+    own_u[...] = gu[:, ff : ff + part]
+    own_d[...] = dn[:part]
+    for k in (1, 2, 3):
+        peers[2 * k - 2][0] = gu[:, k * part : (k + 1) * part].astype(BF)
+        peers[2 * k - 2][1] = gu[:, ff + k * part : ff + (k + 1) * part].astype(BF)
+        peers[2 * k - 1][...] = dn[k * part : (k + 1) * part].astype(BF)
+
+def expert_slopes(x, dgu, h, dy, tile=256):
+    slots, width = x.shape
+    ff = h.shape[1]; part = ff // 4
+    col = pl.BlockSpec((slots, tile), lambda i: (0, i))
+    whole = lambda a: pl.BlockSpec(a.shape, lambda i: (0, 0))
+    tall = pl.BlockSpec((tile, part), lambda i: (i, 0))
+    wide = pl.BlockSpec((part, tile), lambda i: (0, i))
+    pair = pl.BlockSpec((2, tile, part), lambda i: (0, i, 0))
+    S = jax.ShapeDtypeStruct
+    return pl.pallas_call(
+        slope_body,
+        grid=(width // tile,),
+        in_specs=[col, whole(dgu), whole(h), col],
+        out_specs=[tall, tall, wide] + [pair, wide] * 3,
+        out_shape=[S((width, part), F32)] * 2 + [S((part, width), F32)] + [S((2, width, part), BF), S((part, width), BF)] * 3,
+        compiler_params=pltpu.CompilerParams(vmem_limit_bytes=VM),
+        cost_estimate=pl.CostEstimate(flops=6*slots*width*ff, bytes_accessed=8*slots*width, transcendentals=0),
+        name="expert_slopes",
+    )(x, dgu, h, dy)
+
+
+def load_body(h_ref, dqkv_ref, o_ref, da_ref, small_ref, flag_ref, keep_ref, give_ref):
+    step = pl.program_id(0)
+    half = keep_ref.shape[3]
+    count = keep_ref.shape[0] * keep_ref.shape[2]
+    shape = (keep_ref.shape[0], keep_ref.shape[2], half)
+
+    def put(kept, given):
+        keep_ref[:, 0] = kept.reshape(shape)
+        give_ref[:, 0] = given.reshape(shape).astype(BF)
+
+    @pl.when(step < WS)
+    def _():
+        both = tdot(h_ref[...], dqkv_ref[...])
+        none = jnp.zeros((count, half - 128), F32)
+        small = jnp.concatenate([none, small_ref[...]], axis=1)
+        put(both[:, :half] + small * flag_ref[0:1, 0:1], both[:, half:] + small * flag_ref[1:2, 0:1])
+
+    for i in range(2):
+
+        @pl.when(step == WS + i)
+        def _():
+            kept = tdot(o_ref[...], da_ref[:, i * half : (i + 1) * half])
+            given = tdot(o_ref[...], da_ref[:, (2 + i) * half : (3 + i) * half])
+            put(kept, given)
+
+
+def load_terms(h1, dqkv, o, da, small, flag):
+    tree, width = h1.shape
+    half = dqkv.shape[1] // 2
+    sets, step = WS + 2, width // WS // CHIPS
+    whole = lambda a: pl.BlockSpec(a.shape, lambda i: (0, 0))
+    out = pl.BlockSpec((CHIPS, 1, step, half), lambda i: (0, i, 0, 0))
+    return pl.pallas_call(
+        load_body,
+        grid=(sets,),
+        in_specs=[
+            pl.BlockSpec((tree, width // WS), lambda i: (0, jnp.minimum(i, WS - 1))),
+            whole(dqkv),
+            whole(o),
+            whole(da),
+            pl.BlockSpec((width // WS, 128), lambda i: (jnp.minimum(i, WS - 1), 0)),
+            whole(flag),
+        ],
+        out_specs=[out, out],
+        out_shape=[
+            jax.ShapeDtypeStruct((CHIPS, sets, step, half), F32),
+            jax.ShapeDtypeStruct((CHIPS, sets, step, half), BF),
+        ],
+        compiler_params=pltpu.CompilerParams(vmem_limit_bytes=VM),
+        cost_estimate=pl.CostEstimate(
+            flops=4 * tree * sets * (width // WS) * half,
+            bytes_accessed=6 * sets * width * half,
+            transcendentals=0,
+        ),
+        name="load_terms",
+    )(h1, dqkv, o, da, small, flag)
+
+
+def finish_body(a_ref, b_ref, ao_ref, bo_ref, flag_ref, q_ref, k_ref, v_ref, s_ref, o_ref):
+    turn = pl.program_id(0)
+    second = flag_ref[0:1, 0:1]
+    rows = q_ref.shape[0]
+    half = a_ref.shape[3]
+    kv = k_ref.shape[1]
+    mine = a_ref[:, 0].astype(F32).reshape(rows, half)
+    twin = b_ref[:, 0].astype(F32).reshape(rows, half)
+    q_ref[...] = jnp.where(second > 0.5, twin, mine)
+    rest = jnp.where(second > 0.5, mine, twin)
+    k_ref[...] = rest[:, :kv]
+    v_ref[...] = rest[:, kv : 2 * kv]
+
+    @pl.when(turn == 0)
+    def _():
+        s_ref[...] = rest[:, 2 * kv :]
+
+    @pl.when(turn > 0)
+    def _():
+        s_ref[...] += rest[:, 2 * kv :]
+
+    mine = ao_ref[:, 0].astype(F32).reshape(rows, half)
+    twin = bo_ref[:, 0].astype(F32).reshape(rows, half)
+    use_twin = jnp.where(turn < 2, second, 1.0 - second)
+    o_ref[...] = jnp.where(use_twin > 0.5, twin, mine)
+
+
+def finish(mine, twin, flag):
+    chips, sets, step, half = mine.shape
+    rows = chips * step
+    first = pl.BlockSpec((chips, 1, step, half), lambda i: (0, i, 0, 0))
+    later = pl.BlockSpec((chips, 1, step, half), lambda i: (0, WS + i % 2, 0, 0))
+    kv = (half - 128) // 2
+    S = jax.ShapeDtypeStruct
+    return pl.pallas_call(
+        finish_body,
+        grid=(WS,),
+        in_specs=[first, first, later, later, pl.BlockSpec(flag.shape, lambda i: (0, 0))],
+        out_specs=[
+            pl.BlockSpec((rows, half), lambda i: (0, i)),
+            pl.BlockSpec((rows, kv), lambda i: (0, i)),
+            pl.BlockSpec((rows, kv), lambda i: (0, i)),
+            pl.BlockSpec((rows, 128), lambda i: (0, 0)),
+            pl.BlockSpec((rows, half), lambda i: (0, i)),
+        ],
+        out_shape=[
+            S((rows, WS * half), F32),
+            S((rows, WS * kv), F32),
+            S((rows, WS * kv), F32),
+            S((rows, 128), F32),
+            S((rows, WS * half), F32),
+        ],
+        compiler_params=pltpu.CompilerParams(vmem_limit_bytes=VM),
+        cost_estimate=pl.CostEstimate(flops=0, bytes_accessed=16 * rows * WS * half, transcendentals=0),
+        name="finish",
+    )(mine, twin, mine, twin, flag)
 
 
 def shards(
@@ -129,21 +340,6 @@
             out = lax.dynamic_update_index_in_dim(out, part, (me + r) % WS, 0)
         return out.reshape((WS * parts[0].shape[0],) + parts[0].shape[1:])
 
-    x_all16 = jnp.concatenate(gathered(tokens), axis=0)
-    small = jnp.concatenate(
-        [
-            w_router,
-            norm_attn[:, None],
-            norm_moe[:, None],
-            jnp.zeros((shard, 128 - experts - 2), BF),
-        ],
-        axis=1,
-    )
-    small_full = absolute(gathered(small))
-    router = small_full[:, :experts]
-    gain_one = small_full[:, experts].astype(F32)
-    gain_two = small_full[:, experts + 1].astype(F32)
-
     def piece(d):
         return jnp.concatenate(
             [
@@ -154,8 +350,23 @@
             axis=1,
         )
 
-    qkv_parts = [piece(me)] + [from_peer(piece((me - k) % WS), k) for k in (1, 2, 3)]
-    w_qkv = absolute(qkv_parts)
+    small = jnp.concatenate(
+        [
+            w_router,
+            norm_attn[:, None],
+            norm_moe[:, None],
+            jnp.zeros((shard, 128 - experts - 2), BF),
+        ],
+        axis=1,
+    )
+    pieces = [piece((me - k) % WS) for k in range(WS)]
+    pieces, small, routes = lax.optimization_barrier((pieces, small, routes))
+    w_qkv = absolute([pieces[0]] + [from_peer(pieces[k], k) for k in (1, 2, 3)])
+    x_all16 = jnp.concatenate(gathered(tokens), axis=0)
+    small_full = absolute(gathered(small))
+    router = small_full[:, :experts]
+    gain_one = small_full[:, experts].astype(F32)
+    gain_two = small_full[:, experts + 1].astype(F32)
 
     labels = jnp.arange(experts, dtype=jnp.int32)
     chosen = jnp.any(routes[:, :, None] == labels[None, None, :], axis=1)
@@ -222,59 +433,29 @@
     x_slots = lax.all_to_all(x_send, "exp", 0, 0, tiled=True).reshape(slots, width)
     gates = masked_softmax(dot(h2, router), chosen)
 
-    wg = jnp.concatenate(gathered(wg_own), axis=1)
-    wu = jnp.concatenate(gathered(wu_own), axis=1)
-    wd = jnp.concatenate(gathered(wd_own), axis=0)
-    g_pre = dot(x_slots, wg)
-    u_pre = dot(x_slots, wu)
-    sig = jax.nn.sigmoid(g_pre)
-    hidden = (g_pre * sig * u_pre).astype(BF)
-    y = dot(hidden, wd).astype(BF)
-    dy = dy_slots[:, :width].astype(F32)
-    slot_mask = dy_slots[:, width : width + experts] > 0.5
-    slot_gates = masked_softmax(dot(x_slots, router), slot_mask)
-    mine = (labels == expert)[None, :]
-    gate_here = jnp.sum(jnp.where(mine, slot_gates, 0.0), axis=1, keepdims=True)
-    dgate = jnp.sum(dy * y.astype(F32), axis=1, keepdims=True)
-    d_y = (gate_here * dy).astype(BF)
-    d_h = dot_t(d_y, wd)
-    d_g = (d_h * u_pre * sig * (1.0 + g_pre * (1.0 - sig))).astype(BF)
-    d_u = (d_h * g_pre * sig).astype(BF)
-    d_x = (dot_t(d_g, wg) + dot_t(d_u, wu)).astype(BF)
-    hi, lo = split(dgate)
-    none = jnp.zeros((), BF)
-    tail = jnp.concatenate(
+    lane = jnp.arange(128, dtype=jnp.int32)
+    sel = jnp.concatenate(
         [
-            jnp.where(mine, hi, none),
-            jnp.where(mine, lo, none),
-            jnp.zeros((slots, 128 - 2 * experts), BF),
-        ],
-        axis=1,
-    )
-    dx_send = jnp.concatenate([d_x, tail], axis=1).reshape(experts, CAP, width + 128)
-    dx_back = lax.all_to_all(dx_send, "exp", 0, 0, tiled=True).reshape(slots, width + 128)
-    y, dx_back = lax.optimization_barrier((y, dx_back))
+            (lane == expert).astype(F32)[None],
+            (lane == expert + experts).astype(F32)[None],
+            jnp.zeros((6, 128), F32),
+        ],
+        axis=0,
+    )
+    y, dx_send, hidden, d_gu, d_y = expert_pass(
+        x_slots, dy_slots, sel, small_full, gathered(wg_own), gathered(wu_own), gathered(wd_own), 512
+    )
+    dx_back = lax.all_to_all(
+        dx_send.reshape(experts, CAP, width + 128), "exp", 0, 0, tiled=True
+    ).reshape(slots, width + 128)
+
+    own_g, own_u, own_d, gu1, dn1, gu2, dn2, gu3, dn3 = expert_slopes(x_slots, d_gu, hidden, d_y)
+    gu1, dn1 = to_peer(gu1, 1), to_peer(dn1, 1)
+    gu3, dn3 = to_peer(gu3, 3), to_peer(dn3, 3)
+    dx_back, y, gu1, dn1, gu3, dn3 = lax.optimization_barrier((dx_back, y, gu1, dn1, gu3, dn3))
     y_back = lax.all_to_all(y.reshape(experts, CAP, width), "exp", 0, 0, tiled=True).reshape(
         slots, width
     )
-
-    part = w_gate.shape[2]
-
-    def shard_sum(blocks):
-        total = blocks[0]
-        for k in (1, 2, 3):
-            total = total + to_peer(blocks[k].astype(BF), k).astype(F32)
-        return total
-
-    grad_wg = shard_sum(
-        [tdot(x_slots, d_g[:, r * part : (r + 1) * part]) for r in range(WS)]
-    )[None]
-    grad_wu = shard_sum(
-        [tdot(x_slots, d_u[:, r * part : (r + 1) * part]) for r in range(WS)]
-    )[None]
-    grad_wd = shard_sum(
-        [tdot(hidden[:, r * part : (r + 1) * part], d_y) for r in range(WS)]
-    )[None]
 
     back = dot(to_slot, dx_back)
     dgate_dense = back[:, width : width + experts] + back[:, width + experts : width + 2 * experts]
@@ -285,7 +466,11 @@
     dres, grad_gain_two = norm_back(x2, scale_two, gain_two, dh2)
     dx2 = cotangent.astype(F32) + dres
     d_a = jnp.concatenate(gathered(dx2.astype(BF)), axis=0)
-    grad_wout = tdot(o, d_a)
+    d_a, gu2, dn2 = lax.optimization_barrier((d_a, gu2, dn2))
+    gu2, dn2 = to_peer(gu2, 2), to_peer(dn2, 2)
+    grad_gu = jnp.stack([own_g, own_u]) + gu1.astype(F32) + gu2.astype(F32) + gu3.astype(F32)
+    grad_wg, grad_wu = grad_gu[0][None], grad_gu[1][None]
+    grad_wd = (own_d + dn1.astype(F32) + dn2.astype(F32) + dn3.astype(F32))[None]
     d_o = dot_t(d_a, w_out).astype(BF).reshape(tree, my_kv, group, HEAD)
     probs = jnp.exp(score_rows() - logsum)
     d_p = jnp.einsum("tkgd,skd->kgts", d_o, v, preferred_element_type=F32)
@@ -307,12 +492,11 @@
     dh1 = to_owners(dh1_part)
     dres_one, _ = norm_back(tokens.astype(F32), scale_one[:rows], gain_one, dh1)
     grad_tokens = dx2 + dres_one
-    grad_wqkv = tdot(h1, d_qkv)
-
     half = (q_w + 2 * kv_w + 128) // 2
-    load = jnp.concatenate(
+    flag = jnp.broadcast_to(jnp.stack([core, 1 - core]).astype(F32)[:, None], (2, 128))
+    flag = jnp.concatenate([flag, jnp.zeros((6, 128), F32)], axis=0)
+    small_terms = jnp.concatenate(
         [
-            grad_wqkv,
             grad_router,
             grad_gain_two[:, None],
             grad_gain_one[:, None],
@@ -320,15 +504,19 @@
         ],
         axis=1,
     )
-    load_o = jnp.concatenate([grad_wout[:, i * half : (i + 1) * half] for i in range(WS)], axis=0)
-    load_o = jnp.concatenate([load_o[: 2 * shard], load_o[2 * shard :]], axis=1)
-    load = jnp.concatenate([load, load_o], axis=0)
-    keep = jnp.where(core == 0, load[:, :half], load[:, half:])
-    give = jnp.where(core == 0, load[:, half:], load[:, :half]).astype(BF)
-    chip_sum = (keep + other_core(give).astype(F32)).astype(BF)
+    d_kv = jnp.concatenate([d_qkv[:, q_w:], jnp.zeros((tree, 128), BF)], axis=1)
+    d_turned = jnp.where(
+        core == 0,
+        jnp.concatenate([d_qkv[:, :q_w], d_kv], axis=1),
+        jnp.concatenate([d_kv, d_qkv[:, :q_w]], axis=1),
+    )
+    da_turned = jnp.where(
+        core == 0, d_a, jnp.concatenate([d_a[:, width // 2 :], d_a[:, : width // 2]], axis=1)
+    )
+    keep, give = load_terms(h1, d_turned, o, da_turned, small_terms, flag)
+    give, y_back = lax.optimization_barrier((give, y_back))
+    sent = (keep + other_core(give).astype(F32)).astype(BF)
     step = shard // CHIPS
-    sets = chip_sum.shape[0] // shard
-    sent = chip_sum.reshape(sets, CHIPS, step, half).transpose(1, 0, 2, 3)
     got = same_core(sent)
     total = jnp.sum(got.astype(F32), axis=0).astype(BF)
     turned = absolute(
@@ -341,14 +529,7 @@
     final = jnp.concatenate([turned, total[WS:]], axis=0)
     spread_out = same_core(jnp.broadcast_to(final, (CHIPS,) + final.shape))
     twin = other_core(spread_out)
-    first = jnp.where(core == 0, spread_out, twin).transpose(1, 0, 2, 3).reshape(sets, shard, half)
-    second = jnp.where(core == 0, twin, spread_out).transpose(1, 0, 2, 3).reshape(sets, shard, half)
-    first, second = first.astype(F32), second.astype(F32)
-    sum_query = jnp.concatenate([first[i] for i in range(WS)], axis=1)
-    sum_key = jnp.concatenate([second[i][:, :kv_w] for i in range(WS)], axis=1)
-    sum_value = jnp.concatenate([second[i][:, kv_w : 2 * kv_w] for i in range(WS)], axis=1)
-    sum_small = sum(second[i][:, 2 * kv_w :] for i in range(WS))
-    sum_out = jnp.concatenate([first[WS], first[WS + 1], second[WS], second[WS + 1]], axis=1)
+    sum_query, sum_key, sum_value, sum_small, sum_out = finish(spread_out, twin, flag)
 
     gates_slot = jnp.where(taken, dot(split(gates)[0], spread) + dot(split(gates)[1], spread), 0.0)
     gs_hi, gs_lo = split(gates_slot)

time: 582 us -> 483 us (0.83)
  matrix products: 125 us -> 50.4 us
  Pallas kernels: 0 us -> 48.9 us
  local copies, waits for them, and re-layouts: 90.9 us -> 44.4 us
  waiting for transfers between devices: 203 us -> 188 us
  starting transfers between devices: 108 us -> 102 us
    dot_general x18 -> x4, matrix products: 62.5 us -> 7.73 us  [tdot(): lax.dot_general(a, b, (((0,), (0,)), ((), ())), preferred_element_type=F32)]
    pallas_call x0 -> x4, Pallas kernels: none -> 48.9 us  [the longest x1 23 us: expert_pass(): pl.pallas_call(functools.partial(expert_body, width, ff), grid=(slots //...]
    all_to_all x1, waiting for transfers between devices: 62.1 us -> 19.2 us  [shards(): lax.all_to_all(dx_send.reshape(experts, CAP, width + 128), 'exp', 0, 0, t...]
    dot_general x15 -> x11, matrix products: 38.4 us -> 17.7 us  [dot(): return jnp.dot(a, b, preferred_element_type=F32)]
    concatenate x6 -> x4, local copies, waits for them, and re-layouts: 22.5 us -> 1.96 us  [the longest x2 1.23 us: shards(): flag = jnp.concatenate([flag, jnp.zeros((6, 128), F32)], axis=0)]
    concatenate x6 -> x4, other arithmetic: 19.2 us -> 4.24 us  [the longest x1 1.45 us: shards(): d_a = jnp.concatenate(gathered(dx2.astype(BF)), axis=0)]
    ppermute x24, waiting for transfers between devices: 73.4 us -> 84.5 us  [from_peer(): return lax.ppermute(v, 'ws', [(s, (s - k) % WS) for s in range(WS)])]
    unnamed x228 -> x138, local copies, waits for them, and re-layouts: 19.6 us -> 10.7 us
  transfers between devices with their start and end apart: 47 -> 44, of which waited for: 21 -> 24; matrix products, arithmetic and copies ran while one was open for 23% -> 22% of each run, Pallas kernels for 0% -> 4%
where the time goes in v2:
time: 483 us; the launch traced here: 474 us
  waiting for transfers between devices  188 us (39%)
  starting transfers between devices  102 us (21%)
  matrix products  50.4 us (10%)
  Pallas kernels  48.9 us (10%)
  local copies, waits for them, and re-layouts  44.4 us (9%)
  other arithmetic  38.3 us (8%)
    ppermute x24, waiting for transfers between devices, from_peer(): return lax.ppermute(v, 'ws', [(s, (s - k) % WS) for s in range(WS)])  84.5 us
    ppermute x12, waiting for transfers between devices, to_peer(): return lax.ppermute(v, 'ws', [(s, (s + k) % WS) for s in range(WS)])  41.3 us
    ppermute x24, starting transfers between devices, from_peer(): return lax.ppermute(v, 'ws', [(s, (s - k) % WS) for s in range(WS)])  33.6 us
    all_to_all x2, waiting for transfers between devices, same_core(): return lax.all_to_all(v, 'exp', 0, 0, tiled=True, axis_index_groups=groups)  31.9 us
    pallas_call x1, Pallas kernels, expert_pass(): pl.pallas_call(functools.partial(expert_body, width, ff), grid=(slots //...  23 us
    all_to_all x1, waiting for transfers between devices, shards(): lax.all_to_all(dx_send.reshape(experts, CAP, width + 128), 'exp', 0, 0, t...  19.2 us
    dot_general x11, matrix products, dot(): return jnp.dot(a, b, preferred_element_type=F32)  17.7 us
    ppermute x12, starting transfers between devices, to_peer(): return lax.ppermute(v, 'ws', [(s, (s + k) % WS) for s in range(WS)])  15.1 us
  transfers between devices with their start and end apart: 44, of which 24 were waited for; matrix products, arithmetic and copies ran while one was open for 22% of the time, Pallas kernels for 4%

profile of v2, /device:TPU:1, one launch (start us, length us, event | category | flops | bytes accessed | tf_op | source)
XLA Modules:
  0.0 474.4 jit_solution(4880330394353009418)
XLA Ops:
  9.5 3.6 collective-permute-start.3
  18.7 3.8 convolution_convert_fusion
  22.5 10.2 %all-to-all-start.1 = ((bf16[32,48,1664]{2,1,0:T(8,128)(2,1)}), bf16[32,48,1664]{2,1,0:T(8,128)(2,1)}, u32[]{:S(2)}, u32[]{:S(2)}) async-start(bf16[32,48,1664]{2,1,0:T(8,128)(2,1)} %bitcast.157), calls=%async_computation.1 | async-start | bytes 10223616 | tf_op jit(solution)/shard_map/all_to_all | solution.py:385
  46.0 14.8 %collective-permute-done.2 = bf16[128,1536]{1,0:T(8,128)(2,1)S(1)} collective-permute-done((bf16[128,1536]{1,0:T(8,128)(2,1)S(1)}, bf16[128,1536]{1,0:T(8,128)(2,1)S(1)}, u32[]{:S(2)}, u32[]{:S(2)}) %collective-permute-start.2) | collective-permute-done | bytes 393248 | tf_op jit(solution)/shard_map/ppermute | solution.py:42
  64.2 7.6 %collective-permute-done.8 = bf16[384,640]{1,0:T(8,128)(2,1)S(1)} collective-permute-done((bf16[384,640]{1,0:T(8,128)(2,1)}, bf16[384,640]{1,0:T(8,128)(2,1)S(1)}, u32[]{:S(2)}, u32[]{:S(2)}) %collective-permute-start.8) | collective-permute-done | bytes 491552 | tf_op jit(solution)/shard_map/ppermute | solution.py:42
  88.7 9.0 %collective-permute-done.10 = bf16[128,1536]{1,0:T(8,128)(2,1)S(1)} collective-permute-done((bf16[128,1536]{1,0:T(8,128)(2,1)S(1)}, bf16[128,1536]{1,0:T(8,128)(2,1)S(1)}, u32[]{:S(2)}, u32[]{:S(2)}) %collective-permute-start.10) | collective-permute-done | bytes 393248 | tf_op jit(solution)/shard_map/ppermute | solution.py:46
  97.7 5.7 %collective-permute-done.11 = bf16[128,1536]{1,0:T(8,128)(2,1)S(1)} collective-permute-done((bf16[128,1536]{1,0:T(8,128)(2,1)S(1)}, bf16[128,1536]{1,0:T(8,128)(2,1)S(1)}, u32[]{:S(2)}, u32[]{:S(2)}) %collective-permute-start.11) | collective-permute-done | bytes 393248 | tf_op jit(solution)/shard_map/ppermute | solution.py:46
  103.4 4.1 collective-permute-done.9
  108.1 3.6 convolution_convert_fusion.1
  111.7 7.5 %all-to-all-start = ((bf16[32,48,1536]{2,1,0:T(8,128)(2,1)}), bf16[32,48,1536]{2,1,0:T(8,128)(2,1)}, u32[]{:S(2)}, u32[]{:S(2)}) async-start(bf16[32,48,1536]{2,1,0:T(8,128)(2,1)} %bitcast.158), calls=%async_computation | async-start | bytes 9437184 | tf_op jit(solution)/shard_map/all_to_all | solution.py:433
  124.3 5.7 %collective-permute-done.12.rest_1_ = bf16[1536,128]{1,0:T(8,128)(2,1)} collective-permute-done((bf16[1536,128]{1,0:T(8,128)(2,1)}, bf16[1536,128]{1,0:T(8,128)(2,1)}, u32[]{:S(2)}, u32[]{:S(2)}) %collective-permute-start.12) | collective-permute-done | bytes 393248 | tf_op jit(solution)/shard_map/ppermute | solution.py:42
  131.5 9.7 %collective-permute-start.18 = (bf16[128,1536]{1,0:T(8,128)(2,1)}, bf16[128,1536]{1,0:T(8,128)(2,1)}, u32[]{:S(2)}, u32[]{:S(2)}) collective-permute-start(bf16[128,1536]{1,0:T(8,128)(2,1)} %bitcast.199), channel_id=1, source_target_pairs={{0,3},{1,0},{2,1},{3,2},{4,7},{5,4},{6,5},{7,6},{8,11},{9,8},{10,9... | collective-permute-start | bytes 1179656 | tf_op jit(solution)/shard_map/ppermute | solution.py:42
  142.5 4.4 collective-permute-done.15.rest_5_
  148.4 10.1 %collective-permute-done.17.rest_7_ = bf16[1536,128]{1,0:T(8,128)(2,1)} collective-permute-done((bf16[1536,128]{1,0:T(8,128)(2,1)}, bf16[1536,128]{1,0:T(8,128)(2,1)}, u32[]{:S(2)}, u32[]{:S(2)}) %collective-permute-start.17) | collective-permute-done | bytes 393248 | tf_op jit(solution)/shard_map/ppermute | solution.py:42
  158.5 5.2 %collective-permute-done.18.rest_9_ = bf16[128,1536]{1,0:T(8,128)(2,1)} collective-permute-done((bf16[128,1536]{1,0:T(8,128)(2,1)}, bf16[128,1536]{1,0:T(8,128)(2,1)}, u32[]{:S(2)}, u32[]{:S(2)}) %collective-permute-start.18) | collective-permute-done | bytes 393248 | tf_op jit(solution)/shard_map/ppermute | solution.py:42
  165.3 9.2 %collective-permute-done.20.rest_11_ = bf16[128,1536]{1,0:T(8,128)(2,1)} collective-permute-done((bf16[128,1536]{1,0:T(8,128)(2,1)}, bf16[128,1536]{1,0:T(8,128)(2,1)}, u32[]{:S(2)}, u32[]{:S(2)}) %collective-permute-start.20) | collective-permute-done | bytes 393248 | tf_op jit(solution)/shard_map/ppermute | solution.py:42
  174.5 3.0 all-to-all-done
  177.6 23.0 %expert_pass.1 = (bf16[1536,1536]{1,0:T(8,128)(2,1)}, bf16[1536,1664]{1,0:T(8,128)(2,1)}, bf16[1536,512]{1,0:T(8,128)(2,1)}, bf16[1536,1024]{1,0:T(8,128)(2,1)}, bf16[1536,1536]{1,0:T(8,128)(2,1)}) custom-call(bf16[1536,1536]{1,0:T(8,128)(2,1)} %bitcast.36.x_ref, bf16[1536,1664]{1,0:T(8,128)(2,1)} %bitcast.38.dy_ref, ...), custom_call_target="tpu_custom_call" | custom-call | flops 14495514624 | bytes 28311552 | tf_op jit(solution)/shard_map/expert_pass/pallas_call | solution.py:142
  200.5 7.8 %all-to-all-start.2 = ((bf16[32,48,1664]{2,1,0:T(8,128)(2,1)}), bf16[32,48,1664]{2,1,0:T(8,128)(2,1)}, u32[]{:S(2)}, u32[]{:S(2)}) async-start(bf16[32,48,1664]{2,1,0:T(8,128)(2,1)} %bitcast.164), calls=%async_computation.2 | async-start | bytes 10223616 | tf_op jit(solution)/shard_map/all_to_all | solution.py:448
  210.6 12.7 %expert_slopes.1 = (f32[1536,128]{1,0:T(8,128)}, f32[1536,128]{1,0:T(8,128)}, f32[128,1536]{1,0:T(8,128)}, bf16[2,1536,128]{2,1,0:T(8,128)(2,1)}, bf16[128,1536]...) custom-call(bf16[1536,1536]{1,0:T(8,128)(2,1)} %bitcast.36.x_ref, ...), custom_call_target="tpu_custom_call" | custom-call | flops 7247757312 | bytes 18874368 | tf_op jit(solution)/shard_map/expert_slopes/pallas_call | solution.py:176
  223.4 2.7 collective-permute-start.23
  226.7 2.7 collective-permute-start.24
  229.7 22.5 %collective-permute-done.22 = bf16[128,1536]{1,0:T(8,128)(2,1)} collective-permute-done((bf16[128,1536]{1,0:T(8,128)(2,1)}, bf16[128,1536]{1,0:T(8,128)(2,1)}, u32[]{:S(2)}, u32[]{:S(2)}) %collective-permute-start.22) | collective-permute-done | bytes 393248 | tf_op jit(solution)/shard_map/ppermute | solution.py:46
  252.2 19.2 %all-to-all-done.2 = bf16[32,48,1664]{2,1,0:T(8,128)(2,1)} async-done(((bf16[32,48,1664]{2,1,0:T(8,128)(2,1)}), bf16[32,48,1664]{2,1,0:T(8,128)(2,1)}, u32[]{:S(2)}, u32[]{:S(2)}) %all-to-all-start.2) | async-done | bytes 5111840 | tf_op jit(solution)/shard_map/all_to_all | solution.py:448
  271.4 3.3 fusion.109
  283.7 8.6 %all-to-all-start.3 = ((bf16[32,48,1536]{2,1,0:T(8,128)(2,1)}), bf16[32,48,1536]{2,1,0:T(8,128)(2,1)}, u32[]{:S(2)}, u32[]{:S(2)}) async-start(bf16[32,48,1536]{2,1,0:T(8,128)(2,1)} %bitcast.165), calls=%async_computation.3 | async-start | bytes 9437184 | tf_op jit(solution)/shard_map/all_to_all | solution.py:456
  293.0 7.7 %collective-permute-done.27 = bf16[128,1536]{1,0:T(8,128)(2,1)} collective-permute-done((bf16[128,1536]{1,0:T(8,128)(2,1)S(1)}, bf16[128,1536]{1,0:T(8,128)(2,1)}, u32[]{:S(2)}, u32[]{:S(2)}) %collective-permute-start.27) | collective-permute-done | bytes 393248 | tf_op jit(solution)/shard_map/ppermute | solution.py:42
  303.1 4.9 %fusion = (f32[2,3,512]{2,1,0:T(4,128)}, f32[2,512,512,3]{2,1,3,0:T(8,128)S(1)}) fusion(f32[2,3,512,512]{2,3,1,0:T(8,128)} %copy-done.1, f32[2,3,512]{2,1,0:T(4,128)S(1)} %copy-done.44, bf16[512,2,64,1]{0,2,3,1:T(8,128)(2,1)S(1)} %bitcast.183, bf16[512,2,3,64]{0,3,2,1:T(8,128)(2,1)S(1)} %bitcast.173), kind=kOutput, calls=%fused_computation.4 | convolution fusion | flops 206042112 | bytes 13131776 | tf_op jit(solution)/shard_map/tkgd,skd->kgts/dot_general | solution.py:476
  316.1 3.1 fusion.25
  321.6 4.6 fusion.26
  327.9 6.1 %fusion.99 = (bf16[512,1536]{1,0:T(8,128)(2,1)}, f32[1536]{0:T(1024)S(1)}, f32[512,1536]{1,0:T(8,128)}) fusion(f32[512]{0:T(512)} %copy-done.57, bf16[128,1536]{1,0:T(8,128)(2,1)} %copy-done.28, bf16[128,1536]{1,0:T(8,128)(2,1)} %collective-permute-done.1, bf16[128,1536]{1,0:T(8,128)(2,1)} %collective-permute-done, bf16[128,1536]{1,0:T(8,128)(2,1)} %param.15, ...), kind=kOutput, calls=%fused_computation.223 | convolution fusion | flops 1018034688 | bytes 8921088 | tf_op jit(solution)/shard_map/dot_general | solution.py:29
  339.1 7.5 %load_terms.1 = (f32[16,6,24,384]{3,2,1,0:T(8,128)}, bf16[16,6,24,384]{3,2,1,0:T(8,128)(2,1)}) custom-call(bf16[512,1536]{1,0:T(8,128)(2,1)} %copy-done.26, bf16[512,768]{1,0:T(8,128)(2,1)} %maximum_select_fusion.1.dqkv_ref, bf16[512,384]{1,0:T(8,128)(2,1)} %copy.131.o_ref, bf16[512,1536]{1,0:T(8,128)(2,1)} %maximum_select_fusion.da_ref, ...), custom_call_target="tpu_custom_call" | custom-call | flops 1811939328 | bytes 21233664 | tf_op jit(solution)/shard_map/load_terms/pallas_call | solution.py:220
  346.6 4.4 all-to-all-done.3
  352.1 3.5 collective-permute-done.31
  355.7 3.6 add_convert_fusion
  359.2 6.5 %all-to-all-start.4 = ((bf16[16,6,24,384]{3,2,1,0:T(8,128)(2,1)}), bf16[16,6,24,384]{3,2,1,0:T(8,128)(2,1)}, u32[]{:S(2)}, u32[]{:S(2)}) async-start(bf16[16,6,24,384]{3,2,1,0:T(8,128)(2,1)} %add_convert_fusion), calls=%async_computation.4 | async-start | bytes 3538944 | tf_op jit(solution)/shard_map/all_to_all | solution.py:55
  367.6 3.4 collective-permute-start.37
  371.0 19.7 %all-to-all-done.4 = bf16[16,6,24,384]{3,2,1,0:T(8,128)(2,1)} async-done(((bf16[16,6,24,384]{3,2,1,0:T(8,128)(2,1)}), bf16[16,6,24,384]{3,2,1,0:T(8,128)(2,1)}, u32[]{:S(2)}, u32[]{:S(2)}) %all-to-all-start.4) | async-done | bytes 1769504 | tf_op jit(solution)/shard_map/all_to_all | solution.py:55
  397.2 2.8 collective-permute-start.29
  403.0 12.5 %collective-permute-done.33 = bf16[24,384]{1,0:T(8,128)(2,1)S(1)} collective-permute-done((bf16[24,384]{1,0:T(8,128)(2,1)S(1)}, bf16[24,384]{1,0:T(8,128)(2,1)S(1)}, u32[]{:S(2)}, u32[]{:S(2)}) %collective-permute-start.33) | collective-permute-done | bytes 18464 | tf_op jit(solution)/shard_map/ppermute | solution.py:42
  416.4 2.9 collective-permute-done.34
  420.7 6.7 %all-to-all-start.5 = ((bf16[16,6,24,384]{3,2,1,0:T(8,128)(2,1)}), bf16[16,6,24,384]{3,2,1,0:T(8,128)(2,1)}, u32[]{:S(2)}, u32[]{:S(2)}) async-start(bf16[16,6,24,384]{3,2,1,0:T(8,128)(2,1)} %broadcast_in_dim.199), calls=%async_computation.5 | async-start | bytes 3538944 | tf_op jit(solution)/shard_map/all_to_all | solution.py:55
  433.9 3.1 fusion.35
  437.0 12.2 %all-to-all-done.5.a_ref.ao_ref = bf16[16,6,24,384]{3,2,1,0:T(8,128)(2,1)} async-done(((bf16[16,6,24,384]{3,2,1,0:T(8,128)(2,1)}), bf16[16,6,24,384]{3,2,1,0:T(8,128)(2,1)}, u32[]{:S(2)}, u32[]{:S(2)}) %all-to-all-start.5) | async-done | bytes 1769504 | tf_op jit(solution)/shard_map/all_to_all | solution.py:55
  449.2 5.1 %collective-permute-start.35 = (bf16[16,6,24,384]{3,2,1,0:T(8,128)(2,1)}, bf16[16,6,24,384]{3,2,1,0:T(8,128)(2,1)}, u32[]{:S(2)}, u32[]{:S(2)}) collective-permute-start(bf16[16,6,24,384]{3,2,1,0:T(8,128)(2,1)} %all-to-all-done.5.a_ref.ao_ref), channel_id=1, source_target_pairs={{0,4},{4,0},{8,12},{12,8},{16,20},{20,16},{24,28},{28,24},{32,36},... | collective-permute-start | bytes 5308424 | tf_op jit(solution)/shard_map/ppermute | solution.py:50
  457.9 3.1 fusion.47
  461.1 3.9 fusion.16
  465.0 5.6 %finish.1 = (f32[384,1536]{1,0:T(8,128)}, f32[384,512]{1,0:T(8,128)}, f32[384,512]{1,0:T(8,128)}, f32[384,128]{1,0:T(8,128)}, f32[384,1536]{1,0:T(8,128)}) custom-call(bf16[16,6,24,384]{3,2,1,0:T(8,128)(2,1)} %all-to-all-done.5.a_ref.ao_ref, bf16[16,6,24,384]{3,2,1,0:T(8,128)(2,1)} %collective-permute-done.35.b_ref.bo_ref, ...), custom_call_target="tpu_custom_call" | custom-call | bytes 9437184 | tf_op jit(solution)/shard_map/finish/pallas_call | solution.py:280
  (319 shorter events, 119.5 us)
Async XLA Ops:
  9.5 29.5 %collective-permute-start.3 = (bf16[384,128]{1,0:T(8,128)(2,1)}, bf16[384,128]{1,0:T(8,128)(2,1)}, u32[]{:S(2)}, u32[]{:S(2)}) collective-permute-start(bf16[384,128]{1,0:T(8,128)(2,1)} %maximum_maximum_fusion.1), channel_id=1, source_target_pairs={{0,3},{1,0},{2,1},{3,2},{4,7},{5,4},{6,5},{7,6},{8,11},{9,8},{10,9... | collective-permute-start | bytes 294920 | tf_op jit(solution)/shard_map/ppermute | solution.py:42
  13.0 27.0 %collective-permute-start.4 = (bf16[384,128]{1,0:T(8,128)(2,1)}, bf16[384,128]{1,0:T(8,128)(2,1)}, u32[]{:S(2)}, u32[]{:S(2)}) collective-permute-start(bf16[384,128]{1,0:T(8,128)(2,1)} %maximum_maximum_fusion.1), channel_id=1, source_target_pairs={{0,2},{1,3},{2,0},{3,1},{4,6},{5,7},{6,4},{7,5},{8,10},{9,11},{10,... | collective-permute-start | bytes 294920 | tf_op jit(solution)/shard_map/ppermute | solution.py:42
  13.4 30.2 %collective-permute-start.5 = (bf16[384,128]{1,0:T(8,128)(2,1)}, bf16[384,128]{1,0:T(8,128)(2,1)}, u32[]{:S(2)}, u32[]{:S(2)}) collective-permute-start(bf16[384,128]{1,0:T(8,128)(2,1)} %maximum_maximum_fusion.1), channel_id=1, source_target_pairs={{0,1},{1,2},{2,3},{3,0},{4,5},{5,6},{6,7},{7,4},{8,9},{9,10},{10,1... | collective-permute-start | bytes 294920 | tf_op jit(solution)/shard_map/ppermute | solution.py:42
  14.1 31.4 %collective-permute-start = (bf16[128,1536]{1,0:T(8,128)(2,1)S(1)}, bf16[128,1536]{1,0:T(8,128)(2,1)}, u32[]{:S(2)}, u32[]{:S(2)}) collective-permute-start(bf16[128,1536]{1,0:T(8,128)(2,1)S(1)} %copy-done.5), channel_id=1, source_target_pairs={{0,3},{1,0},{2,1},{3,2},{4,7},{5,4},{6,5},{7,6},{8,11},{9,8},{10,9... | collective-permute-start | bytes 1179656 | tf_op jit(solution)/shard_map/ppermute | solution.py:42
  16.1 29.9 %collective-permute-start.1 = (bf16[128,1536]{1,0:T(8,128)(2,1)S(1)}, bf16[128,1536]{1,0:T(8,128)(2,1)}, u32[]{:S(2)}, u32[]{:S(2)}) collective-permute-start(bf16[128,1536]{1,0:T(8,128)(2,1)S(1)} %copy-done.5), channel_id=1, source_target_pairs={{0,2},{1,3},{2,0},{3,1},{4,6},{5,7},{6,4},{7,5},{8,10},{9,11},{10,... | collective-permute-start | bytes 1179656 | tf_op jit(solution)/shard_map/ppermute | solution.py:42
  17.6 258.4 %copy-start.42 = (pred[128,32]{0,1:T(8,128)(4,1)}, pred[128,32]{0,1:T(8,128)(4,1)S(1)}, u32[]{:S(2)}) copy-start(pred[128,32]{0,1:T(8,128)(4,1)S(1)} %fusion.55) | copy-start | bytes 12292
  18.6 252.9 %copy-start.13 = (pred[128,1536]{1,0:T(32,128)(4,1)}, pred[128,1536]{1,0:T(32,128)(4,1)S(1)}, u32[]{:S(2)}) copy-start(pred[128,1536]{1,0:T(32,128)(4,1)S(1)} %convolution_compare_fusion) | copy-start | bytes 589828
  22.5 89.2 %all-to-all-start.1 = ((bf16[32,48,1664]{2,1,0:T(8,128)(2,1)}), bf16[32,48,1664]{2,1,0:T(8,128)(2,1)}, u32[]{:S(2)}, u32[]{:S(2)}) async-start(bf16[32,48,1664]{2,1,0:T(8,128)(2,1)} %bitcast.157), calls=%async_computation.1 | async-start | bytes 10223616 | tf_op jit(solution)/shard_map/all_to_all | solution.py:385
  39.0 21.8 %collective-permute-start.2 = (bf16[128,1536]{1,0:T(8,128)(2,1)S(1)}, bf16[128,1536]{1,0:T(8,128)(2,1)S(1)}, u32[]{:S(2)}, u32[]{:S(2)}) collective-permute-start(bf16[128,1536]{1,0:T(8,128)(2,1)S(1)} %copy-done.5), channel_id=1, source_target_pairs={{0,1},{1,2},{2,3},{3,0},{4,5},{5,6},{6,7},{7,4},{8,9},{9,10},{10,1... | collective-permute-start | bytes 1179656 | tf_op jit(solution)/shard_map/ppermute | solution.py:42
  40.1 24.0 %collective-permute-start.6 = (bf16[384,640]{1,0:T(8,128)(2,1)}, bf16[384,640]{1,0:T(8,128)(2,1)S(1)}, u32[]{:S(2)}, u32[]{:S(2)}) collective-permute-start(bf16[384,640]{1,0:T(8,128)(2,1)} %pad_maximum_fusion.3), channel_id=1, source_target_pairs={{0,3},{1,0},{2,1},{3,2},{4,7},{5,4},{6,5},{7,6},{8,11},{9,8},{10,9... | collective-permute-start | bytes 1474568 | tf_op jit(solution)/shard_map/ppermute | solution.py:42
  43.6 20.5 %collective-permute-start.7 = (bf16[384,640]{1,0:T(8,128)(2,1)}, bf16[384,640]{1,0:T(8,128)(2,1)S(1)}, u32[]{:S(2)}, u32[]{:S(2)}) collective-permute-start(bf16[384,640]{1,0:T(8,128)(2,1)} %pad_maximum_fusion.4), channel_id=1, source_target_pairs={{0,2},{1,3},{2,0},{3,1},{4,6},{5,7},{6,4},{7,5},{8,10},{9,11},{10,... | collective-permute-start | bytes 1474568 | tf_op jit(solution)/shard_map/ppermute | solution.py:42
  45.5 232.4 %copy-start.45 = (f32[1536]{0:T(1024)}, f32[1536]{0:T(1024)S(1)}, u32[]{:S(2)}) copy-start(f32[1536]{0:T(1024)S(1)} %get-tuple-element.146) | copy-start | bytes 18436
  45.5 26.3 %collective-permute-start.8 = (bf16[384,640]{1,0:T(8,128)(2,1)}, bf16[384,640]{1,0:T(8,128)(2,1)S(1)}, u32[]{:S(2)}, u32[]{:S(2)}) collective-permute-start(bf16[384,640]{1,0:T(8,128)(2,1)} %pad_maximum_fusion.5), channel_id=1, source_target_pairs={{0,1},{1,2},{2,3},{3,0},{4,5},{5,6},{6,7},{7,4},{8,9},{9,10},{10,1... | collective-permute-start | bytes 1474568 | tf_op jit(solution)/shard_map/ppermute | solution.py:42
  86.5 11.2 %collective-permute-start.10 = (bf16[128,1536]{1,0:T(8,128)(2,1)S(1)}, bf16[128,1536]{1,0:T(8,128)(2,1)S(1)}, u32[]{:S(2)}, u32[]{:S(2)}) collective-permute-start(bf16[128,1536]{1,0:T(8,128)(2,1)S(1)} %get-tuple-element.167), channel_id=1, source_target_pairs={{0,2},{1,3},{2,0},{3,1},{4,6},{5,7},{6,4},{7,5},{8,10},{9,11},{10,... | collective-permute-start | bytes 1179656 | tf_op jit(solution)/shard_map/ppermute | solution.py:46
  87.3 16.2 %collective-permute-start.11 = (bf16[128,1536]{1,0:T(8,128)(2,1)S(1)}, bf16[128,1536]{1,0:T(8,128)(2,1)S(1)}, u32[]{:S(2)}, u32[]{:S(2)}) collective-permute-start(bf16[128,1536]{1,0:T(8,128)(2,1)S(1)} %get-tuple-element.166), channel_id=1, source_target_pairs={{0,3},{1,0},{2,1},{3,2},{4,7},{5,4},{6,5},{7,6},{8,11},{9,8},{10,9... | collective-permute-start | bytes 1179656 | tf_op jit(solution)/shard_map/ppermute | solution.py:46
  88.1 19.4 %collective-permute-start.9 = (bf16[128,1536]{1,0:T(8,128)(2,1)S(1)}, bf16[128,1536]{1,0:T(8,128)(2,1)S(1)}, u32[]{:S(2)}, u32[]{:S(2)}) collective-permute-start(bf16[128,1536]{1,0:T(8,128)(2,1)S(1)} %get-tuple-element.165), channel_id=1, source_target_pairs={{0,1},{1,2},{2,3},{3,0},{4,5},{5,6},{6,7},{7,4},{8,9},{9,10},{10,1... | collective-permute-start | bytes 1179656 | tf_op jit(solution)/shard_map/ppermute | solution.py:46
  107.9 170.0 %copy-start.53 = (f32[128]{0:T(128)}, f32[128]{0:T(128)S(1)}, u32[]{:S(2)}) copy-start(f32[128]{0:T(128)S(1)} %add_rsqrt_fusion.1) | copy-start | bytes 1540
  111.7 65.9 %all-to-all-start = ((bf16[32,48,1536]{2,1,0:T(8,128)(2,1)}), bf16[32,48,1536]{2,1,0:T(8,128)(2,1)}, u32[]{:S(2)}, u32[]{:S(2)}) async-start(bf16[32,48,1536]{2,1,0:T(8,128)(2,1)} %bitcast.158), calls=%async_computation | async-start | bytes 9437184 | tf_op jit(solution)/shard_map/all_to_all | solution.py:433
  119.1 10.8 %collective-permute-start.12 = (bf16[1536,128]{1,0:T(8,128)(2,1)}, bf16[1536,128]{1,0:T(8,128)(2,1)}, u32[]{:S(2)}, u32[]{:S(2)}) collective-permute-start(bf16[1536,128]{1,0:T(8,128)(2,1)} %bitcast.191), channel_id=1, source_target_pairs={{0,3},{1,0},{2,1},{3,2},{4,7},{5,4},{6,5},{7,6},{8,11},{9,8},{10,9... | collective-permute-start | bytes 1179656 | tf_op jit(solution)/shard_map/ppermute | solution.py:42
  119.5 12.0 %collective-permute-start.13 = (bf16[1536,128]{1,0:T(8,128)(2,1)}, bf16[1536,128]{1,0:T(8,128)(2,1)}, u32[]{:S(2)}, u32[]{:S(2)}) collective-permute-start(bf16[1536,128]{1,0:T(8,128)(2,1)} %bitcast.192), channel_id=1, source_target_pairs={{0,2},{1,3},{2,0},{3,1},{4,6},{5,7},{6,4},{7,5},{8,10},{9,11},{10,... | collective-permute-start | bytes 1179656 | tf_op jit(solution)/shard_map/ppermute | solution.py:42
  120.3 21.4 %collective-permute-start.14 = (bf16[1536,128]{1,0:T(8,128)(2,1)}, bf16[1536,128]{1,0:T(8,128)(2,1)}, u32[]{:S(2)}, u32[]{:S(2)}) collective-permute-start(bf16[1536,128]{1,0:T(8,128)(2,1)} %bitcast.193), channel_id=1, source_target_pairs={{0,1},{1,2},{2,3},{3,0},{4,5},{5,6},{6,7},{7,4},{8,9},{9,10},{10,1... | collective-permute-start | bytes 1179656 | tf_op jit(solution)/shard_map/ppermute | solution.py:42
  120.8 26.0 %collective-permute-start.15 = (bf16[1536,128]{1,0:T(8,128)(2,1)}, bf16[1536,128]{1,0:T(8,128)(2,1)}, u32[]{:S(2)}, u32[]{:S(2)}) collective-permute-start(bf16[1536,128]{1,0:T(8,128)(2,1)} %bitcast.195), channel_id=1, source_target_pairs={{0,3},{1,0},{2,1},{3,2},{4,7},{5,4},{6,5},{7,6},{8,11},{9,8},{10,9... | collective-permute-start | bytes 1179656 | tf_op jit(solution)/shard_map/ppermute | solution.py:42
  123.1 25.3 %collective-permute-start.16 = (bf16[1536,128]{1,0:T(8,128)(2,1)}, bf16[1536,128]{1,0:T(8,128)(2,1)}, u32[]{:S(2)}, u32[]{:S(2)}) collective-permute-start(bf16[1536,128]{1,0:T(8,128)(2,1)} %bitcast.196), channel_id=1, source_target_pairs={{0,2},{1,3},{2,0},{3,1},{4,6},{5,7},{6,4},{7,5},{8,10},{9,11},{10,... | collective-permute-start | bytes 1179656 | tf_op jit(solution)/shard_map/ppermute | solution.py:42
  129.9 28.6 %collective-permute-start.17 = (bf16[1536,128]{1,0:T(8,128)(2,1)}, bf16[1536,128]{1,0:T(8,128)(2,1)}, u32[]{:S(2)}, u32[]{:S(2)}) collective-permute-start(bf16[1536,128]{1,0:T(8,128)(2,1)} %bitcast.197), channel_id=1, source_target_pairs={{0,1},{1,2},{2,3},{3,0},{4,5},{5,6},{6,7},{7,4},{8,9},{9,10},{10,1... | collective-permute-start | bytes 1179656 | tf_op jit(solution)/shard_map/ppermute | solution.py:42
  131.5 32.2 %collective-permute-start.18 = (bf16[128,1536]{1,0:T(8,128)(2,1)}, bf16[128,1536]{1,0:T(8,128)(2,1)}, u32[]{:S(2)}, u32[]{:S(2)}) collective-permute-start(bf16[128,1536]{1,0:T(8,128)(2,1)} %bitcast.199), channel_id=1, source_target_pairs={{0,3},{1,0},{2,1},{3,2},{4,7},{5,4},{6,5},{7,6},{8,11},{9,8},{10,9... | collective-permute-start | bytes 1179656 | tf_op jit(solution)/shard_map/ppermute | solution.py:42
  141.7 23.6 %collective-permute-start.19 = (bf16[128,1536]{1,0:T(8,128)(2,1)}, bf16[128,1536]{1,0:T(8,128)(2,1)}, u32[]{:S(2)}, u32[]{:S(2)}) collective-permute-start(bf16[128,1536]{1,0:T(8,128)(2,1)} %bitcast.200), channel_id=1, source_target_pairs={{0,2},{1,3},{2,0},{3,1},{4,6},{5,7},{6,4},{7,5},{8,10},{9,11},{10,... | collective-permute-start | bytes 1179656 | tf_op jit(solution)/shard_map/ppermute | solution.py:42
  146.8 27.7 %collective-permute-start.20 = (bf16[128,1536]{1,0:T(8,128)(2,1)}, bf16[128,1536]{1,0:T(8,128)(2,1)}, u32[]{:S(2)}, u32[]{:S(2)}) collective-permute-start(bf16[128,1536]{1,0:T(8,128)(2,1)} %bitcast.201), channel_id=1, source_target_pairs={{0,1},{1,2},{2,3},{3,0},{4,5},{5,6},{6,7},{7,4},{8,9},{9,10},{10,1... | collective-permute-start | bytes 1179656 | tf_op jit(solution)/shard_map/ppermute | solution.py:42
  200.5 70.9 %all-to-all-start.2 = ((bf16[32,48,1664]{2,1,0:T(8,128)(2,1)}), bf16[32,48,1664]{2,1,0:T(8,128)(2,1)}, u32[]{:S(2)}, u32[]{:S(2)}) async-start(bf16[32,48,1664]{2,1,0:T(8,128)(2,1)} %bitcast.164), calls=%async_computation.2 | async-start | bytes 10223616 | tf_op jit(solution)/shard_map/all_to_all | solution.py:448
  223.3 28.9 %collective-permute-start.21 = (bf16[2,1536,128]{2,1,0:T(8,128)(2,1)}, bf16[2,1536,128]{2,1,0:T(8,128)(2,1)}, u32[]{:S(2)}, u32[]{:S(2)}) collective-permute-start(bf16[2,1536,128]{2,1,0:T(8,128)(2,1)} %get-tuple-element.69), channel_id=1, source_target_pairs={{0,1},{1,2},{2,3},{3,0},{4,5},{5,6},{6,7},{7,4},{8,9},{9,10},{10,1... | collective-permute-start | bytes 2359304 | tf_op jit(solution)/shard_map/ppermute | solution.py:46
  223.4 28.8 %collective-permute-start.23 = (bf16[2,1536,128]{2,1,0:T(8,128)(2,1)}, bf16[2,1536,128]{2,1,0:T(8,128)(2,1)}, u32[]{:S(2)}, u32[]{:S(2)}) collective-permute-start(bf16[2,1536,128]{2,1,0:T(8,128)(2,1)} %get-tuple-element.71), channel_id=1, source_target_pairs={{0,3},{1,0},{2,1},{3,2},{4,7},{5,4},{6,5},{7,6},{8,11},{9,8},{10,9... | collective-permute-start | bytes 2359304 | tf_op jit(solution)/shard_map/ppermute | solution.py:46
  226.7 25.5 %collective-permute-start.22 = (bf16[128,1536]{1,0:T(8,128)(2,1)}, bf16[128,1536]{1,0:T(8,128)(2,1)}, u32[]{:S(2)}, u32[]{:S(2)}) collective-permute-start(bf16[128,1536]{1,0:T(8,128)(2,1)} %get-tuple-element.70), channel_id=1, source_target_pairs={{0,1},{1,2},{2,3},{3,0},{4,5},{5,6},{6,7},{7,4},{8,9},{9,10},{10,1... | collective-permute-start | bytes 1179656 | tf_op jit(solution)/shard_map/ppermute | solution.py:46
  226.7 25.5 %collective-permute-start.24 = (bf16[128,1536]{1,0:T(8,128)(2,1)}, bf16[128,1536]{1,0:T(8,128)(2,1)}, u32[]{:S(2)}, u32[]{:S(2)}) collective-permute-start(bf16[128,1536]{1,0:T(8,128)(2,1)} %get-tuple-element.72), channel_id=1, source_target_pairs={{0,3},{1,0},{2,1},{3,2},{4,7},{5,4},{6,5},{7,6},{8,11},{9,8},{10,9... | collective-permute-start | bytes 1179656 | tf_op jit(solution)/shard_map/ppermute | solution.py:46
  279.1 13.2 %collective-permute-start.25 = (bf16[128,1536]{1,0:T(8,128)(2,1)S(1)}, bf16[128,1536]{1,0:T(8,128)(2,1)S(1)}, u32[]{:S(2)}, u32[]{:S(2)}) collective-permute-start(bf16[128,1536]{1,0:T(8,128)(2,1)S(1)} %fusion.97), channel_id=1, source_target_pairs={{0,3},{1,0},{2,1},{3,2},{4,7},{5,4},{6,5},{7,6},{8,11},{9,8},{10,9... | collective-permute-start | bytes 1179656 | tf_op jit(solution)/shard_map/ppermute | solution.py:42
  279.7 12.6 %collective-permute-start.26 = (bf16[128,1536]{1,0:T(8,128)(2,1)S(1)}, bf16[128,1536]{1,0:T(8,128)(2,1)}, u32[]{:S(2)}, u32[]{:S(2)}) collective-permute-start(bf16[128,1536]{1,0:T(8,128)(2,1)S(1)} %fusion.97), channel_id=1, source_target_pairs={{0,2},{1,3},{2,0},{3,1},{4,6},{5,7},{6,4},{7,5},{8,10},{9,11},{10,... | collective-permute-start | bytes 1179656 | tf_op jit(solution)/shard_map/ppermute | solution.py:42
  280.4 20.3 %collective-permute-start.27 = (bf16[128,1536]{1,0:T(8,128)(2,1)S(1)}, bf16[128,1536]{1,0:T(8,128)(2,1)}, u32[]{:S(2)}, u32[]{:S(2)}) collective-permute-start(bf16[128,1536]{1,0:T(8,128)(2,1)S(1)} %fusion.97), channel_id=1, source_target_pairs={{0,1},{1,2},{2,3},{3,0},{4,5},{5,6},{6,7},{7,4},{8,9},{9,10},{10,1... | collective-permute-start | bytes 1179656 | tf_op jit(solution)/shard_map/ppermute | solution.py:42
  283.7 67.4 %all-to-all-start.3 = ((bf16[32,48,1536]{2,1,0:T(8,128)(2,1)}), bf16[32,48,1536]{2,1,0:T(8,128)(2,1)}, u32[]{:S(2)}, u32[]{:S(2)}) async-start(bf16[32,48,1536]{2,1,0:T(8,128)(2,1)} %bitcast.165), calls=%async_computation.3 | async-start | bytes 9437184 | tf_op jit(solution)/shard_map/all_to_all | solution.py:456
  351.1 4.6 collective-permute-start.31
  359.2 31.5 %all-to-all-start.4 = ((bf16[16,6,24,384]{3,2,1,0:T(8,128)(2,1)}), bf16[16,6,24,384]{3,2,1,0:T(8,128)(2,1)}, u32[]{:S(2)}, u32[]{:S(2)}) async-start(bf16[16,6,24,384]{3,2,1,0:T(8,128)(2,1)} %add_convert_fusion), calls=%async_computation.4 | async-start | bytes 3538944 | tf_op jit(solution)/shard_map/all_to_all | solution.py:55
  367.6 63.9 %collective-permute-start.37 = (bf16[128,1536]{1,0:T(8,128)(2,1)}, bf16[128,1536]{1,0:T(8,128)(2,1)}, u32[]{:S(2)}, u32[]{:S(2)}) collective-permute-start(bf16[128,1536]{1,0:T(8,128)(2,1)} %get-tuple-element.94), channel_id=1, source_target_pairs={{0,2},{1,3},{2,0},{3,1},{4,6},{5,7},{6,4},{7,5},{8,10},{9,11},{10,... | collective-permute-start | bytes 1179656 | tf_op jit(solution)/shard_map/ppermute | solution.py:46
  393.9 7.5 %collective-permute-start.32 = (bf16[24,384]{1,0:T(8,128)(2,1)S(1)}, bf16[24,384]{1,0:T(8,128)(2,1)S(1)}, u32[]{:S(2)}, u32[]{:S(2)}) collective-permute-start(bf16[24,384]{1,0:T(8,128)(2,1)S(1)} %get-tuple-element.192), channel_id=1, source_target_pairs={{0,3},{1,0},{2,1},{3,2},{4,7},{5,4},{6,5},{7,6},{8,11},{9,8},{10,9... | collective-permute-start | bytes 55304 | tf_op jit(solution)/shard_map/ppermute | solution.py:42
  397.1 32.6 %collective-permute-start.28 = (bf16[128,1536]{1,0:T(8,128)(2,1)}, bf16[128,1536]{1,0:T(8,128)(2,1)}, u32[]{:S(2)}, u32[]{:S(2)}) collective-permute-start(bf16[128,1536]{1,0:T(8,128)(2,1)} %get-tuple-element.160), channel_id=1, source_target_pairs={{0,1},{1,2},{2,3},{3,0},{4,5},{5,6},{6,7},{7,4},{8,9},{9,10},{10,1... | collective-permute-start | bytes 1179656 | tf_op jit(solution)/shard_map/ppermute | solution.py:46
  397.2 32.5 %collective-permute-start.29 = (bf16[128,1536]{1,0:T(8,128)(2,1)}, bf16[128,1536]{1,0:T(8,128)(2,1)}, u32[]{:S(2)}, u32[]{:S(2)}) collective-permute-start(bf16[128,1536]{1,0:T(8,128)(2,1)} %get-tuple-element.162), channel_id=1, source_target_pairs={{0,2},{1,3},{2,0},{3,1},{4,6},{5,7},{6,4},{7,5},{8,10},{9,11},{10,... | collective-permute-start | bytes 1179656 | tf_op jit(solution)/shard_map/ppermute | solution.py:46
  400.0 29.7 %collective-permute-start.30 = (bf16[128,1536]{1,0:T(8,128)(2,1)}, bf16[128,1536]{1,0:T(8,128)(2,1)}, u32[]{:S(2)}, u32[]{:S(2)}) collective-permute-start(bf16[128,1536]{1,0:T(8,128)(2,1)} %get-tuple-element.161), channel_id=1, source_target_pairs={{0,3},{1,0},{2,1},{3,2},{4,7},{5,4},{6,5},{7,6},{8,11},{9,8},{10,9... | collective-permute-start | bytes 1179656 | tf_op jit(solution)/shard_map/ppermute | solution.py:46
  401.4 14.1 %collective-permute-start.33 = (bf16[24,384]{1,0:T(8,128)(2,1)S(1)}, bf16[24,384]{1,0:T(8,128)(2,1)S(1)}, u32[]{:S(2)}, u32[]{:S(2)}) collective-permute-start(bf16[24,384]{1,0:T(8,128)(2,1)S(1)} %get-tuple-element.191), channel_id=1, source_target_pairs={{0,2},{1,3},{2,0},{3,1},{4,6},{5,7},{6,4},{7,5},{8,10},{9,11},{10,... | collective-permute-start | bytes 55304 | tf_op jit(solution)/shard_map/ppermute | solution.py:42
  415.5 3.8 collective-permute-start.34
  420.7 28.5 %all-to-all-start.5 = ((bf16[16,6,24,384]{3,2,1,0:T(8,128)(2,1)}), bf16[16,6,24,384]{3,2,1,0:T(8,128)(2,1)}, u32[]{:S(2)}, u32[]{:S(2)}) async-start(bf16[16,6,24,384]{3,2,1,0:T(8,128)(2,1)} %broadcast_in_dim.199), calls=%async_computation.5 | async-start | bytes 3538944 | tf_op jit(solution)/shard_map/all_to_all | solution.py:55
  429.1 25.2 %collective-permute-start.36 = (bf16[2,1536,128]{2,1,0:T(8,128)(2,1)}, bf16[2,1536,128]{2,1,0:T(8,128)(2,1)}, u32[]{:S(2)}, u32[]{:S(2)}) collective-permute-start(bf16[2,1536,128]{2,1,0:T(8,128)(2,1)} %get-tuple-element.90), channel_id=1, source_target_pairs={{0,2},{1,3},{2,0},{3,1},{4,6},{5,7},{6,4},{7,5},{8,10},{9,11},{10,... | collective-permute-start | bytes 2359304 | tf_op jit(solution)/shard_map/ppermute | solution.py:46
  449.2 15.8 %collective-permute-start.35 = (bf16[16,6,24,384]{3,2,1,0:T(8,128)(2,1)}, bf16[16,6,24,384]{3,2,1,0:T(8,128)(2,1)}, u32[]{:S(2)}, u32[]{:S(2)}) collective-permute-start(bf16[16,6,24,384]{3,2,1,0:T(8,128)(2,1)} %all-to-all-done.5.a_ref.ao_ref), channel_id=1, source_target_pairs={{0,4},{4,0},{8,12},{12,8},{16,20},{20,16},{24,28},{28,24},{32,36},... | collective-permute-start | bytes 5308424 | tf_op jit(solution)/shard_map/ppermute | solution.py:50
  (64 other events, 727.5 us)

commit v3 on v2

v3 whole, which is shorter than its diff:
```python
import functools

import jax
import jax.numpy as jnp
from jax import lax
from jax.experimental import pallas as pl
from jax.experimental.pallas import tpu as pltpu
from jax.sharding import PartitionSpec as P

HEADS = 24
KV_HEADS = 8
HEAD = 64
EPS = 1e-06
THETA = 10000.0
MASKED = -1e30
BF = jnp.bfloat16
F32 = jnp.float32
WS = 4
CHIPS = 16
CAP = 48
VM = 60 * 1024 * 1024


def dot(a, b):
    return jnp.dot(a, b, preferred_element_type=F32)


def dot_t(a, b):
    return lax.dot_general(a, b, (((1,), (1,)), ((), ())), preferred_element_type=F32)


def tdot(a, b):
    return lax.dot_general(a, b, (((0,), (0,)), ((), ())), preferred_element_type=F32)


def split(v):
    hi = v.astype(BF)
    return hi, (v - hi.astype(F32)).astype(BF)


def from_peer(v, k):
    return lax.ppermute(v, "ws", [(s, (s - k) % WS) for s in range(WS)])


def to_peer(v, k):
    return lax.ppermute(v, "ws", [(s, (s + k) % WS) for s in range(WS)])


def other_core(v):
    return lax.ppermute(v, "exp", [(s, s ^ 1) for s in range(2 * CHIPS)])


def same_core(v):
    groups = [[2 * chip + core for chip in range(CHIPS)] for core in range(2)]
    return lax.all_to_all(v, "exp", 0, 0, tiled=True, axis_index_groups=groups)


def tree_layout(lengths, parents, token_index):
    seg = lengths.shape[0]
    labels = jnp.arange(seg, dtype=jnp.int32)
    segment_end = jnp.cumsum(lengths, dtype=jnp.int32)
    starts = segment_end - lengths
    segment = jnp.sum((token_index[:, None] >= segment_end[None, :]).astype(jnp.int32), axis=1)
    reach = ((parents[:, None] == labels[None, :]) | (labels[:, None] == labels[None, :])).astype(
        BF
    )
    for _ in range(4):
        reach = (dot(reach, reach) > 0.5).astype(BF)
    above = jnp.sum(reach.astype(jnp.int32) * lengths[None, :], axis=1) - lengths
    members = segment[:, None] == labels[None, :]
    position = jnp.sum(jnp.where(members, (above - starts)[None, :], 0), axis=1) + token_index
    members = members.astype(BF)
    reaches = dot(members, reach).astype(BF)
    visible = (dot_t(reaches, members) > 0.5) & (token_index[None, :] <= token_index[:, None])
    return visible, position


def expert_body(width, ff, x_ref, dy_ref, sel_ref, wr_ref, *rest):
    wg, wu, wd = rest[0:4], rest[4:8], rest[8:12]
    y_ref, dx_ref, h_ref, dgu_ref, dyo_ref = rest[12:17]
    wgu, wdn = rest[17:]
    part = wg[0].shape[1]

    @pl.when(pl.program_id(0) == 0)
    def _():
        for r in range(4):
            wgu[:, r * part : (r + 1) * part] = wg[r][...]
            wgu[:, ff + r * part : ff + (r + 1) * part] = wu[r][...]
            wdn[r * part : (r + 1) * part, :] = wd[r][...]
        wgu[:, 2 * ff :] = wr_ref[...]

    x = x_ref[...]
    pre = dot(x, wgu[...])
    g, u, logits = pre[:, :ff], pre[:, ff : 2 * ff], pre[:, 2 * ff :]
    mask = dy_ref[:, width:].astype(F32) > 0.5
    logits = jnp.where(mask, logits, MASKED)
    lifted = jnp.where(mask, jnp.exp(logits - jnp.max(logits, axis=1, keepdims=True)), 0.0)
    total = jnp.maximum(jnp.sum(lifted, axis=1, keepdims=True), 1e-30)
    gate = jnp.sum(lifted * sel_ref[0:1, :], axis=1, keepdims=True) / total
    sig = 1.0 / (1.0 + jnp.exp(-g))
    silu = g * sig
    h = (silu * u).astype(BF)
    h_ref[...] = h
    y = dot(h, wdn[...]).astype(BF)
    y_ref[...] = y
    dy = dy_ref[:, :width].astype(F32)
    dgate = jnp.sum(dy * y.astype(F32), axis=1, keepdims=True)
    d_y = (gate * dy).astype(BF)
    dyo_ref[...] = d_y
    dh = dot_t(d_y, wdn[...])
    dgu_ref[:, :ff] = (dh * u * sig * (1.0 + g * (1.0 - sig))).astype(BF)
    dgu_ref[:, ff:] = (dh * silu).astype(BF)
    dx_ref[:, :width] = dot_t(dgu_ref[...], wgu[:, : 2 * ff]).astype(BF)
    hi = dgate.astype(BF).astype(F32)
    dx_ref[:, width:] = (hi * sel_ref[0:1, :] + (dgate - hi) * sel_ref[1:2, :]).astype(BF)

def expert_pass(x, dy, sel, wr, wg, wu, wd, tile):
    slots, width = x.shape
    part = wg[0].shape[1]; ff = 4 * part
    row = lambda w: pl.BlockSpec((tile, w), lambda i: (i, 0))
    whole = lambda a: pl.BlockSpec(a.shape, lambda i: (0, 0))
    return pl.pallas_call(
        functools.partial(expert_body, width, ff),
        grid=(slots // tile,),
        in_specs=[row(width), row(width + 128), whole(sel), whole(wr)] + [whole(a) for a in (*wg, *wu, *wd)],
        out_specs=[row(width), row(width + 128), row(ff), row(2 * ff), row(width)],
        out_shape=[jax.ShapeDtypeStruct((slots, w), BF) for w in (width, width + 128, ff, 2 * ff, width)],
        scratch_shapes=[pltpu.VMEM((width, 2 * ff + 128), BF), pltpu.VMEM((ff, width), BF)],
        compiler_params=pltpu.CompilerParams(vmem_limit_bytes=VM),
        cost_estimate=pl.CostEstimate(flops=12*slots*width*ff, bytes_accessed=12*slots*width, transcendentals=slots*ff),
        name="expert_pass",
    )(x, dy, sel, wr, *wg, *wu, *wd)

def slope_body(x_ref, dgu_ref, h_ref, dy_ref, own_g, own_u, own_d, *peers):
    part = own_g.shape[1]
    ff = h_ref.shape[1]
    gu = tdot(x_ref[...], dgu_ref[...])
    dn = tdot(h_ref[...], dy_ref[...])
    own_g[...] = gu[:, :part]
    own_u[...] = gu[:, ff : ff + part]
    own_d[...] = dn[:part]
    for k in (1, 2, 3):
        peers[2 * k - 2][0] = gu[:, k * part : (k + 1) * part].astype(BF)
        peers[2 * k - 2][1] = gu[:, ff + k * part : ff + (k + 1) * part].astype(BF)
        peers[2 * k - 1][...] = dn[k * part : (k + 1) * part].astype(BF)

def expert_slopes(x, dgu, h, dy, tile=256):
    slots, width = x.shape
    ff = h.shape[1]; part = ff // 4
    col = pl.BlockSpec((slots, tile), lambda i: (0, i))
    whole = lambda a: pl.BlockSpec(a.shape, lambda i: (0, 0))
    tall = pl.BlockSpec((tile, part), lambda i: (i, 0))
    wide = pl.BlockSpec((part, tile), lambda i: (0, i))
    pair = pl.BlockSpec((2, tile, part), lambda i: (0, i, 0))
    S = jax.ShapeDtypeStruct
    return pl.pallas_call(
        slope_body,
        grid=(width // tile,),
        in_specs=[col, whole(dgu), whole(h), col],
        out_specs=[tall, tall, wide] + [pair, wide] * 3,
        out_shape=[S((width, part), F32)] * 2 + [S((part, width), F32)] + [S((2, width, part), BF), S((part, width), BF)] * 3,
        compiler_params=pltpu.CompilerParams(vmem_limit_bytes=VM),
        cost_estimate=pl.CostEstimate(flops=6*slots*width*ff, bytes_accessed=8*slots*width, transcendentals=0),
        name="expert_slopes",
    )(x, dgu, h, dy)


def finish_body(experts, a_ref, b_ref, ao_ref, bo_ref, flag_ref, *refs):
    q_ref, k_ref, v_ref, r_ref, g_ref, o_ref, s_ref = refs
    turn = pl.program_id(0)
    second = flag_ref[0:1, 0:1]
    rows = q_ref.shape[0]
    half = a_ref.shape[3]
    kv = k_ref.shape[1]
    mine = a_ref[:, 0].astype(F32).reshape(rows, half)
    twin = b_ref[:, 0].astype(F32).reshape(rows, half)
    q_ref[...] = jnp.where(second > 0.5, twin, mine)
    rest = jnp.where(second > 0.5, mine, twin)
    k_ref[...] = rest[:, :kv]
    v_ref[...] = rest[:, kv : 2 * kv]

    @pl.when(turn == 0)
    def _():
        s_ref[...] = rest[:, 2 * kv :]

    @pl.when(turn > 0)
    def _():
        s_ref[...] += rest[:, 2 * kv :]

    @pl.when(turn == WS - 1)
    def _():
        turned = s_ref[...].T
        r_ref[...] = turned[:experts]
        g_ref[...] = turned[experts : experts + 8]

    mine = ao_ref[:, 0].astype(F32).reshape(rows, half)
    twin = bo_ref[:, 0].astype(F32).reshape(rows, half)
    use_twin = jnp.where(turn < 2, second, 1.0 - second)
    o_ref[...] = jnp.where(use_twin > 0.5, twin, mine)


def finish(experts, mine, twin, flag):
    chips, sets, step, half = mine.shape
    rows = chips * step
    first = pl.BlockSpec((chips, 1, step, half), lambda i: (0, i, 0, 0))
    later = pl.BlockSpec((chips, 1, step, half), lambda i: (0, WS + i % 2, 0, 0))
    kv = (half - 128) // 2
    S = jax.ShapeDtypeStruct
    return pl.pallas_call(
        functools.partial(finish_body, experts),
        grid=(WS,),
        in_specs=[first, first, later, later, pl.BlockSpec(flag.shape, lambda i: (0, 0))],
        out_specs=[
            pl.BlockSpec((rows, half), lambda i: (0, i)),
            pl.BlockSpec((rows, kv), lambda i: (0, i)),
            pl.BlockSpec((rows, kv), lambda i: (0, i)),
            pl.BlockSpec((experts, rows), lambda i: (0, 0)),
            pl.BlockSpec((8, rows), lambda i: (0, 0)),
            pl.BlockSpec((rows, half), lambda i: (0, i)),
        ],
        scratch_shapes=[pltpu.VMEM((rows, 128), F32)],
        out_shape=[
            S((rows, WS * half), F32),
            S((rows, WS * kv), F32),
            S((rows, WS * kv), F32),
            S((experts, rows), F32),
            S((8, rows), F32),
            S((rows, WS * half), F32),
        ],
        compiler_params=pltpu.CompilerParams(vmem_limit_bytes=VM),
        cost_estimate=pl.CostEstimate(flops=0, bytes_accessed=16 * rows * WS * half, transcendentals=0),
        name="finish",
    )(mine, twin, mine, twin, flag)


def whole(shape):
    return pl.BlockSpec(shape, lambda *_: (0,) * len(shape))


def sds(shape, kind):
    return jax.ShapeDtypeStruct(shape, kind)


def one_step(body, name, scalars, arrays, outs, scratch, flops):
    moved = sum(a.size * a.dtype.itemsize for a in arrays)
    return pl.pallas_call(
        body,
        in_specs=[pl.BlockSpec(memory_space=pltpu.SMEM)] * len(scalars)
        + [pl.BlockSpec(memory_space=pltpu.VMEM)] * len(arrays),
        out_specs=[pl.BlockSpec(memory_space=pltpu.VMEM)] * len(outs),
        out_shape=outs,
        scratch_shapes=scratch,
        compiler_params=pltpu.CompilerParams(vmem_limit_bytes=VM),
        cost_estimate=pl.CostEstimate(flops=flops, bytes_accessed=moved, transcendentals=0),
        name=name,
    )(*scalars, *arrays)


def other_half(v):
    lanes = v.shape[1]
    low = lax.broadcasted_iota(jnp.int32, v.shape, 1) % HEAD < HEAD // 2
    ahead = pltpu.roll(v, lanes - HEAD // 2, 1)
    behind = pltpu.roll(v, HEAD // 2, 1)
    return jnp.where(low, ahead, behind)


def wide(ref, times):
    return jnp.concatenate([ref[...]] * times, axis=1)


def rms(x):
    return lax.rsqrt(jnp.mean(x * x, axis=1, keepdims=True) + EPS)


def column_sum(m, lane):
    hi, lo = split(m)
    pick = (lax.broadcasted_iota(jnp.int32, (m.shape[0], 128), 1) == lane).astype(F32).astype(BF)
    return tdot(hi, pick) + tdot(lo, pick)


def pack_body(experts, place_ref, wq, wk, wv, wr, na, nm, *outs):
    small = outs[WS + 1]
    me, core = place_ref[0], place_ref[1]
    strip = wq.shape[0] // 2
    q_w, kv_w = wq.shape[1] // WS, wk.shape[1] // WS
    shard = wq.shape[0]
    gains = jnp.concatenate(
        [na[...].astype(F32), nm[...].astype(F32), jnp.zeros((6, shard), F32)], axis=0
    ).T
    small[...] = jnp.concatenate(
        [wr[...].astype(F32), gains, jnp.zeros((shard, 128 - experts - 8), F32)], axis=1
    ).astype(BF)
    for r in range(WS + 1):
        side = core if r < WS else 1 - core
        d = lax.rem(me + WS - r % WS, WS)
        part = pl.ds(pl.multiple_of(side * strip, 64), strip)
        outs[r][:, :q_w] = wq[part, pl.ds(pl.multiple_of(d * q_w, 128), q_w)]
        spot = pl.ds(pl.multiple_of(d * kv_w, 128), kv_w)
        outs[r][:, q_w : q_w + kv_w] = wk[part, spot]
        outs[r][:, q_w + kv_w : q_w + 2 * kv_w] = wv[part, spot]
        outs[r][:, q_w + 2 * kv_w :] = small[part, :]


def pack(experts, place, wq, wk, wv, wr, na, nm):
    shard = wq.shape[0]
    wide_w = (wq.shape[1] + 2 * wk.shape[1]) // WS + 128
    return one_step(
        functools.partial(pack_body, experts),
        "pack",
        [place],
        [wq, wk, wv, wr, na[None], nm[None]],
        [sds((shard // 2, wide_w), BF)] * (WS + 1),
        [pltpu.VMEM((shard, 128), BF)],
        0,
    )


def attend_body(experts, place_ref, *refs):
    xs, own, twin = refs[0:4], refs[4:8], refs[8:12]
    cos_ref, sin_ref, bias_ref, wo_ref = refs[12:16]
    h1_ref, qkv_ref, o_ref, lse_ref, w_ref, small_ref, rows_ref = refs[16:23]
    parts = refs[23:27]
    me, core = place_ref[0], place_ref[1]
    rows = xs[0].shape[0]
    strip = own[0].shape[0]
    heads = o_ref.shape[1] // HEAD
    q_w = heads * HEAD
    qkv_w = qkv_ref.shape[1]
    kv_w = (qkv_w - q_w) // 2
    group = q_w // kv_w
    for r in range(WS):
        base = lax.rem(me + r, WS) * (2 * strip)
        for source, side in ((own[r], core), (twin[r], 1 - core)):
            spot = pl.ds(pl.multiple_of(base + side * strip, 64), strip)
            w_ref[spot, :] = source[:, :qkv_w]
            small_ref[spot, :] = source[:, qkv_w:]
    turned = small_ref[...].astype(F32).T
    rows_ref[...] = jnp.concatenate(
        [turned[experts : experts + 2], jnp.zeros((6, turned.shape[1]), F32)], axis=0
    )
    gain = turned[experts : experts + 1]
    for r in range(WS):
        x = xs[r][...].astype(F32)
        h1_ref[r * rows : (r + 1) * rows, :] = (x * rms(x) * gain).astype(BF)
    qkv = dot(h1_ref[...], w_ref[...])
    qk = qkv[:, : q_w + kv_w]
    times = (q_w + kv_w) // 128
    qk = qk * wide(cos_ref, times) + other_half(qk) * wide(sin_ref, times)
    qkv_ref[:, : q_w + kv_w] = qk.astype(BF)
    qkv_ref[:, q_w + kv_w :] = qkv[:, q_w + kv_w :].astype(BF)
    for h in range(heads):
        at = h // group * HEAD
        q = qkv_ref[:, h * HEAD : (h + 1) * HEAD]
        k = qkv_ref[:, q_w + at : q_w + at + HEAD]
        v = qkv_ref[:, q_w + kv_w + at : q_w + kv_w + at + HEAD]
        s = dot_t(q, k) * HEAD ** (-0.5) + bias_ref[...]
        peak = jnp.max(s, axis=1, keepdims=True)
        p = jnp.exp(s - peak)
        total = jnp.sum(p, axis=1, keepdims=True)
        lse_ref[:, h : h + 1] = peak + jnp.log(total)
        o_ref[:, h * HEAD : (h + 1) * HEAD] = dot((p / total).astype(BF), v).astype(BF)
    for r in range(WS):
        part = dot(o_ref[r * rows : (r + 1) * rows, :], wo_ref[...])
        parts[r][...] = part.astype(parts[r].dtype)


def attend(experts, place, xs, own, twin, cos, sin, bias, wo):
    rows, width = xs[0].shape
    tree = rows * WS
    q_w, qkv_w = wo.shape[0], own[0].shape[1] - 128
    outs = [
        sds((tree, width), BF),
        sds((tree, qkv_w), BF),
        sds((tree, q_w), BF),
        sds((tree, 128), F32),
        sds((width, qkv_w), BF),
        sds((width, 128), BF),
        sds((8, width), F32),
        sds((rows, width), F32),
    ] + [sds((rows, width), BF)] * 3
    flops = 2 * tree * width * (qkv_w + q_w) + 4 * tree * tree * q_w
    return one_step(
        functools.partial(attend_body, experts),
        "attend",
        [place],
        [*xs, *own, *twin, cos, sin, bias, wo],
        outs,
        [],
        flops,
    )


def enter_body(x_ref, p0, p1, p2, p3, rows_ref, router_ref, slot_ref, chosen_ref, spread_ref, *outs):
    x2_ref, h2_ref, send_ref, gates_ref, gs_ref = outs
    x2 = x_ref[...].astype(F32) + p0[...]
    for p in (p1, p2, p3):
        x2 = x2 + p[...].astype(F32)
    x2_ref[...] = x2
    h2 = (x2 * rms(x2) * rows_ref[1:2, :]).astype(BF)
    h2_ref[...] = h2
    send_ref[...] = tdot(slot_ref[...], h2).astype(BF)
    logits = dot(h2, router_ref[...])
    mask = chosen_ref[...].astype(F32) > 0.5
    logits = jnp.where(mask, logits, MASKED)
    lifted = jnp.where(mask, jnp.exp(logits - jnp.max(logits, axis=1, keepdims=True)), 0.0)
    gates = lifted / jnp.maximum(jnp.sum(lifted, axis=1, keepdims=True), 1e-30)
    gates_ref[...] = gates
    hi, lo = split(gates)
    on_slots = dot(hi, spread_ref[...]) + dot(lo, spread_ref[...])
    hi, lo = split(on_slots * slot_ref[...].astype(F32))
    rows = x2.shape[0]
    gs_ref[:rows, :] = hi
    gs_ref[rows:, :] = lo


def enter(x, parts, rows, router, to_slot, chosen, spread):
    n, width = x.shape
    slots = to_slot.shape[1]
    outs = [
        sds((n, width), F32),
        sds((n, width), BF),
        sds((slots, width), BF),
        sds((n, 128), F32),
        sds((2 * n, slots), BF),
    ]
    return one_step(
        enter_body,
        "enter",
        [],
        [x, *parts, rows, router, to_slot, chosen, spread],
        outs,
        [],
        2 * n * width * slots,
    )


def leave_body(experts, back_ref, slot_ref, gates_ref, router_ref, x2_ref, h2_ref, rows_ref, cot_ref, *outs):
    dx2_ref, da_ref, small_ref = outs
    width = x2_ref.shape[1]
    back = dot(slot_ref[...], back_ref[...])
    tail = back[:, width:]
    dgate = tail + pltpu.roll(tail, 128 - experts, 1)
    gates = gates_ref[...]
    dl = gates * (dgate - jnp.sum(gates * dgate, axis=1, keepdims=True))
    hi, lo = split(dl)
    dh2 = back[:, :width] + dot_t(hi, router_ref[...]) + dot_t(lo, router_ref[...])
    x2 = x2_ref[...]
    scale, gain = rms(x2), rows_ref[1:2, :]
    inner = jnp.mean(gain * dh2 * x2, axis=1, keepdims=True)
    dx2 = cot_ref[...].astype(F32) + scale * gain * dh2 - x2 * scale * scale * scale * inner
    dx2_ref[...] = dx2
    da_ref[...] = dx2.astype(BF)
    h2 = h2_ref[...]
    small_ref[...] = tdot(h2, hi) + tdot(h2, lo) + column_sum(dh2 * x2 * scale, experts)


def leave(experts, back, to_slot, gates, router, x2, h2, rows, cot):
    n, width = x2.shape
    outs = [sds((n, width), F32), sds((n, width), BF), sds((width, 128), F32)]
    return one_step(
        functools.partial(leave_body, experts),
        "leave",
        [],
        [back, to_slot, gates, router, x2, h2, rows, cot],
        outs,
        [],
        2 * n * back.size,
    )


def attend_back_body(experts, place_ref, *refs):
    das, xs = refs[0:4], refs[4:8]
    wo_ref, qkv_ref, o_ref, lse_ref, h1_ref, w_ref = refs[8:14]
    cos_ref, sin_ref, bias_ref, small_ref = refs[14:18]
    keep_ref, give_ref = refs[18:20]
    parts = refs[20:24]
    da, do, dqk, dqkv = refs[24:28]
    core = place_ref[1]
    rows = xs[0].shape[0]
    q_w, qkv_w = o_ref.shape[1], qkv_ref.shape[1]
    kv_w = (qkv_w - q_w) // 2
    group = q_w // kv_w
    scale = HEAD ** (-0.5)
    for r in range(WS):
        da[r * rows : (r + 1) * rows, :] = das[r][...]
    do[...] = dot_t(da[...], wo_ref[...]).astype(BF)
    for n in range(kv_w // HEAD):
        at = n * HEAD
        k = qkv_ref[:, q_w + at : q_w + at + HEAD]
        v = qkv_ref[:, q_w + kv_w + at : q_w + kv_w + at + HEAD]
        dk, dv = None, None
        for h in range(n * group, (n + 1) * group):
            q = qkv_ref[:, h * HEAD : (h + 1) * HEAD]
            doh = do[:, h * HEAD : (h + 1) * HEAD]
            p = jnp.exp(dot_t(q, k) * scale + bias_ref[...] - lse_ref[:, h : h + 1])
            dp = dot_t(doh, v)
            delta = jnp.sum(p * dp, axis=1, keepdims=True)
            ds = (p * (dp - delta)).astype(BF)
            dqk[:, h * HEAD : (h + 1) * HEAD] = dot(ds, k) * scale
            more_k, more_v = tdot(ds, q), tdot(p.astype(BF), doh)
            dk = more_k if dk is None else dk + more_k
            dv = more_v if dv is None else dv + more_v
        dqk[:, q_w + at : q_w + at + HEAD] = dk * scale
        dqkv[:, q_w + kv_w + at : q_w + kv_w + at + HEAD] = dv.astype(BF)
    dqkv[:, qkv_w:] = jnp.zeros((da.shape[0], 128), BF)
    d = dqk[...]
    times = (q_w + kv_w) // 128
    d = d * wide(cos_ref, times) - other_half(d) * wide(sin_ref, times)
    dqkv[:, : q_w + kv_w] = d.astype(BF)
    small = small_ref[...]
    for r in range(WS):
        dh1 = dot_t(dqkv[r * rows : (r + 1) * rows, :qkv_w], w_ref[...])
        parts[r][...] = dh1.astype(parts[r].dtype)
        x = xs[r][...].astype(F32)
        small = small + column_sum(dh1 * x * rms(x), experts + 1)
    half = keep_ref.shape[3]
    chips, step = keep_ref.shape[0], keep_ref.shape[2]
    count = chips * step

    def put(i, first, second):
        kept = jnp.where(core == 0, first, second)
        given = jnp.where(core == 0, second, first)
        keep_ref[:, i] = kept.reshape(chips, step, half)
        give_ref[:, i] = given.reshape(chips, step, half).astype(BF)

    for i in range(WS):
        both = tdot(h1_ref[:, i * count : (i + 1) * count], dqkv[...])
        mine = small[i * count : (i + 1) * count]
        second = jnp.concatenate([both[:, half : 2 * half - 128], both[:, 2 * half - 128 :] + mine], axis=1)
        put(i, both[:, :half], second)
    slope = tdot(o_ref[...], da[...])
    for i in range(2):
        put(WS + i, slope[:, i * half : (i + 1) * half], slope[:, (2 + i) * half : (3 + i) * half])


def attend_back(experts, place, das, xs, wo, qkv, o, lse, h1, w, cos, sin, bias, small):
    rows, width = xs[0].shape
    tree = rows * WS
    q_w, qkv_w = wo.shape[0], qkv.shape[1]
    half = (qkv_w + 128) // 2
    load = (CHIPS, WS + 2, width // WS // CHIPS, half)
    outs = [sds(load, F32), sds(load, BF), sds((rows, width), F32)] + [sds((rows, width), BF)] * 3
    scratch = [
        pltpu.VMEM((tree, width), BF),
        pltpu.VMEM((tree, q_w), BF),
        pltpu.VMEM((tree, (q_w + qkv_w) // 2), F32),
        pltpu.VMEM((tree, qkv_w + 128), BF),
    ]
    flops = 4 * tree * width * (qkv_w + q_w) + 10 * tree * tree * q_w
    return one_step(
        functools.partial(attend_back_body, experts),
        "attend_back",
        [place],
        [*das, *xs, wo, qkv, o, lse, h1, w, cos, sin, bias, small],
        outs,
        scratch,
        flops,
    )


def shards(
    tokens,
    cotangent,
    seg_lengths,
    parents,
    routes,
    norm_attn,
    w_query,
    w_key,
    w_value,
    w_out,
    norm_moe,
    w_router,
    w_gate,
    w_up,
    w_down,
):
    me = lax.axis_index("ws")
    expert = lax.axis_index("exp")
    core = expert % 2
    place = jnp.stack([me, core]).astype(jnp.int32)
    rows, width = tokens.shape
    shard = width // WS
    strip = shard // 2
    experts = 2 * CHIPS
    q_w, kv_w = HEADS // WS * HEAD, KV_HEADS // WS * HEAD
    slots = experts * CAP

    def gathered(v):
        return [v] + [from_peer(v, k) for k in (1, 2, 3)]

    xs = gathered(tokens)

    pieces = pack(experts, place, w_query, w_key, w_value, w_router, norm_attn, norm_moe)
    pieces, routes = lax.optimization_barrier((pieces, routes))
    own = [pieces[0]] + [from_peer(pieces[k], k) for k in (1, 2, 3)]
    twin = [pieces[WS]] + [other_core(own[k]) for k in (1, 2, 3)]

    labels = jnp.arange(experts, dtype=jnp.int32)
    lane = jnp.arange(128, dtype=jnp.int32)
    chosen = jnp.any(routes[:, :, None] == lane[None, None, :], axis=1)
    row_id = jnp.arange(rows, dtype=jnp.int32)
    before = (row_id[None, :] < row_id[:, None]).astype(BF)
    rank = dot(before, chosen.astype(BF))
    col = jnp.arange(slots, dtype=jnp.int32)
    spread = (col[None, :] // CAP == lane[:, None]).astype(BF)
    spot = dot(jnp.where(chosen, rank + 1.0, 0.0).astype(BF), spread)
    nothing = (xs[1][:1, :1] + xs[3][:1, :1]).astype(F32) * 0.0
    to_slot = (spot == (col % CAP + 1).astype(F32)[None, :] + nothing).astype(BF)
    chosen = chosen.astype(BF)
    extra = jnp.concatenate([cotangent, chosen], axis=1)
    dy_send = tdot(to_slot, extra).astype(BF).reshape(experts, CAP, width + 128)
    dy_slots = lax.all_to_all(dy_send, "exp", 0, 0, tiled=True).reshape(slots, width + 128)

    order = (
        ((me + jnp.arange(WS, dtype=jnp.int32)) % WS)[:, None] * rows + row_id[None, :]
    ).reshape(-1)
    visible, position = tree_layout(seg_lengths[0], parents[0], order)
    bias = jnp.where(visible, 0.0, MASKED).astype(F32)
    inverse = THETA ** (-(lane % (HEAD // 2)).astype(F32) * 2.0 / HEAD)
    angles = position.astype(F32)[:, None] * inverse[None, :]
    cosines = jnp.cos(angles)
    sines = jnp.where((lane % HEAD < HEAD // 2)[None, :], -1.0, 1.0) * jnp.sin(angles)
    h1, qkv, o, lse, w_qkv, small_full, gains, *parts = attend(
        experts, place, xs, own, twin, cosines, sines, bias, w_out
    )
    sums = [parts[0]] + [to_peer(parts[k], k) for k in (1, 2, 3)]
    x2, h2, x_send, gates, gate_slots = enter(
        tokens, sums, gains, small_full, to_slot, chosen, spread
    )
    x_send, wg_own, wu_own, wd_own = lax.optimization_barrier(
        (x_send, w_gate[0], w_up[0], w_down[0])
    )
    x_slots = lax.all_to_all(
        x_send.reshape(experts, CAP, width), "exp", 0, 0, tiled=True
    ).reshape(slots, width)

    sel = jnp.concatenate(
        [
            (lane == expert).astype(F32)[None],
            (lane == expert + experts).astype(F32)[None],
            jnp.zeros((6, 128), F32),
        ],
        axis=0,
    )
    y, dx_send, hidden, d_gu, d_y = expert_pass(
        x_slots, dy_slots, sel, small_full, gathered(wg_own), gathered(wu_own), gathered(wd_own), 512
    )
    dx_back = lax.all_to_all(
        dx_send.reshape(experts, CAP, width + 128), "exp", 0, 0, tiled=True
    ).reshape(slots, width + 128)

    own_g, own_u, own_d, gu1, dn1, gu2, dn2, gu3, dn3 = expert_slopes(x_slots, d_gu, hidden, d_y)
    gu1, dn1 = to_peer(gu1, 1), to_peer(dn1, 1)
    gu3, dn3 = to_peer(gu3, 3), to_peer(dn3, 3)
    gu2, dn2 = to_peer(gu2, 2), to_peer(dn2, 2)
    dx_back, y, gu1, dn1, gu2, dn2, gu3, dn3 = lax.optimization_barrier(
        (dx_back, y, gu1, dn1, gu2, dn2, gu3, dn3)
    )
    y_back = lax.all_to_all(y.reshape(experts, CAP, width), "exp", 0, 0, tiled=True).reshape(
        slots, width
    )

    dx2, d_a, small_terms = leave(
        experts, dx_back, to_slot, gates, small_full, x2, h2, gains, cotangent
    )
    das = gathered(d_a)
    grad_gu = jnp.stack([own_g, own_u]) + gu1.astype(F32) + gu2.astype(F32) + gu3.astype(F32)
    grad_wg, grad_wu = grad_gu[0][None], grad_gu[1][None]
    grad_wd = (own_d + dn1.astype(F32) + dn2.astype(F32) + dn3.astype(F32))[None]
    keep, give, *slopes = attend_back(
        experts, place, das, xs, w_out, qkv, o, lse, h1, w_qkv, cosines, sines, bias, small_terms
    )
    dh1 = slopes[0]
    for k in (1, 2, 3):
        dh1 = dh1 + to_peer(slopes[k], k).astype(F32)
    resid = tokens.astype(F32)
    scale = lax.rsqrt(jnp.mean(resid * resid, axis=-1, keepdims=True) + EPS)
    inner = jnp.mean(gains[0:1] * dh1 * resid, axis=-1, keepdims=True)
    grad_tokens = dx2 + scale * gains[0:1] * dh1 - resid * scale * scale * scale * inner

    half = (q_w + 2 * kv_w + 128) // 2
    flag = jnp.broadcast_to(jnp.stack([core, 1 - core]).astype(F32)[:, None], (2, 128))
    flag = jnp.concatenate([flag, jnp.zeros((6, 128), F32)], axis=0)
    give, y_back = lax.optimization_barrier((give, y_back))
    sent = (keep + other_core(give).astype(F32)).astype(BF)
    step = shard // CHIPS
    both = dot(gate_slots, y_back)
    layer_out = (x2 + both[:rows] + both[rows:]).astype(BF)
    got = same_core(sent)
    got, layer_out, grad_tokens, grad_wg, grad_wu, grad_wd = lax.optimization_barrier(
        (got, layer_out, grad_tokens, grad_wg, grad_wu, grad_wd)
    )
    total = jnp.sum(got.astype(F32), axis=0).astype(BF)
    turned = jnp.stack(
        [lax.dynamic_index_in_dim(total, me, 0, False)]
        + [
            from_peer(lax.dynamic_index_in_dim(total, (me - k) % WS, 0, False), k)
            for k in (1, 2, 3)
        ]
    )
    turned = lax.dynamic_slice_in_dim(jnp.concatenate([turned, turned]), (WS - me) % WS, WS, 0)
    final = jnp.concatenate([turned, total[WS:]], axis=0)
    spread_out = same_core(jnp.broadcast_to(final, (CHIPS,) + final.shape))
    twin_out = other_core(spread_out)
    sum_query, sum_key, sum_value, sum_router, sum_gains, sum_out = finish(
        experts, spread_out, twin_out, flag
    )

    return (
        layer_out,
        grad_tokens,
        sum_gains[1],
        sum_query,
        sum_key,
        sum_value,
        sum_out,
        sum_gains[0],
        sum_router.T,
        grad_wg,
        grad_wu,
        grad_wd,
    )


def solution(mesh):
    rows = P(("exp", "ws"), None)
    placed = (
        rows,
        rows,
        P("exp", None),
        P("exp", None),
        rows,
        P("ws"),
        P("ws", None),
        P("ws", None),
        P("ws", None),
        P("ws", None),
        P("ws"),
        P("ws", None),
        P("exp", None, "ws"),
        P("exp", None, "ws"),
        P("exp", "ws", None),
    )
    return jax.shard_map(
        shards,
        mesh=mesh,
        in_specs=placed,
        out_specs=(
            rows,
            rows,
            P("ws"),
            P("ws", None),
            P("ws", None),
            P("ws", None),
            P("ws", None),
            P("ws"),
            P("ws", None),
            P("exp", None, "ws"),
            P("exp", None, "ws"),
            P("exp", "ws", None),
        ),
        check_vma=False,
    )
```

time: 483 us -> 450 us (0.932)
  matrix products: 50.4 us -> 11 us
  Pallas kernels: 48.9 us -> 87 us
  local copies, waits for them, and re-layouts: 44.4 us -> 14 us
  blocking collectives: 0 us -> 26.3 us
  other arithmetic: 38.3 us -> 14.6 us
  starting transfers between devices: 102 us -> 91.3 us
  waiting for transfers between devices: 188 us -> 197 us
    ppermute x12, waiting for transfers between devices: 41.3 us -> 84.1 us  [to_peer(): return lax.ppermute(v, 'ws', [(s, (s + k) % WS) for s in range(WS)])]
    pallas_call x2 -> x6, Pallas kernels: 13.2 us -> 51.3 us  [the longest x5 45.6 us: one_step(): pl.pallas_call(body, in_specs=[pl.BlockSpec(memory_space=pltpu.SMEM)] * l...]
    all_to_all x0 -> x1, blocking collectives: none -> 26.3 us  [same_core(): return lax.all_to_all(v, 'exp', 0, 0, tiled=True, axis_index_groups=groups)]
    all_to_all x1, waiting for transfers between devices: 19.2 us -> 0.01 us  [shards(): lax.all_to_all(dx_send.reshape(experts, CAP, width + 128), 'exp', 0, 0, t...]
    all_to_all x2 -> x1, waiting for transfers between devices: 31.9 us -> 15.1 us  [same_core(): return lax.all_to_all(v, 'exp', 0, 0, tiled=True, axis_index_groups=groups)]
    dot_general x6 -> x0, matrix products: 15.7 us -> none  [the longest x1 4.94 us: shards(): d_p = jnp.einsum('tkgd,skd->kgts', d_o, v, preferred_element_type=F32)]
    dot_general x11 -> x4, matrix products: 17.7 us -> 5.65 us  [dot(): return jnp.dot(a, b, preferred_element_type=F32)]
    dot_general x5 -> x1, matrix products: 9.31 us -> 1.42 us  [dot_t(): lax.dot_general(a, b, (((1,), (1,)), ((), ())), preferred_element_type=F32)]
  transfers between devices with their start and end apart: 44 -> 43, of which waited for: 24 -> 31; matrix products, arithmetic and copies ran while one was open for 22% -> 6% of each run, Pallas kernels for 4% -> 13%
where the time goes in v3:
time: 450 us; the launch traced here: 444 us
  waiting for transfers between devices  197 us (44%)
  starting transfers between devices  91.3 us (20%)
  Pallas kernels  87 us (19%)
  blocking collectives  26.3 us (6%)
  other arithmetic  14.6 us (3%)
  local copies, waits for them, and re-layouts  14 us (3%)
  matrix products  11 us (2%)
    ppermute x12, waiting for transfers between devices, to_peer(): return lax.ppermute(v, 'ws', [(s, (s + k) % WS) for s in range(WS)])  84.1 us
    ppermute x21, waiting for transfers between devices, from_peer(): return lax.ppermute(v, 'ws', [(s, (s - k) % WS) for s in range(WS)])  83 us
    pallas_call x5, Pallas kernels, one_step(): pl.pallas_call(body, in_specs=[pl.BlockSpec(memory_space=pltpu.SMEM)] * l...  45.6 us
    ppermute x21, starting transfers between devices, from_peer(): return lax.ppermute(v, 'ws', [(s, (s - k) % WS) for s in range(WS)])  30 us
    all_to_all x1, blocking collectives, same_core(): return lax.all_to_all(v, 'exp', 0, 0, tiled=True, axis_index_groups=groups)  26.3 us
    pallas_call x1, Pallas kernels, expert_pass(): pl.pallas_call(functools.partial(expert_body, width, ff), grid=(slots //...  23 us
    all_to_all x1, waiting for transfers between devices, same_core(): return lax.all_to_all(v, 'exp', 0, 0, tiled=True, axis_index_groups=groups)  15.1 us
    pallas_call x1, Pallas kernels, expert_slopes(): pl.pallas_call(slope_body, grid=(width // tile,), in_specs=[col, whole(dg...  12.7 us
  transfers between devices with their start and end apart: 43, of which 31 were waited for; matrix products, arithmetic and copies ran while one was open for 6% of the time, Pallas kernels for 13%

profile of v3, /device:TPU:1, one launch (start us, length us, event | category | flops | bytes accessed | tf_op | source)
XLA Modules:
  0.0 443.9 jit_solution(16872794162051452703)
XLA Ops:
  0.7 3.6 collective-permute-start
  8.9 2.9 pack.1
  12.9 2.4 collective-permute-done.2.refs_3_.refs_7_
  18.5 3.9 convolution_convert_fusion
  22.4 10.0 %all-to-all-start.1 = ((bf16[32,48,1664]{2,1,0:T(8,128)(2,1)}), bf16[32,48,1664]{2,1,0:T(8,128)(2,1)}, u32[]{:S(2)}, u32[]{:S(2)}) async-start(bf16[32,48,1664]{2,1,0:T(8,128)(2,1)} %bitcast.62), calls=%async_computation.1 | async-start | bytes 10223616 | tf_op jit(solution)/shard_map/all_to_all | solution.py:613
  37.6 11.5 %collective-permute-done.3.refs_5_ = bf16[192,768]{1,0:T(8,128)(2,1)S(1)} collective-permute-done((bf16[192,768]{1,0:T(8,128)(2,1)S(1)}, bf16[192,768]{1,0:T(8,128)(2,1)S(1)}, u32[]{:S(2)}, u32[]{:S(2)}) %collective-permute-start.3) | collective-permute-done | bytes 294944 | tf_op jit(solution)/shard_map/ppermute | solution.py:42
  52.6 5.2 %collective-permute-done.5.refs_7_ = bf16[192,768]{1,0:T(8,128)(2,1)S(1)} collective-permute-done((bf16[192,768]{1,0:T(8,128)(2,1)S(1)}, bf16[192,768]{1,0:T(8,128)(2,1)S(1)}, u32[]{:S(2)}, u32[]{:S(2)}) %collective-permute-start.5) | collective-permute-done | bytes 294944 | tf_op jit(solution)/shard_map/ppermute | solution.py:42
  62.7 11.1 %attend.1 = (bf16[512,1536]{1,0:T(8,128)(2,1)}, bf16[512,640]{1,0:T(8,128)(2,1)}, bf16[512,384]{1,0:T(8,128)(2,1)}, f32[512,128]{1,0:T(8,128)}, bf16[1536,640]{1...) custom-call(s32[2]{0:T(128)} %pad_add_fusion.place_ref, ...), custom_call_target="tpu_custom_call" | custom-call | flops 2013265920 | bytes 6684672 | tf_op jit(solution)/shard_map/attend/pallas_call | solution.py:246
  76.2 10.1 %collective-permute-done.10.p2 = bf16[128,1536]{1,0:T(8,128)(2,1)S(1)} collective-permute-done((bf16[128,1536]{1,0:T(8,128)(2,1)}, bf16[128,1536]{1,0:T(8,128)(2,1)S(1)}, u32[]{:S(2)}, u32[]{:S(2)}) %collective-permute-start.10) | collective-permute-done | bytes 393248 | tf_op jit(solution)/shard_map/ppermute | solution.py:46
  86.3 6.5 %collective-permute-done.11.p3 = bf16[128,1536]{1,0:T(8,128)(2,1)S(1)} collective-permute-done((bf16[128,1536]{1,0:T(8,128)(2,1)}, bf16[128,1536]{1,0:T(8,128)(2,1)S(1)}, u32[]{:S(2)}, u32[]{:S(2)}) %collective-permute-start.11) | collective-permute-done | bytes 393248 | tf_op jit(solution)/shard_map/ppermute | solution.py:46
  92.8 2.4 collective-permute-done.9.p1
  95.9 6.4 %enter.1 = (f32[128,1536]{1,0:T(8,128)}, bf16[128,1536]{1,0:T(8,128)(2,1)}, bf16[1536,1536]{1,0:T(8,128)(2,1)}, f32[128,128]{1,0:T(8,128)}, bf16[256,1536]{1,0:T(8,128)(2,1)}) custom-call(bf16[128,1536]{1,0:T(8,128)(2,1)} %refs_4_.1, f32[128,1536]{1,0:T(8,128)} %get-tuple-element.98.p0, bf16[128,1536]{1,0:T(8,128)(2,1)} %copy-done.15, ...), custom_call_target="tpu_custom_call" | custom-call | flops 603979776 | bytes 3620864 | tf_op jit(solution)/shard_map/enter/pallas_call | solution.py:246
  102.3 7.6 %all-to-all-start = ((bf16[32,48,1536]{2,1,0:T(8,128)(2,1)}), bf16[32,48,1536]{2,1,0:T(8,128)(2,1)}, u32[]{:S(2)}, u32[]{:S(2)}) async-start(bf16[32,48,1536]{2,1,0:T(8,128)(2,1)} %bitcast.65), calls=%async_computation | async-start | bytes 9437184 | tf_op jit(solution)/shard_map/all_to_all | solution.py:634
  111.5 2.7 collective-permute-start.15
  115.7 4.8 %collective-permute-done.12.rest_1_ = bf16[1536,128]{1,0:T(8,128)(2,1)S(1)} collective-permute-done((bf16[1536,128]{1,0:T(8,128)(2,1)S(1)}, bf16[1536,128]{1,0:T(8,128)(2,1)S(1)}, u32[]{:S(2)}, u32[]{:S(2)}) %collective-permute-start.12) | collective-permute-done | bytes 393248 | tf_op jit(solution)/shard_map/ppermute | solution.py:42
  122.6 8.8 %collective-permute-start.18 = (bf16[128,1536]{1,0:T(8,128)(2,1)S(1)}, bf16[128,1536]{1,0:T(8,128)(2,1)}, u32[]{:S(2)}, u32[]{:S(2)}) collective-permute-start(bf16[128,1536]{1,0:T(8,128)(2,1)S(1)} %bitcast.80), channel_id=1, source_target_pairs={{0,3},{1,0},{2,1},{3,2},{4,7},{5,4},{6,5},{7,6},{8,11},{9,8},{10,9... | collective-permute-start | bytes 1179656 | tf_op jit(solution)/shard_map/ppermute | solution.py:42
  132.9 4.5 %collective-permute-done.15.rest_5_ = bf16[1536,128]{1,0:T(8,128)(2,1)S(1)} collective-permute-done((bf16[1536,128]{1,0:T(8,128)(2,1)S(1)}, bf16[1536,128]{1,0:T(8,128)(2,1)S(1)}, u32[]{:S(2)}, u32[]{:S(2)}) %collective-permute-start.15) | collective-permute-done | bytes 393248 | tf_op jit(solution)/shard_map/ppermute | solution.py:42
  139.5 9.9 %collective-permute-done.17.rest_7_ = bf16[1536,128]{1,0:T(8,128)(2,1)S(1)} collective-permute-done((bf16[1536,128]{1,0:T(8,128)(2,1)S(1)}, bf16[1536,128]{1,0:T(8,128)(2,1)S(1)}, u32[]{:S(2)}, u32[]{:S(2)}) %collective-permute-start.17) | collective-permute-done | bytes 393248 | tf_op jit(solution)/shard_map/ppermute | solution.py:42
  149.4 4.9 %collective-permute-done.18.rest_9_ = bf16[128,1536]{1,0:T(8,128)(2,1)} collective-permute-done((bf16[128,1536]{1,0:T(8,128)(2,1)S(1)}, bf16[128,1536]{1,0:T(8,128)(2,1)}, u32[]{:S(2)}, u32[]{:S(2)}) %collective-permute-start.18) | collective-permute-done | bytes 393248 | tf_op jit(solution)/shard_map/ppermute | solution.py:42
  156.4 9.1 %collective-permute-done.20.rest_11_ = bf16[128,1536]{1,0:T(8,128)(2,1)} collective-permute-done((bf16[128,1536]{1,0:T(8,128)(2,1)S(1)}, bf16[128,1536]{1,0:T(8,128)(2,1)}, u32[]{:S(2)}, u32[]{:S(2)}) %collective-permute-start.20) | collective-permute-done | bytes 393248 | tf_op jit(solution)/shard_map/ppermute | solution.py:42
  165.5 2.8 all-to-all-done
  168.4 23.0 %expert_pass.1 = (bf16[1536,1536]{1,0:T(8,128)(2,1)}, bf16[1536,1664]{1,0:T(8,128)(2,1)}, bf16[1536,512]{1,0:T(8,128)(2,1)}, bf16[1536,1024]{1,0:T(8,128)(2,1)}, bf16[1536,1536]{1,0:T(8,128)(2,1)}) custom-call(bf16[1536,1536]{1,0:T(8,128)(2,1)} %bitcast.15.x_ref, bf16[1536,1664]{1,0:T(8,128)(2,1)} %bitcast.17.dy_ref, f32[8,128]{1,0:T(8,128)} %maximum_maximum_fusion.sel_ref, ...), custom_call_target="tpu_custom_call" | custom-call | flops 14495514624 | bytes 28311552 | tf_op jit(solution)/shard_map/expert_pass/pallas_call | solution.py:122
  191.4 7.8 %all-to-all-start.2 = ((bf16[32,48,1664]{2,1,0:T(8,128)(2,1)}), bf16[32,48,1664]{2,1,0:T(8,128)(2,1)}, u32[]{:S(2)}, u32[]{:S(2)}) async-start(bf16[32,48,1664]{2,1,0:T(8,128)(2,1)} %bitcast.63), calls=%async_computation.2 | async-start | bytes 10223616 | tf_op jit(solution)/shard_map/all_to_all | solution.py:649
  199.2 12.7 %expert_slopes.1 = (f32[1536,128]{1,0:T(8,128)}, f32[1536,128]{1,0:T(8,128)}, f32[128,1536]{1,0:T(8,128)}, bf16[2,1536,128]{2,1,0:T(8,128)(2,1)}, bf16[128,1536]...) custom-call(bf16[1536,1536]{1,0:T(8,128)(2,1)} %bitcast.15.x_ref, ...), custom_call_target="tpu_custom_call" | custom-call | flops 7247757312 | bytes 18874368 | tf_op jit(solution)/shard_map/expert_slopes/pallas_call | solution.py:156
  212.0 3.8 collective-permute-start.23
  217.1 6.8 %collective-permute-done.22 = bf16[128,1536]{1,0:T(8,128)(2,1)S(1)} collective-permute-done((bf16[128,1536]{1,0:T(8,128)(2,1)}, bf16[128,1536]{1,0:T(8,128)(2,1)S(1)}, u32[]{:S(2)}, u32[]{:S(2)}) %collective-permute-start.22) | collective-permute-done | bytes 393248 | tf_op jit(solution)/shard_map/ppermute | solution.py:46
  223.9 41.4 %collective-permute-done.24 = bf16[128,1536]{1,0:T(8,128)(2,1)S(1)} collective-permute-done((bf16[128,1536]{1,0:T(8,128)(2,1)}, bf16[128,1536]{1,0:T(8,128)(2,1)S(1)}, u32[]{:S(2)}, u32[]{:S(2)}) %collective-permute-start.24) | collective-permute-done | bytes 393248 | tf_op jit(solution)/shard_map/ppermute | solution.py:46
  267.1 8.9 %all-to-all-start.3 = ((bf16[32,48,1536]{2,1,0:T(8,128)(2,1)}), bf16[32,48,1536]{2,1,0:T(8,128)(2,1)}, u32[]{:S(2)}, u32[]{:S(2)}) async-start(bf16[32,48,1536]{2,1,0:T(8,128)(2,1)} %bitcast.64), calls=%async_computation.3 | async-start | bytes 9437184 | tf_op jit(solution)/shard_map/all_to_all | solution.py:660
  276.0 6.3 %leave.1 = (f32[128,1536]{1,0:T(8,128)}, bf16[128,1536]{1,0:T(8,128)(2,1)}, f32[1536,128]{1,0:T(8,128)}) custom-call(bf16[1536,1664]{1,0:T(8,128)(2,1)} %bitcast.19.back_ref, bf16[128,1536]{1,0:T(8,128)(2,1)} %get-tuple-element.178.slot_ref, f32[128,128]{1,0:T(8,128)} %get-tuple-element.122.gates_ref, ...), custom_call_target="tpu_custom_call" | custom-call | flops 654311424 | bytes 7585792 | tf_op jit(solution)/shard_map/leave/pallas_call | solution.py:246
  282.3 2.3 collective-permute-start.27
  286.1 15.4 %collective-permute-done.27.refs_1_ = bf16[128,1536]{1,0:T(8,128)(2,1)S(1)} collective-permute-done((bf16[128,1536]{1,0:T(8,128)(2,1)}, bf16[128,1536]{1,0:T(8,128)(2,1)S(1)}, u32[]{:S(2)}, u32[]{:S(2)}) %collective-permute-start.27) | collective-permute-done | bytes 393248 | tf_op jit(solution)/shard_map/ppermute | solution.py:42
  301.6 4.3 collective-permute-done.29.refs_3_
  306.6 18.9 %attend_back.1 = (f32[16,6,24,384]{3,2,1,0:T(8,128)}, bf16[16,6,24,384]{3,2,1,0:T(8,128)(2,1)}, f32[128,1536]{1,0:T(8,128)}, bf16[128,1536]{1,0:T(8,128)(2,1)}, ...) custom-call(s32[2]{0:T(128)} %pad_add_fusion.place_ref, bf16[128,1536]{1,0:T(8,128)(2,1)} %get-tuple-element.125.refs_0_, ...), custom_call_target="tpu_custom_call" | custom-call | flops 4227858432 | bytes 11534336 | tf_op jit(solution)/shard_map/attend_back/pallas_call | solution.py:246
  325.5 8.6 %all-to-all-done.3 = bf16[32,48,1536]{2,1,0:T(8,128)(2,1)} async-done(((bf16[32,48,1536]{2,1,0:T(8,128)(2,1)}), bf16[32,48,1536]{2,1,0:T(8,128)(2,1)}, u32[]{:S(2)}, u32[]{:S(2)}) %all-to-all-start.3) | async-done | bytes 4718624 | tf_op jit(solution)/shard_map/all_to_all | solution.py:660
  335.0 2.2 add_bitcast_fusion
  340.5 2.2 collective-permute-start.32
  344.6 6.7 %collective-permute-done.31 = bf16[128,1536]{1,0:T(8,128)(2,1)S(1)} collective-permute-done((bf16[128,1536]{1,0:T(8,128)(2,1)S(1)}, bf16[128,1536]{1,0:T(8,128)(2,1)S(1)}, u32[]{:S(2)}, u32[]{:S(2)}) %collective-permute-start.31) | collective-permute-done | bytes 393248 | tf_op jit(solution)/shard_map/ppermute | solution.py:46
  351.2 9.2 %collective-permute-done.32 = bf16[128,1536]{1,0:T(8,128)(2,1)S(1)} collective-permute-done((bf16[128,1536]{1,0:T(8,128)(2,1)S(1)}, bf16[128,1536]{1,0:T(8,128)(2,1)S(1)}, u32[]{:S(2)}, u32[]{:S(2)}) %collective-permute-start.32) | collective-permute-done | bytes 393248 | tf_op jit(solution)/shard_map/ppermute | solution.py:46
  362.9 6.5 %all-to-all-start.4 = ((bf16[16,6,24,384]{3,2,1,0:T(8,128)(2,1)}), bf16[16,6,24,384]{3,2,1,0:T(8,128)(2,1)S(1)}, u32[]{:S(2)}, u32[]{:S(2)}) async-start(bf16[16,6,24,384]{3,2,1,0:T(8,128)(2,1)} %add_convert_fusion), calls=%async_computation.4 | async-start | bytes 3538944 | tf_op jit(solution)/shard_map/all_to_all | solution.py:55
  369.5 2.7 fusion.10
  372.2 3.8 fusion.59
  376.9 15.1 %all-to-all-done.4 = bf16[16,6,24,384]{3,2,1,0:T(8,128)(2,1)S(1)} async-done(((bf16[16,6,24,384]{3,2,1,0:T(8,128)(2,1)}), bf16[16,6,24,384]{3,2,1,0:T(8,128)(2,1)S(1)}, u32[]{:S(2)}, u32[]{:S(2)}) %all-to-all-start.4) | async-done | bytes 1769504 | tf_op jit(solution)/shard_map/all_to_all | solution.py:55
  392.3 4.1 collective-permute-start.34
  397.3 3.2 collective-permute-done.35
  401.2 26.3 %all_to_all.30.a_ref.ao_ref = bf16[16,6,24,384]{3,2,1,0:T(8,128)(2,1)S(1)} all-to-all(bf16[16,6,24,384]{3,2,1,0:T(8,128)(2,1)S(1)} %broadcast_in_dim.84), channel_id=1, replica_groups={{0,8,16,24,32,40,48,56,64,72,80,88,96,104,112,120},{4,12,20,28,36,44,52..., dimensions={0} | all-to-all | bytes 3538944 | tf_op jit(solution)/shard_map/all_to_all | solution.py:55
  427.5 4.6 %collective-permute-start.37 = (bf16[16,6,24,384]{3,2,1,0:T(8,128)(2,1)S(1)}, bf16[16,6,24,384]{3,2,1,0:T(8,128)(2,1)S(1)}, u32[]{:S(2)}, u32[]{:S(2)}) collective-permute-start(bf16[16,6,24,384]{3,2,1,0:T(8,128)(2,1)S(1)} %all_to_all.30.a_ref.ao_ref), channel_id=1, source_target_pairs={{0,4},{4,0},{8,12},{12,8},{16,20},{20,16},{24,28},{28,24},{32,36},... | collective-permute-start | bytes 5308424 | tf_op jit(solution)/shard_map/ppermute | solution.py:50
  432.2 3.2 collective-permute-done.37.b_ref.bo_ref
  436.6 5.7 %finish.1 = (f32[384,1536]{1,0:T(8,128)}, f32[384,512]{1,0:T(8,128)}, f32[384,512]{1,0:T(8,128)}, f32[32,384]{1,0:T(8,128)}, f32[8,384]{1,0:T(8,128)}, /*index=5*/f32[384,1536]{1,0:T(8,128)}) custom-call(bf16[16,6,24,384]{3,2,1,0:T(8,128)(2,1)} %copy-done, bf16[16,6,24,384]{3,2,1,0:T(8,128)(2,1)} %copy-done.1, bf16[16,6,24,384]{3,2,1,0:T(8,128)(2,1)} %copy-done, ...), custom_call_target="tpu_custom_call" | custom-call | bytes 9437184 | tf_op jit(solution)/shard_map/finish/pallas_call | solution.py:209
  (207 shorter events, 54.2 us)
Async XLA Ops:
  0.7 11.7 %collective-permute-start = (bf16[128,1536]{1,0:T(8,128)(2,1)}, bf16[128,1536]{1,0:T(8,128)(2,1)S(1)}, u32[]{:S(2)}, u32[]{:S(2)}) collective-permute-start(bf16[128,1536]{1,0:T(8,128)(2,1)} %refs_4_.1), channel_id=1, source_target_pairs={{0,3},{1,0},{2,1},{3,2},{4,7},{5,4},{6,5},{7,6},{8,11},{9,8},{10,9... | collective-permute-start | bytes 1179656 | tf_op jit(solution)/shard_map/ppermute | solution.py:42
  4.3 11.1 %collective-permute-start.2 = (bf16[128,1536]{1,0:T(8,128)(2,1)}, bf16[128,1536]{1,0:T(8,128)(2,1)S(1)}, u32[]{:S(2)}, u32[]{:S(2)}) collective-permute-start(bf16[128,1536]{1,0:T(8,128)(2,1)} %refs_4_.1), channel_id=1, source_target_pairs={{0,1},{1,2},{2,3},{3,0},{4,5},{5,6},{6,7},{7,4},{8,9},{9,10},{10,1... | collective-permute-start | bytes 1179656 | tf_op jit(solution)/shard_map/ppermute | solution.py:42
  22.4 79.9 %all-to-all-start.1 = ((bf16[32,48,1664]{2,1,0:T(8,128)(2,1)}), bf16[32,48,1664]{2,1,0:T(8,128)(2,1)}, u32[]{:S(2)}, u32[]{:S(2)}) async-start(bf16[32,48,1664]{2,1,0:T(8,128)(2,1)} %bitcast.62), calls=%async_computation.1 | async-start | bytes 10223616 | tf_op jit(solution)/shard_map/all_to_all | solution.py:613
  32.4 29.2 %collective-permute-start.1 = (bf16[128,1536]{1,0:T(8,128)(2,1)S(1)}, bf16[128,1536]{1,0:T(8,128)(2,1)S(1)}, u32[]{:S(2)}, u32[]{:S(2)}) collective-permute-start(bf16[128,1536]{1,0:T(8,128)(2,1)S(1)} %copy-done.3), channel_id=1, source_target_pairs={{0,2},{1,3},{2,0},{3,1},{4,6},{5,7},{6,4},{7,5},{8,10},{9,11},{10,... | collective-permute-start | bytes 1179656 | tf_op jit(solution)/shard_map/ppermute | solution.py:42
  32.5 16.5 %collective-permute-start.3 = (bf16[192,768]{1,0:T(8,128)(2,1)S(1)}, bf16[192,768]{1,0:T(8,128)(2,1)S(1)}, u32[]{:S(2)}, u32[]{:S(2)}) collective-permute-start(bf16[192,768]{1,0:T(8,128)(2,1)S(1)} %copy-done.46), channel_id=1, source_target_pairs={{0,3},{1,0},{2,1},{3,2},{4,7},{5,4},{6,5},{7,6},{8,11},{9,8},{10,9... | collective-permute-start | bytes 884744 | tf_op jit(solution)/shard_map/ppermute | solution.py:42
  33.7 17.2 %collective-permute-start.4 = (bf16[192,768]{1,0:T(8,128)(2,1)S(1)}, bf16[192,768]{1,0:T(8,128)(2,1)S(1)}, u32[]{:S(2)}, u32[]{:S(2)}) collective-permute-start(bf16[192,768]{1,0:T(8,128)(2,1)S(1)} %copy-done.45), channel_id=1, source_target_pairs={{0,2},{1,3},{2,0},{3,1},{4,6},{5,7},{6,4},{7,5},{8,10},{9,11},{10,... | collective-permute-start | bytes 884744 | tf_op jit(solution)/shard_map/ppermute | solution.py:42
  35.6 22.2 %collective-permute-start.5 = (bf16[192,768]{1,0:T(8,128)(2,1)S(1)}, bf16[192,768]{1,0:T(8,128)(2,1)S(1)}, u32[]{:S(2)}, u32[]{:S(2)}) collective-permute-start(bf16[192,768]{1,0:T(8,128)(2,1)S(1)} %copy-done.41), channel_id=1, source_target_pairs={{0,1},{1,2},{2,3},{3,0},{4,5},{5,6},{6,7},{7,4},{8,9},{9,10},{10,1... | collective-permute-start | bytes 884744 | tf_op jit(solution)/shard_map/ppermute | solution.py:42
  49.1 12.5 %collective-permute-start.6 = (bf16[192,768]{1,0:T(8,128)(2,1)S(1)}, bf16[192,768]{1,0:T(8,128)(2,1)S(1)}, u32[]{:S(2)}, u32[]{:S(2)}) collective-permute-start(bf16[192,768]{1,0:T(8,128)(2,1)S(1)} %collective-permute-done.3.refs_5_), channel_id=1, source_target_pairs={{0,4},{4,0},{8,12},{12,8},{16,20},{20,16},{24,28},{28,24},{32,36},... | collective-permute-start | bytes 884744 | tf_op jit(solution)/shard_map/ppermute | solution.py:50
  50.9 10.7 %collective-permute-start.7 = (bf16[192,768]{1,0:T(8,128)(2,1)S(1)}, bf16[192,768]{1,0:T(8,128)(2,1)S(1)}, u32[]{:S(2)}, u32[]{:S(2)}) collective-permute-start(bf16[192,768]{1,0:T(8,128)(2,1)S(1)} %collective-permute-done.4.refs_6_), channel_id=1, source_target_pairs={{0,4},{4,0},{8,12},{12,8},{16,20},{20,16},{24,28},{28,24},{32,36},... | collective-permute-start | bytes 884744 | tf_op jit(solution)/shard_map/ppermute | solution.py:50
  57.8 3.8 collective-permute-start.8
  73.8 12.5 %collective-permute-start.10 = (bf16[128,1536]{1,0:T(8,128)(2,1)}, bf16[128,1536]{1,0:T(8,128)(2,1)S(1)}, u32[]{:S(2)}, u32[]{:S(2)}) collective-permute-start(bf16[128,1536]{1,0:T(8,128)(2,1)} %get-tuple-element.100), channel_id=1, source_target_pairs={{0,2},{1,3},{2,0},{3,1},{4,6},{5,7},{6,4},{7,5},{8,10},{9,11},{10,... | collective-permute-start | bytes 1179656 | tf_op jit(solution)/shard_map/ppermute | solution.py:46
  73.9 18.9 %collective-permute-start.11 = (bf16[128,1536]{1,0:T(8,128)(2,1)}, bf16[128,1536]{1,0:T(8,128)(2,1)S(1)}, u32[]{:S(2)}, u32[]{:S(2)}) collective-permute-start(bf16[128,1536]{1,0:T(8,128)(2,1)} %get-tuple-element.101), channel_id=1, source_target_pairs={{0,3},{1,0},{2,1},{3,2},{4,7},{5,4},{6,5},{7,6},{8,11},{9,8},{10,9... | collective-permute-start | bytes 1179656 | tf_op jit(solution)/shard_map/ppermute | solution.py:46
  75.2 19.9 %collective-permute-start.9 = (bf16[128,1536]{1,0:T(8,128)(2,1)}, bf16[128,1536]{1,0:T(8,128)(2,1)S(1)}, u32[]{:S(2)}, u32[]{:S(2)}) collective-permute-start(bf16[128,1536]{1,0:T(8,128)(2,1)} %get-tuple-element.99), channel_id=1, source_target_pairs={{0,1},{1,2},{2,3},{3,0},{4,5},{5,6},{6,7},{7,4},{8,9},{9,10},{10,1... | collective-permute-start | bytes 1179656 | tf_op jit(solution)/shard_map/ppermute | solution.py:46
  102.3 66.0 %all-to-all-start = ((bf16[32,48,1536]{2,1,0:T(8,128)(2,1)}), bf16[32,48,1536]{2,1,0:T(8,128)(2,1)}, u32[]{:S(2)}, u32[]{:S(2)}) async-start(bf16[32,48,1536]{2,1,0:T(8,128)(2,1)} %bitcast.65), calls=%async_computation | async-start | bytes 9437184 | tf_op jit(solution)/shard_map/all_to_all | solution.py:634
  109.9 10.6 %collective-permute-start.12 = (bf16[1536,128]{1,0:T(8,128)(2,1)S(1)}, bf16[1536,128]{1,0:T(8,128)(2,1)S(1)}, u32[]{:S(2)}, u32[]{:S(2)}) collective-permute-start(bf16[1536,128]{1,0:T(8,128)(2,1)S(1)} %bitcast.72), channel_id=1, source_target_pairs={{0,3},{1,0},{2,1},{3,2},{4,7},{5,4},{6,5},{7,6},{8,11},{9,8},{10,9... | collective-permute-start | bytes 1179656 | tf_op jit(solution)/shard_map/ppermute | solution.py:42
  110.8 11.7 %collective-permute-start.13 = (bf16[1536,128]{1,0:T(8,128)(2,1)S(1)}, bf16[1536,128]{1,0:T(8,128)(2,1)S(1)}, u32[]{:S(2)}, u32[]{:S(2)}) collective-permute-start(bf16[1536,128]{1,0:T(8,128)(2,1)S(1)} %bitcast.73), channel_id=1, source_target_pairs={{0,2},{1,3},{2,0},{3,1},{4,6},{5,7},{6,4},{7,5},{8,10},{9,11},{10,... | collective-permute-start | bytes 1179656 | tf_op jit(solution)/shard_map/ppermute | solution.py:42
  110.9 21.9 %collective-permute-start.14 = (bf16[1536,128]{1,0:T(8,128)(2,1)S(1)}, bf16[1536,128]{1,0:T(8,128)(2,1)S(1)}, u32[]{:S(2)}, u32[]{:S(2)}) collective-permute-start(bf16[1536,128]{1,0:T(8,128)(2,1)S(1)} %bitcast.74), channel_id=1, source_target_pairs={{0,1},{1,2},{2,3},{3,0},{4,5},{5,6},{6,7},{7,4},{8,9},{9,10},{10,1... | collective-permute-start | bytes 1179656 | tf_op jit(solution)/shard_map/ppermute | solution.py:42
  111.5 25.9 %collective-permute-start.15 = (bf16[1536,128]{1,0:T(8,128)(2,1)S(1)}, bf16[1536,128]{1,0:T(8,128)(2,1)S(1)}, u32[]{:S(2)}, u32[]{:S(2)}) collective-permute-start(bf16[1536,128]{1,0:T(8,128)(2,1)S(1)} %bitcast.76), channel_id=1, source_target_pairs={{0,3},{1,0},{2,1},{3,2},{4,7},{5,4},{6,5},{7,6},{8,11},{9,8},{10,9... | collective-permute-start | bytes 1179656 | tf_op jit(solution)/shard_map/ppermute | solution.py:42
  114.2 25.2 %collective-permute-start.16 = (bf16[1536,128]{1,0:T(8,128)(2,1)S(1)}, bf16[1536,128]{1,0:T(8,128)(2,1)S(1)}, u32[]{:S(2)}, u32[]{:S(2)}) collective-permute-start(bf16[1536,128]{1,0:T(8,128)(2,1)S(1)} %bitcast.77), channel_id=1, source_target_pairs={{0,2},{1,3},{2,0},{3,1},{4,6},{5,7},{6,4},{7,5},{8,10},{9,11},{10,... | collective-permute-start | bytes 1179656 | tf_op jit(solution)/shard_map/ppermute | solution.py:42
  120.5 47.8 %copy-start.31 = (bf16[1536,128]{1,0:T(8,128)(2,1)}, bf16[1536,128]{1,0:T(8,128)(2,1)S(1)}, u32[]{:S(2)}) copy-start(bf16[1536,128]{1,0:T(8,128)(2,1)S(1)} %collective-permute-done.12.rest_1_) | copy-start | bytes 1179652
  120.5 28.9 %collective-permute-start.17 = (bf16[1536,128]{1,0:T(8,128)(2,1)S(1)}, bf16[1536,128]{1,0:T(8,128)(2,1)S(1)}, u32[]{:S(2)}, u32[]{:S(2)}) collective-permute-start(bf16[1536,128]{1,0:T(8,128)(2,1)S(1)} %bitcast.78), channel_id=1, source_target_pairs={{0,1},{1,2},{2,3},{3,0},{4,5},{5,6},{6,7},{7,4},{8,9},{9,10},{10,1... | collective-permute-start | bytes 1179656 | tf_op jit(solution)/shard_map/ppermute | solution.py:42
  122.6 45.7 %copy-start.32 = (bf16[1536,128]{1,0:T(8,128)(2,1)}, bf16[1536,128]{1,0:T(8,128)(2,1)S(1)}, u32[]{:S(2)}) copy-start(bf16[1536,128]{1,0:T(8,128)(2,1)S(1)} %collective-permute-done.13.rest_2_) | copy-start | bytes 1179652
  122.6 31.7 %collective-permute-start.18 = (bf16[128,1536]{1,0:T(8,128)(2,1)S(1)}, bf16[128,1536]{1,0:T(8,128)(2,1)}, u32[]{:S(2)}, u32[]{:S(2)}) collective-permute-start(bf16[128,1536]{1,0:T(8,128)(2,1)S(1)} %bitcast.80), channel_id=1, source_target_pairs={{0,3},{1,0},{2,1},{3,2},{4,7},{5,4},{6,5},{7,6},{8,11},{9,8},{10,9... | collective-permute-start | bytes 1179656 | tf_op jit(solution)/shard_map/ppermute | solution.py:42
  132.8 35.5 %copy-start.33 = (bf16[1536,128]{1,0:T(8,128)(2,1)}, bf16[1536,128]{1,0:T(8,128)(2,1)S(1)}, u32[]{:S(2)}) copy-start(bf16[1536,128]{1,0:T(8,128)(2,1)S(1)} %collective-permute-done.14.rest_3_) | copy-start | bytes 1179652
  132.8 23.6 %collective-permute-start.19 = (bf16[128,1536]{1,0:T(8,128)(2,1)S(1)}, bf16[128,1536]{1,0:T(8,128)(2,1)S(1)}, u32[]{:S(2)}, u32[]{:S(2)}) collective-permute-start(bf16[128,1536]{1,0:T(8,128)(2,1)S(1)} %bitcast.81), channel_id=1, source_target_pairs={{0,2},{1,3},{2,0},{3,1},{4,6},{5,7},{6,4},{7,5},{8,10},{9,11},{10,... | collective-permute-start | bytes 1179656 | tf_op jit(solution)/shard_map/ppermute | solution.py:42
  137.4 30.9 %copy-start.34 = (bf16[1536,128]{1,0:T(8,128)(2,1)}, bf16[1536,128]{1,0:T(8,128)(2,1)S(1)}, u32[]{:S(2)}) copy-start(bf16[1536,128]{1,0:T(8,128)(2,1)S(1)} %collective-permute-done.15.rest_5_) | copy-start | bytes 1179652
  137.4 28.1 %collective-permute-start.20 = (bf16[128,1536]{1,0:T(8,128)(2,1)S(1)}, bf16[128,1536]{1,0:T(8,128)(2,1)}, u32[]{:S(2)}, u32[]{:S(2)}) collective-permute-start(bf16[128,1536]{1,0:T(8,128)(2,1)S(1)} %bitcast.82), channel_id=1, source_target_pairs={{0,1},{1,2},{2,3},{3,0},{4,5},{5,6},{6,7},{7,4},{8,9},{9,10},{10,1... | collective-permute-start | bytes 1179656 | tf_op jit(solution)/shard_map/ppermute | solution.py:42
  139.5 28.9 %copy-start.35 = (bf16[1536,128]{1,0:T(8,128)(2,1)}, bf16[1536,128]{1,0:T(8,128)(2,1)S(1)}, u32[]{:S(2)}) copy-start(bf16[1536,128]{1,0:T(8,128)(2,1)S(1)} %collective-permute-done.16.rest_6_) | copy-start | bytes 1179652
  191.4 75.7 %all-to-all-start.2 = ((bf16[32,48,1664]{2,1,0:T(8,128)(2,1)}), bf16[32,48,1664]{2,1,0:T(8,128)(2,1)}, u32[]{:S(2)}, u32[]{:S(2)}) async-start(bf16[32,48,1664]{2,1,0:T(8,128)(2,1)} %bitcast.63), calls=%async_computation.2 | async-start | bytes 10223616 | tf_op jit(solution)/shard_map/all_to_all | solution.py:649
  211.9 12.0 %collective-permute-start.22 = (bf16[128,1536]{1,0:T(8,128)(2,1)}, bf16[128,1536]{1,0:T(8,128)(2,1)S(1)}, u32[]{:S(2)}, u32[]{:S(2)}) collective-permute-start(bf16[128,1536]{1,0:T(8,128)(2,1)} %get-tuple-element.116), channel_id=1, source_target_pairs={{0,1},{1,2},{2,3},{3,0},{4,5},{5,6},{6,7},{7,4},{8,9},{9,10},{10,1... | collective-permute-start | bytes 1179656 | tf_op jit(solution)/shard_map/ppermute | solution.py:46
  212.0 54.4 %collective-permute-start.21 = (bf16[2,1536,128]{2,1,0:T(8,128)(2,1)}, bf16[2,1536,128]{2,1,0:T(8,128)(2,1)S(1)}, u32[]{:S(2)}, u32[]{:S(2)}) collective-permute-start(bf16[2,1536,128]{2,1,0:T(8,128)(2,1)} %get-tuple-element.115), channel_id=1, source_target_pairs={{0,1},{1,2},{2,3},{3,0},{4,5},{5,6},{6,7},{7,4},{8,9},{9,10},{10,1... | collective-permute-start | bytes 2359304 | tf_op jit(solution)/shard_map/ppermute | solution.py:46
  212.0 54.3 %collective-permute-start.23 = (bf16[2,1536,128]{2,1,0:T(8,128)(2,1)}, bf16[2,1536,128]{2,1,0:T(8,128)(2,1)}, u32[]{:S(2)}, u32[]{:S(2)}) collective-permute-start(bf16[2,1536,128]{2,1,0:T(8,128)(2,1)} %get-tuple-element.117), channel_id=1, source_target_pairs={{0,2},{1,3},{2,0},{3,1},{4,6},{5,7},{6,4},{7,5},{8,10},{9,11},{10,... | collective-permute-start | bytes 2359304 | tf_op jit(solution)/shard_map/ppermute | solution.py:46
  215.8 51.3 %collective-permute-start.25 = (bf16[2,1536,128]{2,1,0:T(8,128)(2,1)}, bf16[2,1536,128]{2,1,0:T(8,128)(2,1)}, u32[]{:S(2)}, u32[]{:S(2)}) collective-permute-start(bf16[2,1536,128]{2,1,0:T(8,128)(2,1)} %get-tuple-element.119), channel_id=1, source_target_pairs={{0,3},{1,0},{2,1},{3,2},{4,7},{5,4},{6,5},{7,6},{8,11},{9,8},{10,9... | collective-permute-start | bytes 2359304 | tf_op jit(solution)/shard_map/ppermute | solution.py:46
  216.1 49.2 %collective-permute-start.24 = (bf16[128,1536]{1,0:T(8,128)(2,1)}, bf16[128,1536]{1,0:T(8,128)(2,1)S(1)}, u32[]{:S(2)}, u32[]{:S(2)}) collective-permute-start(bf16[128,1536]{1,0:T(8,128)(2,1)} %get-tuple-element.118), channel_id=1, source_target_pairs={{0,2},{1,3},{2,0},{3,1},{4,6},{5,7},{6,4},{7,5},{8,10},{9,11},{10,... | collective-permute-start | bytes 1179656 | tf_op jit(solution)/shard_map/ppermute | solution.py:46
  223.9 42.5 %collective-permute-start.26 = (bf16[128,1536]{1,0:T(8,128)(2,1)}, bf16[128,1536]{1,0:T(8,128)(2,1)S(1)}, u32[]{:S(2)}, u32[]{:S(2)}) collective-permute-start(bf16[128,1536]{1,0:T(8,128)(2,1)} %get-tuple-element.120), channel_id=1, source_target_pairs={{0,3},{1,0},{2,1},{3,2},{4,7},{5,4},{6,5},{7,6},{8,11},{9,8},{10,9... | collective-permute-start | bytes 1179656 | tf_op jit(solution)/shard_map/ppermute | solution.py:46
  267.1 67.1 %all-to-all-start.3 = ((bf16[32,48,1536]{2,1,0:T(8,128)(2,1)}), bf16[32,48,1536]{2,1,0:T(8,128)(2,1)}, u32[]{:S(2)}, u32[]{:S(2)}) async-start(bf16[32,48,1536]{2,1,0:T(8,128)(2,1)} %bitcast.64), calls=%async_computation.3 | async-start | bytes 9437184 | tf_op jit(solution)/shard_map/all_to_all | solution.py:660
  282.3 19.3 %collective-permute-start.27 = (bf16[128,1536]{1,0:T(8,128)(2,1)}, bf16[128,1536]{1,0:T(8,128)(2,1)S(1)}, u32[]{:S(2)}, u32[]{:S(2)}) collective-permute-start(bf16[128,1536]{1,0:T(8,128)(2,1)} %get-tuple-element.125.refs_0_), channel_id=1, source_target_pairs={{0,3},{1,0},{2,1},{3,2},{4,7},{5,4},{6,5},{7,6},{8,11},{9,8},{10,9... | collective-permute-start | bytes 1179656 | tf_op jit(solution)/shard_map/ppermute | solution.py:42
  284.6 17.0 %collective-permute-start.28 = (bf16[128,1536]{1,0:T(8,128)(2,1)}, bf16[128,1536]{1,0:T(8,128)(2,1)S(1)}, u32[]{:S(2)}, u32[]{:S(2)}) collective-permute-start(bf16[128,1536]{1,0:T(8,128)(2,1)} %get-tuple-element.125.refs_0_), channel_id=1, source_target_pairs={{0,2},{1,3},{2,0},{3,1},{4,6},{5,7},{6,4},{7,5},{8,10},{9,11},{10,... | collective-permute-start | bytes 1179656 | tf_op jit(solution)/shard_map/ppermute | solution.py:42
  285.3 20.5 %collective-permute-start.29 = (bf16[128,1536]{1,0:T(8,128)(2,1)}, bf16[128,1536]{1,0:T(8,128)(2,1)S(1)}, u32[]{:S(2)}, u32[]{:S(2)}) collective-permute-start(bf16[128,1536]{1,0:T(8,128)(2,1)} %get-tuple-element.125.refs_0_), channel_id=1, source_target_pairs={{0,1},{1,2},{2,3},{3,0},{4,5},{5,6},{6,7},{7,4},{8,9},{9,10},{10,1... | collective-permute-start | bytes 1179656 | tf_op jit(solution)/shard_map/ppermute | solution.py:42
  334.2 26.7 %collective-permute-start.30 = (bf16[16,6,24,384]{3,2,1,0:T(8,128)(2,1)}, bf16[16,6,24,384]{3,2,1,0:T(8,128)(2,1)S(1)}, u32[]{:S(2)}, u32[]{:S(2)}) collective-permute-start(bf16[16,6,24,384]{3,2,1,0:T(8,128)(2,1)} %get-tuple-element.135), channel_id=1, source_target_pairs={{0,4},{4,0},{8,12},{12,8},{16,20},{20,16},{24,28},{28,24},{32,36},... | collective-permute-start | bytes 5308424 | tf_op jit(solution)/shard_map/ppermute | solution.py:50
  339.0 12.2 %collective-permute-start.31 = (bf16[128,1536]{1,0:T(8,128)(2,1)S(1)}, bf16[128,1536]{1,0:T(8,128)(2,1)S(1)}, u32[]{:S(2)}, u32[]{:S(2)}) collective-permute-start(bf16[128,1536]{1,0:T(8,128)(2,1)S(1)} %copy-done.39), channel_id=1, source_target_pairs={{0,1},{1,2},{2,3},{3,0},{4,5},{5,6},{6,7},{7,4},{8,9},{9,10},{10,1... | collective-permute-start | bytes 1179656 | tf_op jit(solution)/shard_map/ppermute | solution.py:46
  340.5 19.9 %collective-permute-start.32 = (bf16[128,1536]{1,0:T(8,128)(2,1)S(1)}, bf16[128,1536]{1,0:T(8,128)(2,1)S(1)}, u32[]{:S(2)}, u32[]{:S(2)}) collective-permute-start(bf16[128,1536]{1,0:T(8,128)(2,1)S(1)} %copy-done.38), channel_id=1, source_target_pairs={{0,2},{1,3},{2,0},{3,1},{4,6},{5,7},{6,4},{7,5},{8,10},{9,11},{10,... | collective-permute-start | bytes 1179656 | tf_op jit(solution)/shard_map/ppermute | solution.py:46
  342.8 17.7 %collective-permute-start.33 = (bf16[128,1536]{1,0:T(8,128)(2,1)S(1)}, bf16[128,1536]{1,0:T(8,128)(2,1)S(1)}, u32[]{:S(2)}, u32[]{:S(2)}) collective-permute-start(bf16[128,1536]{1,0:T(8,128)(2,1)S(1)} %copy-done.37), channel_id=1, source_target_pairs={{0,3},{1,0},{2,1},{3,2},{4,7},{5,4},{6,5},{7,6},{8,11},{9,8},{10,9... | collective-permute-start | bytes 1179656 | tf_op jit(solution)/shard_map/ppermute | solution.py:46
  362.9 29.1 %all-to-all-start.4 = ((bf16[16,6,24,384]{3,2,1,0:T(8,128)(2,1)}), bf16[16,6,24,384]{3,2,1,0:T(8,128)(2,1)S(1)}, u32[]{:S(2)}, u32[]{:S(2)}) async-start(bf16[16,6,24,384]{3,2,1,0:T(8,128)(2,1)} %add_convert_fusion), calls=%async_computation.4 | async-start | bytes 3538944 | tf_op jit(solution)/shard_map/all_to_all | solution.py:55
  392.3 5.0 %collective-permute-start.34 = (bf16[24,384]{1,0:T(8,128)(2,1)S(1)}, bf16[24,384]{1,0:T(8,128)(2,1)S(1)}, u32[]{:S(2)}, u32[]{:S(2)}) collective-permute-start(bf16[24,384]{1,0:T(8,128)(2,1)S(1)} %get-tuple-element.173), channel_id=1, source_target_pairs={{0,3},{1,0},{2,1},{3,2},{4,7},{5,4},{6,5},{7,6},{8,11},{9,8},{10,9... | collective-permute-start | bytes 55304 | tf_op jit(solution)/shard_map/ppermute | solution.py:42
  396.4 4.1 collective-permute-start.35
  397.1 3.8 collective-permute-start.36
  427.5 7.9 %collective-permute-start.37 = (bf16[16,6,24,384]{3,2,1,0:T(8,128)(2,1)S(1)}, bf16[16,6,24,384]{3,2,1,0:T(8,128)(2,1)S(1)}, u32[]{:S(2)}, u32[]{:S(2)}) collective-permute-start(bf16[16,6,24,384]{3,2,1,0:T(8,128)(2,1)S(1)} %all_to_all.30.a_ref.ao_ref), channel_id=1, source_target_pairs={{0,4},{4,0},{8,12},{12,8},{16,20},{20,16},{24,28},{28,24},{32,36},... | collective-permute-start | bytes 5308424 | tf_op jit(solution)/shard_map/ppermute | solution.py:50
  (46 other events, 384.4 us)

commit v4 on v3

--- a/solution.py
+++ b/solution.py
@@ -77,65 +77,77 @@
 
 def expert_body(width, ff, x_ref, dy_ref, sel_ref, wr_ref, *rest):
     wg, wu, wd = rest[0:4], rest[4:8], rest[8:12]
-    y_ref, dx_ref, h_ref, dgu_ref, dyo_ref = rest[12:17]
-    wgu, wdn = rest[17:]
+    dx_ref, h_ref, dgu_ref, gate_ref = rest[12:16]
+    wgu, wdn = rest[16:]
     part = wg[0].shape[1]
 
     @pl.when(pl.program_id(0) == 0)
     def _():
-        for r in range(4):
+        for r in range(WS):
             wgu[:, r * part : (r + 1) * part] = wg[r][...]
             wgu[:, ff + r * part : ff + (r + 1) * part] = wu[r][...]
             wdn[r * part : (r + 1) * part, :] = wd[r][...]
         wgu[:, 2 * ff :] = wr_ref[...]
 
-    x = x_ref[...]
-    pre = dot(x, wgu[...])
+    pre = dot(x_ref[...], wgu[...])
     g, u, logits = pre[:, :ff], pre[:, ff : 2 * ff], pre[:, 2 * ff :]
     mask = dy_ref[:, width:].astype(F32) > 0.5
     logits = jnp.where(mask, logits, MASKED)
     lifted = jnp.where(mask, jnp.exp(logits - jnp.max(logits, axis=1, keepdims=True)), 0.0)
     total = jnp.maximum(jnp.sum(lifted, axis=1, keepdims=True), 1e-30)
     gate = jnp.sum(lifted * sel_ref[0:1, :], axis=1, keepdims=True) / total
+    gate_ref[...] = jnp.broadcast_to(gate, gate_ref.shape)
     sig = 1.0 / (1.0 + jnp.exp(-g))
     silu = g * sig
     h = (silu * u).astype(BF)
     h_ref[...] = h
-    y = dot(h, wdn[...]).astype(BF)
-    y_ref[...] = y
-    dy = dy_ref[:, :width].astype(F32)
-    dgate = jnp.sum(dy * y.astype(F32), axis=1, keepdims=True)
-    d_y = (gate * dy).astype(BF)
-    dyo_ref[...] = d_y
-    dh = dot_t(d_y, wdn[...])
+    raw = dot_t(dy_ref[:, :width], wdn[...])
+    dgate = jnp.sum(raw * h.astype(F32), axis=1, keepdims=True)
+    dh = raw * gate
     dgu_ref[:, :ff] = (dh * u * sig * (1.0 + g * (1.0 - sig))).astype(BF)
     dgu_ref[:, ff:] = (dh * silu).astype(BF)
     dx_ref[:, :width] = dot_t(dgu_ref[...], wgu[:, : 2 * ff]).astype(BF)
     hi = dgate.astype(BF).astype(F32)
     dx_ref[:, width:] = (hi * sel_ref[0:1, :] + (dgate - hi) * sel_ref[1:2, :]).astype(BF)
 
+
 def expert_pass(x, dy, sel, wr, wg, wu, wd, tile):
     slots, width = x.shape
-    part = wg[0].shape[1]; ff = 4 * part
+    part = wg[0].shape[1]
+    ff = WS * part
     row = lambda w: pl.BlockSpec((tile, w), lambda i: (i, 0))
-    whole = lambda a: pl.BlockSpec(a.shape, lambda i: (0, 0))
+    once = lambda a: pl.BlockSpec(a.shape, lambda i: (0, 0))
     return pl.pallas_call(
         functools.partial(expert_body, width, ff),
         grid=(slots // tile,),
-        in_specs=[row(width), row(width + 128), whole(sel), whole(wr)] + [whole(a) for a in (*wg, *wu, *wd)],
-        out_specs=[row(width), row(width + 128), row(ff), row(2 * ff), row(width)],
-        out_shape=[jax.ShapeDtypeStruct((slots, w), BF) for w in (width, width + 128, ff, 2 * ff, width)],
+        in_specs=[row(width), row(width + 128), once(sel), once(wr)]
+        + [once(a) for a in (*wg, *wu, *wd)],
+        out_specs=[row(width + 128), row(ff), row(2 * ff), row(128)],
+        out_shape=[
+            jax.ShapeDtypeStruct((slots, width + 128), BF),
+            jax.ShapeDtypeStruct((slots, ff), BF),
+            jax.ShapeDtypeStruct((slots, 2 * ff), BF),
+            jax.ShapeDtypeStruct((slots, 128), F32),
+        ],
         scratch_shapes=[pltpu.VMEM((width, 2 * ff + 128), BF), pltpu.VMEM((ff, width), BF)],
         compiler_params=pltpu.CompilerParams(vmem_limit_bytes=VM),
-        cost_estimate=pl.CostEstimate(flops=12*slots*width*ff, bytes_accessed=12*slots*width, transcendentals=slots*ff),
+        cost_estimate=pl.CostEstimate(
+            flops=10 * slots * width * ff, bytes_accessed=9 * slots * width, transcendentals=0
+        ),
         name="expert_pass",
     )(x, dy, sel, wr, *wg, *wu, *wd)
 
-def slope_body(x_ref, dgu_ref, h_ref, dy_ref, own_g, own_u, own_d, *peers):
+
+def slope_body(x_ref, dgu_ref, h_ref, dy_ref, gate_ref, *refs):
+    wd = refs[0:4]
+    y_ref, own_g, own_u, own_d = refs[4:8]
+    peers = refs[8:]
     part = own_g.shape[1]
     ff = h_ref.shape[1]
     gu = tdot(x_ref[...], dgu_ref[...])
-    dn = tdot(h_ref[...], dy_ref[...])
+    d_y = (gate_ref[:, 0:1] * dy_ref[...].astype(F32)).astype(BF)
+    dn = tdot(h_ref[...], d_y)
+    y_ref[...] = dot(h_ref[...], jnp.concatenate([w[...] for w in wd], axis=0)).astype(BF)
     own_g[...] = gu[:, :part]
     own_u[...] = gu[:, ff : ff + part]
     own_d[...] = dn[:part]
@@ -144,28 +156,35 @@
         peers[2 * k - 2][1] = gu[:, ff + k * part : ff + (k + 1) * part].astype(BF)
         peers[2 * k - 1][...] = dn[k * part : (k + 1) * part].astype(BF)
 
-def expert_slopes(x, dgu, h, dy, tile=256):
+
+def expert_slopes(x, dgu, h, dy, gate, wd, tile=256):
     slots, width = x.shape
-    ff = h.shape[1]; part = ff // 4
+    ff = h.shape[1]
+    part = ff // WS
     col = pl.BlockSpec((slots, tile), lambda i: (0, i))
-    whole = lambda a: pl.BlockSpec(a.shape, lambda i: (0, 0))
+    once = lambda a: pl.BlockSpec(a.shape, lambda i: (0, 0))
     tall = pl.BlockSpec((tile, part), lambda i: (i, 0))
-    wide = pl.BlockSpec((part, tile), lambda i: (0, i))
+    flat = pl.BlockSpec((part, tile), lambda i: (0, i))
     pair = pl.BlockSpec((2, tile, part), lambda i: (0, i, 0))
     S = jax.ShapeDtypeStruct
     return pl.pallas_call(
         slope_body,
         grid=(width // tile,),
-        in_specs=[col, whole(dgu), whole(h), col],
-        out_specs=[tall, tall, wide] + [pair, wide] * 3,
-        out_shape=[S((width, part), F32)] * 2 + [S((part, width), F32)] + [S((2, width, part), BF), S((part, width), BF)] * 3,
+        in_specs=[col, once(dgu), once(h), col, once(gate)] + [flat] * WS,
+        out_specs=[col, tall, tall, flat] + [pair, flat] * 3,
+        out_shape=[S((slots, width), BF)]
+        + [S((width, part), F32)] * 2
+        + [S((part, width), F32)]
+        + [S((2, width, part), BF), S((part, width), BF)] * 3,
         compiler_params=pltpu.CompilerParams(vmem_limit_bytes=VM),
-        cost_estimate=pl.CostEstimate(flops=6*slots*width*ff, bytes_accessed=8*slots*width, transcendentals=0),
+        cost_estimate=pl.CostEstimate(
+            flops=8 * slots * width * ff, bytes_accessed=8 * slots * width, transcendentals=0
+        ),
         name="expert_slopes",
-    )(x, dgu, h, dy)
-
-
-def finish_body(experts, a_ref, b_ref, ao_ref, bo_ref, flag_ref, *refs):
+    )(x, dgu, h, dy, gate, *wd)
+
+
+def finish_body(experts, place_ref, a_ref, b_ref, ao_ref, bo_ref, flag_ref, *refs):
     q_ref, k_ref, v_ref, r_ref, g_ref, o_ref, s_ref = refs
     turn = pl.program_id(0)
     second = flag_ref[0:1, 0:1]
@@ -199,26 +218,30 @@
     o_ref[...] = jnp.where(use_twin > 0.5, twin, mine)
 
 
-def finish(experts, mine, twin, flag):
+def finish(experts, place, mine, twin, flag):
     chips, sets, step, half = mine.shape
     rows = chips * step
-    first = pl.BlockSpec((chips, 1, step, half), lambda i: (0, i, 0, 0))
-    later = pl.BlockSpec((chips, 1, step, half), lambda i: (0, WS + i % 2, 0, 0))
+    first = pl.BlockSpec((chips, 1, step, half), lambda i, p: (0, i, 0, 0))
+    later = pl.BlockSpec((chips, 1, step, half), lambda i, p: (0, WS + i % 2, 0, 0))
+    turned = lambda i, p: (0, lax.rem(p[0] + i, WS))
     kv = (half - 128) // 2
     S = jax.ShapeDtypeStruct
     return pl.pallas_call(
         functools.partial(finish_body, experts),
-        grid=(WS,),
-        in_specs=[first, first, later, later, pl.BlockSpec(flag.shape, lambda i: (0, 0))],
-        out_specs=[
-            pl.BlockSpec((rows, half), lambda i: (0, i)),
-            pl.BlockSpec((rows, kv), lambda i: (0, i)),
-            pl.BlockSpec((rows, kv), lambda i: (0, i)),
-            pl.BlockSpec((experts, rows), lambda i: (0, 0)),
-            pl.BlockSpec((8, rows), lambda i: (0, 0)),
-            pl.BlockSpec((rows, half), lambda i: (0, i)),
-        ],
-        scratch_shapes=[pltpu.VMEM((rows, 128), F32)],
+        grid_spec=pltpu.PrefetchScalarGridSpec(
+            num_scalar_prefetch=1,
+            grid=(WS,),
+            in_specs=[first, first, later, later, whole(flag.shape)],
+            out_specs=[
+                pl.BlockSpec((rows, half), turned),
+                pl.BlockSpec((rows, kv), turned),
+                pl.BlockSpec((rows, kv), turned),
+                whole((experts, rows)),
+                whole((8, rows)),
+                pl.BlockSpec((rows, half), lambda i, p: (0, i)),
+            ],
+            scratch_shapes=[pltpu.VMEM((rows, 128), F32)],
+        ),
         out_shape=[
             S((rows, WS * half), F32),
             S((rows, WS * kv), F32),
@@ -230,7 +253,7 @@
         compiler_params=pltpu.CompilerParams(vmem_limit_bytes=VM),
         cost_estimate=pl.CostEstimate(flops=0, bytes_accessed=16 * rows * WS * half, transcendentals=0),
         name="finish",
-    )(mine, twin, mine, twin, flag)
+    )(place, mine, twin, mine, twin, flag)
 
 
 def whole(shape):
@@ -315,19 +338,34 @@
     )
 
 
+def attend_rows(qkv_ref, bias_ref, o_ref, lse_ref, start, q_w, kv_w):
+    rows = o_ref.shape[0]
+    group = q_w // kv_w
+    here = slice(start, start + rows)
+    for h in range(q_w // HEAD):
+        at = h // group * HEAD
+        q = qkv_ref[here, h * HEAD : (h + 1) * HEAD]
+        k = qkv_ref[:, q_w + at : q_w + at + HEAD]
+        v = qkv_ref[:, q_w + kv_w + at : q_w + kv_w + at + HEAD]
+        s = dot_t(q, k) * HEAD ** (-0.5) + bias_ref[here, :]
+        peak = jnp.max(s, axis=1, keepdims=True)
+        p = jnp.exp(s - peak)
+        total = jnp.sum(p, axis=1, keepdims=True)
+        lse_ref[:, h : h + 1] = peak + jnp.log(total)
+        o_ref[:, h * HEAD : (h + 1) * HEAD] = dot((p / total).astype(BF), v).astype(BF)
+
+
 def attend_body(experts, place_ref, *refs):
     xs, own, twin = refs[0:4], refs[4:8], refs[8:12]
     cos_ref, sin_ref, bias_ref, wo_ref = refs[12:16]
     h1_ref, qkv_ref, o_ref, lse_ref, w_ref, small_ref, rows_ref = refs[16:23]
-    parts = refs[23:27]
+    parts = refs[23:26]
     me, core = place_ref[0], place_ref[1]
     rows = xs[0].shape[0]
     strip = own[0].shape[0]
-    heads = o_ref.shape[1] // HEAD
-    q_w = heads * HEAD
+    q_w = o_ref.shape[1]
     qkv_w = qkv_ref.shape[1]
     kv_w = (qkv_w - q_w) // 2
-    group = q_w // kv_w
     for r in range(WS):
         base = lax.rem(me + r, WS) * (2 * strip)
         for source, side in ((own[r], core), (twin[r], 1 - core)):
@@ -348,20 +386,10 @@
     qk = qk * wide(cos_ref, times) + other_half(qk) * wide(sin_ref, times)
     qkv_ref[:, : q_w + kv_w] = qk.astype(BF)
     qkv_ref[:, q_w + kv_w :] = qkv[:, q_w + kv_w :].astype(BF)
-    for h in range(heads):
-        at = h // group * HEAD
-        q = qkv_ref[:, h * HEAD : (h + 1) * HEAD]
-        k = qkv_ref[:, q_w + at : q_w + at + HEAD]
-        v = qkv_ref[:, q_w + kv_w + at : q_w + kv_w + at + HEAD]
-        s = dot_t(q, k) * HEAD ** (-0.5) + bias_ref[...]
-        peak = jnp.max(s, axis=1, keepdims=True)
-        p = jnp.exp(s - peak)
-        total = jnp.sum(p, axis=1, keepdims=True)
-        lse_ref[:, h : h + 1] = peak + jnp.log(total)
-        o_ref[:, h * HEAD : (h + 1) * HEAD] = dot((p / total).astype(BF), v).astype(BF)
-    for r in range(WS):
+    attend_rows(qkv_ref, bias_ref, o_ref, lse_ref, rows, q_w, kv_w)
+    for r in range(3):
         part = dot(o_ref[r * rows : (r + 1) * rows, :], wo_ref[...])
-        parts[r][...] = part.astype(parts[r].dtype)
+        parts[r][...] = part.astype(BF)
 
 
 def attend(experts, place, xs, own, twin, cos, sin, bias, wo):
@@ -371,12 +399,11 @@
     outs = [
         sds((tree, width), BF),
         sds((tree, qkv_w), BF),
-        sds((tree, q_w), BF),
-        sds((tree, 128), F32),
+        sds((tree - rows, q_w), BF),
+        sds((tree - rows, 128), F32),
         sds((width, qkv_w), BF),
         sds((width, 128), BF),
         sds((8, width), F32),
-        sds((rows, width), F32),
     ] + [sds((rows, width), BF)] * 3
     flops = 2 * tree * width * (qkv_w + q_w) + 4 * tree * tree * q_w
     return one_step(
@@ -390,16 +417,56 @@
     )
 
 
-def enter_body(x_ref, p0, p1, p2, p3, rows_ref, router_ref, slot_ref, chosen_ref, spread_ref, *outs):
-    x2_ref, h2_ref, send_ref, gates_ref, gs_ref = outs
-    x2 = x_ref[...].astype(F32) + p0[...]
-    for p in (p1, p2, p3):
-        x2 = x2 + p[...].astype(F32)
-    x2_ref[...] = x2
-    h2 = (x2 * rms(x2) * rows_ref[1:2, :]).astype(BF)
-    h2_ref[...] = h2
-    send_ref[...] = tdot(slot_ref[...], h2).astype(BF)
-    logits = dot(h2, router_ref[...])
+def attend_own_body(qkv_ref, bias_ref, wo_ref, o_ref, lse_ref, part_ref):
+    q_w = o_ref.shape[1]
+    kv_w = (qkv_ref.shape[1] - q_w) // 2
+    attend_rows(qkv_ref, bias_ref, o_ref, lse_ref, 0, q_w, kv_w)
+    part_ref[...] = dot(o_ref[...], wo_ref[...])
+
+
+def attend_own(rows, qkv, bias, wo):
+    q_w, width = wo.shape
+    outs = [sds((rows, q_w), BF), sds((rows, 128), F32), sds((rows, width), F32)]
+    flops = 2 * rows * width * q_w + 4 * rows * qkv.shape[0] * q_w
+    return one_step(attend_own_body, "attend_own", [], [qkv, bias, wo], outs, [], flops)
+
+
+def enter_body(x_ref, p0, p1, p2, p3, rows_ref, slot_ref, x2_ref, h2_ref, send_ref):
+    @pl.when(pl.program_id(0) == 0)
+    def _():
+        x2 = x_ref[...].astype(F32) + p0[...]
+        for p in (p1, p2, p3):
+            x2 = x2 + p[...].astype(F32)
+        x2_ref[...] = x2
+        h2_ref[...] = (x2 * rms(x2) * rows_ref[1:2, :]).astype(BF)
+
+    send_ref[...] = tdot(slot_ref[...], h2_ref[...]).astype(BF)
+
+
+def enter(x, parts, rows, to_slot, tile=512):
+    n, width = x.shape
+    slots = to_slot.shape[1]
+    arrays = [x, *parts, rows]
+    return pl.pallas_call(
+        enter_body,
+        grid=(slots // tile,),
+        in_specs=[whole(a.shape) for a in arrays] + [pl.BlockSpec((n, tile), lambda i: (0, i))],
+        out_specs=[
+            whole((n, width)),
+            whole((n, width)),
+            pl.BlockSpec((tile, width), lambda i: (i, 0)),
+        ],
+        out_shape=[sds((n, width), F32), sds((n, width), BF), sds((slots, width), BF)],
+        compiler_params=pltpu.CompilerParams(vmem_limit_bytes=VM),
+        cost_estimate=pl.CostEstimate(
+            flops=2 * n * width * slots, bytes_accessed=3 * slots * width, transcendentals=0
+        ),
+        name="enter",
+    )(*arrays, to_slot)
+
+
+def gate_body(h2_ref, router_ref, slot_ref, chosen_ref, spread_ref, gates_ref, gs_ref):
+    logits = dot(h2_ref[...], router_ref[...])
     mask = chosen_ref[...].astype(F32) > 0.5
     logits = jnp.where(mask, logits, MASKED)
     lifted = jnp.where(mask, jnp.exp(logits - jnp.max(logits, axis=1, keepdims=True)), 0.0)
@@ -408,73 +475,100 @@
     hi, lo = split(gates)
     on_slots = dot(hi, spread_ref[...]) + dot(lo, spread_ref[...])
     hi, lo = split(on_slots * slot_ref[...].astype(F32))
-    rows = x2.shape[0]
+    rows = gates.shape[0]
     gs_ref[:rows, :] = hi
     gs_ref[rows:, :] = lo
 
 
-def enter(x, parts, rows, router, to_slot, chosen, spread):
-    n, width = x.shape
-    slots = to_slot.shape[1]
-    outs = [
-        sds((n, width), F32),
-        sds((n, width), BF),
-        sds((slots, width), BF),
-        sds((n, 128), F32),
-        sds((2 * n, slots), BF),
-    ]
+def gate_terms(h2, router, to_slot, chosen, spread):
+    n, slots = to_slot.shape
+    outs = [sds((n, 128), F32), sds((2 * n, slots), BF)]
+    arrays = [h2, router, to_slot, chosen, spread]
+    return one_step(gate_body, "gate_terms", [], arrays, outs, [], 8 * n * 128 * slots)
+
+
+def leave_body(experts, back_ref, slot_ref, gates_ref, router_ref, x2_ref, rows_ref, cot_ref, *outs):
+    dx2_ref, da_ref, dh2_ref, dl_ref, sum_ref = outs
+    width = x2_ref.shape[1]
+    step = pl.program_id(0)
+    more = dot(slot_ref[...], back_ref[...])
+
+    @pl.when(step == 0)
+    def _():
+        sum_ref[...] = more
+
+    @pl.when(step > 0)
+    def _():
+        sum_ref[...] += more
+
+    @pl.when(step == pl.num_programs(0) - 1)
+    def _():
+        tail = sum_ref[:, width:]
+        dgate = tail + pltpu.roll(tail, 128 - experts, 1)
+        gates = gates_ref[...]
+        dl = gates * (dgate - jnp.sum(gates * dgate, axis=1, keepdims=True))
+        dl_ref[...] = dl
+        hi, lo = split(dl)
+        dh2 = sum_ref[:, :width] + dot_t(hi, router_ref[...]) + dot_t(lo, router_ref[...])
+        dh2_ref[...] = dh2
+        x2 = x2_ref[...]
+        scale, gain = rms(x2), rows_ref[1:2, :]
+        inner = jnp.mean(gain * dh2 * x2, axis=1, keepdims=True)
+        dx2 = cot_ref[...].astype(F32) + scale * gain * dh2 - x2 * scale * scale * scale * inner
+        dx2_ref[...] = dx2
+        da_ref[...] = dx2.astype(BF)
+
+
+def leave(experts, back, to_slot, gates, router, x2, rows, cot, tile=512):
+    n, width = x2.shape
+    slots = back.shape[0]
+    outs = [sds((n, width), F32), sds((n, width), BF), sds((n, width), F32), sds((n, 128), F32)]
+    rest = [gates, router, x2, rows, cot]
+    return pl.pallas_call(
+        functools.partial(leave_body, experts),
+        grid=(slots // tile,),
+        in_specs=[
+            pl.BlockSpec((tile, width + 128), lambda i: (i, 0)),
+            pl.BlockSpec((n, tile), lambda i: (0, i)),
+        ]
+        + [whole(a.shape) for a in rest],
+        out_specs=[whole(o.shape) for o in outs],
+        out_shape=outs,
+        scratch_shapes=[pltpu.VMEM((n, width + 128), F32)],
+        compiler_params=pltpu.CompilerParams(vmem_limit_bytes=VM),
+        cost_estimate=pl.CostEstimate(
+            flops=2 * n * width * slots, bytes_accessed=3 * slots * width, transcendentals=0
+        ),
+        name="leave",
+    )(back, to_slot, *rest)
+
+
+def small_body(experts, h2_ref, dl_ref, dh2_ref, x2_ref, out_ref):
+    hi, lo = split(dl_ref[...])
+    h2, x2 = h2_ref[...], x2_ref[...]
+    out_ref[...] = tdot(h2, hi) + tdot(h2, lo) + column_sum(dh2_ref[...] * x2 * rms(x2), experts)
+
+
+def small_slopes(experts, h2, dl, dh2, x2):
+    n, width = x2.shape
     return one_step(
-        enter_body,
-        "enter",
+        functools.partial(small_body, experts),
+        "small_slopes",
         [],
-        [x, *parts, rows, router, to_slot, chosen, spread],
-        outs,
+        [h2, dl, dh2, x2],
+        [sds((width, 128), F32)],
         [],
-        2 * n * width * slots,
-    )
-
-
-def leave_body(experts, back_ref, slot_ref, gates_ref, router_ref, x2_ref, h2_ref, rows_ref, cot_ref, *outs):
-    dx2_ref, da_ref, small_ref = outs
-    width = x2_ref.shape[1]
-    back = dot(slot_ref[...], back_ref[...])
-    tail = back[:, width:]
-    dgate = tail + pltpu.roll(tail, 128 - experts, 1)
-    gates = gates_ref[...]
-    dl = gates * (dgate - jnp.sum(gates * dgate, axis=1, keepdims=True))
-    hi, lo = split(dl)
-    dh2 = back[:, :width] + dot_t(hi, router_ref[...]) + dot_t(lo, router_ref[...])
-    x2 = x2_ref[...]
-    scale, gain = rms(x2), rows_ref[1:2, :]
-    inner = jnp.mean(gain * dh2 * x2, axis=1, keepdims=True)
-    dx2 = cot_ref[...].astype(F32) + scale * gain * dh2 - x2 * scale * scale * scale * inner
-    dx2_ref[...] = dx2
-    da_ref[...] = dx2.astype(BF)
-    h2 = h2_ref[...]
-    small_ref[...] = tdot(h2, hi) + tdot(h2, lo) + column_sum(dh2 * x2 * scale, experts)
-
-
-def leave(experts, back, to_slot, gates, router, x2, h2, rows, cot):
-    n, width = x2.shape
-    outs = [sds((n, width), F32), sds((n, width), BF), sds((width, 128), F32)]
-    return one_step(
-        functools.partial(leave_body, experts),
-        "leave",
-        [],
-        [back, to_slot, gates, router, x2, h2, rows, cot],
-        outs,
-        [],
-        2 * n * back.size,
-    )
+        8 * n * width * 128,
+    )[0]
 
 
 def attend_back_body(experts, place_ref, *refs):
     das, xs = refs[0:4], refs[4:8]
-    wo_ref, qkv_ref, o_ref, lse_ref, h1_ref, w_ref = refs[8:14]
-    cos_ref, sin_ref, bias_ref, small_ref = refs[14:18]
-    keep_ref, give_ref = refs[18:20]
-    parts = refs[20:24]
-    da, do, dqk, dqkv = refs[24:28]
+    wo_ref, qkv_ref, o_own, o_far, lse_own, lse_far, h1_ref, w_ref = refs[8:16]
+    cos_ref, sin_ref, bias_ref, small_ref = refs[16:20]
+    keep_ref, give_ref = refs[20:22]
+    parts = refs[22:26]
+    da, do, dqk, dqkv, o_ref, lse_ref = refs[26:32]
     core = place_ref[1]
     rows = xs[0].shape[0]
     q_w, qkv_w = o_ref.shape[1], qkv_ref.shape[1]
@@ -483,6 +577,10 @@
     scale = HEAD ** (-0.5)
     for r in range(WS):
         da[r * rows : (r + 1) * rows, :] = das[r][...]
+    o_ref[:rows, :] = o_own[...]
+    o_ref[rows:, :] = o_far[...]
+    lse_ref[:rows, :] = lse_own[...]
+    lse_ref[rows:, :] = lse_far[...]
     do[...] = dot_t(da[...], wo_ref[...]).astype(BF)
     for n in range(kv_w // HEAD):
         at = n * HEAD
@@ -533,7 +631,7 @@
         put(WS + i, slope[:, i * half : (i + 1) * half], slope[:, (2 + i) * half : (3 + i) * half])
 
 
-def attend_back(experts, place, das, xs, wo, qkv, o, lse, h1, w, cos, sin, bias, small):
+def attend_back(experts, place, das, xs, wo, qkv, os, lses, h1, w, cos, sin, bias, small):
     rows, width = xs[0].shape
     tree = rows * WS
     q_w, qkv_w = wo.shape[0], qkv.shape[1]
@@ -545,13 +643,15 @@
         pltpu.VMEM((tree, q_w), BF),
         pltpu.VMEM((tree, (q_w + qkv_w) // 2), F32),
         pltpu.VMEM((tree, qkv_w + 128), BF),
+        pltpu.VMEM((tree, q_w), BF),
+        pltpu.VMEM((tree, 128), F32),
     ]
     flops = 4 * tree * width * (qkv_w + q_w) + 10 * tree * tree * q_w
     return one_step(
         functools.partial(attend_back_body, experts),
         "attend_back",
         [place],
-        [*das, *xs, wo, qkv, o, lse, h1, w, cos, sin, bias, small],
+        [*das, *xs, wo, qkv, *os, *lses, h1, w, cos, sin, bias, small],
         outs,
         scratch,
         flops,
@@ -605,11 +705,11 @@
     col = jnp.arange(slots, dtype=jnp.int32)
     spread = (col[None, :] // CAP == lane[:, None]).astype(BF)
     spot = dot(jnp.where(chosen, rank + 1.0, 0.0).astype(BF), spread)
-    nothing = (xs[1][:1, :1] + xs[3][:1, :1]).astype(F32) * 0.0
-    to_slot = (spot == (col % CAP + 1).astype(F32)[None, :] + nothing).astype(BF)
+    to_slot = (spot == (col % CAP + 1).astype(F32)[None, :]).astype(BF)
     chosen = chosen.astype(BF)
     extra = jnp.concatenate([cotangent, chosen], axis=1)
     dy_send = tdot(to_slot, extra).astype(BF).reshape(experts, CAP, width + 128)
+    dy_send, xs[1], xs[3] = lax.optimization_barrier((dy_send, xs[1], xs[3]))
     dy_slots = lax.all_to_all(dy_send, "exp", 0, 0, tiled=True).reshape(slots, width + 128)
 
     order = (
@@ -621,13 +721,12 @@
     angles = position.astype(F32)[:, None] * inverse[None, :]
     cosines = jnp.cos(angles)
     sines = jnp.where((lane % HEAD < HEAD // 2)[None, :], -1.0, 1.0) * jnp.sin(angles)
-    h1, qkv, o, lse, w_qkv, small_full, gains, *parts = attend(
+    h1, qkv, o_far, lse_far, w_qkv, small_full, gains, *parts = attend(
         experts, place, xs, own, twin, cosines, sines, bias, w_out
     )
-    sums = [parts[0]] + [to_peer(parts[k], k) for k in (1, 2, 3)]
-    x2, h2, x_send, gates, gate_slots = enter(
-        tokens, sums, gains, small_full, to_slot, chosen, spread
-    )
+    o_own, lse_own, part_own = attend_own(rows, qkv, bias, w_out)
+    sums = [part_own] + [to_peer(parts[k - 1], k) for k in (1, 2, 3)]
+    x2, h2, x_send = enter(tokens, sums, gains, to_slot)
     x_send, wg_own, wu_own, wd_own = lax.optimization_barrier(
         (x_send, w_gate[0], w_up[0], w_down[0])
     )
@@ -643,34 +742,56 @@
         ],
         axis=0,
     )
-    y, dx_send, hidden, d_gu, d_y = expert_pass(
-        x_slots, dy_slots, sel, small_full, gathered(wg_own), gathered(wu_own), gathered(wd_own), 512
-    )
+    wd = gathered(wd_own)
+    dx_send, hidden, d_gu, slot_gates = expert_pass(
+        x_slots, dy_slots, sel, small_full, gathered(wg_own), gathered(wu_own), wd, 256
+    )
+    gates, gate_slots = gate_terms(h2, small_full, to_slot, chosen, spread)
+    hidden, gates, gate_slots = lax.optimization_barrier((hidden, gates, gate_slots))
     dx_back = lax.all_to_all(
         dx_send.reshape(experts, CAP, width + 128), "exp", 0, 0, tiled=True
     ).reshape(slots, width + 128)
 
-    own_g, own_u, own_d, gu1, dn1, gu2, dn2, gu3, dn3 = expert_slopes(x_slots, d_gu, hidden, d_y)
+    y, own_g, own_u, own_d, gu1, dn1, gu2, dn2, gu3, dn3 = expert_slopes(
+        x_slots, d_gu, hidden, dy_slots, slot_gates, wd
+    )
     gu1, dn1 = to_peer(gu1, 1), to_peer(dn1, 1)
     gu3, dn3 = to_peer(gu3, 3), to_peer(dn3, 3)
-    gu2, dn2 = to_peer(gu2, 2), to_peer(dn2, 2)
-    dx_back, y, gu1, dn1, gu2, dn2, gu3, dn3 = lax.optimization_barrier(
-        (dx_back, y, gu1, dn1, gu2, dn2, gu3, dn3)
+    gu2 = to_peer(gu2, 2)
+    dx_back, y, gu1, dn1, gu2, gu3, dn3 = lax.optimization_barrier(
+        (dx_back, y, gu1, dn1, gu2, gu3, dn3)
     )
     y_back = lax.all_to_all(y.reshape(experts, CAP, width), "exp", 0, 0, tiled=True).reshape(
         slots, width
     )
 
-    dx2, d_a, small_terms = leave(
-        experts, dx_back, to_slot, gates, small_full, x2, h2, gains, cotangent
+    dx2, d_a, dh2, dl = leave(
+        experts, dx_back, to_slot, gates, small_full, x2, gains, cotangent
     )
     das = gathered(d_a)
+    small_terms = small_slopes(experts, h2, dl, dh2, x2)
+    keep, give, *slopes = attend_back(
+        experts,
+        place,
+        das,
+        xs,
+        w_out,
+        qkv,
+        (o_own, o_far),
+        (lse_own, lse_far),
+        h1,
+        w_qkv,
+        cosines,
+        sines,
+        bias,
+        small_terms,
+    )
+    sent = (keep + other_core(give).astype(F32)).astype(BF)
+    sent, y_back, slopes, dn2, gu1 = lax.optimization_barrier((sent, y_back, slopes, dn2, gu1))
+    dn2 = to_peer(dn2, 2)
     grad_gu = jnp.stack([own_g, own_u]) + gu1.astype(F32) + gu2.astype(F32) + gu3.astype(F32)
     grad_wg, grad_wu = grad_gu[0][None], grad_gu[1][None]
     grad_wd = (own_d + dn1.astype(F32) + dn2.astype(F32) + dn3.astype(F32))[None]
-    keep, give, *slopes = attend_back(
-        experts, place, das, xs, w_out, qkv, o, lse, h1, w_qkv, cosines, sines, bias, small_terms
-    )
     dh1 = slopes[0]
     for k in (1, 2, 3):
         dh1 = dh1 + to_peer(slopes[k], k).astype(F32)
@@ -682,8 +803,6 @@
     half = (q_w + 2 * kv_w + 128) // 2
     flag = jnp.broadcast_to(jnp.stack([core, 1 - core]).astype(F32)[:, None], (2, 128))
     flag = jnp.concatenate([flag, jnp.zeros((6, 128), F32)], axis=0)
-    give, y_back = lax.optimization_barrier((give, y_back))
-    sent = (keep + other_core(give).astype(F32)).astype(BF)
     step = shard // CHIPS
     both = dot(gate_slots, y_back)
     layer_out = (x2 + both[:rows] + both[rows:]).astype(BF)
@@ -692,19 +811,18 @@
         (got, layer_out, grad_tokens, grad_wg, grad_wu, grad_wd)
     )
     total = jnp.sum(got.astype(F32), axis=0).astype(BF)
-    turned = jnp.stack(
+    final = jnp.stack(
         [lax.dynamic_index_in_dim(total, me, 0, False)]
         + [
             from_peer(lax.dynamic_index_in_dim(total, (me - k) % WS, 0, False), k)
             for k in (1, 2, 3)
         ]
-    )
-    turned = lax.dynamic_slice_in_dim(jnp.concatenate([turned, turned]), (WS - me) % WS, WS, 0)
-    final = jnp.concatenate([turned, total[WS:]], axis=0)
+        + [total[WS], total[WS + 1]]
+    )
     spread_out = same_core(jnp.broadcast_to(final, (CHIPS,) + final.shape))
     twin_out = other_core(spread_out)
     sum_query, sum_key, sum_value, sum_router, sum_gains, sum_out = finish(
-        experts, spread_out, twin_out, flag
+        experts, place, spread_out, twin_out, flag
     )
 
     return (

time: 450 us -> 420 us (0.933)
  waiting for transfers between devices: 197 us -> 155 us
  Pallas kernels: 87 us -> 97.9 us
    pallas_call x2 -> x4, Pallas kernels: 18.4 us -> 34.1 us  [the longest x1 15.6 us: expert_slopes(): pl.pallas_call(slope_body, grid=(width // tile,), in_specs=[col, once(dgu...]
    all_to_all x1, waiting for transfers between devices: 15.1 us -> 0.01 us  [same_core(): return lax.all_to_all(v, 'exp', 0, 0, tiled=True, axis_index_groups=groups)]
    ppermute x12, waiting for transfers between devices: 84.1 us -> 69.2 us  [to_peer(): return lax.ppermute(v, 'ws', [(s, (s + k) % WS) for s in range(WS)])]
    all_to_all x1, waiting for transfers between devices: 8.63 us -> 1.01 us  [shards(): lax.all_to_all(y.reshape(experts, CAP, width), 'exp', 0, 0, tiled=True)]
    ppermute x21, waiting for transfers between devices: 83 us -> 77 us  [from_peer(): return lax.ppermute(v, 'ws', [(s, (s - k) % WS) for s in range(WS)])]
    pallas_call x5 -> x6, Pallas kernels: 45.6 us -> 43 us  [one_step(): pl.pallas_call(body, in_specs=[pl.BlockSpec(memory_space=pltpu.SMEM)] * l...]
  transfers between devices with their start and end apart: 43 -> 43, of which waited for: 31 -> 28; matrix products, arithmetic and copies ran while one was open for 6% -> 8% of each run, Pallas kernels for 13% -> 17%
where the time goes in v4:
time: 420 us; the launch traced here: 414 us
  waiting for transfers between devices  155 us (37%)
  Pallas kernels  97.9 us (23%)
  starting transfers between devices  93.8 us (22%)
  blocking collectives  25.9 us (6%)
  other arithmetic  15.2 us (4%)
  local copies, waits for them, and re-layouts  13.3 us (3%)
  matrix products  10.9 us (3%)
    ppermute x21, waiting for transfers between devices, from_peer(): return lax.ppermute(v, 'ws', [(s, (s - k) % WS) for s in range(WS)])  77 us
    ppermute x12, waiting for transfers between devices, to_peer(): return lax.ppermute(v, 'ws', [(s, (s + k) % WS) for s in range(WS)])  69.2 us
    pallas_call x6, Pallas kernels, one_step(): pl.pallas_call(body, in_specs=[pl.BlockSpec(memory_space=pltpu.SMEM)] * l...  43 us
    ppermute x21, starting transfers between devices, from_peer(): return lax.ppermute(v, 'ws', [(s, (s - k) % WS) for s in range(WS)])  28.9 us
    all_to_all x1, blocking collectives, same_core(): return lax.all_to_all(v, 'exp', 0, 0, tiled=True, axis_index_groups=groups)  25.9 us
    pallas_call x1, Pallas kernels, expert_pass(): pl.pallas_call(functools.partial(expert_body, width, ff), grid=(slots //...  20.7 us
    pallas_call x1, Pallas kernels, expert_slopes(): pl.pallas_call(slope_body, grid=(width // tile,), in_specs=[col, once(dgu...  15.6 us
    ppermute x12, starting transfers between devices, to_peer(): return lax.ppermute(v, 'ws', [(s, (s + k) % WS) for s in range(WS)])  15.4 us
  transfers between devices with their start and end apart: 43, of which 28 were waited for; matrix products, arithmetic and copies ran while one was open for 8% of the time, Pallas kernels for 17%

profile of v4, /device:TPU:1, one launch (start us, length us, event | category | flops | bytes accessed | tf_op | source)
XLA Modules:
  0.0 413.9 jit_solution(13607866362295277706)
XLA Ops:
  0.7 3.6 collective-permute-start
  8.9 2.9 pack.1
  13.4 3.9 convolution_convert_fusion
  18.2 8.9 %all-to-all-start.1 = ((bf16[32,48,1664]{2,1,0:T(8,128)(2,1)}), bf16[32,48,1664]{2,1,0:T(8,128)(2,1)}, u32[]{:S(2)}, u32[]{:S(2)}) async-start(bf16[32,48,1664]{2,1,0:T(8,128)(2,1)} %bitcast.58), calls=%async_computation.1 | async-start | bytes 10223616 | tf_op jit(solution)/shard_map/all_to_all | solution.py:713
  30.3 2.3 collective-permute-start.4
  33.8 12.4 %collective-permute-done.3.refs_5_ = bf16[192,768]{1,0:T(8,128)(2,1)S(1)} collective-permute-done((bf16[192,768]{1,0:T(8,128)(2,1)S(1)}, bf16[192,768]{1,0:T(8,128)(2,1)S(1)}, u32[]{:S(2)}, u32[]{:S(2)}) %collective-permute-start.3) | collective-permute-done | bytes 294944 | tf_op jit(solution)/shard_map/ppermute | solution.py:42
  48.0 4.5 %collective-permute-done.5.refs_7_ = bf16[192,768]{1,0:T(8,128)(2,1)S(1)} collective-permute-done((bf16[192,768]{1,0:T(8,128)(2,1)S(1)}, bf16[192,768]{1,0:T(8,128)(2,1)S(1)}, u32[]{:S(2)}, u32[]{:S(2)}) %collective-permute-start.5) | collective-permute-done | bytes 294944 | tf_op jit(solution)/shard_map/ppermute | solution.py:42
  57.7 9.6 %attend.1 = (bf16[512,1536]{1,0:T(8,128)(2,1)}, bf16[512,640]{1,0:T(8,128)(2,1)}, bf16[384,384]{1,0:T(8,128)(2,1)}, f32[384,128]{1,0:T(8,128)}, bf16[1536,640]{1...) custom-call(s32[2]{0:T(128)} %pad_add_fusion.place_ref, ...), custom_call_target="tpu_custom_call" | custom-call | flops 2013265920 | bytes 6684672 | tf_op jit(solution)/shard_map/attend/pallas_call | solution.py:269
  68.1 3.6 collective-permute-start.10
  71.7 5.4 %attend_own.1 = (bf16[128,384]{1,0:T(8,128)(2,1)}, f32[128,128]{1,0:T(8,128)}, f32[128,1536]{1,0:T(8,128)}) custom-call(bf16[512,640]{1,0:T(8,128)(2,1)} %get-tuple-element.115.qkv_ref.refs_9_, f32[512,512]{1,0:T(8,128)} %fusion.3.refs_14_.bias_ref.refs_18_, bf16[384,1536]{1,0:T(8,128)(2,1)} %refs_8_.1), custom_call_target="tpu_custom_call" | custom-call | flops 251658240 | bytes 2883584 | tf_op jit(solution)/shard_map/attend_own/pallas_call | solution.py:269
  77.0 2.9 collective-permute-done.9.p1
  79.9 9.3 %collective-permute-done.10.p2 = bf16[128,1536]{1,0:T(8,128)(2,1)S(1)} collective-permute-done((bf16[128,1536]{1,0:T(8,128)(2,1)}, bf16[128,1536]{1,0:T(8,128)(2,1)S(1)}, u32[]{:S(2)}, u32[]{:S(2)}) %collective-permute-start.10) | collective-permute-done | bytes 393248 | tf_op jit(solution)/shard_map/ppermute | solution.py:46
  90.1 5.6 %enter.1 = (f32[128,1536]{1,0:T(8,128)}, bf16[128,1536]{1,0:T(8,128)(2,1)}, bf16[1536,1536]{1,0:T(8,128)(2,1)}) custom-call(bf16[128,1536]{1,0:T(8,128)(2,1)} %refs_4_.1, f32[128,1536]{1,0:T(8,128)} %get-tuple-element.116.p0, bf16[128,1536]{1,0:T(8,128)(2,1)} %copy-done.11, bf16[128,1536]{1,0:T(8,128)(2,1)} %copy-done.12, bf16[128,1536]{1,0:T(8,128)(2,1)} %copy-done.13, ...), custom_call_target="tpu_custom_call" | custom-call | flops 603979776 | bytes 7077888 | tf_op jit(solution)/shard_map/enter/pallas_call | solution.py:450
  95.7 8.3 %all-to-all-start = ((bf16[32,48,1536]{2,1,0:T(8,128)(2,1)}), bf16[32,48,1536]{2,1,0:T(8,128)(2,1)}, u32[]{:S(2)}, u32[]{:S(2)}) async-start(bf16[32,48,1536]{2,1,0:T(8,128)(2,1)} %bitcast.61), calls=%async_computation | async-start | bytes 9437184 | tf_op jit(solution)/shard_map/all_to_all | solution.py:733
  110.4 4.3 %collective-permute-done.12.rest_1_ = bf16[1536,128]{1,0:T(8,128)(2,1)S(1)} collective-permute-done((bf16[1536,128]{1,0:T(8,128)(2,1)S(1)}, bf16[1536,128]{1,0:T(8,128)(2,1)S(1)}, u32[]{:S(2)}, u32[]{:S(2)}) %collective-permute-start.12) | collective-permute-done | bytes 393248 | tf_op jit(solution)/shard_map/ppermute | solution.py:42
  115.0 2.7 collective-permute-done.13.rest_2_
  117.7 7.8 %collective-permute-start.18 = (bf16[128,1536]{1,0:T(8,128)(2,1)S(1)}, bf16[128,1536]{1,0:T(8,128)(2,1)S(1)}, u32[]{:S(2)}, u32[]{:S(2)}) collective-permute-start(bf16[128,1536]{1,0:T(8,128)(2,1)S(1)} %bitcast.77), channel_id=1, source_target_pairs={{0,3},{1,0},{2,1},{3,2},{4,7},{5,4},{6,5},{7,6},{8,11},{9,8},{10,9... | collective-permute-start | bytes 1179656 | tf_op jit(solution)/shard_map/ppermute | solution.py:42
  128.1 3.5 collective-permute-done.15.rest_5_
  134.6 9.3 %collective-permute-done.17.rest_7_ = bf16[1536,128]{1,0:T(8,128)(2,1)} collective-permute-done((bf16[1536,128]{1,0:T(8,128)(2,1)S(1)}, bf16[1536,128]{1,0:T(8,128)(2,1)}, u32[]{:S(2)}, u32[]{:S(2)}) %collective-permute-start.17) | collective-permute-done | bytes 393248 | tf_op jit(solution)/shard_map/ppermute | solution.py:42
  143.9 4.5 %collective-permute-done.18.rest_9_.refs_1_ = bf16[128,1536]{1,0:T(8,128)(2,1)S(1)} collective-permute-done((bf16[128,1536]{1,0:T(8,128)(2,1)S(1)}, bf16[128,1536]{1,0:T(8,128)(2,1)S(1)}, u32[]{:S(2)}, u32[]{:S(2)}) %collective-permute-start.18) | collective-permute-done | bytes 393248 | tf_op jit(solution)/shard_map/ppermute | solution.py:42
  148.5 3.0 collective-permute-done.19.rest_10_.refs_2_
  151.5 8.8 %collective-permute-done.20.rest_11_.refs_3_ = bf16[128,1536]{1,0:T(8,128)(2,1)S(1)} collective-permute-done((bf16[128,1536]{1,0:T(8,128)(2,1)S(1)}, bf16[128,1536]{1,0:T(8,128)(2,1)S(1)}, u32[]{:S(2)}, u32[]{:S(2)}) %collective-permute-start.20) | collective-permute-done | bytes 393248 | tf_op jit(solution)/shard_map/ppermute | solution.py:42
  162.5 20.7 %expert_pass.1 = (bf16[1536,1664]{1,0:T(8,128)(2,1)}, bf16[1536,512]{1,0:T(8,128)(2,1)}, bf16[1536,1024]{1,0:T(8,128)(2,1)}, f32[1536,128]{1,0:T(8,128)}) custom-call(bf16[1536,1536]{1,0:T(8,128)(2,1)} %bitcast.15.x_ref, bf16[1536,1664]{1,0:T(8,128)(2,1)} %bitcast.16.dy_ref, f32[8,128]{1,0:T(8,128)} %maximum_maximum_fusion.sel_ref, ...), custom_call_target="tpu_custom_call" | custom-call | flops 12079595520 | bytes 21233664 | tf_op jit(solution)/shard_map/expert_pass/pallas_call | solution.py:120
  183.3 7.8 %all-to-all-start.2 = ((bf16[32,48,1664]{2,1,0:T(8,128)(2,1)}), bf16[32,48,1664]{2,1,0:T(8,128)(2,1)}, u32[]{:S(2)}, u32[]{:S(2)}) async-start(bf16[32,48,1664]{2,1,0:T(8,128)(2,1)} %bitcast.59), calls=%async_computation.2 | async-start | bytes 10223616 | tf_op jit(solution)/shard_map/all_to_all | solution.py:751
  191.9 3.0 gate_terms.1
  194.9 15.6 %expert_slopes.1 = (bf16[1536,1536]{1,0:T(8,128)(2,1)}, f32[1536,128]{1,0:T(8,128)}, f32[1536,128]{1,0:T(8,128)}, f32[128,1536]{1,0:T(8,128)}, bf16[2,1536,128]{...) custom-call(bf16[1536,1536]{1,0:T(8,128)(2,1)} %bitcast.15.x_ref, ...), custom_call_target="tpu_custom_call" | custom-call | flops 9663676416 | bytes 18874368 | tf_op jit(solution)/shard_map/expert_slopes/pallas_call | solution.py:170
  210.8 2.8 collective-permute-start.23
  216.2 40.0 %collective-permute-done.22 = bf16[128,1536]{1,0:T(8,128)(2,1)} collective-permute-done((bf16[128,1536]{1,0:T(8,128)(2,1)}, bf16[128,1536]{1,0:T(8,128)(2,1)}, u32[]{:S(2)}, u32[]{:S(2)}) %collective-permute-start.22) | collective-permute-done | bytes 393248 | tf_op jit(solution)/shard_map/ppermute | solution.py:46
  256.6 8.5 %all-to-all-start.3 = ((bf16[32,48,1536]{2,1,0:T(8,128)(2,1)}), bf16[32,48,1536]{2,1,0:T(8,128)(2,1)}, u32[]{:S(2)}, u32[]{:S(2)}) async-start(bf16[32,48,1536]{2,1,0:T(8,128)(2,1)} %bitcast.60), calls=%async_computation.3 | async-start | bytes 9437184 | tf_op jit(solution)/shard_map/all_to_all | solution.py:764
  265.1 6.5 %leave.1 = (f32[128,1536]{1,0:T(8,128)}, bf16[128,1536]{1,0:T(8,128)(2,1)}, f32[128,1536]{1,0:T(8,128)}, f32[128,128]{1,0:T(8,128)}) custom-call(bf16[1536,1664]{1,0:T(8,128)(2,1)} %bitcast.18.back_ref, bf16[128,1536]{1,0:T(8,128)(2,1)} %get-tuple-element.206.slot_ref, f32[128,128]{1,0:T(8,128)} %get-tuple-element.143.gates_ref, ...), custom_call_target="tpu_custom_call" | custom-call | flops 603979776 | bytes 7077888 | tf_op jit(solution)/shard_map/leave/pallas_call | solution.py:527
  271.6 2.3 collective-permute-start.26
  274.7 3.2 small_slopes.1.refs_19_
  277.9 5.1 %collective-permute-done.26.refs_1_ = bf16[128,1536]{1,0:T(8,128)(2,1)S(1)} collective-permute-done((bf16[128,1536]{1,0:T(8,128)(2,1)}, bf16[128,1536]{1,0:T(8,128)(2,1)S(1)}, u32[]{:S(2)}, u32[]{:S(2)}) %collective-permute-start.26) | collective-permute-done | bytes 393248 | tf_op jit(solution)/shard_map/ppermute | solution.py:42
  283.0 2.9 collective-permute-done.27.refs_2_
  285.9 9.1 %collective-permute-done.28.refs_3_ = bf16[128,1536]{1,0:T(8,128)(2,1)S(1)} collective-permute-done((bf16[128,1536]{1,0:T(8,128)(2,1)}, bf16[128,1536]{1,0:T(8,128)(2,1)S(1)}, u32[]{:S(2)}, u32[]{:S(2)}) %collective-permute-start.28) | collective-permute-done | bytes 393248 | tf_op jit(solution)/shard_map/ppermute | solution.py:42
  295.7 18.9 %attend_back.1 = (f32[16,6,24,384]{3,2,1,0:T(8,128)}, bf16[16,6,24,384]{3,2,1,0:T(8,128)(2,1)}, f32[128,1536]{1,0:T(8,128)}, bf16[128,1536]{1,0:T(8,128)(2,1)}, ...) custom-call(s32[2]{0:T(128)} %pad_add_fusion.place_ref, bf16[128,1536]{1,0:T(8,128)(2,1)} %get-tuple-element.145.refs_0_, ...), custom_call_target="tpu_custom_call" | custom-call | flops 4227858432 | bytes 11534336 | tf_op jit(solution)/shard_map/attend_back/pallas_call | solution.py:269
  316.2 2.7 collective-permute-done.29
  318.9 3.6 add_convert_fusion
  323.5 6.7 %all-to-all-start.4 = ((bf16[16,6,24,384]{3,2,1,0:T(8,128)(2,1)}), bf16[16,6,24,384]{3,2,1,0:T(8,128)(2,1)S(1)}, u32[]{:S(2)}, u32[]{:S(2)}) async-start(bf16[16,6,24,384]{3,2,1,0:T(8,128)(2,1)} %add_convert_fusion), calls=%async_computation.4 | async-start | bytes 3538944 | tf_op jit(solution)/shard_map/all_to_all | solution.py:55
  330.2 2.4 collective-permute-start.32
  336.4 2.3 collective-permute-start.33
  338.8 3.7 fusion.58
  343.6 10.7 %collective-permute-done.30 = bf16[128,1536]{1,0:T(8,128)(2,1)S(1)} collective-permute-done((bf16[128,1536]{1,0:T(8,128)(2,1)}, bf16[128,1536]{1,0:T(8,128)(2,1)S(1)}, u32[]{:S(2)}, u32[]{:S(2)}) %collective-permute-start.30) | collective-permute-done | bytes 393248 | tf_op jit(solution)/shard_map/ppermute | solution.py:46
  354.7 5.8 %collective-permute-done.33 = bf16[128,1536]{1,0:T(8,128)(2,1)S(1)} collective-permute-done((bf16[128,1536]{1,0:T(8,128)(2,1)S(1)}, bf16[128,1536]{1,0:T(8,128)(2,1)S(1)}, u32[]{:S(2)}, u32[]{:S(2)}) %collective-permute-start.33) | collective-permute-done | bytes 393248 | tf_op jit(solution)/shard_map/ppermute | solution.py:46
  369.4 25.9 %all_to_all.30.a_ref.ao_ref = bf16[16,6,24,384]{3,2,1,0:T(8,128)(2,1)S(1)} all-to-all(bf16[16,6,24,384]{3,2,1,0:T(8,128)(2,1)S(1)} %broadcast_in_dim.84), channel_id=1, replica_groups={{0,8,16,24,32,40,48,56,64,72,80,88,96,104,112,120},{4,12,20,28,36,44,52..., dimensions={0} | all-to-all | bytes 3538944 | tf_op jit(solution)/shard_map/all_to_all | solution.py:55
  395.3 5.8 %collective-permute-start.37 = (bf16[16,6,24,384]{3,2,1,0:T(8,128)(2,1)S(1)}, bf16[16,6,24,384]{3,2,1,0:T(8,128)(2,1)S(1)}, u32[]{:S(2)}, u32[]{:S(2)}) collective-permute-start(bf16[16,6,24,384]{3,2,1,0:T(8,128)(2,1)S(1)} %all_to_all.30.a_ref.ao_ref), channel_id=1, source_target_pairs={{0,4},{4,0},{8,12},{12,8},{16,20},{20,16},{24,28},{28,24},{32,36},... | collective-permute-start | bytes 5308424 | tf_op jit(solution)/shard_map/ppermute | solution.py:50
  401.2 3.2 collective-permute-done.37.b_ref.bo_ref
  405.7 6.4 %finish.1 = (f32[384,1536]{1,0:T(8,128)}, f32[384,512]{1,0:T(8,128)}, f32[384,512]{1,0:T(8,128)}, f32[32,384]{1,0:T(8,128)}, f32[8,384]{1,0:T(8,128)}, /*index=5*/f32[384,1536]{1,0:T(8,128)}) custom-call(s32[2]{0:T(128)} %pad_add_fusion.place_ref, bf16[16,6,24,384]{3,2,1,0:T(8,128)(2,1)} %copy-done, bf16[16,6,24,384]{3,2,1,0:T(8,128)(2,1)} %copy-done.1, ...), custom_call_target="tpu_custom_call" | custom-call | bytes 9437184 | tf_op jit(solution)/shard_map/finish/pallas_call | solution.py:229
  (190 shorter events, 59.4 us)
Async XLA Ops:
  0.7 16.7 %collective-permute-start = (bf16[128,1536]{1,0:T(8,128)(2,1)}, bf16[128,1536]{1,0:T(8,128)(2,1)S(1)}, u32[]{:S(2)}, u32[]{:S(2)}) collective-permute-start(bf16[128,1536]{1,0:T(8,128)(2,1)} %refs_4_.1), channel_id=1, source_target_pairs={{0,3},{1,0},{2,1},{3,2},{4,7},{5,4},{6,5},{7,6},{8,11},{9,8},{10,9... | collective-permute-start | bytes 1179656 | tf_op jit(solution)/shard_map/ppermute | solution.py:42
  4.3 13.0 %collective-permute-start.1 = (bf16[128,1536]{1,0:T(8,128)(2,1)}, bf16[128,1536]{1,0:T(8,128)(2,1)S(1)}, u32[]{:S(2)}, u32[]{:S(2)}) collective-permute-start(bf16[128,1536]{1,0:T(8,128)(2,1)} %refs_4_.1), channel_id=1, source_target_pairs={{0,1},{1,2},{2,3},{3,0},{4,5},{5,6},{6,7},{7,4},{8,9},{9,10},{10,1... | collective-permute-start | bytes 1179656 | tf_op jit(solution)/shard_map/ppermute | solution.py:42
  18.2 77.5 %all-to-all-start.1 = ((bf16[32,48,1664]{2,1,0:T(8,128)(2,1)}), bf16[32,48,1664]{2,1,0:T(8,128)(2,1)}, u32[]{:S(2)}, u32[]{:S(2)}) async-start(bf16[32,48,1664]{2,1,0:T(8,128)(2,1)} %bitcast.58), calls=%async_computation.1 | async-start | bytes 10223616 | tf_op jit(solution)/shard_map/all_to_all | solution.py:713
  27.2 29.4 %collective-permute-start.2 = (bf16[128,1536]{1,0:T(8,128)(2,1)S(1)}, bf16[128,1536]{1,0:T(8,128)(2,1)S(1)}, u32[]{:S(2)}, u32[]{:S(2)}) collective-permute-start(bf16[128,1536]{1,0:T(8,128)(2,1)S(1)} %copy-done.3), channel_id=1, source_target_pairs={{0,2},{1,3},{2,0},{3,1},{4,6},{5,7},{6,4},{7,5},{8,10},{9,11},{10,... | collective-permute-start | bytes 1179656 | tf_op jit(solution)/shard_map/ppermute | solution.py:42
  29.2 17.0 %collective-permute-start.3 = (bf16[192,768]{1,0:T(8,128)(2,1)S(1)}, bf16[192,768]{1,0:T(8,128)(2,1)S(1)}, u32[]{:S(2)}, u32[]{:S(2)}) collective-permute-start(bf16[192,768]{1,0:T(8,128)(2,1)S(1)} %copy-done.40), channel_id=1, source_target_pairs={{0,3},{1,0},{2,1},{3,2},{4,7},{5,4},{6,5},{7,6},{8,11},{9,8},{10,9... | collective-permute-start | bytes 884744 | tf_op jit(solution)/shard_map/ppermute | solution.py:42
  30.3 17.6 %collective-permute-start.4 = (bf16[192,768]{1,0:T(8,128)(2,1)S(1)}, bf16[192,768]{1,0:T(8,128)(2,1)S(1)}, u32[]{:S(2)}, u32[]{:S(2)}) collective-permute-start(bf16[192,768]{1,0:T(8,128)(2,1)S(1)} %copy-done.39), channel_id=1, source_target_pairs={{0,2},{1,3},{2,0},{3,1},{4,6},{5,7},{6,4},{7,5},{8,10},{9,11},{10,... | collective-permute-start | bytes 884744 | tf_op jit(solution)/shard_map/ppermute | solution.py:42
  32.6 20.0 %collective-permute-start.5 = (bf16[192,768]{1,0:T(8,128)(2,1)S(1)}, bf16[192,768]{1,0:T(8,128)(2,1)S(1)}, u32[]{:S(2)}, u32[]{:S(2)}) collective-permute-start(bf16[192,768]{1,0:T(8,128)(2,1)S(1)} %copy-done.38), channel_id=1, source_target_pairs={{0,1},{1,2},{2,3},{3,0},{4,5},{5,6},{6,7},{7,4},{8,9},{9,10},{10,1... | collective-permute-start | bytes 884744 | tf_op jit(solution)/shard_map/ppermute | solution.py:42
  46.2 10.4 %collective-permute-start.6 = (bf16[192,768]{1,0:T(8,128)(2,1)S(1)}, bf16[192,768]{1,0:T(8,128)(2,1)S(1)}, u32[]{:S(2)}, u32[]{:S(2)}) collective-permute-start(bf16[192,768]{1,0:T(8,128)(2,1)S(1)} %collective-permute-done.3.refs_5_), channel_id=1, source_target_pairs={{0,4},{4,0},{8,12},{12,8},{16,20},{20,16},{24,28},{28,24},{32,36},... | collective-permute-start | bytes 884744 | tf_op jit(solution)/shard_map/ppermute | solution.py:50
  47.9 8.7 %collective-permute-start.7 = (bf16[192,768]{1,0:T(8,128)(2,1)S(1)}, bf16[192,768]{1,0:T(8,128)(2,1)S(1)}, u32[]{:S(2)}, u32[]{:S(2)}) collective-permute-start(bf16[192,768]{1,0:T(8,128)(2,1)S(1)} %collective-permute-done.4.refs_6_), channel_id=1, source_target_pairs={{0,4},{4,0},{8,12},{12,8},{16,20},{20,16},{24,28},{28,24},{32,36},... | collective-permute-start | bytes 884744 | tf_op jit(solution)/shard_map/ppermute | solution.py:50
  52.5 4.1 collective-permute-start.8
  67.3 12.6 %collective-permute-start.9 = (bf16[128,1536]{1,0:T(8,128)(2,1)}, bf16[128,1536]{1,0:T(8,128)(2,1)S(1)}, u32[]{:S(2)}, u32[]{:S(2)}) collective-permute-start(bf16[128,1536]{1,0:T(8,128)(2,1)} %get-tuple-element.117), channel_id=1, source_target_pairs={{0,1},{1,2},{2,3},{3,0},{4,5},{5,6},{6,7},{7,4},{8,9},{9,10},{10,1... | collective-permute-start | bytes 1179656 | tf_op jit(solution)/shard_map/ppermute | solution.py:46
  68.1 21.1 %collective-permute-start.10 = (bf16[128,1536]{1,0:T(8,128)(2,1)}, bf16[128,1536]{1,0:T(8,128)(2,1)S(1)}, u32[]{:S(2)}, u32[]{:S(2)}) collective-permute-start(bf16[128,1536]{1,0:T(8,128)(2,1)} %get-tuple-element.118), channel_id=1, source_target_pairs={{0,2},{1,3},{2,0},{3,1},{4,6},{5,7},{6,4},{7,5},{8,10},{9,11},{10,... | collective-permute-start | bytes 1179656 | tf_op jit(solution)/shard_map/ppermute | solution.py:46
  71.7 17.6 %collective-permute-start.11 = (bf16[128,1536]{1,0:T(8,128)(2,1)}, bf16[128,1536]{1,0:T(8,128)(2,1)S(1)}, u32[]{:S(2)}, u32[]{:S(2)}) collective-permute-start(bf16[128,1536]{1,0:T(8,128)(2,1)} %get-tuple-element.119), channel_id=1, source_target_pairs={{0,3},{1,0},{2,1},{3,2},{4,7},{5,4},{6,5},{7,6},{8,11},{9,8},{10,9... | collective-permute-start | bytes 1179656 | tf_op jit(solution)/shard_map/ppermute | solution.py:46
  95.7 22.0 %copy-start.20 = (bf16[1,128,1536]{2,1,0:T(8,128)(2,1)S(1)}, bf16[1,128,1536]{2,1,0:T(8,128)(2,1)}, u32[]{:S(2)}) copy-start(bf16[1,128,1536]{2,1,0:T(8,128)(2,1)} %param.29) | copy-start | bytes 1179652
  95.7 66.8 %all-to-all-start = ((bf16[32,48,1536]{2,1,0:T(8,128)(2,1)}), bf16[32,48,1536]{2,1,0:T(8,128)(2,1)}, u32[]{:S(2)}, u32[]{:S(2)}) async-start(bf16[32,48,1536]{2,1,0:T(8,128)(2,1)} %bitcast.61), calls=%async_computation | async-start | bytes 9437184 | tf_op jit(solution)/shard_map/all_to_all | solution.py:733
  104.1 10.6 %collective-permute-start.12 = (bf16[1536,128]{1,0:T(8,128)(2,1)S(1)}, bf16[1536,128]{1,0:T(8,128)(2,1)S(1)}, u32[]{:S(2)}, u32[]{:S(2)}) collective-permute-start(bf16[1536,128]{1,0:T(8,128)(2,1)S(1)} %bitcast.68), channel_id=1, source_target_pairs={{0,3},{1,0},{2,1},{3,2},{4,7},{5,4},{6,5},{7,6},{8,11},{9,8},{10,9... | collective-permute-start | bytes 1179656 | tf_op jit(solution)/shard_map/ppermute | solution.py:42
  105.9 11.8 %collective-permute-start.13 = (bf16[1536,128]{1,0:T(8,128)(2,1)S(1)}, bf16[1536,128]{1,0:T(8,128)(2,1)S(1)}, u32[]{:S(2)}, u32[]{:S(2)}) collective-permute-start(bf16[1536,128]{1,0:T(8,128)(2,1)S(1)} %bitcast.69), channel_id=1, source_target_pairs={{0,2},{1,3},{2,0},{3,1},{4,6},{5,7},{6,4},{7,5},{8,10},{9,11},{10,... | collective-permute-start | bytes 1179656 | tf_op jit(solution)/shard_map/ppermute | solution.py:42
  106.1 21.3 %collective-permute-start.14 = (bf16[1536,128]{1,0:T(8,128)(2,1)S(1)}, bf16[1536,128]{1,0:T(8,128)(2,1)S(1)}, u32[]{:S(2)}, u32[]{:S(2)}) collective-permute-start(bf16[1536,128]{1,0:T(8,128)(2,1)S(1)} %bitcast.70), channel_id=1, source_target_pairs={{0,1},{1,2},{2,3},{3,0},{4,5},{5,6},{6,7},{7,4},{8,9},{9,10},{10,1... | collective-permute-start | bytes 1179656 | tf_op jit(solution)/shard_map/ppermute | solution.py:42
  106.6 25.0 %collective-permute-start.15 = (bf16[1536,128]{1,0:T(8,128)(2,1)S(1)}, bf16[1536,128]{1,0:T(8,128)(2,1)S(1)}, u32[]{:S(2)}, u32[]{:S(2)}) collective-permute-start(bf16[1536,128]{1,0:T(8,128)(2,1)S(1)} %bitcast.72), channel_id=1, source_target_pairs={{0,3},{1,0},{2,1},{3,2},{4,7},{5,4},{6,5},{7,6},{8,11},{9,8},{10,9... | collective-permute-start | bytes 1179656 | tf_op jit(solution)/shard_map/ppermute | solution.py:42
  108.8 25.8 %collective-permute-start.16 = (bf16[1536,128]{1,0:T(8,128)(2,1)S(1)}, bf16[1536,128]{1,0:T(8,128)(2,1)}, u32[]{:S(2)}, u32[]{:S(2)}) collective-permute-start(bf16[1536,128]{1,0:T(8,128)(2,1)S(1)} %bitcast.73), channel_id=1, source_target_pairs={{0,2},{1,3},{2,0},{3,1},{4,6},{5,7},{6,4},{7,5},{8,10},{9,11},{10,... | collective-permute-start | bytes 1179656 | tf_op jit(solution)/shard_map/ppermute | solution.py:42
  114.7 47.8 %copy-start.26 = (bf16[1536,128]{1,0:T(8,128)(2,1)}, bf16[1536,128]{1,0:T(8,128)(2,1)S(1)}, u32[]{:S(2)}) copy-start(bf16[1536,128]{1,0:T(8,128)(2,1)S(1)} %collective-permute-done.12.rest_1_) | copy-start | bytes 1179652
  114.7 29.2 %collective-permute-start.17 = (bf16[1536,128]{1,0:T(8,128)(2,1)S(1)}, bf16[1536,128]{1,0:T(8,128)(2,1)}, u32[]{:S(2)}, u32[]{:S(2)}) collective-permute-start(bf16[1536,128]{1,0:T(8,128)(2,1)S(1)} %bitcast.74), channel_id=1, source_target_pairs={{0,1},{1,2},{2,3},{3,0},{4,5},{5,6},{6,7},{7,4},{8,9},{9,10},{10,1... | collective-permute-start | bytes 1179656 | tf_op jit(solution)/shard_map/ppermute | solution.py:42
  117.7 44.8 %copy-start.28 = (bf16[1536,128]{1,0:T(8,128)(2,1)}, bf16[1536,128]{1,0:T(8,128)(2,1)S(1)}, u32[]{:S(2)}) copy-start(bf16[1536,128]{1,0:T(8,128)(2,1)S(1)} %collective-permute-done.13.rest_2_) | copy-start | bytes 1179652
  117.7 30.8 %collective-permute-start.18 = (bf16[128,1536]{1,0:T(8,128)(2,1)S(1)}, bf16[128,1536]{1,0:T(8,128)(2,1)S(1)}, u32[]{:S(2)}, u32[]{:S(2)}) collective-permute-start(bf16[128,1536]{1,0:T(8,128)(2,1)S(1)} %bitcast.77), channel_id=1, source_target_pairs={{0,3},{1,0},{2,1},{3,2},{4,7},{5,4},{6,5},{7,6},{8,11},{9,8},{10,9... | collective-permute-start | bytes 1179656 | tf_op jit(solution)/shard_map/ppermute | solution.py:42
  127.3 35.2 %copy-start.29 = (bf16[1536,128]{1,0:T(8,128)(2,1)}, bf16[1536,128]{1,0:T(8,128)(2,1)S(1)}, u32[]{:S(2)}) copy-start(bf16[1536,128]{1,0:T(8,128)(2,1)S(1)} %collective-permute-done.14.rest_3_) | copy-start | bytes 1179652
  127.3 24.2 %collective-permute-start.19 = (bf16[128,1536]{1,0:T(8,128)(2,1)S(1)}, bf16[128,1536]{1,0:T(8,128)(2,1)S(1)}, u32[]{:S(2)}, u32[]{:S(2)}) collective-permute-start(bf16[128,1536]{1,0:T(8,128)(2,1)S(1)} %bitcast.78), channel_id=1, source_target_pairs={{0,2},{1,3},{2,0},{3,1},{4,6},{5,7},{6,4},{7,5},{8,10},{9,11},{10,... | collective-permute-start | bytes 1179656 | tf_op jit(solution)/shard_map/ppermute | solution.py:42
  132.3 28.0 %collective-permute-start.20 = (bf16[128,1536]{1,0:T(8,128)(2,1)S(1)}, bf16[128,1536]{1,0:T(8,128)(2,1)S(1)}, u32[]{:S(2)}, u32[]{:S(2)}) collective-permute-start(bf16[128,1536]{1,0:T(8,128)(2,1)S(1)} %bitcast.79), channel_id=1, source_target_pairs={{0,1},{1,2},{2,3},{3,0},{4,5},{5,6},{6,7},{7,4},{8,9},{9,10},{10,1... | collective-permute-start | bytes 1179656 | tf_op jit(solution)/shard_map/ppermute | solution.py:42
  183.3 73.3 %all-to-all-start.2 = ((bf16[32,48,1664]{2,1,0:T(8,128)(2,1)}), bf16[32,48,1664]{2,1,0:T(8,128)(2,1)}, u32[]{:S(2)}, u32[]{:S(2)}) async-start(bf16[32,48,1664]{2,1,0:T(8,128)(2,1)} %bitcast.59), calls=%async_computation.2 | async-start | bytes 10223616 | tf_op jit(solution)/shard_map/all_to_all | solution.py:751
  210.5 46.1 %collective-permute-start.21 = (bf16[2,1536,128]{2,1,0:T(8,128)(2,1)}, bf16[2,1536,128]{2,1,0:T(8,128)(2,1)}, u32[]{:S(2)}, u32[]{:S(2)}) collective-permute-start(bf16[2,1536,128]{2,1,0:T(8,128)(2,1)} %get-tuple-element.137), channel_id=1, source_target_pairs={{0,1},{1,2},{2,3},{3,0},{4,5},{5,6},{6,7},{7,4},{8,9},{9,10},{10,1... | collective-permute-start | bytes 2359304 | tf_op jit(solution)/shard_map/ppermute | solution.py:46
  210.8 45.9 %collective-permute-start.23 = (bf16[2,1536,128]{2,1,0:T(8,128)(2,1)}, bf16[2,1536,128]{2,1,0:T(8,128)(2,1)}, u32[]{:S(2)}, u32[]{:S(2)}) collective-permute-start(bf16[2,1536,128]{2,1,0:T(8,128)(2,1)} %get-tuple-element.139), channel_id=1, source_target_pairs={{0,2},{1,3},{2,0},{3,1},{4,6},{5,7},{6,4},{7,5},{8,10},{9,11},{10,... | collective-permute-start | bytes 2359304 | tf_op jit(solution)/shard_map/ppermute | solution.py:46
  213.6 43.1 %collective-permute-start.24 = (bf16[2,1536,128]{2,1,0:T(8,128)(2,1)}, bf16[2,1536,128]{2,1,0:T(8,128)(2,1)}, u32[]{:S(2)}, u32[]{:S(2)}) collective-permute-start(bf16[2,1536,128]{2,1,0:T(8,128)(2,1)} %get-tuple-element.140), channel_id=1, source_target_pairs={{0,3},{1,0},{2,1},{3,2},{4,7},{5,4},{6,5},{7,6},{8,11},{9,8},{10,9... | collective-permute-start | bytes 2359304 | tf_op jit(solution)/shard_map/ppermute | solution.py:46
  213.6 42.7 %collective-permute-start.22 = (bf16[128,1536]{1,0:T(8,128)(2,1)}, bf16[128,1536]{1,0:T(8,128)(2,1)}, u32[]{:S(2)}, u32[]{:S(2)}) collective-permute-start(bf16[128,1536]{1,0:T(8,128)(2,1)} %get-tuple-element.138), channel_id=1, source_target_pairs={{0,1},{1,2},{2,3},{3,0},{4,5},{5,6},{6,7},{7,4},{8,9},{9,10},{10,1... | collective-permute-start | bytes 1179656 | tf_op jit(solution)/shard_map/ppermute | solution.py:46
  215.0 41.6 %collective-permute-start.25 = (bf16[128,1536]{1,0:T(8,128)(2,1)}, bf16[128,1536]{1,0:T(8,128)(2,1)}, u32[]{:S(2)}, u32[]{:S(2)}) collective-permute-start(bf16[128,1536]{1,0:T(8,128)(2,1)} %get-tuple-element.141), channel_id=1, source_target_pairs={{0,3},{1,0},{2,1},{3,2},{4,7},{5,4},{6,5},{7,6},{8,11},{9,8},{10,9... | collective-permute-start | bytes 1179656 | tf_op jit(solution)/shard_map/ppermute | solution.py:46
  256.6 66.9 %all-to-all-start.3 = ((bf16[32,48,1536]{2,1,0:T(8,128)(2,1)}), bf16[32,48,1536]{2,1,0:T(8,128)(2,1)}, u32[]{:S(2)}, u32[]{:S(2)}) async-start(bf16[32,48,1536]{2,1,0:T(8,128)(2,1)} %bitcast.60), calls=%async_computation.3 | async-start | bytes 9437184 | tf_op jit(solution)/shard_map/all_to_all | solution.py:764
  271.6 11.4 %collective-permute-start.26 = (bf16[128,1536]{1,0:T(8,128)(2,1)}, bf16[128,1536]{1,0:T(8,128)(2,1)S(1)}, u32[]{:S(2)}, u32[]{:S(2)}) collective-permute-start(bf16[128,1536]{1,0:T(8,128)(2,1)} %get-tuple-element.145.refs_0_), channel_id=1, source_target_pairs={{0,3},{1,0},{2,1},{3,2},{4,7},{5,4},{6,5},{7,6},{8,11},{9,8},{10,9... | collective-permute-start | bytes 1179656 | tf_op jit(solution)/shard_map/ppermute | solution.py:42
  273.9 12.0 %collective-permute-start.27 = (bf16[128,1536]{1,0:T(8,128)(2,1)}, bf16[128,1536]{1,0:T(8,128)(2,1)S(1)}, u32[]{:S(2)}, u32[]{:S(2)}) collective-permute-start(bf16[128,1536]{1,0:T(8,128)(2,1)} %get-tuple-element.145.refs_0_), channel_id=1, source_target_pairs={{0,2},{1,3},{2,0},{3,1},{4,6},{5,7},{6,4},{7,5},{8,10},{9,11},{10,... | collective-permute-start | bytes 1179656 | tf_op jit(solution)/shard_map/ppermute | solution.py:42
  273.9 21.1 %collective-permute-start.28 = (bf16[128,1536]{1,0:T(8,128)(2,1)}, bf16[128,1536]{1,0:T(8,128)(2,1)S(1)}, u32[]{:S(2)}, u32[]{:S(2)}) collective-permute-start(bf16[128,1536]{1,0:T(8,128)(2,1)} %get-tuple-element.145.refs_0_), channel_id=1, source_target_pairs={{0,1},{1,2},{2,3},{3,0},{4,5},{5,6},{6,7},{7,4},{8,9},{9,10},{10,1... | collective-permute-start | bytes 1179656 | tf_op jit(solution)/shard_map/ppermute | solution.py:42
  314.6 4.4 %collective-permute-start.29 = (bf16[16,6,24,384]{3,2,1,0:T(8,128)(2,1)}, bf16[16,6,24,384]{3,2,1,0:T(8,128)(2,1)S(1)}, u32[]{:S(2)}, u32[]{:S(2)}) collective-permute-start(bf16[16,6,24,384]{3,2,1,0:T(8,128)(2,1)} %get-tuple-element.155), channel_id=1, source_target_pairs={{0,4},{4,0},{8,12},{12,8},{16,20},{20,16},{24,28},{28,24},{32,36},... | collective-permute-start | bytes 5308424 | tf_op jit(solution)/shard_map/ppermute | solution.py:50
  323.5 40.4 %all-to-all-start.4 = ((bf16[16,6,24,384]{3,2,1,0:T(8,128)(2,1)}), bf16[16,6,24,384]{3,2,1,0:T(8,128)(2,1)S(1)}, u32[]{:S(2)}, u32[]{:S(2)}) async-start(bf16[16,6,24,384]{3,2,1,0:T(8,128)(2,1)} %add_convert_fusion), calls=%async_computation.4 | async-start | bytes 3538944 | tf_op jit(solution)/shard_map/all_to_all | solution.py:55
  330.2 13.2 %collective-permute-start.32 = (bf16[128,1536]{1,0:T(8,128)(2,1)}, bf16[128,1536]{1,0:T(8,128)(2,1)S(1)}, u32[]{:S(2)}, u32[]{:S(2)}) collective-permute-start(bf16[128,1536]{1,0:T(8,128)(2,1)} %get-tuple-element.170), channel_id=1, source_target_pairs={{0,3},{1,0},{2,1},{3,2},{4,7},{5,4},{6,5},{7,6},{8,11},{9,8},{10,9... | collective-permute-start | bytes 1179656 | tf_op jit(solution)/shard_map/ppermute | solution.py:46
  332.6 11.0 %collective-permute-start.31 = (bf16[128,1536]{1,0:T(8,128)(2,1)}, bf16[128,1536]{1,0:T(8,128)(2,1)S(1)}, u32[]{:S(2)}, u32[]{:S(2)}) collective-permute-start(bf16[128,1536]{1,0:T(8,128)(2,1)} %get-tuple-element.169), channel_id=1, source_target_pairs={{0,2},{1,3},{2,0},{3,1},{4,6},{5,7},{6,4},{7,5},{8,10},{9,11},{10,... | collective-permute-start | bytes 1179656 | tf_op jit(solution)/shard_map/ppermute | solution.py:46
  332.6 21.6 %collective-permute-start.30 = (bf16[128,1536]{1,0:T(8,128)(2,1)}, bf16[128,1536]{1,0:T(8,128)(2,1)S(1)}, u32[]{:S(2)}, u32[]{:S(2)}) collective-permute-start(bf16[128,1536]{1,0:T(8,128)(2,1)} %get-tuple-element.168), channel_id=1, source_target_pairs={{0,1},{1,2},{2,3},{3,0},{4,5},{5,6},{6,7},{7,4},{8,9},{9,10},{10,1... | collective-permute-start | bytes 1179656 | tf_op jit(solution)/shard_map/ppermute | solution.py:46
  336.4 24.0 %collective-permute-start.33 = (bf16[128,1536]{1,0:T(8,128)(2,1)S(1)}, bf16[128,1536]{1,0:T(8,128)(2,1)S(1)}, u32[]{:S(2)}, u32[]{:S(2)}) collective-permute-start(bf16[128,1536]{1,0:T(8,128)(2,1)S(1)} %copy-done.24), channel_id=1, source_target_pairs={{0,2},{1,3},{2,0},{3,1},{4,6},{5,7},{6,4},{7,5},{8,10},{9,11},{10,... | collective-permute-start | bytes 1179656 | tf_op jit(solution)/shard_map/ppermute | solution.py:46
  343.4 17.0 %copy-start.7 = (f32[128,1536]{1,0:T(8,128)S(1)}, f32[128,1536]{1,0:T(8,128)}, u32[]{:S(2)}) copy-start(f32[128,1536]{1,0:T(8,128)} %get-tuple-element.176) | copy-start | bytes 2359300
  364.2 2.7 collective-permute-start.34
  364.3 4.2 %collective-permute-start.35 = (bf16[24,384]{1,0:T(8,128)(2,1)S(1)}, bf16[24,384]{1,0:T(8,128)(2,1)S(1)}, u32[]{:S(2)}, u32[]{:S(2)}) collective-permute-start(bf16[24,384]{1,0:T(8,128)(2,1)S(1)} %get-tuple-element.199), channel_id=1, source_target_pairs={{0,2},{1,3},{2,0},{3,1},{4,6},{5,7},{6,4},{7,5},{8,10},{9,11},{10,... | collective-permute-start | bytes 55304 | tf_op jit(solution)/shard_map/ppermute | solution.py:42
  364.6 4.7 %collective-permute-start.36 = (bf16[24,384]{1,0:T(8,128)(2,1)S(1)}, bf16[24,384]{1,0:T(8,128)(2,1)S(1)}, u32[]{:S(2)}, u32[]{:S(2)}) collective-permute-start(bf16[24,384]{1,0:T(8,128)(2,1)S(1)} %get-tuple-element.198), channel_id=1, source_target_pairs={{0,1},{1,2},{2,3},{3,0},{4,5},{5,6},{6,7},{7,4},{8,9},{9,10},{10,1... | collective-permute-start | bytes 55304 | tf_op jit(solution)/shard_map/ppermute | solution.py:42
  395.3 9.1 %collective-permute-start.37 = (bf16[16,6,24,384]{3,2,1,0:T(8,128)(2,1)S(1)}, bf16[16,6,24,384]{3,2,1,0:T(8,128)(2,1)S(1)}, u32[]{:S(2)}, u32[]{:S(2)}) collective-permute-start(bf16[16,6,24,384]{3,2,1,0:T(8,128)(2,1)S(1)} %all_to_all.30.a_ref.ao_ref), channel_id=1, source_target_pairs={{0,4},{4,0},{8,12},{12,8},{16,20},{20,16},{24,28},{28,24},{32,36},... | collective-permute-start | bytes 5308424 | tf_op jit(solution)/shard_map/ppermute | solution.py:50
  (40 other events, 282.8 us)

commit v5 on v4

--- a/solution.py
+++ b/solution.py
@@ -138,63 +138,82 @@
     )(x, dy, sel, wr, *wg, *wu, *wd)
 
 
-def slope_body(x_ref, dgu_ref, h_ref, dy_ref, gate_ref, *refs):
+def in_slope_body(x_ref, dgu_ref, own_g, own_u, *peers):
+    part = own_g.shape[1]
+    ff = WS * part
+    gu = tdot(x_ref[...], dgu_ref[...])
+    own_g[...] = gu[:, :part]
+    own_u[...] = gu[:, ff : ff + part]
+    for k in (1, 2, 3):
+        peers[k - 1][0] = gu[:, k * part : (k + 1) * part].astype(BF)
+        peers[k - 1][1] = gu[:, ff + k * part : ff + (k + 1) * part].astype(BF)
+
+
+def in_slopes(x, dgu, tile=256):
+    slots, width = x.shape
+    part = dgu.shape[1] // (2 * WS)
+    tall = pl.BlockSpec((tile, part), lambda i: (i, 0))
+    pair = pl.BlockSpec((2, tile, part), lambda i: (0, i, 0))
+    return pl.pallas_call(
+        in_slope_body,
+        grid=(width // tile,),
+        in_specs=[pl.BlockSpec((slots, tile), lambda i: (0, i)), whole(dgu.shape)],
+        out_specs=[tall, tall] + [pair] * 3,
+        out_shape=[sds((width, part), F32)] * 2 + [sds((2, width, part), BF)] * 3,
+        compiler_params=pltpu.CompilerParams(vmem_limit_bytes=VM),
+        cost_estimate=pl.CostEstimate(
+            flops=2 * slots * width * dgu.shape[1],
+            bytes_accessed=4 * slots * width,
+            transcendentals=0,
+        ),
+        name="in_slopes",
+    )(x, dgu)
+
+
+def out_slope_body(h_ref, dy_ref, gate_ref, *refs):
     wd = refs[0:4]
-    y_ref, own_g, own_u, own_d = refs[4:8]
-    peers = refs[8:]
-    part = own_g.shape[1]
-    ff = h_ref.shape[1]
-    gu = tdot(x_ref[...], dgu_ref[...])
+    y_ref, own_d = refs[4:6]
+    part = own_d.shape[0]
     d_y = (gate_ref[:, 0:1] * dy_ref[...].astype(F32)).astype(BF)
     dn = tdot(h_ref[...], d_y)
-    y_ref[...] = dot(h_ref[...], jnp.concatenate([w[...] for w in wd], axis=0)).astype(BF)
-    own_g[...] = gu[:, :part]
-    own_u[...] = gu[:, ff : ff + part]
     own_d[...] = dn[:part]
     for k in (1, 2, 3):
-        peers[2 * k - 2][0] = gu[:, k * part : (k + 1) * part].astype(BF)
-        peers[2 * k - 2][1] = gu[:, ff + k * part : ff + (k + 1) * part].astype(BF)
-        peers[2 * k - 1][...] = dn[k * part : (k + 1) * part].astype(BF)
-
-
-def expert_slopes(x, dgu, h, dy, gate, wd, tile=256):
-    slots, width = x.shape
-    ff = h.shape[1]
+        refs[5 + k][...] = dn[k * part : (k + 1) * part].astype(BF)
+    y_ref[...] = dot(h_ref[...], jnp.concatenate([w[...] for w in wd], axis=0)).astype(BF)
+
+
+def out_slopes(h, dy, gate, wd, tile=256):
+    slots, ff = h.shape
+    width = wd[0].shape[1]
     part = ff // WS
     col = pl.BlockSpec((slots, tile), lambda i: (0, i))
-    once = lambda a: pl.BlockSpec(a.shape, lambda i: (0, 0))
-    tall = pl.BlockSpec((tile, part), lambda i: (i, 0))
     flat = pl.BlockSpec((part, tile), lambda i: (0, i))
-    pair = pl.BlockSpec((2, tile, part), lambda i: (0, i, 0))
-    S = jax.ShapeDtypeStruct
     return pl.pallas_call(
-        slope_body,
+        out_slope_body,
         grid=(width // tile,),
-        in_specs=[col, once(dgu), once(h), col, once(gate)] + [flat] * WS,
-        out_specs=[col, tall, tall, flat] + [pair, flat] * 3,
-        out_shape=[S((slots, width), BF)]
-        + [S((width, part), F32)] * 2
-        + [S((part, width), F32)]
-        + [S((2, width, part), BF), S((part, width), BF)] * 3,
+        in_specs=[whole(h.shape), col, whole(gate.shape)] + [flat] * WS,
+        out_specs=[col, flat] + [flat] * 3,
+        out_shape=[sds((slots, width), BF), sds((part, width), F32)]
+        + [sds((part, width), BF)] * 3,
         compiler_params=pltpu.CompilerParams(vmem_limit_bytes=VM),
         cost_estimate=pl.CostEstimate(
-            flops=8 * slots * width * ff, bytes_accessed=8 * slots * width, transcendentals=0
+            flops=4 * slots * width * ff, bytes_accessed=4 * slots * width, transcendentals=0
         ),
-        name="expert_slopes",
-    )(x, dgu, h, dy, gate, *wd)
-
-
-def finish_body(experts, place_ref, a_ref, b_ref, ao_ref, bo_ref, flag_ref, *refs):
+        name="out_slopes",
+    )(h, dy, gate, *wd)
+
+
+def finish_body(experts, place_ref, a_ref, b_ref, ao_ref, bo_ref, *refs):
     q_ref, k_ref, v_ref, r_ref, g_ref, o_ref, s_ref = refs
     turn = pl.program_id(0)
-    second = flag_ref[0:1, 0:1]
+    second = place_ref[1] == 1
     rows = q_ref.shape[0]
     half = a_ref.shape[3]
     kv = k_ref.shape[1]
     mine = a_ref[:, 0].astype(F32).reshape(rows, half)
     twin = b_ref[:, 0].astype(F32).reshape(rows, half)
-    q_ref[...] = jnp.where(second > 0.5, twin, mine)
-    rest = jnp.where(second > 0.5, mine, twin)
+    q_ref[...] = jnp.where(second, twin, mine)
+    rest = jnp.where(second, mine, twin)
     k_ref[...] = rest[:, :kv]
     v_ref[...] = rest[:, kv : 2 * kv]
 
@@ -214,11 +233,10 @@
 
     mine = ao_ref[:, 0].astype(F32).reshape(rows, half)
     twin = bo_ref[:, 0].astype(F32).reshape(rows, half)
-    use_twin = jnp.where(turn < 2, second, 1.0 - second)
-    o_ref[...] = jnp.where(use_twin > 0.5, twin, mine)
-
-
-def finish(experts, place, mine, twin, flag):
+    o_ref[...] = jnp.where(second == (turn < 2), twin, mine)
+
+
+def finish(experts, place, mine, twin):
     chips, sets, step, half = mine.shape
     rows = chips * step
     first = pl.BlockSpec((chips, 1, step, half), lambda i, p: (0, i, 0, 0))
@@ -231,7 +249,7 @@
         grid_spec=pltpu.PrefetchScalarGridSpec(
             num_scalar_prefetch=1,
             grid=(WS,),
-            in_specs=[first, first, later, later, whole(flag.shape)],
+            in_specs=[first, first, later, later],
             out_specs=[
                 pl.BlockSpec((rows, half), turned),
                 pl.BlockSpec((rows, kv), turned),
@@ -253,7 +271,7 @@
         compiler_params=pltpu.CompilerParams(vmem_limit_bytes=VM),
         cost_estimate=pl.CostEstimate(flops=0, bytes_accessed=16 * rows * WS * half, transcendentals=0),
         name="finish",
-    )(place, mine, twin, mine, twin, flag)
+    )(place, mine, twin, mine, twin)
 
 
 def whole(shape):
@@ -694,7 +712,6 @@
     pieces = pack(experts, place, w_query, w_key, w_value, w_router, norm_attn, norm_moe)
     pieces, routes = lax.optimization_barrier((pieces, routes))
     own = [pieces[0]] + [from_peer(pieces[k], k) for k in (1, 2, 3)]
-    twin = [pieces[WS]] + [other_core(own[k]) for k in (1, 2, 3)]
 
     labels = jnp.arange(experts, dtype=jnp.int32)
     lane = jnp.arange(128, dtype=jnp.int32)
@@ -721,6 +738,8 @@
     angles = position.astype(F32)[:, None] * inverse[None, :]
     cosines = jnp.cos(angles)
     sines = jnp.where((lane % HEAD < HEAD // 2)[None, :], -1.0, 1.0) * jnp.sin(angles)
+    own[1], bias, cosines, sines = lax.optimization_barrier((own[1], bias, cosines, sines))
+    twin = [pieces[WS]] + [other_core(own[k]) for k in (1, 2, 3)]
     h1, qkv, o_far, lse_far, w_qkv, small_full, gains, *parts = attend(
         experts, place, xs, own, twin, cosines, sines, bias, w_out
     )
@@ -743,23 +762,22 @@
         axis=0,
     )
     wd = gathered(wd_own)
+    gates, gate_slots = gate_terms(h2, small_full, to_slot, chosen, spread)
+    wd[1], gates, gate_slots = lax.optimization_barrier((wd[1], gates, gate_slots))
     dx_send, hidden, d_gu, slot_gates = expert_pass(
         x_slots, dy_slots, sel, small_full, gathered(wg_own), gathered(wu_own), wd, 256
     )
-    gates, gate_slots = gate_terms(h2, small_full, to_slot, chosen, spread)
-    hidden, gates, gate_slots = lax.optimization_barrier((hidden, gates, gate_slots))
     dx_back = lax.all_to_all(
         dx_send.reshape(experts, CAP, width + 128), "exp", 0, 0, tiled=True
     ).reshape(slots, width + 128)
 
-    y, own_g, own_u, own_d, gu1, dn1, gu2, dn2, gu3, dn3 = expert_slopes(
-        x_slots, d_gu, hidden, dy_slots, slot_gates, wd
-    )
-    gu1, dn1 = to_peer(gu1, 1), to_peer(dn1, 1)
-    gu3, dn3 = to_peer(gu3, 3), to_peer(dn3, 3)
-    gu2 = to_peer(gu2, 2)
-    dx_back, y, gu1, dn1, gu2, gu3, dn3 = lax.optimization_barrier(
-        (dx_back, y, gu1, dn1, gu2, gu3, dn3)
+    own_g, own_u, gu1, gu2, gu3 = in_slopes(x_slots, d_gu)
+    gu1, gu2, gu3 = to_peer(gu1, 1), to_peer(gu2, 2), to_peer(gu3, 3)
+    hidden, gu1 = lax.optimization_barrier((hidden, gu1))
+    y, own_d, dn1, dn2, dn3 = out_slopes(hidden, dy_slots, slot_gates, wd)
+    dn1, dn2, dn3 = to_peer(dn1, 1), to_peer(dn2, 2), to_peer(dn3, 3)
+    dx_back, y, gu1, dn1, gu2, dn2, gu3, dn3 = lax.optimization_barrier(
+        (dx_back, y, gu1, dn1, gu2, dn2, gu3, dn3)
     )
     y_back = lax.all_to_all(y.reshape(experts, CAP, width), "exp", 0, 0, tiled=True).reshape(
         slots, width
@@ -770,6 +788,10 @@
     )
     das = gathered(d_a)
     small_terms = small_slopes(experts, h2, dl, dh2, x2)
+    grad_gu = jnp.stack([own_g, own_u]) + gu1.astype(F32) + gu2.astype(F32) + gu3.astype(F32)
+    grad_wg, grad_wu = grad_gu[0][None], grad_gu[1][None]
+    grad_wd = (own_d + dn1.astype(F32) + dn2.astype(F32) + dn3.astype(F32))[None]
+    das, grad_wg, grad_wu, grad_wd = lax.optimization_barrier((das, grad_wg, grad_wu, grad_wd))
     keep, give, *slopes = attend_back(
         experts,
         place,
@@ -787,29 +809,21 @@
         small_terms,
     )
     sent = (keep + other_core(give).astype(F32)).astype(BF)
-    sent, y_back, slopes, dn2, gu1 = lax.optimization_barrier((sent, y_back, slopes, dn2, gu1))
-    dn2 = to_peer(dn2, 2)
-    grad_gu = jnp.stack([own_g, own_u]) + gu1.astype(F32) + gu2.astype(F32) + gu3.astype(F32)
-    grad_wg, grad_wu = grad_gu[0][None], grad_gu[1][None]
-    grad_wd = (own_d + dn1.astype(F32) + dn2.astype(F32) + dn3.astype(F32))[None]
+    sent, y_back = lax.optimization_barrier((sent, y_back))
+    step = shard // CHIPS
+    both = dot(gate_slots, y_back)
+    layer_out = (x2 + both[:rows] + both[rows:]).astype(BF)
+    got = same_core(sent)
+    slopes = [slopes[0]] + [to_peer(slopes[k], k) for k in (1, 2, 3)]
+    got, layer_out, slopes = lax.optimization_barrier((got, layer_out, slopes))
     dh1 = slopes[0]
     for k in (1, 2, 3):
-        dh1 = dh1 + to_peer(slopes[k], k).astype(F32)
+        dh1 = dh1 + slopes[k].astype(F32)
     resid = tokens.astype(F32)
     scale = lax.rsqrt(jnp.mean(resid * resid, axis=-1, keepdims=True) + EPS)
     inner = jnp.mean(gains[0:1] * dh1 * resid, axis=-1, keepdims=True)
     grad_tokens = dx2 + scale * gains[0:1] * dh1 - resid * scale * scale * scale * inner
 
-    half = (q_w + 2 * kv_w + 128) // 2
-    flag = jnp.broadcast_to(jnp.stack([core, 1 - core]).astype(F32)[:, None], (2, 128))
-    flag = jnp.concatenate([flag, jnp.zeros((6, 128), F32)], axis=0)
-    step = shard // CHIPS
-    both = dot(gate_slots, y_back)
-    layer_out = (x2 + both[:rows] + both[rows:]).astype(BF)
-    got = same_core(sent)
-    got, layer_out, grad_tokens, grad_wg, grad_wu, grad_wd = lax.optimization_barrier(
-        (got, layer_out, grad_tokens, grad_wg, grad_wu, grad_wd)
-    )
     total = jnp.sum(got.astype(F32), axis=0).astype(BF)
     final = jnp.stack(
         [lax.dynamic_index_in_dim(total, me, 0, False)]
@@ -822,7 +836,7 @@
     spread_out = same_core(jnp.broadcast_to(final, (CHIPS,) + final.shape))
     twin_out = other_core(spread_out)
     sum_query, sum_key, sum_value, sum_router, sum_gains, sum_out = finish(
-        experts, place, spread_out, twin_out, flag
+        experts, place, spread_out, twin_out
     )
 
     return (

time: 420 us -> 407 us (0.969)
  waiting for transfers between devices: 155 us -> 136 us
    ppermute x21, waiting for transfers between devices: 77 us -> 60.3 us  [from_peer(): return lax.ppermute(v, 'ws', [(s, (s - k) % WS) for s in range(WS)])]
    ppermute x21, starting transfers between devices: 28.9 us -> 35.1 us  [from_peer(): return lax.ppermute(v, 'ws', [(s, (s - k) % WS) for s in range(WS)])]
    ppermute x12, waiting for transfers between devices: 69.2 us -> 63.1 us  [to_peer(): return lax.ppermute(v, 'ws', [(s, (s + k) % WS) for s in range(WS)])]
    pallas_call x1 -> x2, Pallas kernels: 15.6 us -> 20 us  [the longest x1 10.2 us: out_slopes(): pl.pallas_call(out_slope_body, grid=(width // tile,), in_specs=[whole(h.s...]
  transfers between devices with their start and end apart: 43 -> 43, of which waited for: 28 -> 28; matrix products, arithmetic and copies ran while one was open for 8% -> 8% of each run, Pallas kernels for 17% -> 19%
where the time goes in v5:
time: 407 us; the launch traced here: 400 us
  waiting for transfers between devices  136 us (33%)
  Pallas kernels  102 us (25%)
  starting transfers between devices  96.9 us (24%)
  blocking collectives  27.1 us (7%)
  other arithmetic  13.7 us (3%)
  local copies, waits for them, and re-layouts  11.6 us (3%)
  matrix products  11.2 us (3%)
    ppermute x12, waiting for transfers between devices, to_peer(): return lax.ppermute(v, 'ws', [(s, (s + k) % WS) for s in range(WS)])  63.1 us
    ppermute x21, waiting for transfers between devices, from_peer(): return lax.ppermute(v, 'ws', [(s, (s - k) % WS) for s in range(WS)])  60.3 us
    pallas_call x6, Pallas kernels, one_step(): pl.pallas_call(body, in_specs=[pl.BlockSpec(memory_space=pltpu.SMEM)] * l...  43.3 us
    ppermute x21, starting transfers between devices, from_peer(): return lax.ppermute(v, 'ws', [(s, (s - k) % WS) for s in range(WS)])  35.1 us
    all_to_all x1, blocking collectives, same_core(): return lax.all_to_all(v, 'exp', 0, 0, tiled=True, axis_index_groups=groups)  27.1 us
    pallas_call x1, Pallas kernels, expert_pass(): pl.pallas_call(functools.partial(expert_body, width, ff), grid=(slots //...  20.7 us
    ppermute x12, starting transfers between devices, to_peer(): return lax.ppermute(v, 'ws', [(s, (s + k) % WS) for s in range(WS)])  14 us
    pallas_call x1, Pallas kernels, out_slopes(): pl.pallas_call(out_slope_body, grid=(width // tile,), in_specs=[whole(h.s...  10.2 us
  transfers between devices with their start and end apart: 43, of which 28 were waited for; matrix products, arithmetic and copies ran while one was open for 8% of the time, Pallas kernels for 19%

profile of v5, /device:TPU:1, one launch (start us, length us, event | category | flops | bytes accessed | tf_op | source)
XLA Modules:
  0.0 400.5 jit_solution(11640003888569556140)
XLA Ops:
  0.7 3.6 collective-permute-start
  8.8 2.9 pack.1
  13.4 3.9 convolution_convert_fusion
  18.2 8.9 %all-to-all-start.1 = ((bf16[32,48,1664]{2,1,0:T(8,128)(2,1)}), bf16[32,48,1664]{2,1,0:T(8,128)(2,1)}, u32[]{:S(2)}, u32[]{:S(2)}) async-start(bf16[32,48,1664]{2,1,0:T(8,128)(2,1)} %bitcast.57), calls=%async_computation.1 | async-start | bytes 10223616 | tf_op jit(solution)/shard_map/all_to_all | solution.py:730
  30.3 2.3 collective-permute-start.4
  37.0 9.1 %collective-permute-done.3.refs_5_ = bf16[192,768]{1,0:T(8,128)(2,1)S(1)} collective-permute-done((bf16[192,768]{1,0:T(8,128)(2,1)S(1)}, bf16[192,768]{1,0:T(8,128)(2,1)S(1)}, u32[]{:S(2)}, u32[]{:S(2)}) %collective-permute-start.3) | collective-permute-done | bytes 294944 | tf_op jit(solution)/shard_map/ppermute | solution.py:42
  48.0 4.5 %collective-permute-done.5.refs_7_ = bf16[192,768]{1,0:T(8,128)(2,1)S(1)} collective-permute-done((bf16[192,768]{1,0:T(8,128)(2,1)S(1)}, bf16[192,768]{1,0:T(8,128)(2,1)S(1)}, u32[]{:S(2)}, u32[]{:S(2)}) %collective-permute-start.5) | collective-permute-done | bytes 294944 | tf_op jit(solution)/shard_map/ppermute | solution.py:42
  55.3 9.6 %attend.1 = (bf16[512,1536]{1,0:T(8,128)(2,1)}, bf16[512,640]{1,0:T(8,128)(2,1)}, bf16[384,384]{1,0:T(8,128)(2,1)}, f32[384,128]{1,0:T(8,128)}, bf16[1536,640]{1...) custom-call(s32[2]{0:T(128)} %pad_add_fusion.place_ref, ...), custom_call_target="tpu_custom_call" | custom-call | flops 2013265920 | bytes 6684672 | tf_op jit(solution)/shard_map/attend/pallas_call | solution.py:287
  69.0 5.4 %attend_own.1 = (bf16[128,384]{1,0:T(8,128)(2,1)}, f32[128,128]{1,0:T(8,128)}, f32[128,1536]{1,0:T(8,128)}) custom-call(bf16[512,640]{1,0:T(8,128)(2,1)} %get-tuple-element.127.qkv_ref.refs_9_, f32[512,512]{1,0:T(8,128)} %fusion.3.refs_14_.bias_ref.refs_18_, bf16[384,1536]{1,0:T(8,128)(2,1)} %refs_8_.1), custom_call_target="tpu_custom_call" | custom-call | flops 251658240 | bytes 2883584 | tf_op jit(solution)/shard_map/attend_own/pallas_call | solution.py:287
  74.4 2.8 collective-permute-done.10.p2
  77.2 9.6 %collective-permute-done.11.p3 = bf16[128,1536]{1,0:T(8,128)(2,1)S(1)} collective-permute-done((bf16[128,1536]{1,0:T(8,128)(2,1)}, bf16[128,1536]{1,0:T(8,128)(2,1)S(1)}, u32[]{:S(2)}, u32[]{:S(2)}) %collective-permute-start.11) | collective-permute-done | bytes 393248 | tf_op jit(solution)/shard_map/ppermute | solution.py:46
  87.6 5.6 %enter.1 = (f32[128,1536]{1,0:T(8,128)}, bf16[128,1536]{1,0:T(8,128)(2,1)}, bf16[1536,1536]{1,0:T(8,128)(2,1)}) custom-call(bf16[128,1536]{1,0:T(8,128)(2,1)} %refs_4_.1, f32[128,1536]{1,0:T(8,128)} %get-tuple-element.128.p0, bf16[128,1536]{1,0:T(8,128)(2,1)} %copy-done.13, bf16[128,1536]{1,0:T(8,128)(2,1)} %copy-done.11, bf16[128,1536]{1,0:T(8,128)(2,1)} %copy-done.12, ...), custom_call_target="tpu_custom_call" | custom-call | flops 603979776 | bytes 7077888 | tf_op jit(solution)/shard_map/enter/pallas_call | solution.py:468
  93.3 8.2 %all-to-all-start = ((bf16[32,48,1536]{2,1,0:T(8,128)(2,1)}), bf16[32,48,1536]{2,1,0:T(8,128)(2,1)}, u32[]{:S(2)}, u32[]{:S(2)}) async-start(bf16[32,48,1536]{2,1,0:T(8,128)(2,1)} %bitcast.60), calls=%async_computation | async-start | bytes 9437184 | tf_op jit(solution)/shard_map/all_to_all | solution.py:752
  105.9 2.4 collective-permute-start.15
  108.3 3.8 collective-permute-done.18.rest_9_.refs_1_
  114.2 6.5 %collective-permute-done.12.rest_1_ = bf16[1536,128]{1,0:T(8,128)(2,1)S(1)} collective-permute-done((bf16[1536,128]{1,0:T(8,128)(2,1)S(1)}, bf16[1536,128]{1,0:T(8,128)(2,1)S(1)}, u32[]{:S(2)}, u32[]{:S(2)}) %collective-permute-start.12) | collective-permute-done | bytes 393248 | tf_op jit(solution)/shard_map/ppermute | solution.py:42
  120.7 12.3 %collective-permute-start.19 = (bf16[128,1536]{1,0:T(8,128)(2,1)S(1)}, bf16[128,1536]{1,0:T(8,128)(2,1)S(1)}, u32[]{:S(2)}, u32[]{:S(2)}) collective-permute-start(bf16[128,1536]{1,0:T(8,128)(2,1)S(1)} %bitcast.77), channel_id=1, source_target_pairs={{0,2},{1,3},{2,0},{3,1},{4,6},{5,7},{6,4},{7,5},{8,10},{9,11},{10,... | collective-permute-start | bytes 1179656 | tf_op jit(solution)/shard_map/ppermute | solution.py:42
  133.8 3.0 gate_terms.1
  139.6 8.7 %collective-permute-done.19.rest_10_.refs_2_ = bf16[128,1536]{1,0:T(8,128)(2,1)S(1)} collective-permute-done((bf16[128,1536]{1,0:T(8,128)(2,1)S(1)}, bf16[128,1536]{1,0:T(8,128)(2,1)S(1)}, u32[]{:S(2)}, u32[]{:S(2)}) %collective-permute-start.19) | collective-permute-done | bytes 393248 | tf_op jit(solution)/shard_map/ppermute | solution.py:42
  148.3 8.2 %collective-permute-done.20.rest_11_.refs_3_ = bf16[128,1536]{1,0:T(8,128)(2,1)S(1)} collective-permute-done((bf16[128,1536]{1,0:T(8,128)(2,1)S(1)}, bf16[128,1536]{1,0:T(8,128)(2,1)S(1)}, u32[]{:S(2)}, u32[]{:S(2)}) %collective-permute-start.20) | collective-permute-done | bytes 393248 | tf_op jit(solution)/shard_map/ppermute | solution.py:42
  156.5 3.4 all-to-all-done
  159.9 20.7 %expert_pass.1 = (bf16[1536,1664]{1,0:T(8,128)(2,1)}, bf16[1536,512]{1,0:T(8,128)(2,1)}, bf16[1536,1024]{1,0:T(8,128)(2,1)}, f32[1536,128]{1,0:T(8,128)}) custom-call(bf16[1536,1536]{1,0:T(8,128)(2,1)} %bitcast.15.x_ref, bf16[1536,1664]{1,0:T(8,128)(2,1)} %bitcast.16.dy_ref, f32[8,128]{1,0:T(8,128)} %maximum_maximum_fusion.sel_ref, ...), custom_call_target="tpu_custom_call" | custom-call | flops 12079595520 | bytes 21233664 | tf_op jit(solution)/shard_map/expert_pass/pallas_call | solution.py:120
  180.6 7.8 %all-to-all-start.2 = ((bf16[32,48,1664]{2,1,0:T(8,128)(2,1)}), bf16[32,48,1664]{2,1,0:T(8,128)(2,1)}, u32[]{:S(2)}, u32[]{:S(2)}) async-start(bf16[32,48,1664]{2,1,0:T(8,128)(2,1)} %bitcast.58), calls=%async_computation.2 | async-start | bytes 10223616 | tf_op jit(solution)/shard_map/all_to_all | solution.py:770
  188.4 9.8 %in_slopes.1 = (f32[1536,128]{1,0:T(8,128)}, f32[1536,128]{1,0:T(8,128)}, bf16[2,1536,128]{2,1,0:T(8,128)(2,1)}, bf16[2,1536,128]{2,1,0:T(8,128)(2,1)}, bf16[2,1536,128]{2,1,0:T(8,128)(2,1)}) custom-call(bf16[1536,1536]{1,0:T(8,128)(2,1)} %bitcast.15.x_ref, bf16[1536,1024]{1,0:T(8,128)(2,1)} %get-tuple-element.146.dgu_ref), custom_call_target="tpu_custom_call" | custom-call | flops 4831838208 | bytes 9437184 | tf_op jit(solution)/shard_map/in_slopes/pallas_call | solution.py:157
  198.2 4.0 %collective-permute-start.23 = (bf16[2,1536,128]{2,1,0:T(8,128)(2,1)}, bf16[2,1536,128]{2,1,0:T(8,128)(2,1)S(1)}, u32[]{:S(2)}, u32[]{:S(2)}) collective-permute-start(bf16[2,1536,128]{2,1,0:T(8,128)(2,1)} %get-tuple-element.153), channel_id=1, source_target_pairs={{0,2},{1,3},{2,0},{3,1},{4,6},{5,7},{6,4},{7,5},{8,10},{9,11},{10,... | collective-permute-start | bytes 2359304 | tf_op jit(solution)/shard_map/ppermute | solution.py:46
  202.3 16.7 %collective-permute-done.21 = bf16[2,1536,128]{2,1,0:T(8,128)(2,1)S(1)} collective-permute-done((bf16[2,1536,128]{2,1,0:T(8,128)(2,1)}, bf16[2,1536,128]{2,1,0:T(8,128)(2,1)S(1)}, u32[]{:S(2)}, u32[]{:S(2)}) %collective-permute-start.21) | collective-permute-done | bytes 786464 | tf_op jit(solution)/shard_map/ppermute | solution.py:46
  219.0 10.2 %out_slopes.1 = (bf16[1536,1536]{1,0:T(8,128)(2,1)}, f32[128,1536]{1,0:T(8,128)}, bf16[128,1536]{1,0:T(8,128)(2,1)}, bf16[128,1536]{1,0:T(8,128)(2,1)}, bf16[128,1536]{1,0:T(8,128)(2,1)}) custom-call(bf16[1536,512]{1,0:T(8,128)(2,1)} %get-tuple-element.148.h_ref, bf16[1536,1664]{1,0:T(8,128)(2,1)} %bitcast.16.dy_ref, ...), custom_call_target="tpu_custom_call" | custom-call | flops 4831838208 | bytes 9437184 | tf_op jit(solution)/shard_map/out_slopes/pallas_call | solution.py:191
  229.2 2.4 collective-permute-start.24
  231.9 5.0 %collective-permute-done.23 = bf16[2,1536,128]{2,1,0:T(8,128)(2,1)S(1)} collective-permute-done((bf16[2,1536,128]{2,1,0:T(8,128)(2,1)}, bf16[2,1536,128]{2,1,0:T(8,128)(2,1)S(1)}, u32[]{:S(2)}, u32[]{:S(2)}) %collective-permute-start.23) | collective-permute-done | bytes 786464 | tf_op jit(solution)/shard_map/ppermute | solution.py:46
  236.8 9.6 %collective-permute-done.22 = bf16[128,1536]{1,0:T(8,128)(2,1)S(1)} collective-permute-done((bf16[128,1536]{1,0:T(8,128)(2,1)}, bf16[128,1536]{1,0:T(8,128)(2,1)S(1)}, u32[]{:S(2)}, u32[]{:S(2)}) %collective-permute-start.22) | collective-permute-done | bytes 393248 | tf_op jit(solution)/shard_map/ppermute | solution.py:46
  246.4 7.1 %collective-permute-done.24 = bf16[128,1536]{1,0:T(8,128)(2,1)S(1)} collective-permute-done((bf16[128,1536]{1,0:T(8,128)(2,1)}, bf16[128,1536]{1,0:T(8,128)(2,1)S(1)}, u32[]{:S(2)}, u32[]{:S(2)}) %collective-permute-start.24) | collective-permute-done | bytes 393248 | tf_op jit(solution)/shard_map/ppermute | solution.py:46
  253.6 8.2 %all-to-all-start.3 = ((bf16[32,48,1536]{2,1,0:T(8,128)(2,1)}), bf16[32,48,1536]{2,1,0:T(8,128)(2,1)}, u32[]{:S(2)}, u32[]{:S(2)}) async-start(bf16[32,48,1536]{2,1,0:T(8,128)(2,1)} %bitcast.59), calls=%async_computation.3 | async-start | bytes 9437184 | tf_op jit(solution)/shard_map/all_to_all | solution.py:782
  261.8 6.5 %leave.1 = (f32[128,1536]{1,0:T(8,128)}, bf16[128,1536]{1,0:T(8,128)(2,1)}, f32[128,1536]{1,0:T(8,128)}, f32[128,128]{1,0:T(8,128)}) custom-call(bf16[1536,1664]{1,0:T(8,128)(2,1)} %bitcast.18.back_ref, bf16[128,1536]{1,0:T(8,128)(2,1)} %get-tuple-element.222.slot_ref, f32[128,128]{1,0:T(8,128)} %get-tuple-element.158.gates_ref, ...), custom_call_target="tpu_custom_call" | custom-call | flops 603979776 | bytes 7077888 | tf_op jit(solution)/shard_map/leave/pallas_call | solution.py:545
  271.1 3.2 small_slopes.1.refs_19_
  279.0 3.2 collective-permute-done.28.refs_2_
  282.3 9.1 %collective-permute-done.29.refs_3_ = bf16[128,1536]{1,0:T(8,128)(2,1)} collective-permute-done((bf16[128,1536]{1,0:T(8,128)(2,1)}, bf16[128,1536]{1,0:T(8,128)(2,1)}, u32[]{:S(2)}, u32[]{:S(2)}) %collective-permute-start.29) | collective-permute-done | bytes 393248 | tf_op jit(solution)/shard_map/ppermute | solution.py:42
  291.3 19.1 %attend_back.1 = (f32[16,6,24,384]{3,2,1,0:T(8,128)}, bf16[16,6,24,384]{3,2,1,0:T(8,128)(2,1)}, f32[128,1536]{1,0:T(8,128)}, bf16[128,1536]{1,0:T(8,128)(2,1)}, ...) custom-call(s32[2]{0:T(128)} %pad_add_fusion.place_ref, bf16[128,1536]{1,0:T(8,128)(2,1)} %get-tuple-element.170.refs_0_, ...), custom_call_target="tpu_custom_call" | custom-call | flops 4227858432 | bytes 11534336 | tf_op jit(solution)/shard_map/attend_back/pallas_call | solution.py:287
  311.1 3.5 collective-permute-done.30
  314.7 3.6 add_convert_fusion
  320.2 6.7 %all-to-all-start.4 = ((bf16[16,6,24,384]{3,2,1,0:T(8,128)(2,1)}), bf16[16,6,24,384]{3,2,1,0:T(8,128)(2,1)S(1)}, u32[]{:S(2)}, u32[]{:S(2)}) async-start(bf16[16,6,24,384]{3,2,1,0:T(8,128)(2,1)} %add_convert_fusion), calls=%async_computation.4 | async-start | bytes 3538944 | tf_op jit(solution)/shard_map/all_to_all | solution.py:55
  327.0 3.1 collective-permute-start.32
  330.1 4.0 %fusion.58 = f32[256,1536]{1,0:T(8,128)S(1)} fusion(bf16[256,1536]{1,0:T(8,128)(2,1)} %get-tuple-element.186, bf16[1536,1536]{1,0:T(8,128)(2,1)} %bitcast.23), kind=kOutput, calls=%fused_computation.112 | convolution fusion | flops 1207959552 | bytes 7077888 | tf_op jit(solution)/shard_map/dot_general | solution.py:25
  335.0 2.9 collective-permute-done.31
  337.9 8.9 %collective-permute-done.32 = bf16[128,1536]{1,0:T(8,128)(2,1)S(1)} collective-permute-done((bf16[128,1536]{1,0:T(8,128)(2,1)}, bf16[128,1536]{1,0:T(8,128)(2,1)S(1)}, u32[]{:S(2)}, u32[]{:S(2)}) %collective-permute-start.32) | collective-permute-done | bytes 393248 | tf_op jit(solution)/shard_map/ppermute | solution.py:46
  352.4 3.2 collective-permute-done.35
  355.9 27.1 %all_to_all.30.a_ref.ao_ref = bf16[16,6,24,384]{3,2,1,0:T(8,128)(2,1)S(1)} all-to-all(bf16[16,6,24,384]{3,2,1,0:T(8,128)(2,1)S(1)} %broadcast_in_dim.84), channel_id=1, replica_groups={{0,8,16,24,32,40,48,56,64,72,80,88,96,104,112,120},{4,12,20,28,36,44,52..., dimensions={0} | all-to-all | bytes 3538944 | tf_op jit(solution)/shard_map/all_to_all | solution.py:55
  383.0 4.8 %collective-permute-start.37 = (bf16[16,6,24,384]{3,2,1,0:T(8,128)(2,1)S(1)}, bf16[16,6,24,384]{3,2,1,0:T(8,128)(2,1)S(1)}, u32[]{:S(2)}, u32[]{:S(2)}) collective-permute-start(bf16[16,6,24,384]{3,2,1,0:T(8,128)(2,1)S(1)} %all_to_all.30.a_ref.ao_ref), channel_id=1, source_target_pairs={{0,4},{4,0},{8,12},{12,8},{16,20},{20,16},{24,28},{28,24},{32,36},... | collective-permute-start | bytes 5308424 | tf_op jit(solution)/shard_map/ppermute | solution.py:50
  392.3 6.3 %finish.1 = (f32[384,1536]{1,0:T(8,128)}, f32[384,512]{1,0:T(8,128)}, f32[384,512]{1,0:T(8,128)}, f32[32,384]{1,0:T(8,128)}, f32[8,384]{1,0:T(8,128)}, /*index=5*/f32[384,1536]{1,0:T(8,128)}) custom-call(s32[2]{0:T(128)} %pad_add_fusion.place_ref, bf16[16,6,24,384]{3,2,1,0:T(8,128)(2,1)} %copy-done, bf16[16,6,24,384]{3,2,1,0:T(8,128)(2,1)} %copy-done.1, ...), custom_call_target="tpu_custom_call" | custom-call | bytes 9437184 | tf_op jit(solution)/shard_map/finish/pallas_call | solution.py:247
  (178 shorter events, 57.5 us)
Async XLA Ops:
  0.7 16.6 %collective-permute-start = (bf16[128,1536]{1,0:T(8,128)(2,1)}, bf16[128,1536]{1,0:T(8,128)(2,1)S(1)}, u32[]{:S(2)}, u32[]{:S(2)}) collective-permute-start(bf16[128,1536]{1,0:T(8,128)(2,1)} %refs_4_.1), channel_id=1, source_target_pairs={{0,3},{1,0},{2,1},{3,2},{4,7},{5,4},{6,5},{7,6},{8,11},{9,8},{10,9... | collective-permute-start | bytes 1179656 | tf_op jit(solution)/shard_map/ppermute | solution.py:42
  4.3 13.0 %collective-permute-start.1 = (bf16[128,1536]{1,0:T(8,128)(2,1)}, bf16[128,1536]{1,0:T(8,128)(2,1)S(1)}, u32[]{:S(2)}, u32[]{:S(2)}) collective-permute-start(bf16[128,1536]{1,0:T(8,128)(2,1)} %refs_4_.1), channel_id=1, source_target_pairs={{0,1},{1,2},{2,3},{3,0},{4,5},{5,6},{6,7},{7,4},{8,9},{9,10},{10,1... | collective-permute-start | bytes 1179656 | tf_op jit(solution)/shard_map/ppermute | solution.py:42
  18.2 75.0 %all-to-all-start.1 = ((bf16[32,48,1664]{2,1,0:T(8,128)(2,1)}), bf16[32,48,1664]{2,1,0:T(8,128)(2,1)}, u32[]{:S(2)}, u32[]{:S(2)}) async-start(bf16[32,48,1664]{2,1,0:T(8,128)(2,1)} %bitcast.57), calls=%async_computation.1 | async-start | bytes 10223616 | tf_op jit(solution)/shard_map/all_to_all | solution.py:730
  27.1 26.2 %collective-permute-start.2 = (bf16[128,1536]{1,0:T(8,128)(2,1)S(1)}, bf16[128,1536]{1,0:T(8,128)(2,1)S(1)}, u32[]{:S(2)}, u32[]{:S(2)}) collective-permute-start(bf16[128,1536]{1,0:T(8,128)(2,1)S(1)} %copy-done.3), channel_id=1, source_target_pairs={{0,2},{1,3},{2,0},{3,1},{4,6},{5,7},{6,4},{7,5},{8,10},{9,11},{10,... | collective-permute-start | bytes 1179656 | tf_op jit(solution)/shard_map/ppermute | solution.py:42
  29.1 17.0 %collective-permute-start.3 = (bf16[192,768]{1,0:T(8,128)(2,1)S(1)}, bf16[192,768]{1,0:T(8,128)(2,1)S(1)}, u32[]{:S(2)}, u32[]{:S(2)}) collective-permute-start(bf16[192,768]{1,0:T(8,128)(2,1)S(1)} %copy-done.35), channel_id=1, source_target_pairs={{0,3},{1,0},{2,1},{3,2},{4,7},{5,4},{6,5},{7,6},{8,11},{9,8},{10,9... | collective-permute-start | bytes 884744 | tf_op jit(solution)/shard_map/ppermute | solution.py:42
  30.3 17.6 %collective-permute-start.4 = (bf16[192,768]{1,0:T(8,128)(2,1)S(1)}, bf16[192,768]{1,0:T(8,128)(2,1)S(1)}, u32[]{:S(2)}, u32[]{:S(2)}) collective-permute-start(bf16[192,768]{1,0:T(8,128)(2,1)S(1)} %copy-done.33), channel_id=1, source_target_pairs={{0,2},{1,3},{2,0},{3,1},{4,6},{5,7},{6,4},{7,5},{8,10},{9,11},{10,... | collective-permute-start | bytes 884744 | tf_op jit(solution)/shard_map/ppermute | solution.py:42
  32.5 20.0 %collective-permute-start.5 = (bf16[192,768]{1,0:T(8,128)(2,1)S(1)}, bf16[192,768]{1,0:T(8,128)(2,1)S(1)}, u32[]{:S(2)}, u32[]{:S(2)}) collective-permute-start(bf16[192,768]{1,0:T(8,128)(2,1)S(1)} %copy-done.30), channel_id=1, source_target_pairs={{0,1},{1,2},{2,3},{3,0},{4,5},{5,6},{6,7},{7,4},{8,9},{9,10},{10,1... | collective-permute-start | bytes 884744 | tf_op jit(solution)/shard_map/ppermute | solution.py:42
  46.2 7.2 %collective-permute-start.6 = (bf16[192,768]{1,0:T(8,128)(2,1)S(1)}, bf16[192,768]{1,0:T(8,128)(2,1)S(1)}, u32[]{:S(2)}, u32[]{:S(2)}) collective-permute-start(bf16[192,768]{1,0:T(8,128)(2,1)S(1)} %collective-permute-done.3.refs_5_), channel_id=1, source_target_pairs={{0,4},{4,0},{8,12},{12,8},{16,20},{20,16},{24,28},{28,24},{32,36},... | collective-permute-start | bytes 884744 | tf_op jit(solution)/shard_map/ppermute | solution.py:50
  47.9 5.5 %collective-permute-start.7 = (bf16[192,768]{1,0:T(8,128)(2,1)S(1)}, bf16[192,768]{1,0:T(8,128)(2,1)S(1)}, u32[]{:S(2)}, u32[]{:S(2)}) collective-permute-start(bf16[192,768]{1,0:T(8,128)(2,1)S(1)} %collective-permute-done.4.refs_6_), channel_id=1, source_target_pairs={{0,4},{4,0},{8,12},{12,8},{16,20},{20,16},{24,28},{28,24},{32,36},... | collective-permute-start | bytes 884744 | tf_op jit(solution)/shard_map/ppermute | solution.py:50
  52.5 2.0 collective-permute-start.8
  64.9 12.2 %collective-permute-start.10 = (bf16[128,1536]{1,0:T(8,128)(2,1)}, bf16[128,1536]{1,0:T(8,128)(2,1)S(1)}, u32[]{:S(2)}, u32[]{:S(2)}) collective-permute-start(bf16[128,1536]{1,0:T(8,128)(2,1)} %get-tuple-element.130), channel_id=1, source_target_pairs={{0,2},{1,3},{2,0},{3,1},{4,6},{5,7},{6,4},{7,5},{8,10},{9,11},{10,... | collective-permute-start | bytes 1179656 | tf_op jit(solution)/shard_map/ppermute | solution.py:46
  66.9 19.9 %collective-permute-start.11 = (bf16[128,1536]{1,0:T(8,128)(2,1)}, bf16[128,1536]{1,0:T(8,128)(2,1)S(1)}, u32[]{:S(2)}, u32[]{:S(2)}) collective-permute-start(bf16[128,1536]{1,0:T(8,128)(2,1)} %get-tuple-element.131), channel_id=1, source_target_pairs={{0,3},{1,0},{2,1},{3,2},{4,7},{5,4},{6,5},{7,6},{8,11},{9,8},{10,9... | collective-permute-start | bytes 1179656 | tf_op jit(solution)/shard_map/ppermute | solution.py:46
  68.5 18.3 %collective-permute-start.9 = (bf16[128,1536]{1,0:T(8,128)(2,1)}, bf16[128,1536]{1,0:T(8,128)(2,1)S(1)}, u32[]{:S(2)}, u32[]{:S(2)}) collective-permute-start(bf16[128,1536]{1,0:T(8,128)(2,1)} %get-tuple-element.129), channel_id=1, source_target_pairs={{0,1},{1,2},{2,3},{3,0},{4,5},{5,6},{6,7},{7,4},{8,9},{9,10},{10,1... | collective-permute-start | bytes 1179656 | tf_op jit(solution)/shard_map/ppermute | solution.py:46
  93.3 66.6 %all-to-all-start = ((bf16[32,48,1536]{2,1,0:T(8,128)(2,1)}), bf16[32,48,1536]{2,1,0:T(8,128)(2,1)}, u32[]{:S(2)}, u32[]{:S(2)}) async-start(bf16[32,48,1536]{2,1,0:T(8,128)(2,1)} %bitcast.60), calls=%async_computation | async-start | bytes 9437184 | tf_op jit(solution)/shard_map/all_to_all | solution.py:752
  101.4 10.6 %collective-permute-start.18 = (bf16[128,1536]{1,0:T(8,128)(2,1)S(1)}, bf16[128,1536]{1,0:T(8,128)(2,1)S(1)}, u32[]{:S(2)}, u32[]{:S(2)}) collective-permute-start(bf16[128,1536]{1,0:T(8,128)(2,1)S(1)} %bitcast.76), channel_id=1, source_target_pairs={{0,3},{1,0},{2,1},{3,2},{4,7},{5,4},{6,5},{7,6},{8,11},{9,8},{10,9... | collective-permute-start | bytes 1179656 | tf_op jit(solution)/shard_map/ppermute | solution.py:42
  103.6 17.1 %collective-permute-start.12 = (bf16[1536,128]{1,0:T(8,128)(2,1)S(1)}, bf16[1536,128]{1,0:T(8,128)(2,1)S(1)}, u32[]{:S(2)}, u32[]{:S(2)}) collective-permute-start(bf16[1536,128]{1,0:T(8,128)(2,1)S(1)} %bitcast.67), channel_id=1, source_target_pairs={{0,3},{1,0},{2,1},{3,2},{4,7},{5,4},{6,5},{7,6},{8,11},{9,8},{10,9... | collective-permute-start | bytes 1179656 | tf_op jit(solution)/shard_map/ppermute | solution.py:42
  103.7 17.0 %collective-permute-start.13 = (bf16[1536,128]{1,0:T(8,128)(2,1)S(1)}, bf16[1536,128]{1,0:T(8,128)(2,1)S(1)}, u32[]{:S(2)}, u32[]{:S(2)}) collective-permute-start(bf16[1536,128]{1,0:T(8,128)(2,1)S(1)} %bitcast.68), channel_id=1, source_target_pairs={{0,2},{1,3},{2,0},{3,1},{4,6},{5,7},{6,4},{7,5},{8,10},{9,11},{10,... | collective-permute-start | bytes 1179656 | tf_op jit(solution)/shard_map/ppermute | solution.py:42
  104.8 28.3 %collective-permute-start.14 = (bf16[1536,128]{1,0:T(8,128)(2,1)S(1)}, bf16[1536,128]{1,0:T(8,128)(2,1)}, u32[]{:S(2)}, u32[]{:S(2)}) collective-permute-start(bf16[1536,128]{1,0:T(8,128)(2,1)S(1)} %bitcast.69), channel_id=1, source_target_pairs={{0,1},{1,2},{2,3},{3,0},{4,5},{5,6},{6,7},{7,4},{8,9},{9,10},{10,1... | collective-permute-start | bytes 1179656 | tf_op jit(solution)/shard_map/ppermute | solution.py:42
  105.9 31.7 %collective-permute-start.15 = (bf16[1536,128]{1,0:T(8,128)(2,1)S(1)}, bf16[1536,128]{1,0:T(8,128)(2,1)S(1)}, u32[]{:S(2)}, u32[]{:S(2)}) collective-permute-start(bf16[1536,128]{1,0:T(8,128)(2,1)S(1)} %bitcast.71), channel_id=1, source_target_pairs={{0,3},{1,0},{2,1},{3,2},{4,7},{5,4},{6,5},{7,6},{8,11},{9,8},{10,9... | collective-permute-start | bytes 1179656 | tf_op jit(solution)/shard_map/ppermute | solution.py:42
  112.0 47.8 %copy-start.24 = (bf16[128,1536]{1,0:T(8,128)(2,1)}, bf16[128,1536]{1,0:T(8,128)(2,1)S(1)}, u32[]{:S(2)}) copy-start(bf16[128,1536]{1,0:T(8,128)(2,1)S(1)} %collective-permute-done.18.rest_9_.refs_1_) | copy-start | bytes 1179652
  112.0 25.5 %collective-permute-start.16 = (bf16[1536,128]{1,0:T(8,128)(2,1)S(1)}, bf16[1536,128]{1,0:T(8,128)(2,1)}, u32[]{:S(2)}, u32[]{:S(2)}) collective-permute-start(bf16[1536,128]{1,0:T(8,128)(2,1)S(1)} %bitcast.72), channel_id=1, source_target_pairs={{0,2},{1,3},{2,0},{3,1},{4,6},{5,7},{6,4},{7,5},{8,10},{9,11},{10,... | collective-permute-start | bytes 1179656 | tf_op jit(solution)/shard_map/ppermute | solution.py:42
  120.7 39.1 %copy-start.25 = (bf16[1536,128]{1,0:T(8,128)(2,1)}, bf16[1536,128]{1,0:T(8,128)(2,1)S(1)}, u32[]{:S(2)}) copy-start(bf16[1536,128]{1,0:T(8,128)(2,1)S(1)} %collective-permute-done.12.rest_1_) | copy-start | bytes 1179652
  120.7 18.9 %collective-permute-start.17 = (bf16[1536,128]{1,0:T(8,128)(2,1)S(1)}, bf16[1536,128]{1,0:T(8,128)(2,1)}, u32[]{:S(2)}, u32[]{:S(2)}) collective-permute-start(bf16[1536,128]{1,0:T(8,128)(2,1)S(1)} %bitcast.73), channel_id=1, source_target_pairs={{0,1},{1,2},{2,3},{3,0},{4,5},{5,6},{6,7},{7,4},{8,9},{9,10},{10,1... | collective-permute-start | bytes 1179656 | tf_op jit(solution)/shard_map/ppermute | solution.py:42
  120.7 39.1 %copy-start.26 = (bf16[1536,128]{1,0:T(8,128)(2,1)}, bf16[1536,128]{1,0:T(8,128)(2,1)S(1)}, u32[]{:S(2)}) copy-start(bf16[1536,128]{1,0:T(8,128)(2,1)S(1)} %collective-permute-done.13.rest_2_) | copy-start | bytes 1179652
  120.7 27.6 %collective-permute-start.19 = (bf16[128,1536]{1,0:T(8,128)(2,1)S(1)}, bf16[128,1536]{1,0:T(8,128)(2,1)S(1)}, u32[]{:S(2)}, u32[]{:S(2)}) collective-permute-start(bf16[128,1536]{1,0:T(8,128)(2,1)S(1)} %bitcast.77), channel_id=1, source_target_pairs={{0,2},{1,3},{2,0},{3,1},{4,6},{5,7},{6,4},{7,5},{8,10},{9,11},{10,... | collective-permute-start | bytes 1179656 | tf_op jit(solution)/shard_map/ppermute | solution.py:42
  133.0 23.4 %collective-permute-start.20 = (bf16[128,1536]{1,0:T(8,128)(2,1)S(1)}, bf16[128,1536]{1,0:T(8,128)(2,1)S(1)}, u32[]{:S(2)}, u32[]{:S(2)}) collective-permute-start(bf16[128,1536]{1,0:T(8,128)(2,1)S(1)} %bitcast.78), channel_id=1, source_target_pairs={{0,1},{1,2},{2,3},{3,0},{4,5},{5,6},{6,7},{7,4},{8,9},{9,10},{10,1... | collective-permute-start | bytes 1179656 | tf_op jit(solution)/shard_map/ppermute | solution.py:42
  180.6 73.0 %all-to-all-start.2 = ((bf16[32,48,1664]{2,1,0:T(8,128)(2,1)}), bf16[32,48,1664]{2,1,0:T(8,128)(2,1)}, u32[]{:S(2)}, u32[]{:S(2)}) async-start(bf16[32,48,1664]{2,1,0:T(8,128)(2,1)} %bitcast.58), calls=%async_computation.2 | async-start | bytes 10223616 | tf_op jit(solution)/shard_map/all_to_all | solution.py:770
  198.2 20.7 %collective-permute-start.21 = (bf16[2,1536,128]{2,1,0:T(8,128)(2,1)}, bf16[2,1536,128]{2,1,0:T(8,128)(2,1)S(1)}, u32[]{:S(2)}, u32[]{:S(2)}) collective-permute-start(bf16[2,1536,128]{2,1,0:T(8,128)(2,1)} %get-tuple-element.147), channel_id=1, source_target_pairs={{0,1},{1,2},{2,3},{3,0},{4,5},{5,6},{6,7},{7,4},{8,9},{9,10},{10,1... | collective-permute-start | bytes 2359304 | tf_op jit(solution)/shard_map/ppermute | solution.py:46
  198.2 38.6 %collective-permute-start.23 = (bf16[2,1536,128]{2,1,0:T(8,128)(2,1)}, bf16[2,1536,128]{2,1,0:T(8,128)(2,1)S(1)}, u32[]{:S(2)}, u32[]{:S(2)}) collective-permute-start(bf16[2,1536,128]{2,1,0:T(8,128)(2,1)} %get-tuple-element.153), channel_id=1, source_target_pairs={{0,2},{1,3},{2,0},{3,1},{4,6},{5,7},{6,4},{7,5},{8,10},{9,11},{10,... | collective-permute-start | bytes 2359304 | tf_op jit(solution)/shard_map/ppermute | solution.py:46
  202.3 34.6 %collective-permute-start.25 = (bf16[2,1536,128]{2,1,0:T(8,128)(2,1)}, bf16[2,1536,128]{2,1,0:T(8,128)(2,1)S(1)}, u32[]{:S(2)}, u32[]{:S(2)}) collective-permute-start(bf16[2,1536,128]{2,1,0:T(8,128)(2,1)} %get-tuple-element.155), channel_id=1, source_target_pairs={{0,3},{1,0},{2,1},{3,2},{4,7},{5,4},{6,5},{7,6},{8,11},{9,8},{10,9... | collective-permute-start | bytes 2359304 | tf_op jit(solution)/shard_map/ppermute | solution.py:46
  229.1 17.3 %collective-permute-start.22 = (bf16[128,1536]{1,0:T(8,128)(2,1)}, bf16[128,1536]{1,0:T(8,128)(2,1)S(1)}, u32[]{:S(2)}, u32[]{:S(2)}) collective-permute-start(bf16[128,1536]{1,0:T(8,128)(2,1)} %get-tuple-element.152), channel_id=1, source_target_pairs={{0,1},{1,2},{2,3},{3,0},{4,5},{5,6},{6,7},{7,4},{8,9},{9,10},{10,1... | collective-permute-start | bytes 1179656 | tf_op jit(solution)/shard_map/ppermute | solution.py:46
  229.2 24.4 %collective-permute-start.24 = (bf16[128,1536]{1,0:T(8,128)(2,1)}, bf16[128,1536]{1,0:T(8,128)(2,1)S(1)}, u32[]{:S(2)}, u32[]{:S(2)}) collective-permute-start(bf16[128,1536]{1,0:T(8,128)(2,1)} %get-tuple-element.154), channel_id=1, source_target_pairs={{0,2},{1,3},{2,0},{3,1},{4,6},{5,7},{6,4},{7,5},{8,10},{9,11},{10,... | collective-permute-start | bytes 1179656 | tf_op jit(solution)/shard_map/ppermute | solution.py:46
  231.6 21.9 %collective-permute-start.26 = (bf16[128,1536]{1,0:T(8,128)(2,1)}, bf16[128,1536]{1,0:T(8,128)(2,1)}, u32[]{:S(2)}, u32[]{:S(2)}) collective-permute-start(bf16[128,1536]{1,0:T(8,128)(2,1)} %get-tuple-element.156), channel_id=1, source_target_pairs={{0,3},{1,0},{2,1},{3,2},{4,7},{5,4},{6,5},{7,6},{8,11},{9,8},{10,9... | collective-permute-start | bytes 1179656 | tf_op jit(solution)/shard_map/ppermute | solution.py:46
  253.6 66.6 %all-to-all-start.3 = ((bf16[32,48,1536]{2,1,0:T(8,128)(2,1)}), bf16[32,48,1536]{2,1,0:T(8,128)(2,1)}, u32[]{:S(2)}, u32[]{:S(2)}) async-start(bf16[32,48,1536]{2,1,0:T(8,128)(2,1)} %bitcast.59), calls=%async_computation.3 | async-start | bytes 9437184 | tf_op jit(solution)/shard_map/all_to_all | solution.py:782
  268.3 10.8 %collective-permute-start.27 = (bf16[128,1536]{1,0:T(8,128)(2,1)}, bf16[128,1536]{1,0:T(8,128)(2,1)}, u32[]{:S(2)}, u32[]{:S(2)}) collective-permute-start(bf16[128,1536]{1,0:T(8,128)(2,1)} %get-tuple-element.170.refs_0_), channel_id=1, source_target_pairs={{0,3},{1,0},{2,1},{3,2},{4,7},{5,4},{6,5},{7,6},{8,11},{9,8},{10,9... | collective-permute-start | bytes 1179656 | tf_op jit(solution)/shard_map/ppermute | solution.py:42
  270.2 12.0 %collective-permute-start.28 = (bf16[128,1536]{1,0:T(8,128)(2,1)}, bf16[128,1536]{1,0:T(8,128)(2,1)}, u32[]{:S(2)}, u32[]{:S(2)}) collective-permute-start(bf16[128,1536]{1,0:T(8,128)(2,1)} %get-tuple-element.170.refs_0_), channel_id=1, source_target_pairs={{0,2},{1,3},{2,0},{3,1},{4,6},{5,7},{6,4},{7,5},{8,10},{9,11},{10,... | collective-permute-start | bytes 1179656 | tf_op jit(solution)/shard_map/ppermute | solution.py:42
  270.2 21.1 %collective-permute-start.29 = (bf16[128,1536]{1,0:T(8,128)(2,1)}, bf16[128,1536]{1,0:T(8,128)(2,1)}, u32[]{:S(2)}, u32[]{:S(2)}) collective-permute-start(bf16[128,1536]{1,0:T(8,128)(2,1)} %get-tuple-element.170.refs_0_), channel_id=1, source_target_pairs={{0,1},{1,2},{2,3},{3,0},{4,5},{5,6},{6,7},{7,4},{8,9},{9,10},{10,1... | collective-permute-start | bytes 1179656 | tf_op jit(solution)/shard_map/ppermute | solution.py:42
  310.5 4.2 %collective-permute-start.30 = (bf16[16,6,24,384]{3,2,1,0:T(8,128)(2,1)}, bf16[16,6,24,384]{3,2,1,0:T(8,128)(2,1)S(1)}, u32[]{:S(2)}, u32[]{:S(2)}) collective-permute-start(bf16[16,6,24,384]{3,2,1,0:T(8,128)(2,1)} %get-tuple-element.183), channel_id=1, source_target_pairs={{0,4},{4,0},{8,12},{12,8},{16,20},{20,16},{24,28},{28,24},{32,36},... | collective-permute-start | bytes 5308424 | tf_op jit(solution)/shard_map/ppermute | solution.py:50
  320.2 29.1 %all-to-all-start.4 = ((bf16[16,6,24,384]{3,2,1,0:T(8,128)(2,1)}), bf16[16,6,24,384]{3,2,1,0:T(8,128)(2,1)S(1)}, u32[]{:S(2)}, u32[]{:S(2)}) async-start(bf16[16,6,24,384]{3,2,1,0:T(8,128)(2,1)} %add_convert_fusion), calls=%async_computation.4 | async-start | bytes 3538944 | tf_op jit(solution)/shard_map/all_to_all | solution.py:55
  327.0 10.9 %collective-permute-start.31 = (bf16[128,1536]{1,0:T(8,128)(2,1)}, bf16[128,1536]{1,0:T(8,128)(2,1)S(1)}, u32[]{:S(2)}, u32[]{:S(2)}) collective-permute-start(bf16[128,1536]{1,0:T(8,128)(2,1)} %get-tuple-element.189), channel_id=1, source_target_pairs={{0,1},{1,2},{2,3},{3,0},{4,5},{5,6},{6,7},{7,4},{8,9},{9,10},{10,1... | collective-permute-start | bytes 1179656 | tf_op jit(solution)/shard_map/ppermute | solution.py:46
  327.0 19.7 %collective-permute-start.32 = (bf16[128,1536]{1,0:T(8,128)(2,1)}, bf16[128,1536]{1,0:T(8,128)(2,1)S(1)}, u32[]{:S(2)}, u32[]{:S(2)}) collective-permute-start(bf16[128,1536]{1,0:T(8,128)(2,1)} %get-tuple-element.190), channel_id=1, source_target_pairs={{0,2},{1,3},{2,0},{3,1},{4,6},{5,7},{6,4},{7,5},{8,10},{9,11},{10,... | collective-permute-start | bytes 1179656 | tf_op jit(solution)/shard_map/ppermute | solution.py:46
  330.1 17.2 %collective-permute-start.33 = (bf16[128,1536]{1,0:T(8,128)(2,1)S(1)}, bf16[128,1536]{1,0:T(8,128)(2,1)S(1)}, u32[]{:S(2)}, u32[]{:S(2)}) collective-permute-start(bf16[128,1536]{1,0:T(8,128)(2,1)S(1)} %copy-done.23), channel_id=1, source_target_pairs={{0,3},{1,0},{2,1},{3,2},{4,7},{5,4},{6,5},{7,6},{8,11},{9,8},{10,9... | collective-permute-start | bytes 1179656 | tf_op jit(solution)/shard_map/ppermute | solution.py:46
  349.5 2.9 collective-permute-start.34
  351.5 4.1 %collective-permute-start.35 = (bf16[24,384]{1,0:T(8,128)(2,1)S(1)}, bf16[24,384]{1,0:T(8,128)(2,1)S(1)}, u32[]{:S(2)}, u32[]{:S(2)}) collective-permute-start(bf16[24,384]{1,0:T(8,128)(2,1)S(1)} %get-tuple-element.215), channel_id=1, source_target_pairs={{0,2},{1,3},{2,0},{3,1},{4,6},{5,7},{6,4},{7,5},{8,10},{9,11},{10,... | collective-permute-start | bytes 55304 | tf_op jit(solution)/shard_map/ppermute | solution.py:42
  351.5 4.1 %collective-permute-start.36 = (bf16[24,384]{1,0:T(8,128)(2,1)S(1)}, bf16[24,384]{1,0:T(8,128)(2,1)S(1)}, u32[]{:S(2)}, u32[]{:S(2)}) collective-permute-start(bf16[24,384]{1,0:T(8,128)(2,1)S(1)} %get-tuple-element.214), channel_id=1, source_target_pairs={{0,1},{1,2},{2,3},{3,0},{4,5},{5,6},{6,7},{7,4},{8,9},{9,10},{10,1... | collective-permute-start | bytes 55304 | tf_op jit(solution)/shard_map/ppermute | solution.py:42
  355.8 32.8 %copy-start.4 = (bf16[128,1536]{1,0:T(8,128)(2,1)S(1)}, bf16[128,1536]{1,0:T(8,128)(2,1)}, u32[]{:S(2)}) copy-start(bf16[128,1536]{1,0:T(8,128)(2,1)} %refs_4_.1) | copy-start | bytes 1179652
  355.9 32.8 %copy-start.5 = (f32[128,1536]{1,0:T(8,128)S(1)}, f32[128,1536]{1,0:T(8,128)}, u32[]{:S(2)}) copy-start(f32[128,1536]{1,0:T(8,128)} %get-tuple-element.194) | copy-start | bytes 2359300
  383.0 8.1 %collective-permute-start.37 = (bf16[16,6,24,384]{3,2,1,0:T(8,128)(2,1)S(1)}, bf16[16,6,24,384]{3,2,1,0:T(8,128)(2,1)S(1)}, u32[]{:S(2)}, u32[]{:S(2)}) collective-permute-start(bf16[16,6,24,384]{3,2,1,0:T(8,128)(2,1)S(1)} %all_to_all.30.a_ref.ao_ref), channel_id=1, source_target_pairs={{0,4},{4,0},{8,12},{12,8},{16,20},{20,16},{24,28},{28,24},{32,36},... | collective-permute-start | bytes 5308424 | tf_op jit(solution)/shard_map/ppermute | solution.py:50
  (35 other events, 231.5 us)

commit v6 on v5

--- a/solution.py
+++ b/solution.py
@@ -319,38 +319,49 @@
     return tdot(hi, pick) + tdot(lo, pick)
 
 
-def pack_body(experts, place_ref, wq, wk, wv, wr, na, nm, *outs):
+def pack_body(experts, place_ref, x_ref, wq, wk, wv, wr, norms, *outs):
     small = outs[WS + 1]
     me, core = place_ref[0], place_ref[1]
+    rows = x_ref.shape[0]
     strip = wq.shape[0] // 2
     q_w, kv_w = wq.shape[1] // WS, wk.shape[1] // WS
     shard = wq.shape[0]
-    gains = jnp.concatenate(
-        [na[...].astype(F32), nm[...].astype(F32), jnp.zeros((6, shard), F32)], axis=0
-    ).T
-    small[...] = jnp.concatenate(
-        [wr[...].astype(F32), gains, jnp.zeros((shard, 128 - experts - 8), F32)], axis=1
-    ).astype(BF)
+    few = [wr[...].astype(F32), norms[...].astype(F32), jnp.zeros((126 - experts, shard), F32)]
+    small[...] = jnp.concatenate(few, axis=0).T.astype(BF)
+
+    def place(out, top, left, side, d, start, count):
+        part = pl.ds(pl.multiple_of(side * strip + start, 32), count)
+        here = slice(top, top + count)
+        spot = pl.ds(pl.multiple_of(d * kv_w, 128), kv_w)
+        out[here, left : left + q_w] = wq[part, pl.ds(pl.multiple_of(d * q_w, 128), q_w)]
+        out[here, left + q_w : left + q_w + kv_w] = wk[part, spot]
+        out[here, left + q_w + kv_w : left + q_w + 2 * kv_w] = wv[part, spot]
+        out[here, left + q_w + 2 * kv_w : left + q_w + 2 * kv_w + 128] = small[part, :]
+
     for r in range(WS + 1):
         side = core if r < WS else 1 - core
         d = lax.rem(me + WS - r % WS, WS)
-        part = pl.ds(pl.multiple_of(side * strip, 64), strip)
-        outs[r][:, :q_w] = wq[part, pl.ds(pl.multiple_of(d * q_w, 128), q_w)]
-        spot = pl.ds(pl.multiple_of(d * kv_w, 128), kv_w)
-        outs[r][:, q_w : q_w + kv_w] = wk[part, spot]
-        outs[r][:, q_w + kv_w : q_w + 2 * kv_w] = wv[part, spot]
-        outs[r][:, q_w + 2 * kv_w :] = small[part, :]
-
-
-def pack(experts, place, wq, wk, wv, wr, na, nm):
+        if r == 2:
+            outs[r][:rows, :] = x_ref[...]
+            for half in range(2):
+                left = half * (q_w + 2 * kv_w + 128)
+                place(outs[r], rows, left, side, d, half * strip // 2, strip // 2)
+        else:
+            place(outs[r], 0, 0, side, d, 0, strip)
+
+
+def pack(experts, place, x, wq, wk, wv, wr, norms):
     shard = wq.shape[0]
+    rows, width = x.shape
     wide_w = (wq.shape[1] + 2 * wk.shape[1]) // WS + 128
+    outs = [sds((shard // 2, wide_w), BF)] * (WS + 1)
+    outs[2] = sds((rows + shard // 4, 2 * wide_w), BF)
     return one_step(
         functools.partial(pack_body, experts),
         "pack",
         [place],
-        [wq, wk, wv, wr, na[None], nm[None]],
-        [sds((shard // 2, wide_w), BF)] * (WS + 1),
+        [x, wq, wk, wv, wr, norms],
+        outs,
         [pltpu.VMEM((shard, 128), BF)],
         0,
     )
@@ -381,22 +392,27 @@
     me, core = place_ref[0], place_ref[1]
     rows = xs[0].shape[0]
     strip = own[0].shape[0]
+    wide_w = own[0].shape[1]
     q_w = o_ref.shape[1]
     qkv_w = qkv_ref.shape[1]
     kv_w = (qkv_w - q_w) // 2
     for r in range(WS):
         base = lax.rem(me + r, WS) * (2 * strip)
         for source, side in ((own[r], core), (twin[r], 1 - core)):
-            spot = pl.ds(pl.multiple_of(base + side * strip, 64), strip)
-            w_ref[spot, :] = source[:, :qkv_w]
-            small_ref[spot, :] = source[:, qkv_w:]
+            folds = source.shape[1] // wide_w
+            count = strip // folds
+            for f in range(folds):
+                left = f * wide_w
+                spot = pl.ds(pl.multiple_of(base + side * strip + f * count, 32), count)
+                w_ref[spot, :] = source[:, left : left + qkv_w]
+                small_ref[spot, :] = source[:, left + qkv_w : left + wide_w]
     turned = small_ref[...].astype(F32).T
     rows_ref[...] = jnp.concatenate(
         [turned[experts : experts + 2], jnp.zeros((6, turned.shape[1]), F32)], axis=0
     )
     gain = turned[experts : experts + 1]
     for r in range(WS):
-        x = xs[r][...].astype(F32)
+        x = xs[r][:rows, :].astype(F32)
         h1_ref[r * rows : (r + 1) * rows, :] = (x * rms(x) * gain).astype(BF)
     qkv = dot(h1_ref[...], w_ref[...])
     qk = qkv[:, : q_w + kv_w]
@@ -423,7 +439,7 @@
         sds((width, 128), BF),
         sds((8, width), F32),
     ] + [sds((rows, width), BF)] * 3
-    flops = 2 * tree * width * (qkv_w + q_w) + 4 * tree * tree * q_w
+    flops = 27 * tree * width * (qkv_w + q_w)
     return one_step(
         functools.partial(attend_body, experts),
         "attend",
@@ -627,7 +643,7 @@
     for r in range(WS):
         dh1 = dot_t(dqkv[r * rows : (r + 1) * rows, :qkv_w], w_ref[...])
         parts[r][...] = dh1.astype(parts[r].dtype)
-        x = xs[r][...].astype(F32)
+        x = xs[r][:rows, :].astype(F32)
         small = small + column_sum(dh1 * x * rms(x), experts + 1)
     half = keep_ref.shape[3]
     chips, step = keep_ref.shape[0], keep_ref.shape[2]
@@ -707,11 +723,11 @@
     def gathered(v):
         return [v] + [from_peer(v, k) for k in (1, 2, 3)]
 
-    xs = gathered(tokens)
-
-    pieces = pack(experts, place, w_query, w_key, w_value, w_router, norm_attn, norm_moe)
-    pieces, routes = lax.optimization_barrier((pieces, routes))
-    own = [pieces[0]] + [from_peer(pieces[k], k) for k in (1, 2, 3)]
+    norms = jnp.stack([norm_attn, norm_moe])
+    pieces = pack(experts, place, tokens, w_query, w_key, w_value, w_router.T, norms)
+    came = [None] + [from_peer(pieces[k], k) for k in (1, 2, 3)]
+    xs = [tokens, from_peer(tokens, 1), came[2], from_peer(tokens, 3)]
+    own = [pieces[0], came[1], came[2][rows:], came[3]]
 
     labels = jnp.arange(experts, dtype=jnp.int32)
     lane = jnp.arange(128, dtype=jnp.int32)
@@ -726,7 +742,6 @@
     chosen = chosen.astype(BF)
     extra = jnp.concatenate([cotangent, chosen], axis=1)
     dy_send = tdot(to_slot, extra).astype(BF).reshape(experts, CAP, width + 128)
-    dy_send, xs[1], xs[3] = lax.optimization_barrier((dy_send, xs[1], xs[3]))
     dy_slots = lax.all_to_all(dy_send, "exp", 0, 0, tiled=True).reshape(slots, width + 128)
 
     order = (

time: 407 us -> 418 us (1.027)
  waiting for transfers between devices: 136 us -> 158 us
  starting transfers between devices: 96.9 us -> 90.1 us
  local copies, waits for them, and re-layouts: 11.6 us -> 7.42 us
    ppermute x12, waiting for transfers between devices: 63.1 us -> 76.6 us  [to_peer(): return lax.ppermute(v, 'ws', [(s, (s + k) % WS) for s in range(WS)])]
    ppermute x21 -> x20, waiting for transfers between devices: 60.3 us -> 69.8 us  [from_peer(): return lax.ppermute(v, 'ws', [(s, (s - k) % WS) for s in range(WS)])]
    ppermute x21 -> x20, starting transfers between devices: 35.1 us -> 29.9 us  [from_peer(): return lax.ppermute(v, 'ws', [(s, (s - k) % WS) for s in range(WS)])]
  transfers between devices with their start and end apart: 43 -> 42, of which waited for: 28 -> 29; matrix products, arithmetic and copies ran while one was open for 8% -> 7% of each run, Pallas kernels for 19% -> 18%
where the time goes in v6:
time: 418 us; the launch traced here: 412 us
  waiting for transfers between devices  158 us (38%)
  Pallas kernels  103 us (25%)
  starting transfers between devices  90.1 us (22%)
  blocking collectives  27.1 us (6%)
  other arithmetic  14.2 us (3%)
  matrix products  11.2 us (3%)
  local copies, waits for them, and re-layouts  7.42 us (2%)
    ppermute x12, waiting for transfers between devices, to_peer(): return lax.ppermute(v, 'ws', [(s, (s + k) % WS) for s in range(WS)])  76.6 us
    ppermute x20, waiting for transfers between devices, from_peer(): return lax.ppermute(v, 'ws', [(s, (s - k) % WS) for s in range(WS)])  69.8 us
    pallas_call x6, Pallas kernels, one_step(): pl.pallas_call(body, in_specs=[pl.BlockSpec(memory_space=pltpu.SMEM)] * l...  43.5 us
    ppermute x20, starting transfers between devices, from_peer(): return lax.ppermute(v, 'ws', [(s, (s - k) % WS) for s in range(WS)])  29.9 us
    all_to_all x1, blocking collectives, same_core(): return lax.all_to_all(v, 'exp', 0, 0, tiled=True, axis_index_groups=groups)  27.1 us
    pallas_call x1, Pallas kernels, expert_pass(): pl.pallas_call(functools.partial(expert_body, width, ff), grid=(slots //...  20.7 us
    ppermute x12, starting transfers between devices, to_peer(): return lax.ppermute(v, 'ws', [(s, (s + k) % WS) for s in range(WS)])  11.1 us
    pallas_call x1, Pallas kernels, out_slopes(): pl.pallas_call(out_slope_body, grid=(width // tile,), in_specs=[whole(h.s...  10.1 us
  transfers between devices with their start and end apart: 42, of which 29 were waited for; matrix products, arithmetic and copies ran while one was open for 7% of the time, Pallas kernels for 18%

profile of v6, /device:TPU:1, one launch (start us, length us, event | category | flops | bytes accessed | tf_op | source)
XLA Modules:
  0.0 412.3 jit_solution(4040337899892400070)
XLA Ops:
  0.7 3.6 collective-permute-start
  6.6 3.9 convolution_convert_fusion
  10.5 9.1 %all-to-all-start.1 = ((bf16[32,48,1664]{2,1,0:T(8,128)(2,1)}), bf16[32,48,1664]{2,1,0:T(8,128)(2,1)}, u32[]{:S(2)}, u32[]{:S(2)}) async-start(bf16[32,48,1664]{2,1,0:T(8,128)(2,1)} %bitcast.58), calls=%async_computation.1 | async-start | bytes 10223616 | tf_op jit(solution)/shard_map/all_to_all | solution.py:745
  20.8 3.0 pack.1
  23.8 2.9 collective-permute-start.3
  31.8 16.0 %collective-permute-done.3.refs_5_ = bf16[192,768]{1,0:T(8,128)(2,1)S(1)} collective-permute-done((bf16[192,768]{1,0:T(8,128)(2,1)}, bf16[192,768]{1,0:T(8,128)(2,1)S(1)}, u32[]{:S(2)}, u32[]{:S(2)}) %collective-permute-start.3) | collective-permute-done | bytes 294944 | tf_op jit(solution)/shard_map/ppermute | solution.py:42
  49.0 2.6 collective-permute-done.4.refs_7_
  55.2 9.7 %attend.1 = (bf16[512,1536]{1,0:T(8,128)(2,1)}, bf16[512,640]{1,0:T(8,128)(2,1)}, bf16[384,384]{1,0:T(8,128)(2,1)}, f32[384,128]{1,0:T(8,128)}, bf16[1536,640]{1...) custom-call(s32[2]{0:T(128)} %pad_add_fusion.place_ref, ...), custom_call_target="tpu_custom_call" | custom-call | flops 21743271936 | bytes 6979584 | tf_op jit(solution)/shard_map/attend/pallas_call | solution.py:287
  66.9 5.4 %attend_own.1 = (bf16[128,384]{1,0:T(8,128)(2,1)}, f32[128,128]{1,0:T(8,128)}, f32[128,1536]{1,0:T(8,128)}) custom-call(bf16[512,640]{1,0:T(8,128)(2,1)} %get-tuple-element.110.qkv_ref.refs_9_, f32[512,512]{1,0:T(8,128)} %fusion.3.refs_14_.bias_ref.refs_18_, bf16[384,1536]{1,0:T(8,128)(2,1)} %refs_8_.1), custom_call_target="tpu_custom_call" | custom-call | flops 251658240 | bytes 2883584 | tf_op jit(solution)/shard_map/attend_own/pallas_call | solution.py:287
  72.2 3.6 collective-permute-done.10.p3
  75.9 9.8 %collective-permute-done.8.p1 = bf16[128,1536]{1,0:T(8,128)(2,1)S(1)} collective-permute-done((bf16[128,1536]{1,0:T(8,128)(2,1)}, bf16[128,1536]{1,0:T(8,128)(2,1)S(1)}, u32[]{:S(2)}, u32[]{:S(2)}) %collective-permute-start.8) | collective-permute-done | bytes 393248 | tf_op jit(solution)/shard_map/ppermute | solution.py:46
  86.6 5.6 %enter.1 = (f32[128,1536]{1,0:T(8,128)}, bf16[128,1536]{1,0:T(8,128)(2,1)}, bf16[1536,1536]{1,0:T(8,128)(2,1)}) custom-call(bf16[128,1536]{1,0:T(8,128)(2,1)} %refs_4_.1, f32[128,1536]{1,0:T(8,128)} %get-tuple-element.111.p0, bf16[128,1536]{1,0:T(8,128)(2,1)} %copy-done.11, bf16[128,1536]{1,0:T(8,128)(2,1)} %copy-done.12, bf16[128,1536]{1,0:T(8,128)(2,1)} %copy-done.10, ...), custom_call_target="tpu_custom_call" | custom-call | flops 603979776 | bytes 7077888 | tf_op jit(solution)/shard_map/enter/pallas_call | solution.py:484
  92.2 8.5 %all-to-all-start = ((bf16[32,48,1536]{2,1,0:T(8,128)(2,1)}), bf16[32,48,1536]{2,1,0:T(8,128)(2,1)}, u32[]{:S(2)}, u32[]{:S(2)}) async-start(bf16[32,48,1536]{2,1,0:T(8,128)(2,1)} %bitcast.61), calls=%async_computation | async-start | bytes 9437184 | tf_op jit(solution)/shard_map/all_to_all | solution.py:767
  104.8 2.7 collective-permute-start.14
  107.4 3.8 collective-permute-done.17.rest_9_.refs_1_
  112.3 7.4 %collective-permute-done.11.rest_1_ = bf16[1536,128]{1,0:T(8,128)(2,1)S(1)} collective-permute-done((bf16[1536,128]{1,0:T(8,128)(2,1)S(1)}, bf16[1536,128]{1,0:T(8,128)(2,1)S(1)}, u32[]{:S(2)}, u32[]{:S(2)}) %collective-permute-start.11) | collective-permute-done | bytes 393248 | tf_op jit(solution)/shard_map/ppermute | solution.py:42
  119.7 3.0 collective-permute-start.18
  124.3 7.0 %collective-permute-start.19 = (bf16[128,1536]{1,0:T(8,128)(2,1)S(1)}, bf16[128,1536]{1,0:T(8,128)(2,1)S(1)}, u32[]{:S(2)}, u32[]{:S(2)}) collective-permute-start(bf16[128,1536]{1,0:T(8,128)(2,1)S(1)} %bitcast.80), channel_id=1, source_target_pairs={{0,1},{1,2},{2,3},{3,0},{4,5},{5,6},{6,7},{7,4},{8,9},{9,10},{10,1... | collective-permute-start | bytes 1179656 | tf_op jit(solution)/shard_map/ppermute | solution.py:42
  132.1 3.0 gate_terms.1
  136.6 4.3 %collective-permute-done.16.rest_7_ = bf16[1536,128]{1,0:T(8,128)(2,1)} collective-permute-done((bf16[1536,128]{1,0:T(8,128)(2,1)S(1)}, bf16[1536,128]{1,0:T(8,128)(2,1)}, u32[]{:S(2)}, u32[]{:S(2)}) %collective-permute-start.16) | collective-permute-done | bytes 393248 | tf_op jit(solution)/shard_map/ppermute | solution.py:42
  140.9 6.3 %collective-permute-done.18.rest_10_.refs_2_ = bf16[128,1536]{1,0:T(8,128)(2,1)S(1)} collective-permute-done((bf16[128,1536]{1,0:T(8,128)(2,1)S(1)}, bf16[128,1536]{1,0:T(8,128)(2,1)S(1)}, u32[]{:S(2)}, u32[]{:S(2)}) %collective-permute-start.18) | collective-permute-done | bytes 393248 | tf_op jit(solution)/shard_map/ppermute | solution.py:42
  147.3 9.4 %collective-permute-done.19.rest_11_.refs_3_ = bf16[128,1536]{1,0:T(8,128)(2,1)S(1)} collective-permute-done((bf16[128,1536]{1,0:T(8,128)(2,1)S(1)}, bf16[128,1536]{1,0:T(8,128)(2,1)S(1)}, u32[]{:S(2)}, u32[]{:S(2)}) %collective-permute-start.19) | collective-permute-done | bytes 393248 | tf_op jit(solution)/shard_map/ppermute | solution.py:42
  156.7 2.4 all-to-all-done
  159.1 20.7 %expert_pass.1 = (bf16[1536,1664]{1,0:T(8,128)(2,1)}, bf16[1536,512]{1,0:T(8,128)(2,1)}, bf16[1536,1024]{1,0:T(8,128)(2,1)}, f32[1536,128]{1,0:T(8,128)}) custom-call(bf16[1536,1536]{1,0:T(8,128)(2,1)} %bitcast.15.x_ref, bf16[1536,1664]{1,0:T(8,128)(2,1)} %bitcast.17.dy_ref, f32[8,128]{1,0:T(8,128)} %maximum_maximum_fusion.sel_ref, ...), custom_call_target="tpu_custom_call" | custom-call | flops 12079595520 | bytes 21233664 | tf_op jit(solution)/shard_map/expert_pass/pallas_call | solution.py:120
  179.9 7.8 %all-to-all-start.2 = ((bf16[32,48,1664]{2,1,0:T(8,128)(2,1)}), bf16[32,48,1664]{2,1,0:T(8,128)(2,1)}, u32[]{:S(2)}, u32[]{:S(2)}) async-start(bf16[32,48,1664]{2,1,0:T(8,128)(2,1)} %bitcast.59), calls=%async_computation.2 | async-start | bytes 10223616 | tf_op jit(solution)/shard_map/all_to_all | solution.py:785
  187.7 9.8 %in_slopes.1 = (f32[1536,128]{1,0:T(8,128)}, f32[1536,128]{1,0:T(8,128)}, bf16[2,1536,128]{2,1,0:T(8,128)(2,1)}, bf16[2,1536,128]{2,1,0:T(8,128)(2,1)}, bf16[2,1536,128]{2,1,0:T(8,128)(2,1)}) custom-call(bf16[1536,1536]{1,0:T(8,128)(2,1)} %bitcast.15.x_ref, bf16[1536,1024]{1,0:T(8,128)(2,1)} %get-tuple-element.128.dgu_ref), custom_call_target="tpu_custom_call" | custom-call | flops 4831838208 | bytes 9437184 | tf_op jit(solution)/shard_map/in_slopes/pallas_call | solution.py:157
  200.6 33.6 %collective-permute-done.20 = bf16[2,1536,128]{2,1,0:T(8,128)(2,1)S(1)} collective-permute-done((bf16[2,1536,128]{2,1,0:T(8,128)(2,1)}, bf16[2,1536,128]{2,1,0:T(8,128)(2,1)S(1)}, u32[]{:S(2)}, u32[]{:S(2)}) %collective-permute-start.20) | collective-permute-done | bytes 786464 | tf_op jit(solution)/shard_map/ppermute | solution.py:46
  234.2 10.1 %out_slopes.1 = (bf16[1536,1536]{1,0:T(8,128)(2,1)}, f32[128,1536]{1,0:T(8,128)}, bf16[128,1536]{1,0:T(8,128)(2,1)}, bf16[128,1536]{1,0:T(8,128)(2,1)}, bf16[128,1536]{1,0:T(8,128)(2,1)}) custom-call(bf16[1536,512]{1,0:T(8,128)(2,1)} %get-tuple-element.130.h_ref, bf16[1536,1664]{1,0:T(8,128)(2,1)} %bitcast.17.dy_ref, ...), custom_call_target="tpu_custom_call" | custom-call | flops 4831838208 | bytes 9437184 | tf_op jit(solution)/shard_map/out_slopes/pallas_call | solution.py:191
  244.5 2.6 collective-permute-start.25
  247.1 17.1 %collective-permute-done.21 = bf16[128,1536]{1,0:T(8,128)(2,1)S(1)} collective-permute-done((bf16[128,1536]{1,0:T(8,128)(2,1)}, bf16[128,1536]{1,0:T(8,128)(2,1)S(1)}, u32[]{:S(2)}, u32[]{:S(2)}) %collective-permute-start.21) | collective-permute-done | bytes 393248 | tf_op jit(solution)/shard_map/ppermute | solution.py:46
  264.3 9.1 %all-to-all-start.3 = ((bf16[32,48,1536]{2,1,0:T(8,128)(2,1)}), bf16[32,48,1536]{2,1,0:T(8,128)(2,1)}, u32[]{:S(2)}, u32[]{:S(2)}) async-start(bf16[32,48,1536]{2,1,0:T(8,128)(2,1)} %bitcast.60), calls=%async_computation.3 | async-start | bytes 9437184 | tf_op jit(solution)/shard_map/all_to_all | solution.py:797
  273.5 6.5 %leave.1 = (f32[128,1536]{1,0:T(8,128)}, bf16[128,1536]{1,0:T(8,128)(2,1)}, f32[128,1536]{1,0:T(8,128)}, f32[128,128]{1,0:T(8,128)}) custom-call(bf16[1536,1664]{1,0:T(8,128)(2,1)} %bitcast.19.back_ref, bf16[128,1536]{1,0:T(8,128)(2,1)} %get-tuple-element.204.slot_ref, f32[128,128]{1,0:T(8,128)} %get-tuple-element.140.gates_ref, ...), custom_call_target="tpu_custom_call" | custom-call | flops 603979776 | bytes 7077888 | tf_op jit(solution)/shard_map/leave/pallas_call | solution.py:561
  282.9 3.2 small_slopes.1.refs_19_
  286.1 2.2 add_bitcast_fusion
  290.9 3.1 collective-permute-done.27.refs_2_
  294.0 9.1 %collective-permute-done.28.refs_3_ = bf16[128,1536]{1,0:T(8,128)(2,1)} collective-permute-done((bf16[128,1536]{1,0:T(8,128)(2,1)}, bf16[128,1536]{1,0:T(8,128)(2,1)}, u32[]{:S(2)}, u32[]{:S(2)}) %collective-permute-start.28) | collective-permute-done | bytes 393248 | tf_op jit(solution)/shard_map/ppermute | solution.py:42
  303.1 19.2 %attend_back.1 = (f32[16,6,24,384]{3,2,1,0:T(8,128)}, bf16[16,6,24,384]{3,2,1,0:T(8,128)(2,1)}, f32[128,1536]{1,0:T(8,128)}, bf16[128,1536]{1,0:T(8,128)(2,1)}, ...) custom-call(s32[2]{0:T(128)} %pad_add_fusion.place_ref, bf16[128,1536]{1,0:T(8,128)(2,1)} %get-tuple-element.152.refs_0_, ...), custom_call_target="tpu_custom_call" | custom-call | flops 4227858432 | bytes 11829248 | tf_op jit(solution)/shard_map/attend_back/pallas_call | solution.py:287
  323.0 3.5 collective-permute-done.29
  326.5 3.6 add_convert_fusion
  331.9 6.7 %all-to-all-start.4 = ((bf16[16,6,24,384]{3,2,1,0:T(8,128)(2,1)}), bf16[16,6,24,384]{3,2,1,0:T(8,128)(2,1)S(1)}, u32[]{:S(2)}, u32[]{:S(2)}) async-start(bf16[16,6,24,384]{3,2,1,0:T(8,128)(2,1)} %add_convert_fusion), calls=%async_computation.4 | async-start | bytes 3538944 | tf_op jit(solution)/shard_map/all_to_all | solution.py:55
  338.7 3.2 collective-permute-start.31
  341.9 4.0 fusion.58
  346.8 2.7 collective-permute-done.30
  349.6 9.0 %collective-permute-done.31 = bf16[128,1536]{1,0:T(8,128)(2,1)S(1)} collective-permute-done((bf16[128,1536]{1,0:T(8,128)(2,1)}, bf16[128,1536]{1,0:T(8,128)(2,1)S(1)}, u32[]{:S(2)}, u32[]{:S(2)}) %collective-permute-start.31) | collective-permute-done | bytes 393248 | tf_op jit(solution)/shard_map/ppermute | solution.py:46
  364.2 3.2 collective-permute-done.34
  367.7 27.1 %all_to_all.30.a_ref.ao_ref = bf16[16,6,24,384]{3,2,1,0:T(8,128)(2,1)S(1)} all-to-all(bf16[16,6,24,384]{3,2,1,0:T(8,128)(2,1)S(1)} %broadcast_in_dim.76), channel_id=1, replica_groups={{0,8,16,24,32,40,48,56,64,72,80,88,96,104,112,120},{4,12,20,28,36,44,52..., dimensions={0} | all-to-all | bytes 3538944 | tf_op jit(solution)/shard_map/all_to_all | solution.py:55
  394.8 4.8 %collective-permute-start.36 = (bf16[16,6,24,384]{3,2,1,0:T(8,128)(2,1)S(1)}, bf16[16,6,24,384]{3,2,1,0:T(8,128)(2,1)S(1)}, u32[]{:S(2)}, u32[]{:S(2)}) collective-permute-start(bf16[16,6,24,384]{3,2,1,0:T(8,128)(2,1)S(1)} %all_to_all.30.a_ref.ao_ref), channel_id=1, source_target_pairs={{0,4},{4,0},{8,12},{12,8},{16,20},{20,16},{24,28},{28,24},{32,36},... | collective-permute-start | bytes 5308424 | tf_op jit(solution)/shard_map/ppermute | solution.py:50
  404.1 6.3 %finish.1 = (f32[384,1536]{1,0:T(8,128)}, f32[384,512]{1,0:T(8,128)}, f32[384,512]{1,0:T(8,128)}, f32[32,384]{1,0:T(8,128)}, f32[8,384]{1,0:T(8,128)}, /*index=5*/f32[384,1536]{1,0:T(8,128)}) custom-call(s32[2]{0:T(128)} %pad_add_fusion.place_ref, bf16[16,6,24,384]{3,2,1,0:T(8,128)(2,1)} %copy-done, bf16[16,6,24,384]{3,2,1,0:T(8,128)(2,1)} %copy-done.1, ...), custom_call_target="tpu_custom_call" | custom-call | bytes 9437184 | tf_op jit(solution)/shard_map/finish/pallas_call | solution.py:247
  (171 shorter events, 49.3 us)
Async XLA Ops:
  0.7 52.3 %collective-permute-start = (bf16[128,1536]{1,0:T(8,128)(2,1)}, bf16[128,1536]{1,0:T(8,128)(2,1)S(1)}, u32[]{:S(2)}, u32[]{:S(2)}) collective-permute-start(bf16[128,1536]{1,0:T(8,128)(2,1)} %refs_4_.1), channel_id=1, source_target_pairs={{0,3},{1,0},{2,1},{3,2},{4,7},{5,4},{6,5},{7,6},{8,11},{9,8},{10,9... | collective-permute-start | bytes 1179656 | tf_op jit(solution)/shard_map/ppermute | solution.py:42
  4.3 48.7 %collective-permute-start.2 = (bf16[128,1536]{1,0:T(8,128)(2,1)}, bf16[128,1536]{1,0:T(8,128)(2,1)S(1)}, u32[]{:S(2)}, u32[]{:S(2)}) collective-permute-start(bf16[128,1536]{1,0:T(8,128)(2,1)} %refs_4_.1), channel_id=1, source_target_pairs={{0,1},{1,2},{2,3},{3,0},{4,5},{5,6},{6,7},{7,4},{8,9},{9,10},{10,1... | collective-permute-start | bytes 1179656 | tf_op jit(solution)/shard_map/ppermute | solution.py:42
  10.5 81.7 %all-to-all-start.1 = ((bf16[32,48,1664]{2,1,0:T(8,128)(2,1)}), bf16[32,48,1664]{2,1,0:T(8,128)(2,1)}, u32[]{:S(2)}, u32[]{:S(2)}) async-start(bf16[32,48,1664]{2,1,0:T(8,128)(2,1)} %bitcast.58), calls=%async_computation.1 | async-start | bytes 10223616 | tf_op jit(solution)/shard_map/all_to_all | solution.py:745
  23.8 24.0 %collective-permute-start.3 = (bf16[192,768]{1,0:T(8,128)(2,1)}, bf16[192,768]{1,0:T(8,128)(2,1)S(1)}, u32[]{:S(2)}, u32[]{:S(2)}) collective-permute-start(bf16[192,768]{1,0:T(8,128)(2,1)} %get-tuple-element.103), channel_id=1, source_target_pairs={{0,3},{1,0},{2,1},{3,2},{4,7},{5,4},{6,5},{7,6},{8,11},{9,8},{10,9... | collective-permute-start | bytes 884744 | tf_op jit(solution)/shard_map/ppermute | solution.py:42
  26.7 25.6 %collective-permute-start.1 = (bf16[224,1536]{1,0:T(8,128)(2,1)}, bf16[224,1536]{1,0:T(8,128)(2,1)S(1)}, u32[]{:S(2)}, u32[]{:S(2)}) collective-permute-start(bf16[224,1536]{1,0:T(8,128)(2,1)} %get-tuple-element.101), channel_id=1, source_target_pairs={{0,2},{1,3},{2,0},{3,1},{4,6},{5,7},{6,4},{7,5},{8,10},{9,11},{10,... | collective-permute-start | bytes 2064392 | tf_op jit(solution)/shard_map/ppermute | solution.py:42
  26.7 24.9 %collective-permute-start.4 = (bf16[192,768]{1,0:T(8,128)(2,1)}, bf16[192,768]{1,0:T(8,128)(2,1)S(1)}, u32[]{:S(2)}, u32[]{:S(2)}) collective-permute-start(bf16[192,768]{1,0:T(8,128)(2,1)} %get-tuple-element.105), channel_id=1, source_target_pairs={{0,1},{1,2},{2,3},{3,0},{4,5},{5,6},{6,7},{7,4},{8,9},{9,10},{10,1... | collective-permute-start | bytes 884744 | tf_op jit(solution)/shard_map/ppermute | solution.py:42
  47.7 5.2 %collective-permute-start.5 = (bf16[192,768]{1,0:T(8,128)(2,1)S(1)}, bf16[192,768]{1,0:T(8,128)(2,1)S(1)}, u32[]{:S(2)}, u32[]{:S(2)}) collective-permute-start(bf16[192,768]{1,0:T(8,128)(2,1)S(1)} %collective-permute-done.3.refs_5_), channel_id=1, source_target_pairs={{0,4},{4,0},{8,12},{12,8},{16,20},{20,16},{24,28},{28,24},{32,36},... | collective-permute-start | bytes 884744 | tf_op jit(solution)/shard_map/ppermute | solution.py:50
  51.6 1.9 collective-permute-start.7
  52.4 2.1 collective-permute-start.6
  64.9 11.0 %collective-permute-start.10 = (bf16[128,1536]{1,0:T(8,128)(2,1)}, bf16[128,1536]{1,0:T(8,128)(2,1)S(1)}, u32[]{:S(2)}, u32[]{:S(2)}) collective-permute-start(bf16[128,1536]{1,0:T(8,128)(2,1)} %get-tuple-element.114), channel_id=1, source_target_pairs={{0,3},{1,0},{2,1},{3,2},{4,7},{5,4},{6,5},{7,6},{8,11},{9,8},{10,9... | collective-permute-start | bytes 1179656 | tf_op jit(solution)/shard_map/ppermute | solution.py:46
  65.6 20.1 %collective-permute-start.8 = (bf16[128,1536]{1,0:T(8,128)(2,1)}, bf16[128,1536]{1,0:T(8,128)(2,1)S(1)}, u32[]{:S(2)}, u32[]{:S(2)}) collective-permute-start(bf16[128,1536]{1,0:T(8,128)(2,1)} %get-tuple-element.112), channel_id=1, source_target_pairs={{0,1},{1,2},{2,3},{3,0},{4,5},{5,6},{6,7},{7,4},{8,9},{9,10},{10,1... | collective-permute-start | bytes 1179656 | tf_op jit(solution)/shard_map/ppermute | solution.py:46
  66.4 19.3 %collective-permute-start.9 = (bf16[128,1536]{1,0:T(8,128)(2,1)}, bf16[128,1536]{1,0:T(8,128)(2,1)S(1)}, u32[]{:S(2)}, u32[]{:S(2)}) collective-permute-start(bf16[128,1536]{1,0:T(8,128)(2,1)} %get-tuple-element.113), channel_id=1, source_target_pairs={{0,2},{1,3},{2,0},{3,1},{4,6},{5,7},{6,4},{7,5},{8,10},{9,11},{10,... | collective-permute-start | bytes 1179656 | tf_op jit(solution)/shard_map/ppermute | solution.py:46
  92.2 12.6 %copy-start.20 = (bf16[1,1536,128]{2,1,0:T(8,128)(2,1)S(1)}, bf16[1,1536,128]{2,1,0:T(8,128)(2,1)}, u32[]{:S(2)}) copy-start(bf16[1,1536,128]{2,1,0:T(8,128)(2,1)} %param.28) | copy-start | bytes 1179652
  92.2 66.9 %all-to-all-start = ((bf16[32,48,1536]{2,1,0:T(8,128)(2,1)}), bf16[32,48,1536]{2,1,0:T(8,128)(2,1)}, u32[]{:S(2)}, u32[]{:S(2)}) async-start(bf16[32,48,1536]{2,1,0:T(8,128)(2,1)} %bitcast.61), calls=%async_computation | async-start | bytes 9437184 | tf_op jit(solution)/shard_map/all_to_all | solution.py:767
  100.7 10.6 %collective-permute-start.17 = (bf16[128,1536]{1,0:T(8,128)(2,1)S(1)}, bf16[128,1536]{1,0:T(8,128)(2,1)S(1)}, u32[]{:S(2)}, u32[]{:S(2)}) collective-permute-start(bf16[128,1536]{1,0:T(8,128)(2,1)S(1)} %bitcast.78), channel_id=1, source_target_pairs={{0,3},{1,0},{2,1},{3,2},{4,7},{5,4},{6,5},{7,6},{8,11},{9,8},{10,9... | collective-permute-start | bytes 1179656 | tf_op jit(solution)/shard_map/ppermute | solution.py:42
  101.2 18.5 %collective-permute-start.11 = (bf16[1536,128]{1,0:T(8,128)(2,1)S(1)}, bf16[1536,128]{1,0:T(8,128)(2,1)S(1)}, u32[]{:S(2)}, u32[]{:S(2)}) collective-permute-start(bf16[1536,128]{1,0:T(8,128)(2,1)S(1)} %bitcast.69), channel_id=1, source_target_pairs={{0,3},{1,0},{2,1},{3,2},{4,7},{5,4},{6,5},{7,6},{8,11},{9,8},{10,9... | collective-permute-start | bytes 1179656 | tf_op jit(solution)/shard_map/ppermute | solution.py:42
  102.1 17.6 %collective-permute-start.12 = (bf16[1536,128]{1,0:T(8,128)(2,1)S(1)}, bf16[1536,128]{1,0:T(8,128)(2,1)S(1)}, u32[]{:S(2)}, u32[]{:S(2)}) collective-permute-start(bf16[1536,128]{1,0:T(8,128)(2,1)S(1)} %bitcast.70), channel_id=1, source_target_pairs={{0,2},{1,3},{2,0},{3,1},{4,6},{5,7},{6,4},{7,5},{8,10},{9,11},{10,... | collective-permute-start | bytes 1179656 | tf_op jit(solution)/shard_map/ppermute | solution.py:42
  104.0 20.3 %collective-permute-start.13 = (bf16[1536,128]{1,0:T(8,128)(2,1)S(1)}, bf16[1536,128]{1,0:T(8,128)(2,1)}, u32[]{:S(2)}, u32[]{:S(2)}) collective-permute-start(bf16[1536,128]{1,0:T(8,128)(2,1)S(1)} %bitcast.71), channel_id=1, source_target_pairs={{0,1},{1,2},{2,3},{3,0},{4,5},{5,6},{6,7},{7,4},{8,9},{9,10},{10,1... | collective-permute-start | bytes 1179656 | tf_op jit(solution)/shard_map/ppermute | solution.py:42
  104.8 31.8 %collective-permute-start.14 = (bf16[1536,128]{1,0:T(8,128)(2,1)S(1)}, bf16[1536,128]{1,0:T(8,128)(2,1)S(1)}, u32[]{:S(2)}, u32[]{:S(2)}) collective-permute-start(bf16[1536,128]{1,0:T(8,128)(2,1)S(1)} %bitcast.73), channel_id=1, source_target_pairs={{0,3},{1,0},{2,1},{3,2},{4,7},{5,4},{6,5},{7,6},{8,11},{9,8},{10,9... | collective-permute-start | bytes 1179656 | tf_op jit(solution)/shard_map/ppermute | solution.py:42
  111.3 47.8 %copy-start.25 = (bf16[128,1536]{1,0:T(8,128)(2,1)}, bf16[128,1536]{1,0:T(8,128)(2,1)S(1)}, u32[]{:S(2)}) copy-start(bf16[128,1536]{1,0:T(8,128)(2,1)S(1)} %collective-permute-done.17.rest_9_.refs_1_) | copy-start | bytes 1179652
  111.3 25.3 %collective-permute-start.15 = (bf16[1536,128]{1,0:T(8,128)(2,1)S(1)}, bf16[1536,128]{1,0:T(8,128)(2,1)}, u32[]{:S(2)}, u32[]{:S(2)}) collective-permute-start(bf16[1536,128]{1,0:T(8,128)(2,1)S(1)} %bitcast.74), channel_id=1, source_target_pairs={{0,2},{1,3},{2,0},{3,1},{4,6},{5,7},{6,4},{7,5},{8,10},{9,11},{10,... | collective-permute-start | bytes 1179656 | tf_op jit(solution)/shard_map/ppermute | solution.py:42
  119.7 39.4 %copy-start.26 = (bf16[1536,128]{1,0:T(8,128)(2,1)}, bf16[1536,128]{1,0:T(8,128)(2,1)S(1)}, u32[]{:S(2)}) copy-start(bf16[1536,128]{1,0:T(8,128)(2,1)S(1)} %collective-permute-done.11.rest_1_) | copy-start | bytes 1179652
  119.7 21.2 %collective-permute-start.16 = (bf16[1536,128]{1,0:T(8,128)(2,1)S(1)}, bf16[1536,128]{1,0:T(8,128)(2,1)}, u32[]{:S(2)}, u32[]{:S(2)}) collective-permute-start(bf16[1536,128]{1,0:T(8,128)(2,1)S(1)} %bitcast.75), channel_id=1, source_target_pairs={{0,1},{1,2},{2,3},{3,0},{4,5},{5,6},{6,7},{7,4},{8,9},{9,10},{10,1... | collective-permute-start | bytes 1179656 | tf_op jit(solution)/shard_map/ppermute | solution.py:42
  119.7 39.4 %copy-start.27 = (bf16[1536,128]{1,0:T(8,128)(2,1)}, bf16[1536,128]{1,0:T(8,128)(2,1)S(1)}, u32[]{:S(2)}) copy-start(bf16[1536,128]{1,0:T(8,128)(2,1)S(1)} %collective-permute-done.12.rest_2_) | copy-start | bytes 1179652
  119.7 27.6 %collective-permute-start.18 = (bf16[128,1536]{1,0:T(8,128)(2,1)S(1)}, bf16[128,1536]{1,0:T(8,128)(2,1)S(1)}, u32[]{:S(2)}, u32[]{:S(2)}) collective-permute-start(bf16[128,1536]{1,0:T(8,128)(2,1)S(1)} %bitcast.79), channel_id=1, source_target_pairs={{0,2},{1,3},{2,0},{3,1},{4,6},{5,7},{6,4},{7,5},{8,10},{9,11},{10,... | collective-permute-start | bytes 1179656 | tf_op jit(solution)/shard_map/ppermute | solution.py:42
  124.3 32.4 %collective-permute-start.19 = (bf16[128,1536]{1,0:T(8,128)(2,1)S(1)}, bf16[128,1536]{1,0:T(8,128)(2,1)S(1)}, u32[]{:S(2)}, u32[]{:S(2)}) collective-permute-start(bf16[128,1536]{1,0:T(8,128)(2,1)S(1)} %bitcast.80), channel_id=1, source_target_pairs={{0,1},{1,2},{2,3},{3,0},{4,5},{5,6},{6,7},{7,4},{8,9},{9,10},{10,1... | collective-permute-start | bytes 1179656 | tf_op jit(solution)/shard_map/ppermute | solution.py:42
  179.9 84.5 %all-to-all-start.2 = ((bf16[32,48,1664]{2,1,0:T(8,128)(2,1)}), bf16[32,48,1664]{2,1,0:T(8,128)(2,1)}, u32[]{:S(2)}, u32[]{:S(2)}) async-start(bf16[32,48,1664]{2,1,0:T(8,128)(2,1)} %bitcast.59), calls=%async_computation.2 | async-start | bytes 10223616 | tf_op jit(solution)/shard_map/all_to_all | solution.py:785
  197.5 36.7 %collective-permute-start.20 = (bf16[2,1536,128]{2,1,0:T(8,128)(2,1)}, bf16[2,1536,128]{2,1,0:T(8,128)(2,1)S(1)}, u32[]{:S(2)}, u32[]{:S(2)}) collective-permute-start(bf16[2,1536,128]{2,1,0:T(8,128)(2,1)} %get-tuple-element.129), channel_id=1, source_target_pairs={{0,1},{1,2},{2,3},{3,0},{4,5},{5,6},{6,7},{7,4},{8,9},{9,10},{10,1... | collective-permute-start | bytes 2359304 | tf_op jit(solution)/shard_map/ppermute | solution.py:46
  197.5 49.6 %collective-permute-start.22 = (bf16[2,1536,128]{2,1,0:T(8,128)(2,1)}, bf16[2,1536,128]{2,1,0:T(8,128)(2,1)S(1)}, u32[]{:S(2)}, u32[]{:S(2)}) collective-permute-start(bf16[2,1536,128]{2,1,0:T(8,128)(2,1)} %get-tuple-element.135), channel_id=1, source_target_pairs={{0,2},{1,3},{2,0},{3,1},{4,6},{5,7},{6,4},{7,5},{8,10},{9,11},{10,... | collective-permute-start | bytes 2359304 | tf_op jit(solution)/shard_map/ppermute | solution.py:46
  199.1 48.0 %collective-permute-start.24 = (bf16[2,1536,128]{2,1,0:T(8,128)(2,1)}, bf16[2,1536,128]{2,1,0:T(8,128)(2,1)S(1)}, u32[]{:S(2)}, u32[]{:S(2)}) collective-permute-start(bf16[2,1536,128]{2,1,0:T(8,128)(2,1)} %get-tuple-element.137), channel_id=1, source_target_pairs={{0,3},{1,0},{2,1},{3,2},{4,7},{5,4},{6,5},{7,6},{8,11},{9,8},{10,9... | collective-permute-start | bytes 2359304 | tf_op jit(solution)/shard_map/ppermute | solution.py:46
  244.4 19.8 %collective-permute-start.21 = (bf16[128,1536]{1,0:T(8,128)(2,1)}, bf16[128,1536]{1,0:T(8,128)(2,1)S(1)}, u32[]{:S(2)}, u32[]{:S(2)}) collective-permute-start(bf16[128,1536]{1,0:T(8,128)(2,1)} %get-tuple-element.134), channel_id=1, source_target_pairs={{0,1},{1,2},{2,3},{3,0},{4,5},{5,6},{6,7},{7,4},{8,9},{9,10},{10,1... | collective-permute-start | bytes 1179656 | tf_op jit(solution)/shard_map/ppermute | solution.py:46
  244.4 19.8 %collective-permute-start.23 = (bf16[128,1536]{1,0:T(8,128)(2,1)}, bf16[128,1536]{1,0:T(8,128)(2,1)S(1)}, u32[]{:S(2)}, u32[]{:S(2)}) collective-permute-start(bf16[128,1536]{1,0:T(8,128)(2,1)} %get-tuple-element.136), channel_id=1, source_target_pairs={{0,2},{1,3},{2,0},{3,1},{4,6},{5,7},{6,4},{7,5},{8,10},{9,11},{10,... | collective-permute-start | bytes 1179656 | tf_op jit(solution)/shard_map/ppermute | solution.py:46
  244.5 19.8 %collective-permute-start.25 = (bf16[128,1536]{1,0:T(8,128)(2,1)}, bf16[128,1536]{1,0:T(8,128)(2,1)}, u32[]{:S(2)}, u32[]{:S(2)}) collective-permute-start(bf16[128,1536]{1,0:T(8,128)(2,1)} %get-tuple-element.138), channel_id=1, source_target_pairs={{0,3},{1,0},{2,1},{3,2},{4,7},{5,4},{6,5},{7,6},{8,11},{9,8},{10,9... | collective-permute-start | bytes 1179656 | tf_op jit(solution)/shard_map/ppermute | solution.py:46
  264.3 67.5 %all-to-all-start.3 = ((bf16[32,48,1536]{2,1,0:T(8,128)(2,1)}), bf16[32,48,1536]{2,1,0:T(8,128)(2,1)}, u32[]{:S(2)}, u32[]{:S(2)}) async-start(bf16[32,48,1536]{2,1,0:T(8,128)(2,1)} %bitcast.60), calls=%async_computation.3 | async-start | bytes 9437184 | tf_op jit(solution)/shard_map/all_to_all | solution.py:797
  279.9 11.0 %collective-permute-start.26 = (bf16[128,1536]{1,0:T(8,128)(2,1)}, bf16[128,1536]{1,0:T(8,128)(2,1)}, u32[]{:S(2)}, u32[]{:S(2)}) collective-permute-start(bf16[128,1536]{1,0:T(8,128)(2,1)} %get-tuple-element.152.refs_0_), channel_id=1, source_target_pairs={{0,3},{1,0},{2,1},{3,2},{4,7},{5,4},{6,5},{7,6},{8,11},{9,8},{10,9... | collective-permute-start | bytes 1179656 | tf_op jit(solution)/shard_map/ppermute | solution.py:42
  282.0 12.0 %collective-permute-start.27 = (bf16[128,1536]{1,0:T(8,128)(2,1)}, bf16[128,1536]{1,0:T(8,128)(2,1)}, u32[]{:S(2)}, u32[]{:S(2)}) collective-permute-start(bf16[128,1536]{1,0:T(8,128)(2,1)} %get-tuple-element.152.refs_0_), channel_id=1, source_target_pairs={{0,2},{1,3},{2,0},{3,1},{4,6},{5,7},{6,4},{7,5},{8,10},{9,11},{10,... | collective-permute-start | bytes 1179656 | tf_op jit(solution)/shard_map/ppermute | solution.py:42
  282.0 21.1 %collective-permute-start.28 = (bf16[128,1536]{1,0:T(8,128)(2,1)}, bf16[128,1536]{1,0:T(8,128)(2,1)}, u32[]{:S(2)}, u32[]{:S(2)}) collective-permute-start(bf16[128,1536]{1,0:T(8,128)(2,1)} %get-tuple-element.152.refs_0_), channel_id=1, source_target_pairs={{0,1},{1,2},{2,3},{3,0},{4,5},{5,6},{6,7},{7,4},{8,9},{9,10},{10,1... | collective-permute-start | bytes 1179656 | tf_op jit(solution)/shard_map/ppermute | solution.py:42
  322.4 4.2 %collective-permute-start.29 = (bf16[16,6,24,384]{3,2,1,0:T(8,128)(2,1)}, bf16[16,6,24,384]{3,2,1,0:T(8,128)(2,1)S(1)}, u32[]{:S(2)}, u32[]{:S(2)}) collective-permute-start(bf16[16,6,24,384]{3,2,1,0:T(8,128)(2,1)} %get-tuple-element.165), channel_id=1, source_target_pairs={{0,4},{4,0},{8,12},{12,8},{16,20},{20,16},{24,28},{28,24},{32,36},... | collective-permute-start | bytes 5308424 | tf_op jit(solution)/shard_map/ppermute | solution.py:50
  331.9 29.1 %all-to-all-start.4 = ((bf16[16,6,24,384]{3,2,1,0:T(8,128)(2,1)}), bf16[16,6,24,384]{3,2,1,0:T(8,128)(2,1)S(1)}, u32[]{:S(2)}, u32[]{:S(2)}) async-start(bf16[16,6,24,384]{3,2,1,0:T(8,128)(2,1)} %add_convert_fusion), calls=%async_computation.4 | async-start | bytes 3538944 | tf_op jit(solution)/shard_map/all_to_all | solution.py:55
  338.6 10.9 %collective-permute-start.30 = (bf16[128,1536]{1,0:T(8,128)(2,1)}, bf16[128,1536]{1,0:T(8,128)(2,1)S(1)}, u32[]{:S(2)}, u32[]{:S(2)}) collective-permute-start(bf16[128,1536]{1,0:T(8,128)(2,1)} %get-tuple-element.171), channel_id=1, source_target_pairs={{0,1},{1,2},{2,3},{3,0},{4,5},{5,6},{6,7},{7,4},{8,9},{9,10},{10,1... | collective-permute-start | bytes 1179656 | tf_op jit(solution)/shard_map/ppermute | solution.py:46
  338.7 19.9 %collective-permute-start.31 = (bf16[128,1536]{1,0:T(8,128)(2,1)}, bf16[128,1536]{1,0:T(8,128)(2,1)S(1)}, u32[]{:S(2)}, u32[]{:S(2)}) collective-permute-start(bf16[128,1536]{1,0:T(8,128)(2,1)} %get-tuple-element.172), channel_id=1, source_target_pairs={{0,2},{1,3},{2,0},{3,1},{4,6},{5,7},{6,4},{7,5},{8,10},{9,11},{10,... | collective-permute-start | bytes 1179656 | tf_op jit(solution)/shard_map/ppermute | solution.py:46
  341.9 17.2 %collective-permute-start.32 = (bf16[128,1536]{1,0:T(8,128)(2,1)S(1)}, bf16[128,1536]{1,0:T(8,128)(2,1)S(1)}, u32[]{:S(2)}, u32[]{:S(2)}) collective-permute-start(bf16[128,1536]{1,0:T(8,128)(2,1)S(1)} %copy-done.24), channel_id=1, source_target_pairs={{0,3},{1,0},{2,1},{3,2},{4,7},{5,4},{6,5},{7,6},{8,11},{9,8},{10,9... | collective-permute-start | bytes 1179656 | tf_op jit(solution)/shard_map/ppermute | solution.py:46
  361.2 3.0 collective-permute-start.33
  363.3 4.1 collective-permute-start.34
  363.3 4.1 %collective-permute-start.35 = (bf16[24,384]{1,0:T(8,128)(2,1)S(1)}, bf16[24,384]{1,0:T(8,128)(2,1)S(1)}, u32[]{:S(2)}, u32[]{:S(2)}) collective-permute-start(bf16[24,384]{1,0:T(8,128)(2,1)S(1)} %get-tuple-element.196), channel_id=1, source_target_pairs={{0,1},{1,2},{2,3},{3,0},{4,5},{5,6},{6,7},{7,4},{8,9},{9,10},{10,1... | collective-permute-start | bytes 55304 | tf_op jit(solution)/shard_map/ppermute | solution.py:42
  367.6 32.8 %copy-start.3 = (bf16[128,1536]{1,0:T(8,128)(2,1)S(1)}, bf16[128,1536]{1,0:T(8,128)(2,1)}, u32[]{:S(2)}) copy-start(bf16[128,1536]{1,0:T(8,128)(2,1)} %refs_4_.1) | copy-start | bytes 1179652
  367.7 32.8 %copy-start.4 = (f32[128,1536]{1,0:T(8,128)S(1)}, f32[128,1536]{1,0:T(8,128)}, u32[]{:S(2)}) copy-start(f32[128,1536]{1,0:T(8,128)} %get-tuple-element.176) | copy-start | bytes 2359300
  394.8 8.1 %collective-permute-start.36 = (bf16[16,6,24,384]{3,2,1,0:T(8,128)(2,1)S(1)}, bf16[16,6,24,384]{3,2,1,0:T(8,128)(2,1)S(1)}, u32[]{:S(2)}, u32[]{:S(2)}) collective-permute-start(bf16[16,6,24,384]{3,2,1,0:T(8,128)(2,1)S(1)} %all_to_all.30.a_ref.ao_ref), channel_id=1, source_target_pairs={{0,4},{4,0},{8,12},{12,8},{16,20},{20,16},{24,28},{28,24},{32,36},... | collective-permute-start | bytes 5308424 | tf_op jit(solution)/shard_map/ppermute | solution.py:50
  (31 other events, 158.8 us)
